TPU v7x, 128 devices: a whole 4x4x4 slice. The times are simulated.
128 devices in a mesh: dp: 32 (over x, y, z_hi), ctx: 4 (over z_lo, core).
Axes of the slice: x: 4, y: 4, z: 4 (z_hi: 2, z_lo: 2; z = z_hi * 2 + z_lo), core: 2. Of those that a mesh axis runs over, the one named last changes fastest.
Arguments:
- tokens: bfloat16 [32768, 4096], P(('dp', 'ctx')), may hold values from -28 to 28
- projection: bfloat16 [4096, 3072], P('dp'), may hold values from -0.09375 to 0.09375
- placement: int32 [128, 128], P(('dp', 'ctx')), may hold values from 0 to 127, each once within a row
- doc_lengths: int32 [32, 8], P('dp'), may hold values from 1 to 512, 1024 in all within a row
Outputs:
- attended: bfloat16 [32768, 2048], P(('dp', 'ctx'))
Inputs may be any that keep to these rules, and one draw needn't show every extreme that they name: `placement`: row i lists for each of the 2-row pieces of loader block i the device that computes it; every device appears once in each row. `doc_lengths`: each row holds the documents of one packed sequence of 1024 tokens in order, one of exactly 512 tokens.
All inputs are finite; a program needn't handle non-finite values.
Results may differ from a plain program's by a relative error of at most 0.006.
The roundings to bfloat16 on the way count: a program that leaves them out, or rounds other values in their place, can miss the bound.
Values may be sent and summed in bfloat16 or wider, within the bound.
No kernel may reach another device: no remote copies, remote signals or barrier semaphores. Data moves between devices by JAX's collectives and lax.ppermute only.
A program may use at most 128 MiB of HBM per device.

v0:
```python
import jax
import jax.numpy as jnp
from jax import lax
from jax.sharding import PartitionSpec as P

HEAD_DIM = 128
HEADS = 16
KV_HEADS = 4


theta_base = 500000.0


def doc_tables(lengths, position):
    doc_ends = jnp.cumsum(lengths)
    doc_starts = doc_ends - lengths
    segment = jnp.sum((position[:, None] >= doc_ends[None, :]).astype(jnp.int32), axis=1)
    one_hot = segment[:, None] == jnp.arange(lengths.shape[0], dtype=jnp.int32)[None, :]
    begins = jnp.sum(jnp.where(one_hot, doc_starts[None, :], 0), axis=1)
    return (segment, position - begins)


def rotate(values, offsets, head_count):
    row_count = values.shape[0]
    half_dim = HEAD_DIM // 2
    frequency = theta_base ** (-2.0 * jnp.arange(half_dim, dtype=jnp.float32) / HEAD_DIM)
    angles = offsets.astype(jnp.float32)[:, None] * frequency[None, :]
    cosine = jnp.cos(angles)[:, None, :]
    sine = jnp.sin(angles)[:, None, :]
    halves = values.astype(jnp.float32).reshape(row_count, head_count, 2, half_dim)
    former = halves[:, :, 0]
    latter = halves[:, :, 1]
    result = jnp.stack([former * cosine - latter * sine, latter * cosine + former * sine], axis=2)
    return result.reshape(row_count, head_count * HEAD_DIM).astype(jnp.bfloat16)


def on_device(tokens, projection, placement, doc_lengths):
    row_count = tokens.shape[0]
    dev_count = placement.shape[1]
    piece_rows = row_count // dev_count
    destinations = placement[0]
    slot_of = (
        jnp.zeros((dev_count,), jnp.int32)
        .at[destinations]
        .set(jnp.arange(dev_count, dtype=jnp.int32))
    )
    outgoing = tokens.reshape(dev_count, piece_rows, tokens.shape[1])[slot_of]
    arrived = lax.all_to_all(
        outgoing, ("dp", "ctx"), split_axis=0, concat_axis=0, tiled=True
    ).reshape(row_count, tokens.shape[1])
    summed = jnp.dot(
        arrived,
        lax.all_gather(projection, "dp", axis=0, tiled=True),
        preferred_element_type=jnp.float32,
    )
    projected = summed.astype(jnp.bfloat16)
    lengths = doc_lengths[0]
    position = lax.axis_index("ctx") * row_count + jnp.arange(row_count, dtype=jnp.int32)
    segment, offsets = doc_tables(lengths, position)
    query_width = HEADS * HEAD_DIM
    key_width = KV_HEADS * HEAD_DIM
    queries = rotate(projected[:, :query_width], offsets, HEADS)
    key_rows = rotate(projected[:, query_width : query_width + key_width], offsets, KV_HEADS)
    value_rows = projected[:, query_width + key_width :]
    group_size = HEADS // KV_HEADS
    query_major = jnp.transpose(
        queries.reshape(row_count, KV_HEADS, group_size, HEAD_DIM), (1, 0, 2, 3)
    )
    score_scale = HEAD_DIM ** (-0.5)
    key_block = lax.all_gather(key_rows, "ctx", axis=0, tiled=True)
    value_block = lax.all_gather(value_rows, "ctx", axis=0, tiled=True)
    key_count = key_block.shape[0]
    key_index = jnp.arange(key_count, dtype=jnp.int32)
    key_segment, unused = doc_tables(lengths, key_index)
    allowed = (segment[:, None] == key_segment[None, :]) & (key_index[None, :] <= position[:, None])
    key_major = jnp.transpose(key_block.reshape(key_count, KV_HEADS, HEAD_DIM), (1, 0, 2))
    value_major = jnp.transpose(value_block.reshape(key_count, KV_HEADS, HEAD_DIM), (1, 0, 2))

    def per_head(inputs):
        query_head, key_head, value_head, row_max, row_sum, weighted = inputs
        scores = (
            jnp.einsum("tgd,sd->tgs", query_head, key_head, preferred_element_type=jnp.float32)
            * score_scale
        )
        scores = jnp.where(allowed[:, None, :], scores, -jnp.inf)
        new_max = jnp.maximum(row_max, jnp.max(scores, axis=-1))
        factor = jnp.exp(row_max - new_max)
        weights = jnp.exp(scores - new_max[..., None])
        row_sum = row_sum * factor + jnp.sum(weights, axis=-1)
        weighted = weighted * factor[..., None] + jnp.einsum(
            "tgs,sd->tgd",
            weights.astype(jnp.bfloat16),
            value_head,
            preferred_element_type=jnp.float32,
        )
        return (new_max, row_sum, weighted)

    row_max = jnp.full((KV_HEADS, row_count, group_size), -1e30, jnp.float32)
    row_sum = jnp.zeros((KV_HEADS, row_count, group_size), jnp.float32)
    weighted = jnp.zeros((KV_HEADS, row_count, group_size, HEAD_DIM), jnp.float32)
    row_max, row_sum, weighted = lax.map(
        per_head, (query_major, key_major, value_major, row_max, row_sum, weighted)
    )
    mixed = (
        jnp.transpose(weighted / row_sum[..., None], (1, 0, 2, 3))
        .reshape(row_count, query_width)
        .astype(jnp.bfloat16)
    )
    returned = lax.all_to_all(
        mixed.reshape(dev_count, piece_rows, query_width),
        ("dp", "ctx"),
        split_axis=0,
        concat_axis=0,
        tiled=True,
    )
    return returned[destinations].reshape(row_count, query_width)


def solution(mesh):
    return jax.shard_map(
        on_device,
        mesh=mesh,
        in_specs=(P(("dp", "ctx"), None), P("dp", None), P(("dp", "ctx"), None), P("dp", None)),
        out_specs=P(("dp", "ctx"), None),
        check_vma=False,
    )
```

profile of v0, /device:TPU:1, one launch (start us, length us, event | category | flops | bytes accessed | tf_op | source)
XLA Modules:
  0.0 361.6 jit_solution(6989466363896268674)
XLA Ops:
  6.5 0.0 all-gather.4.cloned.1.call-start
  6.5 0.7 all-gather.4.cloned.1.call-update
  7.3 0.0 all-gather.8.cloned.1.call-start
  7.3 0.0 copy-start.1
  7.3 3.2 reshape.179
  10.5 0.0 copy-done.1
  10.5 1.0 scatter_custom_fusion
  11.5 8.0 %gather_fusion = bf16[128,2,4096]{2,1,0:T(2,128)(2,1)} fusion(bf16[128,2,4096]{2,1,0:T(2,128)(2,1)S(1)} %reshape.179, s32[1024]{0:T(1024)S(1)} %pad_clamp_fusion.1), kind=kCustom, calls=%fused_computation | custom fusion | bytes 4194816 | tf_op jit(solution)/shard_map/gather | solution.py:47
  19.5 46.0 %all_to_all.10 = bf16[128,2,4096]{2,1,0:T(2,128)(2,1)S(1)} all-to-all(bf16[128,2,4096]{2,1,0:T(2,128)(2,1)} %gather_fusion), channel_id=1, replica_groups=mesh['dp'=32,'ctx'=4] {'dp','ctx'}, dimensions={0} | all-to-all | bytes 4194304 | tf_op jit(solution)/shard_map/all_to_all | solution.py:48
  65.5 2.2 reshape.180
  67.7 0.0 copy-start.2
  67.8 173.6 %all-gather.4.cloned.1.call-done = bf16[4096,3072]{1,0:T(8,128)(2,1)} async-done(((bf16[128,3072]{1,0:T(8,128)(2,1)}), bf16[4096,3072]{1,0:T(8,128)(2,1)}) %all-gather.4.cloned.1.call-update) | async-done | bytes 25165840 | tf_op jit(solution)/shard_map/all_gather | solution.py:53
  241.4 12.2 %convolution_convert_fusion = bf16[256,3072]{1,0:T(8,128)(2,1)S(1)} fusion(bf16[256,4096]{1,0:T(8,128)(2,1)} %reshape.180, bf16[4096,3072]{1,0:T(8,128)(2,1)} %all-gather.4.cloned.1.call-done), kind=kOutput, calls=%fused_computation.30 | convolution fusion | flops 6443237376 | bytes 28835840 | tf_op jit(solution)/shard_map/dot_general | solution.py:51
  253.6 0.8 fusion.34
  254.3 0.0 all-gather.8.cloned.1.call-update
  254.3 0.2 all-gather.6.cloned.1.call-start
  254.6 0.0 copy-done.2
  254.6 0.2 reduce-window.4
  254.8 0.1 convert_reduce_fusion.1
  254.9 0.1 select_reduce_fusion
  255.0 0.3 multiply_cosine_fusion
  255.3 0.2 copy.14
  255.5 0.1 subtract_convert_fusion.1
  255.6 0.7 pad_maximum_fusion.1
  256.3 0.0 all-gather.6.cloned.1.call-update
  256.4 0.1 convert_reduce_fusion
  256.4 1.5 slice_convert_fusion
  258.0 1.9 copy.13
  259.9 0.3 subtract_convert_fusion
  260.2 0.0 copy-start
  260.2 0.1 pad_maximum_fusion
  260.4 13.4 %all-gather.8.cloned.1.call-done = bf16[1024,512]{1,0:T(8,128)(2,1)} async-done(((bf16[256,512]{1,0:T(8,128)(2,1)}), bf16[1024,512]{1,0:T(8,128)(2,1)}) %all-gather.8.cloned.1.call-update) | async-done | bytes 1048592 | tf_op jit(solution)/shard_map/all_gather | solution.py:71
  273.7 2.4 bitcast_bitcast_fusion
  276.1 20.8 %all-gather.6.cloned.1.call-done = bf16[1024,512]{0,1:T(8,128)(2,1)} async-done(((bf16[256,512]{0,1:T(8,128)(2,1)}), bf16[1024,512]{0,1:T(8,128)(2,1)}) %all-gather.6.cloned.1.call-update) | async-done | bytes 1048592 | tf_op jit(solution)/shard_map/all_gather | solution.py:70
  296.9 0.0 copy-done
  296.9 22.9 %while.13 = (s32[]{:T(128)}, f32[4,256,4]{1,2,0:T(4,128)S(1)}, f32[4,256,4,128]{3,1,2,0:T(8,128)S(1)}, bf16[4,256,4,128]{1,3,2,0:T(8,128)(2,1)S(1)}, bf16[4,1024...) while((s32[]{:T(128)}, f32[4,256,4]{1,2,0:T(4,128)S(1)}, ...), condition=%wide.region_8.9_spmd.clone, body=%wide.region_5.8_spmd.clone.sunk | while | flops 549327872 | bytes 14995561 | solution.py:101
  296.9 0.4 fusion.46
  297.3 1.9 fusion.47
  299.2 2.2 fusion.49
  301.4 1.2 fusion.48
  302.6 0.4 fusion.46
  303.0 1.9 fusion.47
  304.9 2.2 fusion.49
  307.1 1.2 fusion.48
  308.4 0.4 fusion.46
  308.7 1.9 fusion.47
  310.6 2.2 fusion.49
  312.8 1.2 fusion.48
  314.1 0.4 fusion.46
  314.5 1.9 fusion.47
  316.4 2.2 fusion.49
  318.6 1.2 fusion.48
  319.8 0.7 fusion.29
  320.5 0.8 copy.18
  321.4 1.1 convert_element_type.49
  322.5 9.5 %all-to-all-start.1 = ((bf16[128,2,2048]{2,1,0:T(2,128)(2,1)}), bf16[128,2,2048]{2,1,0:T(2,128)(2,1)S(1)}, u32[]{:S(2)}, u32[]{:S(2)}) async-start(bf16[128,2,2048]{2,1,0:T(2,128)(2,1)} %convert_element_type.49), calls=%async_computation.1 | async-start | bytes 2097152 | tf_op jit(solution)/shard_map/all_to_all | solution.py:109
  331.9 19.3 %all-to-all-done.1 = bf16[128,2,2048]{2,1,0:T(2,128)(2,1)S(1)} async-done(((bf16[128,2,2048]{2,1,0:T(2,128)(2,1)}), bf16[128,2,2048]{2,1,0:T(2,128)(2,1)S(1)}, u32[]{:S(2)}, u32[]{:S(2)}) %all-to-all-start.1) | async-done | bytes 1048608 | tf_op jit(solution)/shard_map/all_to_all | solution.py:109
  351.2 2.7 gather_fusion.1
  353.9 1.2 reshape.188
  (19 shorter events, 0.2 us)
Async XLA Ops:
  6.5 234.8 %all-gather.4.cloned.1.call-start = ((), (), s32[]{:S(2)}) async-start(), calls=%async_computation.2 | async-start | bytes 25952256 | tf_op jit(solution)/shard_map/all_gather | solution.py:53
  7.3 266.5 %all-gather.8.cloned.1.call-start = ((), (), s32[]{:S(2)}) async-start(), calls=%async_computation.4 | async-start | bytes 1310720 | tf_op jit(solution)/shard_map/all_gather | solution.py:71
  7.3 3.2 copy-start.1
  67.7 186.8 %copy-start.2 = (s32[1,8]{1,0:T(1,128)S(1)}, s32[1,8]{1,0:T(1,128)}, u32[]{:S(2)}) copy-start(s32[1,8]{1,0:T(1,128)} %param.9) | copy-start | bytes 100
  254.3 42.6 %all-gather.6.cloned.1.call-start = ((), (), s32[]{:S(2)}) async-start(), calls=%async_computation.3 | async-start | bytes 1310720 | tf_op jit(solution)/shard_map/all_gather | solution.py:70
  260.2 36.7 %copy-start = (f32[4,256,4,128]{3,1,2,0:T(8,128)S(1)}, f32[4,256,4,128]{3,1,2,0:T(8,128)}, u32[]{:S(2)}) copy-start(f32[4,256,4,128]{3,1,2,0:T(8,128)} %custom-call.5) | copy-start | bytes 6291460
  322.5 28.7 %all-to-all-start.1 = ((bf16[128,2,2048]{2,1,0:T(2,128)(2,1)}), bf16[128,2,2048]{2,1,0:T(2,128)(2,1)S(1)}, u32[]{:S(2)}, u32[]{:S(2)}) async-start(bf16[128,2,2048]{2,1,0:T(2,128)(2,1)} %convert_element_type.49), calls=%async_computation.1 | async-start | bytes 2097152 | tf_op jit(solution)/shard_map/all_to_all | solution.py:109
Sparse Core Ops, SparseCore 0:
  10.3 231.0 all-gather.3
  254.5 19.2 all-gather.7
  275.4 21.4 all-gather.5
where the time goes:
time: 362 us
  waiting for transfers between devices  228 us (63%)
  blocking collectives  46 us (13%)
  matrix products  28.5 us (8%)
  local copies, waits for them, and re-layouts  24.7 us (7%)
  between operations  13.3 us (4%)
  other arithmetic  11.5 us (3%)
  starting transfers between devices  9.72 us (3%)
    all_gather x1, waiting for transfers between devices, on_device(): lax.all_gather(projection, 'dp', axis=0, tiled=True)  174 us
    all_to_all x1, blocking collectives, on_device(): lax.all_to_all(outgoing, ('dp', 'ctx'), split_axis=0, concat_axis=0, tile...  46 us
    all_gather x1, waiting for transfers between devices, on_device(): key_block = lax.all_gather(key_rows, 'ctx', axis=0, tiled=True)  20.8 us
    all_to_all x1, waiting for transfers between devices, on_device(): lax.all_to_all(mixed.reshape(dev_count, piece_rows, query_width), ('dp',...  19.3 us
    all_gather x1, waiting for transfers between devices, on_device(): value_block = lax.all_gather(value_rows, 'ctx', axis=0, tiled=True)  13.4 us
    dot_general x1, matrix products, on_device(): jnp.dot(arrived, lax.all_gather(projection, 'dp', axis=0, tiled=True), pr...  12.2 us
    all_to_all x1, starting transfers between devices, on_device(): lax.all_to_all(mixed.reshape(dev_count, piece_rows, query_width), ('dp',...  9.45 us
    dot_general x4, matrix products, per_head(): jnp.einsum('tgs,sd->tgd', weights.astype(jnp.bfloat16), value_head, prefe...  8.74 us
  transfers between devices with their start and end apart: 4, of which 4 were waited for; matrix products, arithmetic and copies ran while one was open for 6% of the time, Pallas kernels for 0%

commit v1 on v0

v1 whole, which is shorter than its diff:
```python
import functools

import jax
import jax.numpy as jnp
from jax import lax
from jax.experimental import pallas as pl
from jax.experimental.pallas import tpu as pltpu
from jax.sharding import Mesh, PartitionSpec as P

HEAD_DIM = 128
HEADS = 16
KV_HEADS = 4
GROUP = HEADS // KV_HEADS
THETA = 500000.0
MOST = 512
DP = ("x", "y", "zh")
CTX = ("zl", "core")
EVERY = DP + CTX
BLOCK = 256


def frequencies():
    half = HEAD_DIM // 2
    return THETA ** (-2.0 * jnp.arange(half, dtype=jnp.float32) / HEAD_DIM)


def rotary_tables(lengths, count):
    position = jnp.arange(count, dtype=jnp.int32)
    ends = jnp.cumsum(lengths)
    begins = jnp.sum(jnp.where(position[:, None] >= ends[None, :], lengths[None, :], 0), axis=1)
    angles = (position - begins).astype(jnp.float32)[:, None] * frequencies()[None, :]
    cosine, sine = jnp.cos(angles), jnp.sin(angles)
    return jnp.concatenate([cosine, cosine], axis=1), jnp.concatenate([-sine, sine], axis=1)


def sort_kernel(target_ref, rows_ref, out_ref):
    count = rows_ref.shape[0]
    order = lax.broadcasted_iota(jnp.int32, (count, count), 0)
    one_hot = jnp.where(order == target_ref[...], 1.0, 0.0).astype(jnp.bfloat16)
    moved = jnp.dot(one_hot, rows_ref[...], preferred_element_type=jnp.float32).astype(jnp.bfloat16)
    groups, copies, rows, width = out_ref.shape
    for copy in range(copies):
        out_ref[:, copy] = moved.reshape(groups, rows, width)


def sort_rows(tokens, target, groups, copies):
    count, width = tokens.shape
    rows = count // groups
    tile = 1024
    return pl.pallas_call(
        sort_kernel,
        out_shape=jax.ShapeDtypeStruct((groups, copies, rows, width), tokens.dtype),
        grid=(width // tile,),
        in_specs=[
            pl.BlockSpec((1, count), lambda i: (0, 0)),
            pl.BlockSpec((count, tile), lambda i: (0, i)),
        ],
        out_specs=pl.BlockSpec((groups, copies, rows, tile), lambda i: (0, 0, 0, i)),
        compiler_params=pltpu.CompilerParams(vmem_limit_bytes=32 * 2**20),
        name="sort_rows",
    )(target.reshape(1, count), tokens)


def unsort_kernel(target_ref, rows_ref, out_ref):
    count = out_ref.shape[0]
    order = lax.broadcasted_iota(jnp.int32, (count, count), 1)
    one_hot = jnp.where(order == target_ref[...], 1.0, 0.0).astype(jnp.bfloat16)
    rows = rows_ref[...].reshape(count, out_ref.shape[1])
    out_ref[...] = jnp.dot(one_hot, rows, preferred_element_type=jnp.float32).astype(jnp.bfloat16)


def unsort_rows(returned, target):
    groups, blocks, rows, width = returned.shape
    count = groups * rows
    return pl.pallas_call(
        unsort_kernel,
        out_shape=jax.ShapeDtypeStruct((count, blocks * width), returned.dtype),
        grid=(blocks,),
        in_specs=[
            pl.BlockSpec((count, 1), lambda i: (0, 0)),
            pl.BlockSpec((groups, None, rows, width), lambda i: (0, i, 0, 0)),
        ],
        out_specs=pl.BlockSpec((count, width), lambda i: (0, i)),
        compiler_params=pltpu.CompilerParams(vmem_limit_bytes=32 * 2**20),
        name="unsort_rows",
    )(target.reshape(count, 1), returned)


def attention_kernel(core_ref, lengths_ref, own_ref, other_ref, cos_ref, sin_ref, out_ref, queries, keys, values, mixed):
    count = cos_ref.shape[0]
    blocks = count // BLOCK
    part = BLOCK // blocks
    half = HEAD_DIM // 2
    core = core_ref[0]

    taken = lax.broadcasted_iota(jnp.int32, (BLOCK, BLOCK), 1)
    lane, rest = taken // (BLOCK // 2), taken % (BLOCK // 2)
    pair, slot, row = rest // (2 * blocks), (rest // 2) % blocks, rest % 2
    placed = slot * part + (pair * 2 + jnp.where(core == 0, lane, 1 - lane)) * 2 + row
    wanted = lax.broadcasted_iota(jnp.int32, (BLOCK, BLOCK), 0)
    forward = jnp.where(wanted == placed, 1.0, 0.0).astype(jnp.bfloat16)
    for h in range(blocks):
        span = slice(h * BLOCK // 2, (h + 1) * BLOCK // 2)
        chunk = jnp.concatenate([own_ref[span], other_ref[span]], axis=0)
        chunk = jnp.dot(forward, chunk, preferred_element_type=jnp.float32)
        for s in range(blocks):
            rows = slice(s * BLOCK + h * part, s * BLOCK + (h + 1) * part)
            here = chunk[s * part : (s + 1) * part]
            cosine, sine = cos_ref[rows], sin_ref[rows]

            def rotate(x):
                return (x * cosine + pltpu.roll(x, half, 1) * sine).astype(jnp.bfloat16)

            for g in range(GROUP):
                queries[g, rows] = rotate(here[:, g * HEAD_DIM : (g + 1) * HEAD_DIM])
            keys[rows] = rotate(here[:, GROUP * HEAD_DIM : (GROUP + 1) * HEAD_DIM])
            values[rows] = here[:, (GROUP + 1) * HEAD_DIM :].astype(jnp.bfloat16)

    scale = HEAD_DIM ** (-0.5)
    reach = (MOST - 1 + BLOCK - 1) // BLOCK
    for b in range(blocks):
        first = max(0, b - reach)
        width = (b + 1 - first) * BLOCK
        position = b * BLOCK + lax.broadcasted_iota(jnp.int32, (BLOCK, 1), 0)
        begin, end = jnp.zeros_like(position), jnp.int32(0)
        for j in range(lengths_ref.shape[1]):
            end = end + lengths_ref[0, j]
            begin = jnp.where(position >= end, end, begin)
        key_at = first * BLOCK + lax.broadcasted_iota(jnp.int32, (BLOCK, width), 1)
        allowed = (key_at >= begin) & (key_at <= position)
        key_block = keys[first * BLOCK : (b + 1) * BLOCK]
        value_block = values[first * BLOCK : (b + 1) * BLOCK]
        for g in range(GROUP):
            scores = lax.dot_general(
                queries[g, b * BLOCK : (b + 1) * BLOCK],
                key_block,
                (((1,), (1,)), ((), ())),
                preferred_element_type=jnp.float32,
            )
            scores = jnp.where(allowed, scores * scale, -1e30)
            weights = jnp.exp(scores - jnp.max(scores, axis=1, keepdims=True))
            total = jnp.sum(weights, axis=1, keepdims=True)
            weighted = jnp.dot(
                weights.astype(jnp.bfloat16), value_block, preferred_element_type=jnp.float32
            )
            mixed[b * BLOCK : (b + 1) * BLOCK, g * HEAD_DIM : (g + 1) * HEAD_DIM] = (
                weighted / total
            ).astype(jnp.bfloat16)

    left = lax.broadcasted_iota(jnp.int32, (BLOCK, BLOCK), 0)
    source = ((left // 2) % blocks) * part + (left // (2 * blocks)) * 2 + left % 2
    backward = jnp.where(taken == source, 1.0, 0.0).astype(jnp.bfloat16)
    for h in range(blocks):
        chunk = jnp.concatenate(
            [mixed[s * BLOCK + h * part : s * BLOCK + (h + 1) * part] for s in range(blocks)], axis=0
        )
        out_ref[h * BLOCK : (h + 1) * BLOCK] = jnp.dot(
            backward, chunk, preferred_element_type=jnp.float32
        ).astype(jnp.bfloat16)


def attend(core, lengths, own, other, cosine, sine):
    count = cosine.shape[0]
    whole = pl.BlockSpec(memory_space=pltpu.VMEM)
    scalars = pl.BlockSpec(memory_space=pltpu.SMEM)
    return pl.pallas_call(
        attention_kernel,
        out_shape=jax.ShapeDtypeStruct((count, GROUP * HEAD_DIM), jnp.bfloat16),
        in_specs=[scalars, scalars, whole, whole, whole, whole],
        out_specs=whole,
        scratch_shapes=[
            pltpu.VMEM((GROUP, count, HEAD_DIM), jnp.bfloat16),
            pltpu.VMEM((count, HEAD_DIM), jnp.bfloat16),
            pltpu.VMEM((count, HEAD_DIM), jnp.bfloat16),
            pltpu.VMEM((count, GROUP * HEAD_DIM), jnp.bfloat16),
        ],
        compiler_params=pltpu.CompilerParams(vmem_limit_bytes=48 * 2**20),
        name="attend",
    )(core, lengths, own, other, cosine, sine)


def on_device(tokens, projection, placement, doc_lengths):
    row_count, width = tokens.shape
    devices = placement.shape[1]
    members = lax.axis_size(CTX)
    groups = devices // members
    piece = row_count // devices
    member, core = lax.axis_index(CTX), lax.axis_index("core")

    query_width, key_width = HEADS * HEAD_DIM, KV_HEADS * HEAD_DIM
    columns = jnp.concatenate(
        [
            lax.dynamic_slice_in_dim(projection, member * GROUP * HEAD_DIM, GROUP * HEAD_DIM, 1),
            lax.dynamic_slice_in_dim(projection, query_width + member * HEAD_DIM, HEAD_DIM, 1),
            lax.dynamic_slice_in_dim(projection, query_width + key_width + member * HEAD_DIM, HEAD_DIM, 1),
        ],
        axis=1,
    )
    weights = lax.all_gather(columns, DP, axis=0, tiled=True)

    target = (placement[0][:, None] * piece + jnp.arange(piece, dtype=jnp.int32)[None, :]).reshape(row_count)
    outgoing = sort_rows(tokens, target, groups, 2)
    arrived = lax.all_to_all(
        outgoing.reshape(groups * 2, row_count // groups, width), DP + ("zl",), 0, 0, tiled=True
    )
    own_rows = arrived.reshape(2 * row_count, width)
    other_rows = lax.ppermute(own_rows, "core", [(0, 1), (1, 0)])
    own = jnp.dot(own_rows, weights, preferred_element_type=jnp.float32).astype(jnp.bfloat16)
    other = jnp.dot(other_rows, weights, preferred_element_type=jnp.float32).astype(jnp.bfloat16)
    cosine, sine = rotary_tables(doc_lengths[0], members * row_count)
    mixed = attend(core.reshape(1), doc_lengths, own, other, cosine, sine)
    returned = lax.all_to_all(
        mixed.reshape(devices, members * piece, GROUP * HEAD_DIM), EVERY, 0, 0, tiled=True
    )
    return unsort_rows(returned.reshape(groups, members, members * piece, GROUP * HEAD_DIM), target)


def solution(mesh):
    sizes = {"x": 4, "y": 4, "zh": 2, "zl": 2, "core": 2}
    fine = Mesh(mesh.devices.reshape(tuple(sizes.values())), tuple(sizes))
    return jax.shard_map(
        on_device,
        mesh=fine,
        in_specs=(P(EVERY, None), P(DP, None), P(EVERY, None), P(DP, None)),
        out_specs=P(EVERY, None),
        check_vma=False,
    )
```

time: 362 us -> 205 us (0.57)
  waiting for transfers between devices: 228 us -> 85.3 us
  local copies, waits for them, and re-layouts: 24.7 us -> 3.52 us
  blocking collectives: 46 us -> 64.1 us
  matrix products: 28.5 us -> 13.2 us
  Pallas kernels: 0 us -> 12.5 us
  other arithmetic: 11.5 us -> 3.95 us
    all_gather x3 -> x1, waiting for transfers between devices: 208 us -> 66.1 us  [on_device(): weights = lax.all_gather(columns, DP, axis=0, tiled=True)]
    all_to_all x1, blocking collectives: 46 us -> 64.1 us  [on_device(): lax.all_to_all(outgoing.reshape(groups * 2, row_count // groups, width),...]
    dot_general x9 -> x2, matrix products: 28.5 us -> 13.2 us  [the longest x1 7.6 us: on_device(): jnp.dot(own_rows, weights, preferred_element_type=jnp.float32)]
    pallas_call x0 -> x3, Pallas kernels: none -> 12.5 us  [the longest x1 8.6 us: attend(): pl.pallas_call(attention_kernel, out_shape=jax.ShapeDtypeStruct((count, G...]
    gather x2 -> x0, local copies, waits for them, and re-layouts: 10.6 us -> none  [the longest x1 7.97 us: on_device(): outgoing = tokens.reshape(dev_count, piece_rows, tokens.shape[1])[slot_of]]
    reshape x5 -> x0, local copies, waits for them, and re-layouts: 8.74 us -> none  [the longest x1 3.17 us: on_device(): outgoing = tokens.reshape(dev_count, piece_rows, tokens.shape[1])[slot_of]]
    reduce_sum x7 -> x1, other arithmetic: 5.13 us -> 0.08 us  [rotary_tables(): jnp.sum(jnp.where(position[:, None] >= ends[None, :], lengths[None, :], 0...]
  transfers between devices with their start and end apart: 4 -> 3, of which waited for: 4 -> 2; matrix products, arithmetic and copies ran while one was open for 6% -> 5% of each run, Pallas kernels for 0% -> 1%
where the time goes in v1:
time: 205 us
  waiting for transfers between devices  85.3 us (42%)
  blocking collectives  64.1 us (31%)
  between operations  13.5 us (7%)
  matrix products  13.2 us (6%)
  Pallas kernels  12.5 us (6%)
  starting transfers between devices  9.04 us (4%)
  other arithmetic  3.95 us (2%)
  local copies, waits for them, and re-layouts  3.52 us (2%)
    all_gather x1, waiting for transfers between devices, on_device(): weights = lax.all_gather(columns, DP, axis=0, tiled=True)  66.1 us
    all_to_all x1, blocking collectives, on_device(): lax.all_to_all(outgoing.reshape(groups * 2, row_count // groups, width),...  64.1 us
    all_to_all x1, waiting for transfers between devices, on_device(): lax.all_to_all(mixed.reshape(devices, members * piece, GROUP * HEAD_DIM),...  19.2 us
    pallas_call x1, Pallas kernels, attend(): pl.pallas_call(attention_kernel, out_shape=jax.ShapeDtypeStruct((count, G...  8.6 us
    dot_general x1, matrix products, on_device(): jnp.dot(own_rows, weights, preferred_element_type=jnp.float32)  7.6 us
    all_to_all x1, starting transfers between devices, on_device(): lax.all_to_all(mixed.reshape(devices, members * piece, GROUP * HEAD_DIM),...  6.41 us
    dot_general x1, matrix products, on_device(): jnp.dot(other_rows, weights, preferred_element_type=jnp.float32)  5.59 us
  transfers between devices with their start and end apart: 3, of which 2 were waited for; matrix products, arithmetic and copies ran while one was open for 5% of the time, Pallas kernels for 1%

profile of v1, /device:TPU:1, one launch (start us, length us, event | category | flops | bytes accessed | tf_op | source)
XLA Modules:
  0.0 205.1 jit_solution(15272816550129006945)
XLA Ops:
  6.5 0.0 all-gather.2.cloned.1.call-start
  6.5 0.9 constant_dynamic-slice_fusion.2
  7.5 0.8 constant_dynamic-slice_fusion.1
  8.2 0.7 pad_maximum_fusion.2
  8.9 0.0 all-gather.2.cloned.1.call-update
  9.0 0.7 multiply_bitcast_fusion
  9.6 0.1 iota_add_fusion
  9.7 0.1 add.53.target_ref
  9.8 0.0 copy-start
  9.9 1.6 copy-done
  11.4 1.7 sort_rows.1
  13.1 0.0 copy-start.1
  13.1 64.1 %all_to_all.10 = bf16[64,8,4096]{2,1,0:T(8,128)(2,1)} all-to-all(bf16[64,8,4096]{2,1,0:T(8,128)(2,1)S(1)} %bitcast.15), channel_id=1, replica_groups=mesh['x'=4,'y'=4,'zh'=2,'zl'=2,'core'=2] {'x','y','zh','zl'}, dimensions={0} | all-to-all | bytes 8388608 | tf_op jit(solution)/shard_map/all_to_all | solution.py:203
  77.2 2.6 %collective-permute-start = (bf16[512,4096]{1,0:T(8,128)(2,1)}, bf16[512,4096]{1,0:T(8,128)(2,1)}, u32[]{:S(2)}, u32[]{:S(2)}) collective-permute-start(bf16[512,4096]{1,0:T(8,128)(2,1)} %bitcast.3), channel_id=1, source_target_pairs={{0,1},{1,0},{2,3},{3,2},{4,5},{5,4},{6,7},{7,6},{8,9},{9,8},{10,11... | collective-permute-start | bytes 12582920 | tf_op jit(solution)/shard_map/ppermute | solution.py:207
  79.8 0.0 copy-done.1
  79.8 0.2 reduce-window.8
  80.0 0.1 select_reduce_fusion
  80.1 1.9 fusion
  82.0 0.3 pad_maximum_fusion
  82.4 66.1 %all-gather.2.cloned.1.call-done = bf16[4096,768]{1,0:T(8,128)(2,1)} async-done(((bf16[128,768]{1,0:T(8,128)(2,1)}), bf16[4096,768]{1,0:T(8,128)(2,1)}) %all-gather.2.cloned.1.call-update) | async-done | bytes 6291472 | tf_op jit(solution)/shard_map/all_gather | solution.py:199
  148.4 0.0 copy-start.2
  148.4 7.6 %convolution_convert_fusion.1.own_ref = bf16[512,768]{1,0:T(8,128)(2,1)S(1)} fusion(bf16[4096,768]{1,0:T(8,128)(2,1)} %all-gather.2.cloned.1.call-done, bf16[64,8,4096]{2,1,0:T(8,128)(2,1)} %all_to_all.10), kind=kOutput, calls=%fused_computation.1 | convolution fusion | flops 3221618688 | bytes 11272192 | tf_op jit(solution)/shard_map/dot_general | solution.py:208
  156.0 0.0 collective-permute-done
  156.0 0.0 copy-done.2
  156.0 5.6 %convolution_convert_fusion.other_ref = bf16[512,768]{1,0:T(8,128)(2,1)S(1)} fusion(bf16[512,4096]{1,0:T(8,128)(2,1)} %collective-permute-done, bf16[4096,768]{1,0:T(8,128)(2,1)S(1)} %copy-done.2), kind=kOutput, calls=%fused_computation | convolution fusion | flops 3221618688 | bytes 11272192 | tf_op jit(solution)/shard_map/dot_general | solution.py:209
  161.6 8.6 %attend.1 = bf16[1024,512]{1,0:T(8,128)(2,1)} custom-call(s32[1]{0:T(128)} %bitcast.1.core_ref, s32[1,8]{1,0:T(1,128)S(1)} %copy-done.1, bf16[512,768]{1,0:T(8,128)(2,1)S(1)} %convolution_convert_fusion.1.own_ref, bf16[512,768]{1,0:T(8,128)(2,1)S(1)} %convolution_convert_fusion.other_ref, f32[1024,128]{1,0:T(8,128)S(1)} %get-tuple-element.10.cos_ref, ...), custom_call_target="tpu_custom_call" | custom-call | tf_op jit(solution)/shard_map/attend/pallas_call | solution.py:166
  170.2 6.4 %all-to-all-start.1 = ((bf16[128,8,512]{2,1,0:T(8,128)(2,1)}), bf16[128,8,512]{2,1,0:T(8,128)(2,1)S(1)}, u32[]{:S(2)}, u32[]{:S(2)}) async-start(bf16[128,8,512]{2,1,0:T(8,128)(2,1)} %bitcast.7), calls=%async_computation.1 | async-start | bytes 2097152 | tf_op jit(solution)/shard_map/all_to_all | solution.py:212
  176.7 0.1 add.58.target_ref
  176.8 19.2 %all-to-all-done.1 = bf16[128,8,512]{2,1,0:T(8,128)(2,1)S(1)} async-done(((bf16[128,8,512]{2,1,0:T(8,128)(2,1)}), bf16[128,8,512]{2,1,0:T(8,128)(2,1)S(1)}, u32[]{:S(2)}, u32[]{:S(2)}) %all-to-all-start.1) | async-done | bytes 1048608 | tf_op jit(solution)/shard_map/all_to_all | solution.py:212
  195.9 2.3 %unsort_rows.1 = bf16[256,2048]{1,0:T(8,128)(2,1)} custom-call(s32[256,1]{1,0:T(8,128)S(1)} %add.58.target_ref, bf16[32,4,8,512]{3,2,1,0:T(8,128)(2,1)S(1)} %bitcast.16), custom_call_target="tpu_custom_call" | custom-call | tf_op jit(solution)/shard_map/unsort_rows/pallas_call | solution.py:75
  (2 shorter events, 0.0 us)
Async XLA Ops:
  6.5 141.9 %all-gather.2.cloned.1.call-start = ((), (), s32[]{:S(2)}) async-start(), calls=%async_computation.2 | async-start | bytes 6488064 | tf_op jit(solution)/shard_map/all_gather | solution.py:199
  9.8 1.6 copy-start
  13.1 66.7 %copy-start.1 = (s32[1,8]{1,0:T(1,128)S(1)}, s32[1,8]{1,0:T(1,128)}, u32[]{:S(2)}) copy-start(s32[1,8]{1,0:T(1,128)} %lengths_ref.1) | copy-start | bytes 100
  77.2 78.8 %collective-permute-start = (bf16[512,4096]{1,0:T(8,128)(2,1)}, bf16[512,4096]{1,0:T(8,128)(2,1)}, u32[]{:S(2)}, u32[]{:S(2)}) collective-permute-start(bf16[512,4096]{1,0:T(8,128)(2,1)} %bitcast.3), channel_id=1, source_target_pairs={{0,1},{1,0},{2,3},{3,2},{4,5},{5,4},{6,7},{7,6},{8,9},{9,8},{10,11... | collective-permute-start | bytes 12582920 | tf_op jit(solution)/shard_map/ppermute | solution.py:207
  148.4 7.6 %copy-start.2 = (bf16[4096,768]{1,0:T(8,128)(2,1)S(1)}, bf16[4096,768]{1,0:T(8,128)(2,1)}, u32[]{:S(2)}) copy-start(bf16[4096,768]{1,0:T(8,128)(2,1)} %all-gather.2.cloned.1.call-done) | copy-start | bytes 18874372
  170.2 25.7 %all-to-all-start.1 = ((bf16[128,8,512]{2,1,0:T(8,128)(2,1)}), bf16[128,8,512]{2,1,0:T(8,128)(2,1)S(1)}, u32[]{:S(2)}, u32[]{:S(2)}) async-start(bf16[128,8,512]{2,1,0:T(8,128)(2,1)} %bitcast.7), calls=%async_computation.1 | async-start | bytes 2097152 | tf_op jit(solution)/shard_map/all_to_all | solution.py:212
Sparse Core Ops, SparseCore 0:
  10.3 138.0 all-gather.1

commit v2 on v1

--- a/solution.py
+++ b/solution.py
@@ -38,24 +38,22 @@
     order = lax.broadcasted_iota(jnp.int32, (count, count), 0)
     one_hot = jnp.where(order == target_ref[...], 1.0, 0.0).astype(jnp.bfloat16)
     moved = jnp.dot(one_hot, rows_ref[...], preferred_element_type=jnp.float32).astype(jnp.bfloat16)
-    groups, copies, rows, width = out_ref.shape
-    for copy in range(copies):
-        out_ref[:, copy] = moved.reshape(groups, rows, width)
-
-
-def sort_rows(tokens, target, groups, copies):
+    out_ref[...] = moved.reshape(out_ref.shape)
+
+
+def sort_rows(tokens, target, groups):
     count, width = tokens.shape
     rows = count // groups
     tile = 1024
     return pl.pallas_call(
         sort_kernel,
-        out_shape=jax.ShapeDtypeStruct((groups, copies, rows, width), tokens.dtype),
+        out_shape=jax.ShapeDtypeStruct((groups, rows, width), tokens.dtype),
         grid=(width // tile,),
         in_specs=[
             pl.BlockSpec((1, count), lambda i: (0, 0)),
             pl.BlockSpec((count, tile), lambda i: (0, i)),
         ],
-        out_specs=pl.BlockSpec((groups, copies, rows, tile), lambda i: (0, 0, 0, i)),
+        out_specs=pl.BlockSpec((groups, rows, tile), lambda i: (0, 0, i)),
         compiler_params=pltpu.CompilerParams(vmem_limit_bytes=32 * 2**20),
         name="sort_rows",
     )(target.reshape(1, count), tokens)
@@ -86,22 +84,113 @@
     )(target.reshape(count, 1), returned)
 
 
-def attention_kernel(core_ref, lengths_ref, own_ref, other_ref, cos_ref, sin_ref, out_ref, queries, keys, values, mixed):
+def own_columns(projection, member):
+    query_width, key_width = HEADS * HEAD_DIM, KV_HEADS * HEAD_DIM
+    return jnp.concatenate(
+        [
+            lax.dynamic_slice_in_dim(projection, member * GROUP * HEAD_DIM, GROUP * HEAD_DIM, 1),
+            lax.dynamic_slice_in_dim(projection, query_width + member * HEAD_DIM, HEAD_DIM, 1),
+            lax.dynamic_slice_in_dim(projection, query_width + key_width + member * HEAD_DIM, HEAD_DIM, 1),
+        ],
+        axis=1,
+    )
+
+
+def spread(block, axis):
+    up, down = [(i, (i + 1) % 4) for i in range(4)], [(i, (i + 3) % 4) for i in range(4)]
+    half = block.shape[0] // 2
+    below, above = lax.ppermute(block, axis, up), lax.ppermute(block, axis, down)
+    far_low = lax.ppermute(below[:half], axis, up)
+    far_high = lax.ppermute(above[half:], axis, down)
+    return [block, below, above, far_low, far_high]
+
+
+RING = (0, 3, 1, 2)
+SPAN = ((0, (0, 1, 2, 3)), (3, (0, 1, 2, 3)), (1, (0, 1, 2, 3)), (2, (0, 1)), (2, (2, 3)))
+
+
+def gather_weights(projection, member):
+    x, y, zh = lax.axis_index("x"), lax.axis_index("y"), lax.axis_index("zh")
+    rows = projection.shape[0]
+    mine = lax.all_gather(own_columns(projection, member), ("x", "y"), axis=0, tiled=True)
+    theirs = lax.ppermute(own_columns(projection, member ^ 2), ("zh", "zl"), [(0, 3), (3, 0), (1, 2), (2, 1)])
+    half = theirs.shape[1] // 2
+    pieces = [mine]
+    places = [(i * 2 + zh) * rows for i in range(16)]
+    for side, (one, two) in enumerate((("y", "x"), ("x", "y"))):
+        block = theirs[:, side * half : (side + 1) * half]
+        pieces += spread(jnp.concatenate(spread(block, one), axis=0), two)
+        for outer, inners in SPAN:
+            for inner in inners:
+                near, far = (outer, RING[inner]) if side == 0 else (RING[inner], outer)
+                places.append(((x + near) % 4 * 8 + (y + far) % 4 * 2 + 1 - zh) * rows)
+    return jnp.stack(places), pieces
+
+
+def project_kernel(places_ref, rows_ref, *refs):
+    pieces, out_ref, ordered = refs[:-2], refs[-2], refs[-1]
+    width = out_ref.shape[1]
+    half = width // 2
+    step = 128
+
+    def take(first, count):
+        for i in range(count):
+            column = pl.multiple_of(places_ref[first + i], step)
+            ordered[:, i * step : (i + 1) * step] = rows_ref[:, pl.ds(column, step)]
+
+    def product(parts):
+        total, at = None, 0
+        for part in parts:
+            depth = part.shape[0]
+            term = jnp.dot(ordered[:, at : at + depth], part[...], preferred_element_type=jnp.float32)
+            total = term if total is None else total + term
+            at += depth
+        return total
+
+    take(0, 16)
+    out = product(pieces[:1])
+    for side in range(2):
+        take(16 + side * 16, 16)
+        other = product(pieces[1 + side * 5 : 6 + side * 5])
+        columns = slice(side * half, (side + 1) * half)
+        out_ref[:, columns] = (out[:, columns] + other).astype(jnp.bfloat16)
+
+
+def project(places, pieces, rows):
+    count, depth = rows.shape
+    width = pieces[0].shape[1]
+    whole = pl.BlockSpec(memory_space=pltpu.VMEM)
+    return pl.pallas_call(
+        project_kernel,
+        out_shape=jax.ShapeDtypeStruct((count, width), jnp.bfloat16),
+        in_specs=[pl.BlockSpec(memory_space=pltpu.SMEM)] + [whole] * (1 + len(pieces)),
+        out_specs=whole,
+        scratch_shapes=[pltpu.VMEM((count, depth // 2), jnp.bfloat16)],
+        compiler_params=pltpu.CompilerParams(vmem_limit_bytes=24 * 2**20),
+        cost_estimate=pl.CostEstimate(
+            flops=2 * count * depth * width, bytes_accessed=2 * depth * (width + count), transcendentals=0
+        ),
+        name="project",
+    )(places, rows, *pieces)
+
+
+def attention_kernel(member_ref, lengths_ref, *refs):
+    lanes = refs[:4]
+    cos_ref, sin_ref, out_ref, queries, keys, values, mixed = refs[4:]
     count = cos_ref.shape[0]
     blocks = count // BLOCK
     part = BLOCK // blocks
     half = HEAD_DIM // 2
-    core = core_ref[0]
+    member = member_ref[0]
 
     taken = lax.broadcasted_iota(jnp.int32, (BLOCK, BLOCK), 1)
-    lane, rest = taken // (BLOCK // 2), taken % (BLOCK // 2)
-    pair, slot, row = rest // (2 * blocks), (rest // 2) % blocks, rest % 2
-    placed = slot * part + (pair * 2 + jnp.where(core == 0, lane, 1 - lane)) * 2 + row
+    lane, rest = taken // part, taken % part
+    group, slot, row = rest // (2 * blocks), (rest // 2) % blocks, rest % 2
+    placed = slot * part + (group * 4 + (lane ^ member)) * 2 + row
     wanted = lax.broadcasted_iota(jnp.int32, (BLOCK, BLOCK), 0)
     forward = jnp.where(wanted == placed, 1.0, 0.0).astype(jnp.bfloat16)
     for h in range(blocks):
-        span = slice(h * BLOCK // 2, (h + 1) * BLOCK // 2)
-        chunk = jnp.concatenate([own_ref[span], other_ref[span]], axis=0)
+        chunk = jnp.concatenate([lane_ref[h * part : (h + 1) * part] for lane_ref in lanes], axis=0)
         chunk = jnp.dot(forward, chunk, preferred_element_type=jnp.float32)
         for s in range(blocks):
             rows = slice(s * BLOCK + h * part, s * BLOCK + (h + 1) * part)
@@ -159,14 +248,14 @@
         ).astype(jnp.bfloat16)
 
 
-def attend(core, lengths, own, other, cosine, sine):
+def attend(member, lengths, lanes, cosine, sine):
     count = cosine.shape[0]
     whole = pl.BlockSpec(memory_space=pltpu.VMEM)
     scalars = pl.BlockSpec(memory_space=pltpu.SMEM)
     return pl.pallas_call(
         attention_kernel,
         out_shape=jax.ShapeDtypeStruct((count, GROUP * HEAD_DIM), jnp.bfloat16),
-        in_specs=[scalars, scalars, whole, whole, whole, whole],
+        in_specs=[scalars, scalars] + [whole] * 6,
         out_specs=whole,
         scratch_shapes=[
             pltpu.VMEM((GROUP, count, HEAD_DIM), jnp.bfloat16),
@@ -174,9 +263,9 @@
             pltpu.VMEM((count, HEAD_DIM), jnp.bfloat16),
             pltpu.VMEM((count, GROUP * HEAD_DIM), jnp.bfloat16),
         ],
-        compiler_params=pltpu.CompilerParams(vmem_limit_bytes=48 * 2**20),
+        compiler_params=pltpu.CompilerParams(vmem_limit_bytes=24 * 2**20),
         name="attend",
-    )(core, lengths, own, other, cosine, sine)
+    )(member, lengths, *lanes, cosine, sine)
 
 
 def on_device(tokens, projection, placement, doc_lengths):
@@ -185,30 +274,21 @@
     members = lax.axis_size(CTX)
     groups = devices // members
     piece = row_count // devices
-    member, core = lax.axis_index(CTX), lax.axis_index("core")
-
-    query_width, key_width = HEADS * HEAD_DIM, KV_HEADS * HEAD_DIM
-    columns = jnp.concatenate(
-        [
-            lax.dynamic_slice_in_dim(projection, member * GROUP * HEAD_DIM, GROUP * HEAD_DIM, 1),
-            lax.dynamic_slice_in_dim(projection, query_width + member * HEAD_DIM, HEAD_DIM, 1),
-            lax.dynamic_slice_in_dim(projection, query_width + key_width + member * HEAD_DIM, HEAD_DIM, 1),
-        ],
-        axis=1,
-    )
-    weights = lax.all_gather(columns, DP, axis=0, tiled=True)
-
+    member = lax.axis_index(CTX)
+
+    places, pieces = gather_weights(projection, member)
     target = (placement[0][:, None] * piece + jnp.arange(piece, dtype=jnp.int32)[None, :]).reshape(row_count)
-    outgoing = sort_rows(tokens, target, groups, 2)
-    arrived = lax.all_to_all(
-        outgoing.reshape(groups * 2, row_count // groups, width), DP + ("zl",), 0, 0, tiled=True
-    )
-    own_rows = arrived.reshape(2 * row_count, width)
-    other_rows = lax.ppermute(own_rows, "core", [(0, 1), (1, 0)])
-    own = jnp.dot(own_rows, weights, preferred_element_type=jnp.float32).astype(jnp.bfloat16)
-    other = jnp.dot(other_rows, weights, preferred_element_type=jnp.float32).astype(jnp.bfloat16)
-    cosine, sine = rotary_tables(doc_lengths[0], members * row_count)
-    mixed = attend(core.reshape(1), doc_lengths, own, other, cosine, sine)
+    outgoing = sort_rows(tokens, target, groups)
+    arrived = lax.all_to_all(outgoing, DP, 0, 0, tiled=True).reshape(row_count, width)
+    across = [(0, 1), (1, 0)]
+    far = lax.ppermute(arrived, "zl", across)
+    near = lax.ppermute(arrived, "core", across)
+    lanes = [project(places, pieces, arrived), project(places, pieces, near)]
+    tables = rotary_tables(doc_lengths[0], members * row_count)
+    far, lanes, tables = lax.optimization_barrier((far, lanes, tables))
+    last = lax.ppermute(far, "core", across)
+    lanes = lanes + [project(places, pieces, far), project(places, pieces, last)]
+    mixed = attend(member.reshape(1), doc_lengths, lanes, *tables)
     returned = lax.all_to_all(
         mixed.reshape(devices, members * piece, GROUP * HEAD_DIM), EVERY, 0, 0, tiled=True
     )

time: 205 us -> 173 us (0.84)
  blocking collectives: 64.1 us -> 0 us
  starting transfers between devices: 9.04 us -> 42.3 us
  waiting for transfers between devices: 85.3 us -> 63.1 us
  Pallas kernels: 12.5 us -> 29.6 us
  matrix products: 13.2 us -> 0 us
  local copies, waits for them, and re-layouts: 3.52 us -> 15.8 us
  other arithmetic: 3.95 us -> 7.88 us
    all_gather x1, waiting for transfers between devices: 66.1 us -> 0.02 us  [gather_weights(): lax.all_gather(own_columns(projection, member), ('x', 'y'), axis=0, tiled...]
    all_to_all x1 -> x0, blocking collectives: 64.1 us -> none  [on_device(): lax.all_to_all(outgoing.reshape(groups * 2, row_count // groups, width),...]
    all_to_all x0 -> x1, waiting for transfers between devices: none -> 28.5 us  [on_device(): lax.all_to_all(outgoing, DP, 0, 0, tiled=True).reshape(row_count, width)]
    ppermute x1 -> x20, starting transfers between devices: 2.63 us -> 25.3 us  [the longest x4 7.99 us: spread(): far_high = lax.ppermute(above[half:], axis, down)]
    pallas_call x1 -> x5, Pallas kernels: 1.66 us -> 18.9 us  [the longest x4 17.4 us: project(): pl.pallas_call(project_kernel, out_shape=jax.ShapeDtypeStruct((count, wid...]
    ppermute x1 -> x20, waiting for transfers between devices: 0.01 us -> 15.4 us  [the longest x4 11 us: spread(): lax.ppermute(block, axis, up)]
    dot_general x2 -> x0, matrix products: 13.2 us -> none  [the longest x1 7.6 us: on_device(): jnp.dot(own_rows, weights, preferred_element_type=jnp.float32)]
    all_to_all x0 -> x1, starting transfers between devices: none -> 11.2 us  [on_device(): lax.all_to_all(outgoing, DP, 0, 0, tiled=True).reshape(row_count, width)]
  transfers between devices with their start and end apart: 3 -> 23, of which waited for: 2 -> 10; matrix products, arithmetic and copies ran while one was open for 5% -> 9% of each run, Pallas kernels for 1% -> 9%
where the time goes in v2:
time: 173 us; the launch traced here: 172 us
  waiting for transfers between devices  63.1 us (36%)
  starting transfers between devices  42.3 us (24%)
  Pallas kernels  29.6 us (17%)
  local copies, waits for them, and re-layouts  15.8 us (9%)
  between operations  13.6 us (8%)
  other arithmetic  7.88 us (5%)
    all_to_all x1, waiting for transfers between devices, on_device(): lax.all_to_all(outgoing, DP, 0, 0, tiled=True).reshape(row_count, width)  28.5 us
    all_to_all x1, waiting for transfers between devices, on_device(): lax.all_to_all(mixed.reshape(devices, members * piece, GROUP * HEAD_DIM),...  19.2 us
    pallas_call x4, Pallas kernels, project(): pl.pallas_call(project_kernel, out_shape=jax.ShapeDtypeStruct((count, wid...  17.4 us
    all_to_all x1, starting transfers between devices, on_device(): lax.all_to_all(outgoing, DP, 0, 0, tiled=True).reshape(row_count, width)  11.2 us
    ppermute x4, waiting for transfers between devices, spread(): lax.ppermute(block, axis, up)  11 us
    unnamed x20, local copies, waits for them, and re-layouts  8.63 us
    pallas_call x1, Pallas kernels, attend(): pl.pallas_call(attention_kernel, out_shape=jax.ShapeDtypeStruct((count, G...  8.41 us
    ppermute x4, starting transfers between devices, spread(): far_high = lax.ppermute(above[half:], axis, down)  7.99 us
  transfers between devices with their start and end apart: 23, of which 10 were waited for; matrix products, arithmetic and copies ran while one was open for 9% of the time, Pallas kernels for 9%

profile of v2, /device:TPU:1, one launch (start us, length us, event | category | flops | bytes accessed | tf_op | source)
XLA Modules:
  0.0 172.4 jit_solution(11104455601372839273)
XLA Ops:
  6.5 1.0 constant_dynamic-slice_fusion.2
  7.5 0.8 constant_dynamic-slice_fusion.1
  8.4 0.7 pad_maximum_fusion.2
  9.1 0.7 multiply_bitcast_fusion
  9.7 0.1 iota_add_fusion
  9.8 0.1 add.357.target_ref
  10.0 1.6 copy-done.3
  11.6 1.5 sort_rows.1
  13.1 1.3 copy-done.2
  14.4 11.2 %all-to-all-start = ((bf16[32,8,4096]{2,1,0:T(8,128)(2,1)}), bf16[32,8,4096]{2,1,0:T(8,128)(2,1)S(1)}, u32[]{:S(2)}, u32[]{:S(2)}) async-start(bf16[32,8,4096]{2,1,0:T(8,128)(2,1)} %copy-done.2), calls=%async_computation | async-start | bytes 4194304 | tf_op jit(solution)/shard_map/all_to_all | solution.py:282
  25.6 3.0 %collective-permute-start.1 = (bf16[128,768]{1,0:T(8,128)(2,1)S(1)}, bf16[128,768]{1,0:T(8,128)(2,1)S(1)}, u32[]{:S(2)}, u32[]{:S(2)}) collective-permute-start(bf16[128,768]{1,0:T(8,128)(2,1)S(1)} %pad_maximum_fusion.3), channel_id=1, source_target_pairs={{0,6},{6,0},{2,4},{4,2},{1,7},{7,1},{3,5},{5,3},{8,14},{14,8},{10,... | collective-permute-start | bytes 589832 | tf_op jit(solution)/shard_map/ppermute | solution.py:116
  28.6 28.5 %all-to-all-done = bf16[32,8,4096]{2,1,0:T(8,128)(2,1)S(1)} async-done(((bf16[32,8,4096]{2,1,0:T(8,128)(2,1)}), bf16[32,8,4096]{2,1,0:T(8,128)(2,1)S(1)}, u32[]{:S(2)}, u32[]{:S(2)}) %all-to-all-start) | async-done | bytes 2097184 | tf_op jit(solution)/shard_map/all_to_all | solution.py:282
  57.1 1.1 collective-permute-start.18
  58.2 0.7 fusion.1
  58.9 0.4 collective-permute-start
  59.3 2.7 %collective-permute-start.11 = (bf16[128,384]{1,0:T(8,128)(2,1)S(1)}, bf16[128,384]{1,0:T(8,128)(2,1)S(1)}, u32[]{:S(2)}, u32[]{:S(2)}) collective-permute-start(bf16[128,384]{1,0:T(8,128)(2,1)S(1)} %get-tuple-element.21), channel_id=1, source_target_pairs={{0,96},{32,0},{64,32},{96,64},{1,97},{33,1},{65,33},{97,65},{2,98}... | collective-permute-start | bytes 294920 | tf_op jit(solution)/shard_map/ppermute | solution.py:102
  62.0 0.6 collective-permute-start.2
  62.6 2.0 %collective-permute-done.10 = bf16[128,384]{1,0:T(8,128)(2,1)S(1)} collective-permute-done((bf16[128,384]{1,0:T(8,128)(2,1)S(1)}, bf16[128,384]{1,0:T(8,128)(2,1)S(1)}, u32[]{:S(2)}, u32[]{:S(2)}) %collective-permute-start.10) | collective-permute-done | bytes 98336 | tf_op jit(solution)/shard_map/ppermute | solution.py:102
  64.6 0.1 collective-permute-start.3
  64.7 0.6 constant_dynamic-update-slice_fusion.8
  65.4 0.7 collective-permute-done.11
  66.1 0.6 constant_dynamic-update-slice_fusion.7
  66.8 2.8 %collective-permute-done.2 = bf16[128,384]{1,0:T(8,128)(2,1)S(1)} collective-permute-done((bf16[128,384]{1,0:T(8,128)(2,1)S(1)}, bf16[128,384]{1,0:T(8,128)(2,1)S(1)}, u32[]{:S(2)}, u32[]{:S(2)}) %collective-permute-start.2) | collective-permute-done | bytes 98336 | tf_op jit(solution)/shard_map/ppermute | solution.py:102
  69.6 0.8 collective-permute-start.13
  70.3 0.6 collective-permute-done.3
  70.9 0.6 collective-permute-start.4
  71.5 0.4 collective-permute-done.12
  71.9 1.8 %collective-permute-start.5 = (bf16[64,384]{1,0:T(8,128)(2,1)S(1)}, bf16[64,384]{1,0:T(8,128)(2,1)S(1)}, u32[]{:S(2)}, u32[]{:S(2)}) collective-permute-start(bf16[64,384]{1,0:T(8,128)(2,1)S(1)} %slice.42), channel_id=1, source_target_pairs={{0,24},{8,0},{16,8},{24,16},{1,25},{9,1},{17,9},{25,17},{2,26},{10... | collective-permute-start | bytes 147464 | tf_op jit(solution)/shard_map/ppermute | solution.py:104
  73.7 0.6 constant_dynamic-update-slice_fusion.6
  74.3 0.6 constant_dynamic-update-slice_fusion.5.refs_6_
  74.9 0.6 constant_dynamic-update-slice_fusion.3
  75.6 0.6 constant_dynamic-update-slice_fusion.2
  76.2 0.3 collective-permute-done.4
  76.5 2.4 %collective-permute-start.15 = (bf16[512,384]{1,0:T(8,128)(2,1)}, bf16[512,384]{1,0:T(8,128)(2,1)S(1)}, u32[]{:S(2)}, u32[]{:S(2)}) collective-permute-start(bf16[512,384]{1,0:T(8,128)(2,1)} %constant_dynamic-update-slice_fusion.5.refs_6_), channel_id=1, source_target_pairs={{0,24},{8,0},{16,8},{24,16},{1,25},{9,1},{17,9},{25,17},{2,26},{10... | collective-permute-start | bytes 1179656 | tf_op jit(solution)/shard_map/ppermute | solution.py:102
  78.9 0.6 constant_dynamic-update-slice_fusion.1
  79.5 0.6 constant_dynamic-update-slice_fusion.refs_1_
  80.1 0.2 collective-permute-start.6
  80.3 6.2 %collective-permute-done.14.refs_7_ = bf16[512,384]{1,0:T(8,128)(2,1)S(1)} collective-permute-done((bf16[512,384]{1,0:T(8,128)(2,1)}, bf16[512,384]{1,0:T(8,128)(2,1)S(1)}, u32[]{:S(2)}, u32[]{:S(2)}) %collective-permute-start.14) | collective-permute-done | bytes 393248 | tf_op jit(solution)/shard_map/ppermute | solution.py:102
  86.6 2.1 %collective-permute-start.7 = (bf16[512,384]{1,0:T(8,128)(2,1)}, bf16[512,384]{1,0:T(8,128)(2,1)}, u32[]{:S(2)}, u32[]{:S(2)}) collective-permute-start(bf16[512,384]{1,0:T(8,128)(2,1)} %constant_dynamic-update-slice_fusion.refs_1_), channel_id=1, source_target_pairs={{0,96},{32,0},{64,32},{96,64},{1,97},{33,1},{65,33},{97,65},{2,98}... | collective-permute-start | bytes 1179656 | tf_op jit(solution)/shard_map/ppermute | solution.py:102
  88.7 0.2 reduce-window.8
  88.9 0.1 select_reduce_fusion
  89.0 0.5 collective-permute-start.16
  89.6 0.7 slice.49
  90.3 2.2 %collective-permute-start.17 = (bf16[256,384]{1,0:T(8,128)(2,1)}, bf16[256,384]{1,0:T(8,128)(2,1)}, u32[]{:S(2)}, u32[]{:S(2)}) collective-permute-start(bf16[256,384]{1,0:T(8,128)(2,1)} %slice.49), channel_id=1, source_target_pairs={{0,24},{8,0},{16,8},{24,16},{1,25},{9,1},{17,9},{25,17},{2,26},{10... | collective-permute-start | bytes 589832 | tf_op jit(solution)/shard_map/ppermute | solution.py:104
  92.5 0.7 slice.43
  93.2 2.4 %collective-permute-done.7.refs_3_ = bf16[512,384]{1,0:T(8,128)(2,1)} collective-permute-done((bf16[512,384]{1,0:T(8,128)(2,1)}, bf16[512,384]{1,0:T(8,128)(2,1)}, u32[]{:S(2)}, u32[]{:S(2)}) %collective-permute-start.7) | collective-permute-done | bytes 393248 | tf_op jit(solution)/shard_map/ppermute | solution.py:102
  95.6 0.2 collective-permute-start.8
  95.8 1.6 slice.44
  97.4 3.2 %collective-permute-start.9 = (bf16[256,384]{1,0:T(8,128)(2,1)}, bf16[256,384]{1,0:T(8,128)(2,1)}, u32[]{:S(2)}, u32[]{:S(2)}) collective-permute-start(bf16[256,384]{1,0:T(8,128)(2,1)} %slice.44), channel_id=1, source_target_pairs={{0,96},{32,0},{64,32},{96,64},{1,97},{33,1},{65,33},{97,65},{2,98}... | collective-permute-start | bytes 589832 | tf_op jit(solution)/shard_map/ppermute | solution.py:104
  100.6 3.1 %fusion = (f32[1024,64]{1,0:T(8,128)}, f32[1024,64]{1,0:T(8,128)}, f32[1024,64]{1,0:T(8,128)}) fusion(f32[64]{0:T(128)S(1)} %multiply_power_fusion, f32[1024]{0:T(1024)S(1)} %subtract_convert_fusion), kind=kLoop, calls=%fused_computation.6 | loop fusion | flops 131072 | bytes 790784 | tf_op jit(solution)/shard_map/neg | solution.py:33
  103.8 0.1 stack.147.places_ref
  103.9 3.0 %pad_maximum_fusion = (f32[1024,128]{1,0:T(8,128)}, f32[1024,128]{1,0:T(8,128)}) fusion(f32[1024,64]{1,0:T(8,128)} %get-tuple-element.27, f32[1024,64]{1,0:T(8,128)} %get-tuple-element.26, f32[1024,64]{1,0:T(8,128)} %get-tuple-element.25), kind=kLoop, calls=%fused_computation.2 | loop fusion | flops 262144 | bytes 1835008 | tf_op jit(solution)/shard_map/concatenate | solution.py:33
  106.9 0.0 all-gather.2.cloned.1.call-done.refs_0_
  107.0 1.9 %copy-done = bf16[2048,768]{1,0:T(8,128)(2,1)S(1)} copy-done((bf16[2048,768]{1,0:T(8,128)(2,1)S(1)}, bf16[2048,768]{1,0:T(8,128)(2,1)}, u32[]{:S(2)}) %copy-start) | copy-done | bytes 3145752
  108.9 4.1 %project.4.refs_0_ = bf16[256,768]{1,0:T(8,128)(2,1)S(1)} custom-call(s32[48]{0:T(128)S(1)} %stack.147.places_ref, bf16[256,4096]{1,0:T(8,128)(2,1)S(1)} %bitcast.43, bf16[2048,768]{1,0:T(8,128)(2,1)S(1)} %copy-done, bf16[512,384]{1,0:T(8,128)(2,1)} %constant_dynamic-update-slice_fusion.refs_1_, bf16[512,384]{1,0:T(8,128)(2,1)S(1)} %collective-permute-done.6.refs_2_, ...), custom_call_target="tpu_custom_call" | custom-call | flops 1610612736 | bytes 8388608 | tf_op jit(solution)/shard_map/project/pallas_call | solution.py:163
  113.0 4.6 %project.5.refs_1_ = bf16[256,768]{1,0:T(8,128)(2,1)S(1)} custom-call(s32[48]{0:T(128)S(1)} %stack.147.places_ref, bf16[256,4096]{1,0:T(8,128)(2,1)} %collective-permute-done.18.rows_ref, bf16[2048,768]{1,0:T(8,128)(2,1)S(1)} %copy-done.1, bf16[512,384]{1,0:T(8,128)(2,1)} %constant_dynamic-update-slice_fusion.refs_1_, ...), custom_call_target="tpu_custom_call" | custom-call | flops 1610612736 | bytes 8388608 | tf_op jit(solution)/shard_map/project/pallas_call | solution.py:163
  117.7 3.3 %collective-permute-start.19 = (bf16[256,4096]{1,0:T(8,128)(2,1)}, bf16[256,4096]{1,0:T(8,128)(2,1)S(1)}, u32[]{:S(2)}, u32[]{:S(2)}) collective-permute-start(bf16[256,4096]{1,0:T(8,128)(2,1)} %collective-permute-done.rows_ref), channel_id=1, source_target_pairs={{0,1},{1,0},{2,3},{3,2},{4,5},{5,4},{6,7},{7,6},{8,9},{9,8},{10,11... | collective-permute-start | bytes 6291464 | tf_op jit(solution)/shard_map/ppermute | solution.py:289
  121.0 4.6 %project.6.refs_2_ = bf16[256,768]{1,0:T(8,128)(2,1)S(1)} custom-call(s32[48]{0:T(128)S(1)} %stack.147.places_ref, bf16[256,4096]{1,0:T(8,128)(2,1)} %collective-permute-done.rows_ref, bf16[2048,768]{1,0:T(8,128)(2,1)S(1)} %copy-done.1, bf16[512,384]{1,0:T(8,128)(2,1)} %constant_dynamic-update-slice_fusion.refs_1_, ...), custom_call_target="tpu_custom_call" | custom-call | flops 1610612736 | bytes 8388608 | tf_op jit(solution)/shard_map/project/pallas_call | solution.py:163
  125.6 4.1 %project.7.refs_3_ = bf16[256,768]{1,0:T(8,128)(2,1)S(1)} custom-call(s32[48]{0:T(128)S(1)} %stack.147.places_ref, bf16[256,4096]{1,0:T(8,128)(2,1)S(1)} %collective-permute-done.19.rows_ref, bf16[2048,768]{1,0:T(8,128)(2,1)S(1)} %copy-done.1, bf16[512,384]{1,0:T(8,128)(2,1)} %constant_dynamic-update-slice_fusion.refs_1_, ...), custom_call_target="tpu_custom_call" | custom-call | flops 1610612736 | bytes 8388608 | tf_op jit(solution)/shard_map/project/pallas_call | solution.py:163
  129.7 8.4 %attend.1 = bf16[1024,512]{1,0:T(8,128)(2,1)} custom-call(s32[1]{0:T(128)} %bitcast.1.member_ref, s32[1,8]{1,0:T(1,128)S(1)} %copy-done.6, bf16[256,768]{1,0:T(8,128)(2,1)S(1)} %project.4.refs_0_, bf16[256,768]{1,0:T(8,128)(2,1)S(1)} %project.5.refs_1_, bf16[256,768]{1,0:T(8,128)(2,1)S(1)} %project.6.refs_2_, bf16[256,768]{1,0:T(8,128)(2,1)S(1)} %project.7.refs_3_, ...), custom_call_target="tpu_custom_call" | custom-call | tf_op jit(solution)/shard_map/attend/pallas_call | solution.py:255
  138.2 5.8 %all-to-all-start.1 = ((bf16[128,8,512]{2,1,0:T(8,128)(2,1)}), bf16[128,8,512]{2,1,0:T(8,128)(2,1)S(1)}, u32[]{:S(2)}, u32[]{:S(2)}) async-start(bf16[128,8,512]{2,1,0:T(8,128)(2,1)} %bitcast.38), calls=%async_computation.1 | async-start | bytes 2097152 | tf_op jit(solution)/shard_map/all_to_all | solution.py:292
  144.0 0.1 add.417.target_ref
  144.1 19.2 %all-to-all-done.1 = bf16[128,8,512]{2,1,0:T(8,128)(2,1)S(1)} async-done(((bf16[128,8,512]{2,1,0:T(8,128)(2,1)}), bf16[128,8,512]{2,1,0:T(8,128)(2,1)S(1)}, u32[]{:S(2)}, u32[]{:S(2)}) %all-to-all-start.1) | async-done | bytes 1048608 | tf_op jit(solution)/shard_map/all_to_all | solution.py:292
  163.3 2.3 %unsort_rows.1 = bf16[256,2048]{1,0:T(8,128)(2,1)} custom-call(s32[256,1]{1,0:T(8,128)S(1)} %add.417.target_ref, bf16[32,4,8,512]{3,2,1,0:T(8,128)(2,1)S(1)} %bitcast.44), custom_call_target="tpu_custom_call" | custom-call | tf_op jit(solution)/shard_map/unsort_rows/pallas_call | solution.py:73
  (36 shorter events, 0.2 us)
Async XLA Ops:
  6.5 100.4 %all-gather.2.cloned.1.call-start = ((), (), s32[]{:S(2)}) async-start(), calls=%async_computation.2 | async-start | bytes 3342336 | tf_op jit(solution)/shard_map/all_gather | solution.py:115
  10.0 1.6 copy-start.3
  13.1 1.3 copy-start.2
  14.4 42.7 %all-to-all-start = ((bf16[32,8,4096]{2,1,0:T(8,128)(2,1)}), bf16[32,8,4096]{2,1,0:T(8,128)(2,1)S(1)}, u32[]{:S(2)}, u32[]{:S(2)}) async-start(bf16[32,8,4096]{2,1,0:T(8,128)(2,1)} %copy-done.2), calls=%async_computation | async-start | bytes 4194304 | tf_op jit(solution)/shard_map/all_to_all | solution.py:282
  25.6 63.1 %copy-start.6 = (s32[1,8]{1,0:T(1,128)S(1)}, s32[1,8]{1,0:T(1,128)}, u32[]{:S(2)}) copy-start(s32[1,8]{1,0:T(1,128)} %lengths_ref.1) | copy-start | bytes 100
  25.6 32.6 %collective-permute-start.1 = (bf16[128,768]{1,0:T(8,128)(2,1)S(1)}, bf16[128,768]{1,0:T(8,128)(2,1)S(1)}, u32[]{:S(2)}, u32[]{:S(2)}) collective-permute-start(bf16[128,768]{1,0:T(8,128)(2,1)S(1)} %pad_maximum_fusion.3), channel_id=1, source_target_pairs={{0,6},{6,0},{2,4},{4,2},{1,7},{7,1},{3,5},{5,3},{8,14},{14,8},{10,... | collective-permute-start | bytes 589832 | tf_op jit(solution)/shard_map/ppermute | solution.py:116
  57.1 55.9 %collective-permute-start.18 = (bf16[256,4096]{1,0:T(8,128)(2,1)S(1)}, bf16[256,4096]{1,0:T(8,128)(2,1)}, u32[]{:S(2)}, u32[]{:S(2)}) collective-permute-start(bf16[256,4096]{1,0:T(8,128)(2,1)S(1)} %bitcast.41), channel_id=1, source_target_pairs={{0,1},{1,0},{2,3},{3,2},{4,5},{5,4},{6,7},{7,6},{8,9},{9,8},{10,11... | collective-permute-start | bytes 6291464 | tf_op jit(solution)/shard_map/ppermute | solution.py:285
  58.9 5.7 %collective-permute-start.10 = (bf16[128,384]{1,0:T(8,128)(2,1)S(1)}, bf16[128,384]{1,0:T(8,128)(2,1)S(1)}, u32[]{:S(2)}, u32[]{:S(2)}) collective-permute-start(bf16[128,384]{1,0:T(8,128)(2,1)S(1)} %get-tuple-element.21), channel_id=1, source_target_pairs={{0,32},{32,64},{64,96},{96,0},{1,33},{33,65},{65,97},{97,1},{2,34}... | collective-permute-start | bytes 294920 | tf_op jit(solution)/shard_map/ppermute | solution.py:102
  58.9 58.7 %collective-permute-start = (bf16[256,4096]{1,0:T(8,128)(2,1)S(1)}, bf16[256,4096]{1,0:T(8,128)(2,1)}, u32[]{:S(2)}, u32[]{:S(2)}) collective-permute-start(bf16[256,4096]{1,0:T(8,128)(2,1)S(1)} %bitcast.42), channel_id=1, source_target_pairs={{0,2},{2,0},{1,3},{3,1},{4,6},{6,4},{5,7},{7,5},{8,10},{10,8},{9,1... | collective-permute-start | bytes 6291464 | tf_op jit(solution)/shard_map/ppermute | solution.py:284
  59.3 6.8 %collective-permute-start.11 = (bf16[128,384]{1,0:T(8,128)(2,1)S(1)}, bf16[128,384]{1,0:T(8,128)(2,1)S(1)}, u32[]{:S(2)}, u32[]{:S(2)}) collective-permute-start(bf16[128,384]{1,0:T(8,128)(2,1)S(1)} %get-tuple-element.21), channel_id=1, source_target_pairs={{0,96},{32,0},{64,32},{96,64},{1,97},{33,1},{65,33},{97,65},{2,98}... | collective-permute-start | bytes 294920 | tf_op jit(solution)/shard_map/ppermute | solution.py:102
  62.0 7.6 %collective-permute-start.2 = (bf16[128,384]{1,0:T(8,128)(2,1)S(1)}, bf16[128,384]{1,0:T(8,128)(2,1)S(1)}, u32[]{:S(2)}, u32[]{:S(2)}) collective-permute-start(bf16[128,384]{1,0:T(8,128)(2,1)S(1)} %get-tuple-element.24), channel_id=1, source_target_pairs={{0,8},{8,16},{16,24},{24,0},{1,9},{9,17},{17,25},{25,1},{2,10},{10... | collective-permute-start | bytes 294920 | tf_op jit(solution)/shard_map/ppermute | solution.py:102
  64.6 6.3 %collective-permute-start.3 = (bf16[128,384]{1,0:T(8,128)(2,1)S(1)}, bf16[128,384]{1,0:T(8,128)(2,1)S(1)}, u32[]{:S(2)}, u32[]{:S(2)}) collective-permute-start(bf16[128,384]{1,0:T(8,128)(2,1)S(1)} %get-tuple-element.24), channel_id=1, source_target_pairs={{0,24},{8,0},{16,8},{24,16},{1,25},{9,1},{17,9},{25,17},{2,26},{10... | collective-permute-start | bytes 294920 | tf_op jit(solution)/shard_map/ppermute | solution.py:102
  66.1 5.8 %collective-permute-start.12 = (bf16[64,384]{1,0:T(8,128)(2,1)S(1)}, bf16[64,384]{1,0:T(8,128)(2,1)S(1)}, u32[]{:S(2)}, u32[]{:S(2)}) collective-permute-start(bf16[64,384]{1,0:T(8,128)(2,1)S(1)} %slice.46), channel_id=1, source_target_pairs={{0,32},{32,64},{64,96},{96,0},{1,33},{33,65},{65,97},{97,1},{2,34}... | collective-permute-start | bytes 147464 | tf_op jit(solution)/shard_map/ppermute | solution.py:103
  69.6 4.7 %collective-permute-start.13 = (bf16[64,384]{1,0:T(8,128)(2,1)S(1)}, bf16[64,384]{1,0:T(8,128)(2,1)S(1)}, u32[]{:S(2)}, u32[]{:S(2)}) collective-permute-start(bf16[64,384]{1,0:T(8,128)(2,1)S(1)} %slice.47), channel_id=1, source_target_pairs={{0,96},{32,0},{64,32},{96,64},{1,97},{33,1},{65,33},{97,65},{2,98}... | collective-permute-start | bytes 147464 | tf_op jit(solution)/shard_map/ppermute | solution.py:104
  70.9 5.6 %collective-permute-start.4 = (bf16[64,384]{1,0:T(8,128)(2,1)S(1)}, bf16[64,384]{1,0:T(8,128)(2,1)S(1)}, u32[]{:S(2)}, u32[]{:S(2)}) collective-permute-start(bf16[64,384]{1,0:T(8,128)(2,1)S(1)} %slice.41), channel_id=1, source_target_pairs={{0,8},{8,16},{16,24},{24,0},{1,9},{9,17},{17,25},{25,1},{2,10},{10... | collective-permute-start | bytes 147464 | tf_op jit(solution)/shard_map/ppermute | solution.py:103
  71.9 7.6 %collective-permute-start.5 = (bf16[64,384]{1,0:T(8,128)(2,1)S(1)}, bf16[64,384]{1,0:T(8,128)(2,1)S(1)}, u32[]{:S(2)}, u32[]{:S(2)}) collective-permute-start(bf16[64,384]{1,0:T(8,128)(2,1)S(1)} %slice.42), channel_id=1, source_target_pairs={{0,24},{8,0},{16,8},{24,16},{1,25},{9,1},{17,9},{25,17},{2,26},{10... | collective-permute-start | bytes 147464 | tf_op jit(solution)/shard_map/ppermute | solution.py:104
  74.9 11.6 %collective-permute-start.14 = (bf16[512,384]{1,0:T(8,128)(2,1)}, bf16[512,384]{1,0:T(8,128)(2,1)S(1)}, u32[]{:S(2)}, u32[]{:S(2)}) collective-permute-start(bf16[512,384]{1,0:T(8,128)(2,1)} %constant_dynamic-update-slice_fusion.5.refs_6_), channel_id=1, source_target_pairs={{0,8},{8,16},{16,24},{24,0},{1,9},{9,17},{17,25},{25,1},{2,10},{10... | collective-permute-start | bytes 1179656 | tf_op jit(solution)/shard_map/ppermute | solution.py:102
  76.5 12.6 %collective-permute-start.15 = (bf16[512,384]{1,0:T(8,128)(2,1)}, bf16[512,384]{1,0:T(8,128)(2,1)S(1)}, u32[]{:S(2)}, u32[]{:S(2)}) collective-permute-start(bf16[512,384]{1,0:T(8,128)(2,1)} %constant_dynamic-update-slice_fusion.5.refs_6_), channel_id=1, source_target_pairs={{0,24},{8,0},{16,8},{24,16},{1,25},{9,1},{17,9},{25,17},{2,26},{10... | collective-permute-start | bytes 1179656 | tf_op jit(solution)/shard_map/ppermute | solution.py:102
  80.1 10.2 %collective-permute-start.6 = (bf16[512,384]{1,0:T(8,128)(2,1)}, bf16[512,384]{1,0:T(8,128)(2,1)S(1)}, u32[]{:S(2)}, u32[]{:S(2)}) collective-permute-start(bf16[512,384]{1,0:T(8,128)(2,1)} %constant_dynamic-update-slice_fusion.refs_1_), channel_id=1, source_target_pairs={{0,32},{32,64},{64,96},{96,0},{1,33},{33,65},{65,97},{97,1},{2,34}... | collective-permute-start | bytes 1179656 | tf_op jit(solution)/shard_map/ppermute | solution.py:102
  86.6 9.0 %collective-permute-start.7 = (bf16[512,384]{1,0:T(8,128)(2,1)}, bf16[512,384]{1,0:T(8,128)(2,1)}, u32[]{:S(2)}, u32[]{:S(2)}) collective-permute-start(bf16[512,384]{1,0:T(8,128)(2,1)} %constant_dynamic-update-slice_fusion.refs_1_), channel_id=1, source_target_pairs={{0,96},{32,0},{64,32},{96,64},{1,97},{33,1},{65,33},{97,65},{2,98}... | collective-permute-start | bytes 1179656 | tf_op jit(solution)/shard_map/ppermute | solution.py:102
  89.0 8.4 %collective-permute-start.16 = (bf16[256,384]{1,0:T(8,128)(2,1)S(1)}, bf16[256,384]{1,0:T(8,128)(2,1)S(1)}, u32[]{:S(2)}, u32[]{:S(2)}) collective-permute-start(bf16[256,384]{1,0:T(8,128)(2,1)S(1)} %slice.48), channel_id=1, source_target_pairs={{0,8},{8,16},{16,24},{24,0},{1,9},{9,17},{17,25},{25,1},{2,10},{10... | collective-permute-start | bytes 589832 | tf_op jit(solution)/shard_map/ppermute | solution.py:103
  90.3 16.6 %collective-permute-start.17 = (bf16[256,384]{1,0:T(8,128)(2,1)}, bf16[256,384]{1,0:T(8,128)(2,1)}, u32[]{:S(2)}, u32[]{:S(2)}) collective-permute-start(bf16[256,384]{1,0:T(8,128)(2,1)} %slice.49), channel_id=1, source_target_pairs={{0,24},{8,0},{16,8},{24,16},{1,25},{9,1},{17,9},{25,17},{2,26},{10... | collective-permute-start | bytes 589832 | tf_op jit(solution)/shard_map/ppermute | solution.py:104
  95.6 11.3 %collective-permute-start.8 = (bf16[256,384]{1,0:T(8,128)(2,1)}, bf16[256,384]{1,0:T(8,128)(2,1)}, u32[]{:S(2)}, u32[]{:S(2)}) collective-permute-start(bf16[256,384]{1,0:T(8,128)(2,1)} %slice.43), channel_id=1, source_target_pairs={{0,32},{32,64},{64,96},{96,0},{1,33},{33,65},{65,97},{97,1},{2,34}... | collective-permute-start | bytes 589832 | tf_op jit(solution)/shard_map/ppermute | solution.py:103
  97.4 9.5 %collective-permute-start.9 = (bf16[256,384]{1,0:T(8,128)(2,1)}, bf16[256,384]{1,0:T(8,128)(2,1)}, u32[]{:S(2)}, u32[]{:S(2)}) collective-permute-start(bf16[256,384]{1,0:T(8,128)(2,1)} %slice.44), channel_id=1, source_target_pairs={{0,96},{32,0},{64,32},{96,64},{1,97},{33,1},{65,33},{97,65},{2,98}... | collective-permute-start | bytes 589832 | tf_op jit(solution)/shard_map/ppermute | solution.py:104
  107.0 1.9 %copy-start = (bf16[2048,768]{1,0:T(8,128)(2,1)S(1)}, bf16[2048,768]{1,0:T(8,128)(2,1)}, u32[]{:S(2)}) copy-start(bf16[2048,768]{1,0:T(8,128)(2,1)} %all-gather.2.cloned.1.call-done.refs_0_) | copy-start | bytes 9437188
  108.9 4.2 %copy-start.1 = (bf16[2048,768]{1,0:T(8,128)(2,1)S(1)}, bf16[2048,768]{1,0:T(8,128)(2,1)}, u32[]{:S(2)}) copy-start(bf16[2048,768]{1,0:T(8,128)(2,1)} %all-gather.2.cloned.1.call-done.refs_0_) | copy-start | bytes 9437188
  117.7 8.0 %collective-permute-start.19 = (bf16[256,4096]{1,0:T(8,128)(2,1)}, bf16[256,4096]{1,0:T(8,128)(2,1)S(1)}, u32[]{:S(2)}, u32[]{:S(2)}) collective-permute-start(bf16[256,4096]{1,0:T(8,128)(2,1)} %collective-permute-done.rows_ref), channel_id=1, source_target_pairs={{0,1},{1,0},{2,3},{3,2},{4,5},{5,4},{6,7},{7,6},{8,9},{9,8},{10,11... | collective-permute-start | bytes 6291464 | tf_op jit(solution)/shard_map/ppermute | solution.py:289
  125.6 4.1 %copy-start.4 = (f32[1024,128]{1,0:T(8,128)S(1)}, f32[1024,128]{1,0:T(8,128)}, u32[]{:S(2)}) copy-start(f32[1024,128]{1,0:T(8,128)} %get-tuple-element.13.refs_4_) | copy-start | bytes 1572868
  125.6 4.1 %copy-start.5 = (f32[1024,128]{1,0:T(8,128)S(1)}, f32[1024,128]{1,0:T(8,128)}, u32[]{:S(2)}) copy-start(f32[1024,128]{1,0:T(8,128)} %get-tuple-element.14.refs_5_) | copy-start | bytes 1572868
  138.2 25.1 %all-to-all-start.1 = ((bf16[128,8,512]{2,1,0:T(8,128)(2,1)}), bf16[128,8,512]{2,1,0:T(8,128)(2,1)S(1)}, u32[]{:S(2)}, u32[]{:S(2)}) async-start(bf16[128,8,512]{2,1,0:T(8,128)(2,1)} %bitcast.38), calls=%async_computation.1 | async-start | bytes 2097152 | tf_op jit(solution)/shard_map/all_to_all | solution.py:292
Sparse Core Ops, SparseCore 0:
  9.5 71.4 all-gather.1

commit v3 on v2

v3 whole, which is shorter than its diff:
```python
import functools

import jax
import jax.numpy as jnp
from jax import lax
from jax.experimental import pallas as pl
from jax.experimental.pallas import tpu as pltpu
from jax.sharding import Mesh, PartitionSpec as P

HEAD_DIM = 128
HEADS = 16
KV_HEADS = 4
GROUP = HEADS // KV_HEADS
THETA = 500000.0
MOST = 512
DP = ("x", "y", "zh")
CTX = ("zl", "core")
EVERY = DP + CTX
BLOCK = 256


def frequencies():
    half = HEAD_DIM // 2
    return THETA ** (-2.0 * jnp.arange(half, dtype=jnp.float32) / HEAD_DIM)


def rotary_tables(lengths, count):
    position = jnp.arange(count, dtype=jnp.int32)
    ends = jnp.cumsum(lengths)
    begins = jnp.sum(jnp.where(position[:, None] >= ends[None, :], lengths[None, :], 0), axis=1)
    angles = (position - begins).astype(jnp.float32)[:, None] * frequencies()[None, :]
    cosine, sine = jnp.cos(angles), jnp.sin(angles)
    return jnp.concatenate([cosine, cosine], axis=1), jnp.concatenate([-sine, sine], axis=1)


def sort_kernel(placement_ref, rows_ref, out_ref):
    count = rows_ref.shape[0]
    devices = placement_ref.shape[1]
    piece = count // devices
    device = lax.broadcasted_iota(jnp.int32, (devices, devices), 0)
    pieces = jnp.where(device == placement_ref[...], 1.0, 0.0).astype(jnp.bfloat16)
    down = lax.broadcasted_iota(jnp.int32, (count, devices), 0) // piece
    tall = jnp.where(down == lax.broadcasted_iota(jnp.int32, (count, devices), 1), 1.0, 0.0).astype(jnp.bfloat16)
    along = lax.broadcasted_iota(jnp.int32, (devices, count), 1) // piece
    wide = jnp.where(along == lax.broadcasted_iota(jnp.int32, (devices, count), 0), 1.0, 0.0).astype(jnp.bfloat16)
    rows = jnp.dot(tall, pieces, preferred_element_type=jnp.float32).astype(jnp.bfloat16)
    both = jnp.dot(rows, wide, preferred_element_type=jnp.float32)
    same = lax.broadcasted_iota(jnp.int32, (count, count), 0) % piece == lax.broadcasted_iota(jnp.int32, (count, count), 1) % piece
    one_hot = jnp.where(same, both, 0.0).astype(jnp.bfloat16)
    moved = jnp.dot(one_hot, rows_ref[...], preferred_element_type=jnp.float32).astype(jnp.bfloat16)
    out_ref[...] = moved.reshape(out_ref.shape)


def sort_rows(tokens, placement, groups):
    count, width = tokens.shape
    rows = count // groups
    tile = 1024
    return pl.pallas_call(
        sort_kernel,
        out_shape=jax.ShapeDtypeStruct((groups, rows, width), tokens.dtype),
        grid=(width // tile,),
        in_specs=[
            pl.BlockSpec(placement.shape, lambda i: (0, 0)),
            pl.BlockSpec((count, tile), lambda i: (0, i)),
        ],
        out_specs=pl.BlockSpec((groups, rows, tile), lambda i: (0, 0, i)),
        compiler_params=pltpu.CompilerParams(vmem_limit_bytes=60 * 2**20),
        name="sort_rows",
    )(placement, tokens)


def unsort_kernel(target_ref, rows_ref, out_ref):
    count = out_ref.shape[0]
    order = lax.broadcasted_iota(jnp.int32, (count, count), 1)
    one_hot = jnp.where(order == target_ref[...], 1.0, 0.0).astype(jnp.bfloat16)
    rows = rows_ref[...].reshape(count, out_ref.shape[1])
    out_ref[...] = jnp.dot(one_hot, rows, preferred_element_type=jnp.float32).astype(jnp.bfloat16)


def unsort_rows(returned, target):
    groups, blocks, rows, width = returned.shape
    count = groups * rows
    return pl.pallas_call(
        unsort_kernel,
        out_shape=jax.ShapeDtypeStruct((count, blocks * width), returned.dtype),
        grid=(blocks,),
        in_specs=[
            pl.BlockSpec((count, 1), lambda i: (0, 0)),
            pl.BlockSpec((groups, None, rows, width), lambda i: (0, i, 0, 0)),
        ],
        out_specs=pl.BlockSpec((count, width), lambda i: (0, i)),
        compiler_params=pltpu.CompilerParams(vmem_limit_bytes=32 * 2**20),
        name="unsort_rows",
    )(target.reshape(count, 1), returned)


def own_columns(projection, member):
    query_width, key_width = HEADS * HEAD_DIM, KV_HEADS * HEAD_DIM
    return jnp.concatenate(
        [
            lax.dynamic_slice_in_dim(projection, member * GROUP * HEAD_DIM, GROUP * HEAD_DIM, 1),
            lax.dynamic_slice_in_dim(projection, query_width + member * HEAD_DIM, HEAD_DIM, 1),
            lax.dynamic_slice_in_dim(projection, query_width + key_width + member * HEAD_DIM, HEAD_DIM, 1),
        ],
        axis=1,
    )


UP, DOWN, OVER = (tuple((i, (i + d) % 4) for i in range(4)) for d in (1, 3, 2))


def ring_blocks(block, axis):
    others = [lax.ppermute(block, axis, way) for way in (UP, DOWN, OVER)]
    return jnp.concatenate([block] + others, axis=0)


def both_ways(block, axis):
    return [block, lax.ppermute(block, axis, UP), lax.ppermute(block, axis, DOWN)]


def far_halves(blocks, axis):
    half = blocks[0].shape[0] // 2
    return [lax.ppermute(blocks[1][:half], axis, UP), lax.ppermute(blocks[2][half:], axis, DOWN)]


RING = (0, 3, 1, 2)
SPAN = ((0, (0, 1, 2, 3)), (3, (0, 1, 2, 3)), (1, (0, 1, 2, 3)), (2, (0, 1)), (2, (2, 3)))


def weight_places(rows):
    x, y, zh = lax.axis_index("x"), lax.axis_index("y"), lax.axis_index("zh")
    places = [(i * 2 + zh) * rows for i in range(16)]
    for side in range(2):
        for outer, inners in SPAN:
            for inner in inners:
                near, far = (outer, RING[inner]) if side == 0 else (RING[inner], outer)
                places.append(((x + near) % 4 * 8 + (y + far) % 4 * 2 + 1 - zh) * rows)
    return jnp.stack(places)


def project_kernel(parts, places_ref, *refs):
    row_refs, refs = refs[:parts], refs[parts:]
    pieces, out_refs, ordered = refs[: -parts - 1], refs[-parts - 1 : -1], refs[-1]
    half = out_refs[0].shape[1] // 2
    step = 128

    def take(first, count):
        for i in range(count):
            column = pl.multiple_of(places_ref[first + i], step)
            at = 0
            for rows in row_refs:
                ordered[at : at + rows.shape[0], i * step : (i + 1) * step] = rows[:, pl.ds(column, step)]
                at += rows.shape[0]

    def product(pieces):
        total, at = None, 0
        for piece in pieces:
            depth = piece.shape[0]
            term = jnp.dot(ordered[:, at : at + depth], piece[...], preferred_element_type=jnp.float32)
            total = term if total is None else total + term
            at += depth
        return total

    take(0, 16)
    out = product(pieces[:1])
    for side in range(2):
        take(16 + side * 16, 16)
        columns = slice(side * half, (side + 1) * half)
        here = (out[:, columns] + product(pieces[1 + side * 5 : 6 + side * 5])).astype(jnp.bfloat16)
        at = 0
        for out_ref in out_refs:
            out_ref[:, columns] = here[at : at + out_ref.shape[0]]
            at += out_ref.shape[0]


def project(places, pieces, rows):
    count, depth = sum(r.shape[0] for r in rows), rows[0].shape[1]
    width = pieces[0].shape[1]
    whole = pl.BlockSpec(memory_space=pltpu.VMEM)
    return pl.pallas_call(
        functools.partial(project_kernel, len(rows)),
        out_shape=[jax.ShapeDtypeStruct((r.shape[0], width), jnp.bfloat16) for r in rows],
        in_specs=[pl.BlockSpec(memory_space=pltpu.SMEM)] + [whole] * (len(rows) + len(pieces)),
        out_specs=[whole] * len(rows),
        scratch_shapes=[pltpu.VMEM((count, depth // 2), jnp.bfloat16)],
        compiler_params=pltpu.CompilerParams(vmem_limit_bytes=24 * 2**20),
        cost_estimate=pl.CostEstimate(flops=1, bytes_accessed=1, transcendentals=0),
        name="project",
    )(places, *rows, *pieces)


def attention_kernel(late, member_ref, lengths_ref, *refs):
    lanes, (cos_ref, sin_ref) = refs[:4], refs[4:6]
    if late:
        early_keys, early_values, early_mixed, out_ref, queries, keys, values, mixed = refs[6:]
    else:
        keys, values, mixed, queries = refs[6:]
    blocks = 2
    part = BLOCK // 4
    span = BLOCK // blocks
    half = HEAD_DIM // 2
    member = member_ref[0]

    taken = lax.broadcasted_iota(jnp.int32, (BLOCK, BLOCK), 1)
    lane, rest = taken // part, taken % part
    group, block, row = rest // (2 * blocks), (rest // 2) % blocks, rest % 2
    placed = block * span + (group * 4 + (lane ^ member)) * 2 + row
    wanted = lax.broadcasted_iota(jnp.int32, (BLOCK, BLOCK), 0)
    forward = jnp.where(wanted == placed, 1.0, 0.0).astype(jnp.bfloat16)
    first_row = blocks * BLOCK if late else 0
    for h in range(2):
        chunk = jnp.concatenate([lane_ref[h * part : (h + 1) * part] for lane_ref in lanes], axis=0)
        chunk = jnp.dot(forward, chunk, preferred_element_type=jnp.float32)
        for s in range(blocks):
            at = s * BLOCK + h * span
            rows = slice(at, at + span)
            here = chunk[s * span : (s + 1) * span]
            cosine, sine = cos_ref[first_row + at : first_row + at + span], sin_ref[first_row + at : first_row + at + span]

            def rotate(x):
                return (x * cosine + pltpu.roll(x, half, 1) * sine).astype(jnp.bfloat16)

            for g in range(GROUP):
                queries[g, rows] = rotate(here[:, g * HEAD_DIM : (g + 1) * HEAD_DIM])
            keys[rows] = rotate(here[:, GROUP * HEAD_DIM : (GROUP + 1) * HEAD_DIM])
            values[rows] = here[:, (GROUP + 1) * HEAD_DIM :].astype(jnp.bfloat16)

    def reached(early, own, first, stop):
        base = blocks if late else 0
        parts = []
        if first < base:
            parts.append(early[first * BLOCK : base * BLOCK])
        parts.append(own[max(first - base, 0) * BLOCK : (stop - base) * BLOCK])
        return parts[0] if len(parts) == 1 else jnp.concatenate(parts, axis=0)

    scale = HEAD_DIM ** (-0.5)
    reach = (MOST - 1 + BLOCK - 1) // BLOCK
    for local in range(blocks):
        b = local + (blocks if late else 0)
        first = max(0, b - reach)
        width = (b + 1 - first) * BLOCK
        position = b * BLOCK + lax.broadcasted_iota(jnp.int32, (BLOCK, 1), 0)
        begin, end = jnp.zeros_like(position), jnp.int32(0)
        for j in range(lengths_ref.shape[1]):
            end = end + lengths_ref[0, j]
            begin = jnp.where(position >= end, end, begin)
        key_at = first * BLOCK + lax.broadcasted_iota(jnp.int32, (BLOCK, width), 1)
        allowed = (key_at >= begin) & (key_at <= position)
        key_block = reached(early_keys if late else None, keys, first, b + 1)
        value_block = reached(early_values if late else None, values, first, b + 1)
        rows = slice(local * BLOCK, (local + 1) * BLOCK)
        for g in range(GROUP):
            scores = lax.dot_general(
                queries[g, rows], key_block, (((1,), (1,)), ((), ())), preferred_element_type=jnp.float32
            )
            scores = jnp.where(allowed, scores * scale, -1e30)
            weights = jnp.exp(scores - jnp.max(scores, axis=1, keepdims=True))
            total = jnp.sum(weights, axis=1, keepdims=True)
            weighted = jnp.dot(
                weights.astype(jnp.bfloat16), value_block, preferred_element_type=jnp.float32
            )
            mixed[rows, g * HEAD_DIM : (g + 1) * HEAD_DIM] = (weighted / total).astype(jnp.bfloat16)

    if not late:
        return
    slots = 2 * blocks
    left = lax.broadcasted_iota(jnp.int32, (BLOCK, BLOCK), 0)
    source = ((left // 2) % slots) * part + (left // (2 * slots)) * 2 + left % 2
    backward = jnp.where(taken == source, 1.0, 0.0).astype(jnp.bfloat16)
    for h in range(slots):
        chunk = jnp.concatenate(
            [
                held[s * BLOCK + h * part : s * BLOCK + (h + 1) * part]
                for held in (early_mixed, mixed)
                for s in range(blocks)
            ],
            axis=0,
        )
        out_ref[h * BLOCK : (h + 1) * BLOCK] = jnp.dot(
            backward, chunk, preferred_element_type=jnp.float32
        ).astype(jnp.bfloat16)


def attend(member, lengths, lanes, tables, early=None):
    count = 2 * BLOCK
    late = early is not None
    whole = pl.BlockSpec(memory_space=pltpu.VMEM)
    scalars = pl.BlockSpec(memory_space=pltpu.SMEM)
    queries = (GROUP, count, HEAD_DIM)
    held = [(count, HEAD_DIM), (count, HEAD_DIM), (count, GROUP * HEAD_DIM)]
    outs = [(2 * count, GROUP * HEAD_DIM)] if late else held
    scratch = [queries] + held if late else [queries]
    early = list(early) if late else []
    return pl.pallas_call(
        functools.partial(attention_kernel, late),
        out_shape=[jax.ShapeDtypeStruct(shape, jnp.bfloat16) for shape in outs],
        in_specs=[scalars, scalars] + [whole] * (6 + len(early)),
        out_specs=[whole] * len(outs),
        scratch_shapes=[pltpu.VMEM(shape, jnp.bfloat16) for shape in scratch],
        compiler_params=pltpu.CompilerParams(vmem_limit_bytes=24 * 2**20),
        cost_estimate=pl.CostEstimate(flops=1, bytes_accessed=1, transcendentals=0),
        name="attend",
    )(member, lengths, *lanes, *tables, *early)


def on_device(tokens, projection, placement, doc_lengths):
    row_count, width = tokens.shape
    devices = placement.shape[1]
    members = lax.axis_size(CTX)
    groups = devices // members
    piece = row_count // devices
    member = lax.axis_index(CTX)
    across = [(0, 1), (1, 0)]
    depth = projection.shape[0]
    tie = lax.optimization_barrier

    mine = lax.all_gather(own_columns(projection, member), ("x", "y"), axis=0, tiled=True)
    places = weight_places(depth)
    outgoing = sort_rows(tokens, placement, groups)
    arrived = lax.all_to_all(outgoing, DP, 0, 0, tiled=True)

    theirs = lax.ppermute(own_columns(projection, member ^ 2), ("zh", "zl"), [(0, 3), (3, 0), (1, 2), (2, 1)])
    half = theirs.shape[1] // 2
    first, second = ring_blocks(theirs[:, :half], "y"), ring_blocks(theirs[:, half:], "x")
    first, second = both_ways(first, "x"), both_ways(second, "y")
    tables = rotary_tables(doc_lengths[0], members * row_count)
    arrived, first, second, tables, places = tie((arrived, first, second, tables, places))

    rows = members * piece // 2
    early, late = (
        arrived[:, i * rows : (i + 1) * rows].reshape(groups * rows, width) for i in range(2)
    )
    far_early = lax.ppermute(early, "zl", across)
    first_far, second_far = far_halves(first, "x"), far_halves(second, "y")
    far_early, early, late, first_far, second_far = tie((far_early, early, late, first_far, second_far))

    far_late = lax.ppermute(late, "zl", across)
    near_early, near_late, last_early = (lax.ppermute(r, "core", across) for r in (early, late, far_early))
    pieces = [mine, *first, *first_far, *second, *second_far]
    own = project(places, pieces, [early, near_early, late, near_late])
    others = project(places, pieces, [far_early, last_early])
    held = attend(member.reshape(1), doc_lengths, [own[0], own[1], *others], tables)
    far_late, held = tie((far_late, held))
    last_late = lax.ppermute(far_late, "core", across)
    others = project(places, pieces, [far_late, last_late])
    mixed = attend(member.reshape(1), doc_lengths, [own[2], own[3], *others], tables, held)[0]

    returned = lax.all_to_all(
        mixed.reshape(devices, members * piece, GROUP * HEAD_DIM), EVERY, 0, 0, tiled=True
    )
    target = (placement[0][:, None] * piece + jnp.arange(piece, dtype=jnp.int32)[None, :]).reshape(row_count)
    return unsort_rows(returned.reshape(groups, members, members * piece, GROUP * HEAD_DIM), target)


def solution(mesh):
    sizes = {"x": 4, "y": 4, "zh": 2, "zl": 2, "core": 2}
    fine = Mesh(mesh.devices.reshape(tuple(sizes.values())), tuple(sizes))
    return jax.shard_map(
        on_device,
        mesh=fine,
        in_specs=(P(EVERY, None), P(DP, None), P(EVERY, None), P(DP, None)),
        out_specs=P(EVERY, None),
        check_vma=False,
    )
```

time: 173 us -> 193 us (1.12)
  waiting for transfers between devices: 63.1 us -> 78.6 us
  starting transfers between devices: 42.3 us -> 47.6 us
  other arithmetic: 7.88 us -> 3.38 us
  local copies, waits for them, and re-layouts: 15.8 us -> 18 us
  Pallas kernels: 29.6 us -> 31.6 us
    ppermute x20 -> x21, waiting for transfers between devices: 15.4 us -> 59.5 us  [the longest x1 22.5 us: on_device(): lax.ppermute(own_columns(projection, member ^ 2), ('zh', 'zl'), [(0, 3),...]
    all_to_all x1, waiting for transfers between devices: 28.5 us -> 0.01 us  [on_device(): arrived = lax.all_to_all(outgoing, DP, 0, 0, tiled=True)]
    ppermute x20 -> x21, starting transfers between devices: 25.3 us -> 30.9 us  [the longest x6 13.1 us: ring_blocks(): others = [lax.ppermute(block, axis, way) for way in (UP, DOWN, OVER)]]
    unnamed x20 -> x16, local copies, waits for them, and re-layouts: 8.63 us -> 4.1 us
    reshape x0 -> x2, local copies, waits for them, and re-layouts: none -> 4.34 us  [on_device(): arrived[:, i * rows:(i + 1) * rows].reshape(groups * rows, width)]
    slice x9 -> x6, local copies, waits for them, and re-layouts: 3.78 us -> 7.54 us  [the longest x1 4.72 us: on_device(): arrived[:, i * rows:(i + 1) * rows].reshape(groups * rows, width)]
    pallas_call x1, Pallas kernels: 1.49 us -> 4.97 us  [sort_rows(): pl.pallas_call(sort_kernel, out_shape=jax.ShapeDtypeStruct((groups, rows,...]
    concatenate x1, other arithmetic: 3.02 us -> 0.34 us  [rotary_tables(): jnp.concatenate([cosine, cosine], axis=1)]
  transfers between devices with their start and end apart: 23 -> 24, of which waited for: 10 -> 13; matrix products, arithmetic and copies ran while one was open for 9% -> 8% of each run, Pallas kernels for 9% -> 10%
where the time goes in v3:
time: 193 us
  waiting for transfers between devices  78.6 us (41%)
  starting transfers between devices  47.6 us (25%)
  Pallas kernels  31.6 us (16%)
  local copies, waits for them, and re-layouts  18 us (9%)
  between operations  13.6 us (7%)
  other arithmetic  3.38 us (2%)
    ppermute x1, waiting for transfers between devices, on_device(): lax.ppermute(own_columns(projection, member ^ 2), ('zh', 'zl'), [(0, 3),...  22.5 us
    all_to_all x1, waiting for transfers between devices, on_device(): lax.all_to_all(mixed.reshape(devices, members * piece, GROUP * HEAD_DIM),...  19.1 us
    pallas_call x3, Pallas kernels, project(): pl.pallas_call(functools.partial(project_kernel, len(rows)), out_shape=[j...  15 us
    ppermute x6, starting transfers between devices, ring_blocks(): others = [lax.ppermute(block, axis, way) for way in (UP, DOWN, OVER)]  13.1 us
    ppermute x1, waiting for transfers between devices, on_device(): far_early = lax.ppermute(early, 'zl', across)  12.3 us
    all_to_all x1, starting transfers between devices, on_device(): arrived = lax.all_to_all(outgoing, DP, 0, 0, tiled=True)  11.5 us
    pallas_call x2, Pallas kernels, attend(): pl.pallas_call(functools.partial(attention_kernel, late), out_shape=[jax....  9.3 us
    ppermute x2, waiting for transfers between devices, both_ways(): lax.ppermute(block, axis, DOWN)  7.71 us
  transfers between devices with their start and end apart: 24, of which 13 were waited for; matrix products, arithmetic and copies ran while one was open for 8% of the time, Pallas kernels for 10%

profile of v3, /device:TPU:1, one launch (start us, length us, event | category | flops | bytes accessed | tf_op | source)
XLA Modules:
  0.0 192.8 jit_solution(16095953525231064912)
XLA Ops:
  6.5 1.0 constant_dynamic-slice_fusion.1
  7.5 0.8 constant_dynamic-slice_fusion
  8.4 0.7 pad_maximum_fusion.5
  9.0 0.0 all-gather.2.cloned.1.call-update
  9.1 5.0 %sort_rows.1 = bf16[32,8,4096]{2,1,0:T(8,128)(2,1)} custom-call(s32[1,128]{1,0:T(1,128)} %placement_ref.1, bf16[256,4096]{1,0:T(8,128)(2,1)} %rows_ref.1), custom_call_target="tpu_custom_call" | custom-call | tf_op jit(solution)/shard_map/sort_rows/pallas_call | solution.py:58
  14.0 11.5 %all-to-all-start = ((bf16[32,8,4096]{2,1,0:T(8,128)(2,1)}), bf16[32,8,4096]{2,1,0:T(8,128)(2,1)}, u32[]{:S(2)}, u32[]{:S(2)}) async-start(bf16[32,8,4096]{2,1,0:T(8,128)(2,1)} %sort_rows.1), calls=%async_computation | async-start | bytes 4194304 | tf_op jit(solution)/shard_map/all_to_all | solution.py:320
  25.5 2.9 %collective-permute-start = (bf16[128,768]{1,0:T(8,128)(2,1)S(1)}, bf16[128,768]{1,0:T(8,128)(2,1)S(1)}, u32[]{:S(2)}, u32[]{:S(2)}) collective-permute-start(bf16[128,768]{1,0:T(8,128)(2,1)S(1)} %pad_maximum_fusion.4), channel_id=1, source_target_pairs={{0,6},{6,0},{2,4},{4,2},{1,7},{7,1},{3,5},{5,3},{8,14},{14,8},{10,... | collective-permute-start | bytes 589832 | tf_op jit(solution)/shard_map/ppermute | solution.py:322
  28.4 0.2 reduce-window.8
  28.6 0.1 stack.147.places_ref
  28.7 0.1 select_reduce_fusion
  28.8 22.5 %collective-permute-done = bf16[128,768]{1,0:T(8,128)(2,1)S(1)} collective-permute-done((bf16[128,768]{1,0:T(8,128)(2,1)S(1)}, bf16[128,768]{1,0:T(8,128)(2,1)S(1)}, u32[]{:S(2)}, u32[]{:S(2)}) %collective-permute-start) | collective-permute-done | bytes 196640 | tf_op jit(solution)/shard_map/ppermute | solution.py:322
  51.3 0.1 collective-permute-start.6
  51.4 6.7 %collective-permute-start.7 = (bf16[128,384]{1,0:T(8,128)(2,1)S(1)}, bf16[128,384]{1,0:T(8,128)(2,1)S(1)}, u32[]{:S(2)}, u32[]{:S(2)}) collective-permute-start(bf16[128,384]{1,0:T(8,128)(2,1)S(1)} %get-tuple-element.77), channel_id=1, source_target_pairs={{0,96},{32,0},{64,32},{96,64},{1,97},{33,1},{65,33},{97,65},{2,98}... | collective-permute-start | bytes 294920 | tf_op jit(solution)/shard_map/ppermute | solution.py:113
  58.1 1.1 collective-permute-start.8
  59.2 2.3 %collective-permute-start.1 = (bf16[128,384]{1,0:T(8,128)(2,1)S(1)}, bf16[128,384]{1,0:T(8,128)(2,1)S(1)}, u32[]{:S(2)}, u32[]{:S(2)}) collective-permute-start(bf16[128,384]{1,0:T(8,128)(2,1)S(1)} %get-tuple-element.78), channel_id=1, source_target_pairs={{0,8},{8,16},{16,24},{24,0},{1,9},{9,17},{17,25},{25,1},{2,10},{10... | collective-permute-start | bytes 294920 | tf_op jit(solution)/shard_map/ppermute | solution.py:113
  61.5 1.4 collective-permute-start.2
  62.9 1.6 collective-permute-start.3
  64.5 1.8 collective-permute-done.8
  66.2 3.1 %collective-permute-start.10 = (bf16[512,384]{1,0:T(8,128)(2,1)S(1)}, bf16[512,384]{1,0:T(8,128)(2,1)S(1)}, u32[]{:S(2)}, u32[]{:S(2)}) collective-permute-start(bf16[512,384]{1,0:T(8,128)(2,1)S(1)} %pad_maximum_fusion.3.refs_10_.refs_8_), channel_id=1, source_target_pairs={{0,24},{8,0},{16,8},{24,16},{1,25},{9,1},{17,9},{25,17},{2,26},{10... | collective-permute-start | bytes 1179656 | tf_op jit(solution)/shard_map/ppermute | solution.py:118
  69.3 3.7 %collective-permute-done.3 = bf16[128,384]{1,0:T(8,128)(2,1)S(1)} collective-permute-done((bf16[128,384]{1,0:T(8,128)(2,1)S(1)}, bf16[128,384]{1,0:T(8,128)(2,1)S(1)}, u32[]{:S(2)}, u32[]{:S(2)}) %collective-permute-start.3) | collective-permute-done | bytes 98336 | tf_op jit(solution)/shard_map/ppermute | solution.py:113
  73.1 0.1 collective-permute-start.4
  73.2 2.7 %collective-permute-start.5 = (bf16[512,384]{1,0:T(8,128)(2,1)S(1)}, bf16[512,384]{1,0:T(8,128)(2,1)S(1)}, u32[]{:S(2)}, u32[]{:S(2)}) collective-permute-start(bf16[512,384]{1,0:T(8,128)(2,1)S(1)} %pad_maximum_fusion.2.refs_5_.refs_3_), channel_id=1, source_target_pairs={{0,96},{32,0},{64,32},{96,64},{1,97},{33,1},{65,33},{97,65},{2,98}... | collective-permute-start | bytes 1179656 | tf_op jit(solution)/shard_map/ppermute | solution.py:118
  75.8 1.9 fusion
  77.7 0.3 pad_maximum_fusion
  78.1 7.7 %collective-permute-done.10.refs_12_.refs_10_ = bf16[512,384]{1,0:T(8,128)(2,1)S(1)} collective-permute-done((bf16[512,384]{1,0:T(8,128)(2,1)S(1)}, bf16[512,384]{1,0:T(8,128)(2,1)S(1)}, u32[]{:S(2)}, u32[]{:S(2)}) %collective-permute-start.10) | collective-permute-done | bytes 393248 | tf_op jit(solution)/shard_map/ppermute | solution.py:118
  85.8 1.3 collective-permute-done.9.refs_11_.refs_9_
  87.1 0.4 collective-permute-done.4.refs_6_.refs_4_
  87.4 0.0 collective-permute-done.5.refs_7_.refs_5_
  87.5 0.0 all-to-all-done
  87.5 4.7 %fusion.1 = (bf16[32,4,4096]{2,1,0:T(4,128)(2,1)}, bf16[32,4,4096]{2,1,0:T(4,128)(2,1)}) fusion(bf16[32,8,4096]{2,1,0:T(8,128)(2,1)} %all-to-all-done), kind=kLoop, calls=%fused_computation.21 | loop fusion | bytes 4194304 | tf_op jit(solution)/shard_map/slice | solution.py:331
  92.2 2.2 %reshape.86.refs_0_ = bf16[128,4096]{1,0:T(8,128)(2,1)} reshape(bf16[32,4,4096]{2,1,0:T(4,128)(2,1)} %get-tuple-element.70) | data formatting | bytes 2097152 | tf_op jit(solution)/shard_map/reshape | solution.py:331
  94.4 0.7 slice.28
  95.0 0.2 collective-permute-start.12
  95.3 0.7 slice.29
  96.0 2.4 %collective-permute-start.13 = (bf16[256,384]{1,0:T(8,128)(2,1)}, bf16[256,384]{1,0:T(8,128)(2,1)}, u32[]{:S(2)}, u32[]{:S(2)}) collective-permute-start(bf16[256,384]{1,0:T(8,128)(2,1)} %slice.29), channel_id=1, source_target_pairs={{0,96},{32,0},{64,32},{96,64},{1,97},{33,1},{65,33},{97,65},{2,98}... | collective-permute-start | bytes 589832 | tf_op jit(solution)/shard_map/ppermute | solution.py:123
  98.4 0.7 slice.30
  99.1 0.7 slice.31
  99.8 2.7 %collective-permute-start.15 = (bf16[256,384]{1,0:T(8,128)(2,1)}, bf16[256,384]{1,0:T(8,128)(2,1)}, u32[]{:S(2)}, u32[]{:S(2)}) collective-permute-start(bf16[256,384]{1,0:T(8,128)(2,1)} %slice.31), channel_id=1, source_target_pairs={{0,24},{8,0},{16,8},{24,16},{1,25},{9,1},{17,9},{25,17},{2,26},{10... | collective-permute-start | bytes 589832 | tf_op jit(solution)/shard_map/ppermute | solution.py:123
  102.5 2.2 %reshape.87.refs_2_ = bf16[128,4096]{1,0:T(8,128)(2,1)} reshape(bf16[32,4,4096]{2,1,0:T(4,128)(2,1)} %get-tuple-element.69) | data formatting | bytes 2097152 | tf_op jit(solution)/shard_map/reshape | solution.py:331
  104.7 0.5 collective-permute-done.14.refs_13_.refs_11_
  105.2 0.3 collective-permute-done.15.refs_14_.refs_12_
  105.4 12.3 %collective-permute-done.11.refs_0_ = bf16[128,4096]{1,0:T(8,128)(2,1)} collective-permute-done((bf16[128,4096]{1,0:T(8,128)(2,1)}, bf16[128,4096]{1,0:T(8,128)(2,1)}, u32[]{:S(2)}, u32[]{:S(2)}) %collective-permute-start.11) | collective-permute-done | bytes 1048608 | tf_op jit(solution)/shard_map/ppermute | solution.py:333
  117.7 2.5 %collective-permute-start.19 = (bf16[128,4096]{1,0:T(8,128)(2,1)}, bf16[128,4096]{1,0:T(8,128)(2,1)S(1)}, u32[]{:S(2)}, u32[]{:S(2)}) collective-permute-start(bf16[128,4096]{1,0:T(8,128)(2,1)} %collective-permute-done.11.refs_0_), channel_id=1, source_target_pairs={{0,1},{1,0},{2,3},{3,2},{4,5},{5,4},{6,7},{7,6},{8,9},{9,8},{10,11... | collective-permute-start | bytes 3145736 | tf_op jit(solution)/shard_map/ppermute | solution.py:338
  120.2 0.0 collective-permute-start.16
  120.2 0.5 collective-permute-start.17
  120.8 0.0 collective-permute-start.18
  120.8 3.4 %collective-permute-done.19.refs_1_ = bf16[128,4096]{1,0:T(8,128)(2,1)S(1)} collective-permute-done((bf16[128,4096]{1,0:T(8,128)(2,1)}, bf16[128,4096]{1,0:T(8,128)(2,1)S(1)}, u32[]{:S(2)}, u32[]{:S(2)}) %collective-permute-start.19) | collective-permute-done | bytes 1048608 | tf_op jit(solution)/shard_map/ppermute | solution.py:338
  124.2 1.0 copy-done.4
  125.2 1.9 copy-done
  127.1 1.2 copy-done.5
  128.3 4.2 %project.4 = (bf16[128,768]{1,0:T(8,128)(2,1)S(1)}, bf16[128,768]{1,0:T(8,128)(2,1)S(1)}) custom-call(s32[48]{0:T(128)S(1)} %stack.147.places_ref, bf16[128,4096]{1,0:T(8,128)(2,1)} %collective-permute-done.11.refs_0_, bf16[128,4096]{1,0:T(8,128)(2,1)S(1)} %copy-done.5, bf16[2048,768]{1,0:T(8,128)(2,1)S(1)} %copy-done, ...), custom_call_target="tpu_custom_call" | custom-call | flops 1 | bytes 1 | tf_op jit(solution)/shard_map/project/pallas_call | solution.py:180
  132.5 6.8 %project.3 = (bf16[128,768]{1,0:T(8,128)(2,1)S(1)}, bf16[128,768]{1,0:T(8,128)(2,1)S(1)}, bf16[128,768]{1,0:T(8,128)(2,1)S(1)}, bf16[128,768]{1,0:T(8,128)(2,1)S(1)}) custom-call(s32[48]{0:T(128)S(1)} %stack.147.places_ref, bf16[128,4096]{1,0:T(8,128)(2,1)S(1)} %copy-done.2, bf16[128,4096]{1,0:T(8,128)(2,1)} %collective-permute-done.16.refs_1_, ...), custom_call_target="tpu_custom_call" | custom-call | flops 1 | bytes 1 | tf_op jit(solution)/shard_map/project/pallas_call | solution.py:180
  139.3 3.4 %attend.2 = (bf16[512,128]{1,0:T(8,128)(2,1)S(1)}, bf16[512,128]{1,0:T(8,128)(2,1)S(1)}, bf16[512,512]{1,0:T(8,128)(2,1)S(1)}) custom-call(s32[1]{0:T(128)} %bitcast.1.member_ref, s32[1,8]{1,0:T(1,128)S(1)} %copy-done.6, bf16[128,768]{1,0:T(8,128)(2,1)S(1)} %get-tuple-element.53.refs_0_, bf16[128,768]{1,0:T(8,128)(2,1)S(1)} %get-tuple-element.54.refs_1_, ...), custom_call_target="tpu_custom_call" | custom-call | flops 1 | bytes 1 | tf_op jit(solution)/shard_map/attend/pallas_call | solution.py:294
  142.7 3.1 %collective-permute-done.18.refs_0_ = bf16[128,4096]{1,0:T(8,128)(2,1)} collective-permute-done((bf16[128,4096]{1,0:T(8,128)(2,1)}, bf16[128,4096]{1,0:T(8,128)(2,1)}, u32[]{:S(2)}, u32[]{:S(2)}) %collective-permute-start.18) | collective-permute-done | bytes 1048608 | tf_op jit(solution)/shard_map/ppermute | solution.py:337
  145.9 0.8 collective-permute-start.20
  146.6 2.5 %collective-permute-done.20.refs_1_ = bf16[128,4096]{1,0:T(8,128)(2,1)S(1)} collective-permute-done((bf16[128,4096]{1,0:T(8,128)(2,1)}, bf16[128,4096]{1,0:T(8,128)(2,1)S(1)}, u32[]{:S(2)}, u32[]{:S(2)}) %collective-permute-start.20) | collective-permute-done | bytes 1048608 | tf_op jit(solution)/shard_map/ppermute | solution.py:344
  149.1 4.1 %project.5 = (bf16[128,768]{1,0:T(8,128)(2,1)S(1)}, bf16[128,768]{1,0:T(8,128)(2,1)S(1)}) custom-call(s32[48]{0:T(128)S(1)} %stack.147.places_ref, bf16[128,4096]{1,0:T(8,128)(2,1)} %collective-permute-done.18.refs_0_, bf16[128,4096]{1,0:T(8,128)(2,1)S(1)} %collective-permute-done.20.refs_1_, bf16[2048,768]{1,0:T(8,128)(2,1)S(1)} %copy-done.1, ...), custom_call_target="tpu_custom_call" | custom-call | flops 1 | bytes 1 | tf_op jit(solution)/shard_map/project/pallas_call | solution.py:180
  153.2 0.0 copy-start.7
  153.2 5.9 %attend.3 = bf16[1024,512]{1,0:T(8,128)(2,1)} custom-call(s32[1]{0:T(128)} %bitcast.1.member_ref, s32[1,8]{1,0:T(1,128)S(1)} %copy-done.6, bf16[128,768]{1,0:T(8,128)(2,1)S(1)} %get-tuple-element.51.refs_0_, bf16[128,768]{1,0:T(8,128)(2,1)S(1)} %get-tuple-element.52.refs_1_, bf16[128,768]{1,0:T(8,128)(2,1)S(1)} %get-tuple-element.64.refs_2_, ...), custom_call_target="tpu_custom_call" | custom-call | flops 1 | bytes 1 | tf_op jit(solution)/shard_map/attend/pallas_call | solution.py:294
  159.1 5.2 %all-to-all-start.1 = ((bf16[128,8,512]{2,1,0:T(8,128)(2,1)}), bf16[128,8,512]{2,1,0:T(8,128)(2,1)S(1)}, u32[]{:S(2)}, u32[]{:S(2)}) async-start(bf16[128,8,512]{2,1,0:T(8,128)(2,1)} %bitcast.37), calls=%async_computation.1 | async-start | bytes 2097152 | tf_op jit(solution)/shard_map/all_to_all | solution.py:348
  164.4 0.1 iota_add_fusion
  164.5 0.1 add.406.target_ref
  164.6 19.1 %all-to-all-done.1 = bf16[128,8,512]{2,1,0:T(8,128)(2,1)S(1)} async-done(((bf16[128,8,512]{2,1,0:T(8,128)(2,1)}), bf16[128,8,512]{2,1,0:T(8,128)(2,1)S(1)}, u32[]{:S(2)}, u32[]{:S(2)}) %all-to-all-start.1) | async-done | bytes 1048608 | tf_op jit(solution)/shard_map/all_to_all | solution.py:348
  183.6 2.3 %unsort_rows.1 = bf16[256,2048]{1,0:T(8,128)(2,1)} custom-call(s32[256,1]{1,0:T(8,128)S(1)} %add.406.target_ref, bf16[32,4,8,512]{3,2,1,0:T(8,128)(2,1)S(1)} %bitcast.40), custom_call_target="tpu_custom_call" | custom-call | tf_op jit(solution)/shard_map/unsort_rows/pallas_call | solution.py:83
  (32 shorter events, 0.2 us)
Async XLA Ops:
  6.5 118.6 %all-gather.2.cloned.1.call-start = ((), (), s32[]{:S(2)}) async-start(), calls=%async_computation.2 | async-start | bytes 3342336 | tf_op jit(solution)/shard_map/all_gather | solution.py:317
  14.0 14.4 %copy-start.6 = (s32[1,8]{1,0:T(1,128)S(1)}, s32[1,8]{1,0:T(1,128)}, u32[]{:S(2)}) copy-start(s32[1,8]{1,0:T(1,128)} %lengths_ref.3) | copy-start | bytes 100
  14.0 73.4 %all-to-all-start = ((bf16[32,8,4096]{2,1,0:T(8,128)(2,1)}), bf16[32,8,4096]{2,1,0:T(8,128)(2,1)}, u32[]{:S(2)}, u32[]{:S(2)}) async-start(bf16[32,8,4096]{2,1,0:T(8,128)(2,1)} %sort_rows.1), calls=%async_computation | async-start | bytes 4194304 | tf_op jit(solution)/shard_map/all_to_all | solution.py:320
  25.5 25.8 %collective-permute-start = (bf16[128,768]{1,0:T(8,128)(2,1)S(1)}, bf16[128,768]{1,0:T(8,128)(2,1)S(1)}, u32[]{:S(2)}, u32[]{:S(2)}) collective-permute-start(bf16[128,768]{1,0:T(8,128)(2,1)S(1)} %pad_maximum_fusion.4), channel_id=1, source_target_pairs={{0,6},{6,0},{2,4},{4,2},{1,7},{7,1},{3,5},{5,3},{8,14},{14,8},{10,... | collective-permute-start | bytes 589832 | tf_op jit(solution)/shard_map/ppermute | solution.py:322
  51.3 11.6 %collective-permute-start.6 = (bf16[128,384]{1,0:T(8,128)(2,1)S(1)}, bf16[128,384]{1,0:T(8,128)(2,1)S(1)}, u32[]{:S(2)}, u32[]{:S(2)}) collective-permute-start(bf16[128,384]{1,0:T(8,128)(2,1)S(1)} %get-tuple-element.77), channel_id=1, source_target_pairs={{0,32},{32,64},{64,96},{96,0},{1,33},{33,65},{65,97},{97,1},{2,34}... | collective-permute-start | bytes 294920 | tf_op jit(solution)/shard_map/ppermute | solution.py:113
  51.4 13.0 %collective-permute-start.7 = (bf16[128,384]{1,0:T(8,128)(2,1)S(1)}, bf16[128,384]{1,0:T(8,128)(2,1)S(1)}, u32[]{:S(2)}, u32[]{:S(2)}) collective-permute-start(bf16[128,384]{1,0:T(8,128)(2,1)S(1)} %get-tuple-element.77), channel_id=1, source_target_pairs={{0,96},{32,0},{64,32},{96,64},{1,97},{33,1},{65,33},{97,65},{2,98}... | collective-permute-start | bytes 294920 | tf_op jit(solution)/shard_map/ppermute | solution.py:113
  58.1 8.1 %collective-permute-start.8 = (bf16[128,384]{1,0:T(8,128)(2,1)S(1)}, bf16[128,384]{1,0:T(8,128)(2,1)S(1)}, u32[]{:S(2)}, u32[]{:S(2)}) collective-permute-start(bf16[128,384]{1,0:T(8,128)(2,1)S(1)} %get-tuple-element.77), channel_id=1, source_target_pairs={{0,64},{32,96},{64,0},{96,32},{1,65},{33,97},{65,1},{97,33},{2,66}... | collective-permute-start | bytes 294920 | tf_op jit(solution)/shard_map/ppermute | solution.py:113
  59.2 10.1 %collective-permute-start.1 = (bf16[128,384]{1,0:T(8,128)(2,1)S(1)}, bf16[128,384]{1,0:T(8,128)(2,1)S(1)}, u32[]{:S(2)}, u32[]{:S(2)}) collective-permute-start(bf16[128,384]{1,0:T(8,128)(2,1)S(1)} %get-tuple-element.78), channel_id=1, source_target_pairs={{0,8},{8,16},{16,24},{24,0},{1,9},{9,17},{17,25},{25,1},{2,10},{10... | collective-permute-start | bytes 294920 | tf_op jit(solution)/shard_map/ppermute | solution.py:113
  61.5 7.8 %collective-permute-start.2 = (bf16[128,384]{1,0:T(8,128)(2,1)S(1)}, bf16[128,384]{1,0:T(8,128)(2,1)S(1)}, u32[]{:S(2)}, u32[]{:S(2)}) collective-permute-start(bf16[128,384]{1,0:T(8,128)(2,1)S(1)} %get-tuple-element.78), channel_id=1, source_target_pairs={{0,24},{8,0},{16,8},{24,16},{1,25},{9,1},{17,9},{25,17},{2,26},{10... | collective-permute-start | bytes 294920 | tf_op jit(solution)/shard_map/ppermute | solution.py:113
  62.9 10.1 %collective-permute-start.3 = (bf16[128,384]{1,0:T(8,128)(2,1)S(1)}, bf16[128,384]{1,0:T(8,128)(2,1)S(1)}, u32[]{:S(2)}, u32[]{:S(2)}) collective-permute-start(bf16[128,384]{1,0:T(8,128)(2,1)S(1)} %get-tuple-element.78), channel_id=1, source_target_pairs={{0,16},{8,24},{16,0},{24,8},{1,17},{9,25},{17,1},{25,9},{2,18},{10... | collective-permute-start | bytes 294920 | tf_op jit(solution)/shard_map/ppermute | solution.py:113
  66.2 19.5 %collective-permute-start.10 = (bf16[512,384]{1,0:T(8,128)(2,1)S(1)}, bf16[512,384]{1,0:T(8,128)(2,1)S(1)}, u32[]{:S(2)}, u32[]{:S(2)}) collective-permute-start(bf16[512,384]{1,0:T(8,128)(2,1)S(1)} %pad_maximum_fusion.3.refs_10_.refs_8_), channel_id=1, source_target_pairs={{0,24},{8,0},{16,8},{24,16},{1,25},{9,1},{17,9},{25,17},{2,26},{10... | collective-permute-start | bytes 1179656 | tf_op jit(solution)/shard_map/ppermute | solution.py:118
  69.3 17.8 %collective-permute-start.9 = (bf16[512,384]{1,0:T(8,128)(2,1)S(1)}, bf16[512,384]{1,0:T(8,128)(2,1)S(1)}, u32[]{:S(2)}, u32[]{:S(2)}) collective-permute-start(bf16[512,384]{1,0:T(8,128)(2,1)S(1)} %pad_maximum_fusion.3.refs_10_.refs_8_), channel_id=1, source_target_pairs={{0,8},{8,16},{16,24},{24,0},{1,9},{9,17},{17,25},{25,1},{2,10},{10... | collective-permute-start | bytes 1179656 | tf_op jit(solution)/shard_map/ppermute | solution.py:118
  73.1 14.4 %collective-permute-start.4 = (bf16[512,384]{1,0:T(8,128)(2,1)S(1)}, bf16[512,384]{1,0:T(8,128)(2,1)S(1)}, u32[]{:S(2)}, u32[]{:S(2)}) collective-permute-start(bf16[512,384]{1,0:T(8,128)(2,1)S(1)} %pad_maximum_fusion.2.refs_5_.refs_3_), channel_id=1, source_target_pairs={{0,32},{32,64},{64,96},{96,0},{1,33},{33,65},{65,97},{97,1},{2,34}... | collective-permute-start | bytes 1179656 | tf_op jit(solution)/shard_map/ppermute | solution.py:118
  73.2 14.3 %collective-permute-start.5 = (bf16[512,384]{1,0:T(8,128)(2,1)S(1)}, bf16[512,384]{1,0:T(8,128)(2,1)S(1)}, u32[]{:S(2)}, u32[]{:S(2)}) collective-permute-start(bf16[512,384]{1,0:T(8,128)(2,1)S(1)} %pad_maximum_fusion.2.refs_5_.refs_3_), channel_id=1, source_target_pairs={{0,96},{32,0},{64,32},{96,64},{1,97},{33,1},{65,33},{97,65},{2,98}... | collective-permute-start | bytes 1179656 | tf_op jit(solution)/shard_map/ppermute | solution.py:118
  94.3 23.4 %collective-permute-start.11 = (bf16[128,4096]{1,0:T(8,128)(2,1)}, bf16[128,4096]{1,0:T(8,128)(2,1)}, u32[]{:S(2)}, u32[]{:S(2)}) collective-permute-start(bf16[128,4096]{1,0:T(8,128)(2,1)} %reshape.86.refs_0_), channel_id=1, source_target_pairs={{0,2},{2,0},{1,3},{3,1},{4,6},{6,4},{5,7},{7,5},{8,10},{10,8},{9,1... | collective-permute-start | bytes 3145736 | tf_op jit(solution)/shard_map/ppermute | solution.py:333
  95.0 9.6 %collective-permute-start.12 = (bf16[256,384]{1,0:T(8,128)(2,1)}, bf16[256,384]{1,0:T(8,128)(2,1)}, u32[]{:S(2)}, u32[]{:S(2)}) collective-permute-start(bf16[256,384]{1,0:T(8,128)(2,1)} %slice.28), channel_id=1, source_target_pairs={{0,32},{32,64},{64,96},{96,0},{1,33},{33,65},{65,97},{97,1},{2,34}... | collective-permute-start | bytes 589832 | tf_op jit(solution)/shard_map/ppermute | solution.py:123
  96.0 8.7 %collective-permute-start.13 = (bf16[256,384]{1,0:T(8,128)(2,1)}, bf16[256,384]{1,0:T(8,128)(2,1)}, u32[]{:S(2)}, u32[]{:S(2)}) collective-permute-start(bf16[256,384]{1,0:T(8,128)(2,1)} %slice.29), channel_id=1, source_target_pairs={{0,96},{32,0},{64,32},{96,64},{1,97},{33,1},{65,33},{97,65},{2,98}... | collective-permute-start | bytes 589832 | tf_op jit(solution)/shard_map/ppermute | solution.py:123
  99.1 6.0 %collective-permute-start.14 = (bf16[256,384]{1,0:T(8,128)(2,1)}, bf16[256,384]{1,0:T(8,128)(2,1)}, u32[]{:S(2)}, u32[]{:S(2)}) collective-permute-start(bf16[256,384]{1,0:T(8,128)(2,1)} %slice.30), channel_id=1, source_target_pairs={{0,8},{8,16},{16,24},{24,0},{1,9},{9,17},{17,25},{25,1},{2,10},{10... | collective-permute-start | bytes 589832 | tf_op jit(solution)/shard_map/ppermute | solution.py:123
  99.8 5.6 %collective-permute-start.15 = (bf16[256,384]{1,0:T(8,128)(2,1)}, bf16[256,384]{1,0:T(8,128)(2,1)}, u32[]{:S(2)}, u32[]{:S(2)}) collective-permute-start(bf16[256,384]{1,0:T(8,128)(2,1)} %slice.31), channel_id=1, source_target_pairs={{0,24},{8,0},{16,8},{24,16},{1,25},{9,1},{17,9},{25,17},{2,26},{10... | collective-permute-start | bytes 589832 | tf_op jit(solution)/shard_map/ppermute | solution.py:123
  117.7 6.5 %collective-permute-start.19 = (bf16[128,4096]{1,0:T(8,128)(2,1)}, bf16[128,4096]{1,0:T(8,128)(2,1)S(1)}, u32[]{:S(2)}, u32[]{:S(2)}) collective-permute-start(bf16[128,4096]{1,0:T(8,128)(2,1)} %collective-permute-done.11.refs_0_), channel_id=1, source_target_pairs={{0,1},{1,0},{2,3},{3,2},{4,5},{5,4},{6,7},{7,6},{8,9},{9,8},{10,11... | collective-permute-start | bytes 3145736 | tf_op jit(solution)/shard_map/ppermute | solution.py:338
  120.2 12.3 %collective-permute-start.16 = (bf16[128,4096]{1,0:T(8,128)(2,1)}, bf16[128,4096]{1,0:T(8,128)(2,1)}, u32[]{:S(2)}, u32[]{:S(2)}) collective-permute-start(bf16[128,4096]{1,0:T(8,128)(2,1)} %reshape.86.refs_0_), channel_id=1, source_target_pairs={{0,1},{1,0},{2,3},{3,2},{4,5},{5,4},{6,7},{7,6},{8,9},{9,8},{10,11... | collective-permute-start | bytes 3145736 | tf_op jit(solution)/shard_map/ppermute | solution.py:338
  120.2 12.3 %collective-permute-start.17 = (bf16[128,4096]{1,0:T(8,128)(2,1)}, bf16[128,4096]{1,0:T(8,128)(2,1)}, u32[]{:S(2)}, u32[]{:S(2)}) collective-permute-start(bf16[128,4096]{1,0:T(8,128)(2,1)} %reshape.87.refs_2_), channel_id=1, source_target_pairs={{0,1},{1,0},{2,3},{3,2},{4,5},{5,4},{6,7},{7,6},{8,9},{9,8},{10,11... | collective-permute-start | bytes 3145736 | tf_op jit(solution)/shard_map/ppermute | solution.py:338
  120.8 25.1 %collective-permute-start.18 = (bf16[128,4096]{1,0:T(8,128)(2,1)}, bf16[128,4096]{1,0:T(8,128)(2,1)}, u32[]{:S(2)}, u32[]{:S(2)}) collective-permute-start(bf16[128,4096]{1,0:T(8,128)(2,1)} %reshape.87.refs_2_), channel_id=1, source_target_pairs={{0,2},{2,0},{1,3},{3,1},{4,6},{6,4},{5,7},{7,5},{8,10},{10,8},{9,1... | collective-permute-start | bytes 3145736 | tf_op jit(solution)/shard_map/ppermute | solution.py:337
  124.2 1.0 copy-start.4
  125.2 1.9 copy-start
  127.1 1.2 copy-start.5
  128.3 4.2 %copy-start.1 = (bf16[2048,768]{1,0:T(8,128)(2,1)S(1)}, bf16[2048,768]{1,0:T(8,128)(2,1)}, u32[]{:S(2)}) copy-start(bf16[2048,768]{1,0:T(8,128)(2,1)} %all-gather.2.cloned.1.call-done.refs_4_.refs_2_) | copy-start | bytes 9437188
  128.3 4.2 %copy-start.2 = (bf16[128,4096]{1,0:T(8,128)(2,1)S(1)}, bf16[128,4096]{1,0:T(8,128)(2,1)}, u32[]{:S(2)}) copy-start(bf16[128,4096]{1,0:T(8,128)(2,1)} %reshape.86.refs_0_) | copy-start | bytes 3145732
  128.3 4.2 %copy-start.3 = (bf16[128,4096]{1,0:T(8,128)(2,1)S(1)}, bf16[128,4096]{1,0:T(8,128)(2,1)}, u32[]{:S(2)}) copy-start(bf16[128,4096]{1,0:T(8,128)(2,1)} %reshape.87.refs_2_) | copy-start | bytes 3145732
  145.9 3.3 %collective-permute-start.20 = (bf16[128,4096]{1,0:T(8,128)(2,1)}, bf16[128,4096]{1,0:T(8,128)(2,1)S(1)}, u32[]{:S(2)}, u32[]{:S(2)}) collective-permute-start(bf16[128,4096]{1,0:T(8,128)(2,1)} %collective-permute-done.18.refs_0_), channel_id=1, source_target_pairs={{0,1},{1,0},{2,3},{3,2},{4,5},{5,4},{6,7},{7,6},{8,9},{9,8},{10,11... | collective-permute-start | bytes 3145736 | tf_op jit(solution)/shard_map/ppermute | solution.py:344
  153.2 11.2 %copy-start.7 = (s32[1,128]{1,0:T(1,128)S(1)}, s32[1,128]{1,0:T(1,128)}, u32[]{:S(2)}) copy-start(s32[1,128]{1,0:T(1,128)} %placement_ref.1) | copy-start | bytes 1540
  159.1 24.5 %all-to-all-start.1 = ((bf16[128,8,512]{2,1,0:T(8,128)(2,1)}), bf16[128,8,512]{2,1,0:T(8,128)(2,1)S(1)}, u32[]{:S(2)}, u32[]{:S(2)}) async-start(bf16[128,8,512]{2,1,0:T(8,128)(2,1)} %bitcast.37), calls=%async_computation.1 | async-start | bytes 2097152 | tf_op jit(solution)/shard_map/all_to_all | solution.py:348
Sparse Core Ops, SparseCore 0:
  9.5 74.6 all-gather.1

commit v4 on v2

--- a/solution.py
+++ b/solution.py
@@ -33,30 +33,46 @@
     return jnp.concatenate([cosine, cosine], axis=1), jnp.concatenate([-sine, sine], axis=1)
 
 
-def sort_kernel(target_ref, rows_ref, out_ref):
+def sort_kernel(placement_ref, rows_ref, out_ref, one_hot):
     count = rows_ref.shape[0]
-    order = lax.broadcasted_iota(jnp.int32, (count, count), 0)
-    one_hot = jnp.where(order == target_ref[...], 1.0, 0.0).astype(jnp.bfloat16)
-    moved = jnp.dot(one_hot, rows_ref[...], preferred_element_type=jnp.float32).astype(jnp.bfloat16)
+    devices = placement_ref.shape[1]
+    piece = count // devices
+
+    @pl.when(pl.program_id(0) == 0)
+    def _():
+        device = lax.broadcasted_iota(jnp.int32, (devices, devices), 0)
+        pieces = jnp.where(device == placement_ref[...], 1.0, 0.0).astype(jnp.bfloat16)
+        down = lax.broadcasted_iota(jnp.int32, (count, devices), 0) // piece
+        tall = jnp.where(down == lax.broadcasted_iota(jnp.int32, (count, devices), 1), 1.0, 0.0).astype(jnp.bfloat16)
+        along = lax.broadcasted_iota(jnp.int32, (devices, count), 1) // piece
+        wide = jnp.where(along == lax.broadcasted_iota(jnp.int32, (devices, count), 0), 1.0, 0.0).astype(jnp.bfloat16)
+        rows = jnp.dot(tall, pieces, preferred_element_type=jnp.float32).astype(jnp.bfloat16)
+        both = jnp.dot(rows, wide, preferred_element_type=jnp.float32)
+        row = lax.broadcasted_iota(jnp.int32, (count, count), 0) % piece
+        same = row == lax.broadcasted_iota(jnp.int32, (count, count), 1) % piece
+        one_hot[...] = jnp.where(same, both, 0.0).astype(jnp.bfloat16)
+
+    moved = jnp.dot(one_hot[...], rows_ref[...], preferred_element_type=jnp.float32).astype(jnp.bfloat16)
     out_ref[...] = moved.reshape(out_ref.shape)
 
 
-def sort_rows(tokens, target, groups):
+def sort_rows(tokens, placement, groups):
     count, width = tokens.shape
     rows = count // groups
-    tile = 1024
+    tile = 512
     return pl.pallas_call(
         sort_kernel,
         out_shape=jax.ShapeDtypeStruct((groups, rows, width), tokens.dtype),
         grid=(width // tile,),
         in_specs=[
-            pl.BlockSpec((1, count), lambda i: (0, 0)),
+            pl.BlockSpec(placement.shape, lambda i: (0, 0)),
             pl.BlockSpec((count, tile), lambda i: (0, i)),
         ],
         out_specs=pl.BlockSpec((groups, rows, tile), lambda i: (0, 0, i)),
-        compiler_params=pltpu.CompilerParams(vmem_limit_bytes=32 * 2**20),
+        scratch_shapes=[pltpu.VMEM((count, count), jnp.bfloat16)],
+        compiler_params=pltpu.CompilerParams(vmem_limit_bytes=60 * 2**20),
         name="sort_rows",
-    )(target.reshape(1, count), tokens)
+    )(placement, tokens)
 
 
 def unsort_kernel(target_ref, rows_ref, out_ref):
@@ -84,65 +100,88 @@
     )(target.reshape(count, 1), returned)
 
 
-def own_columns(projection, member):
-    query_width, key_width = HEADS * HEAD_DIM, KV_HEADS * HEAD_DIM
-    return jnp.concatenate(
-        [
-            lax.dynamic_slice_in_dim(projection, member * GROUP * HEAD_DIM, GROUP * HEAD_DIM, 1),
-            lax.dynamic_slice_in_dim(projection, query_width + member * HEAD_DIM, HEAD_DIM, 1),
-            lax.dynamic_slice_in_dim(projection, query_width + key_width + member * HEAD_DIM, HEAD_DIM, 1),
-        ],
-        axis=1,
-    )
-
-
-def spread(block, axis):
-    up, down = [(i, (i + 1) % 4) for i in range(4)], [(i, (i + 3) % 4) for i in range(4)]
-    half = block.shape[0] // 2
-    below, above = lax.ppermute(block, axis, up), lax.ppermute(block, axis, down)
-    far_low = lax.ppermute(below[:half], axis, up)
-    far_high = lax.ppermute(above[half:], axis, down)
-    return [block, below, above, far_low, far_high]
+def columns_kernel(members_ref, projection_ref, *refs):
+    outs, sems = refs[:-1], refs[-1]
+    copies = []
+    for i, out in enumerate(outs):
+        member, at, source = members_ref[i], 0, 0
+        for heads, width in ((KV_HEADS, GROUP * HEAD_DIM), (KV_HEADS, HEAD_DIM), (KV_HEADS, HEAD_DIM)):
+            copy = pltpu.make_async_copy(
+                projection_ref.at[:, pl.ds(pl.multiple_of(source + member * width, HEAD_DIM), width)],
+                out.at[:, pl.ds(at, width)],
+                sems.at[len(copies)],
+            )
+            copy.start()
+            copies.append(copy)
+            at, source = at + width, source + heads * width
+    for copy in copies:
+        copy.wait()
+
+
+def columns_of(projection, members):
+    anywhere = pl.BlockSpec(memory_space=pl.ANY)
+    shape = jax.ShapeDtypeStruct((projection.shape[0], (GROUP + 2) * HEAD_DIM), projection.dtype)
+    return pl.pallas_call(
+        columns_kernel,
+        out_shape=[shape] * len(members),
+        in_specs=[pl.BlockSpec(memory_space=pltpu.SMEM), anywhere],
+        out_specs=[anywhere] * len(members),
+        scratch_shapes=[pltpu.SemaphoreType.DMA((3 * len(members),))],
+        name="columns",
+    )(jnp.stack(members), projection)
+
+
+UP, DOWN, OVER = (tuple((i, (i + d) % 4) for i in range(4)) for d in (1, 3, 2))
+
+
+def ring_blocks(block, axis):
+    others = [lax.ppermute(block, axis, way) for way in (UP, DOWN, OVER)]
+    return jnp.concatenate([block] + others, axis=0)
+
+
+def both_ways(block, axis):
+    return [block, lax.ppermute(block, axis, UP), lax.ppermute(block, axis, DOWN)]
+
+
+def far_halves(blocks, axis):
+    half = blocks[0].shape[0] // 2
+    return [lax.ppermute(blocks[1][:half], axis, UP), lax.ppermute(blocks[2][half:], axis, DOWN)]
 
 
 RING = (0, 3, 1, 2)
 SPAN = ((0, (0, 1, 2, 3)), (3, (0, 1, 2, 3)), (1, (0, 1, 2, 3)), (2, (0, 1)), (2, (2, 3)))
 
 
-def gather_weights(projection, member):
+def weight_places(rows):
     x, y, zh = lax.axis_index("x"), lax.axis_index("y"), lax.axis_index("zh")
-    rows = projection.shape[0]
-    mine = lax.all_gather(own_columns(projection, member), ("x", "y"), axis=0, tiled=True)
-    theirs = lax.ppermute(own_columns(projection, member ^ 2), ("zh", "zl"), [(0, 3), (3, 0), (1, 2), (2, 1)])
-    half = theirs.shape[1] // 2
-    pieces = [mine]
     places = [(i * 2 + zh) * rows for i in range(16)]
-    for side, (one, two) in enumerate((("y", "x"), ("x", "y"))):
-        block = theirs[:, side * half : (side + 1) * half]
-        pieces += spread(jnp.concatenate(spread(block, one), axis=0), two)
+    for side in range(2):
         for outer, inners in SPAN:
             for inner in inners:
                 near, far = (outer, RING[inner]) if side == 0 else (RING[inner], outer)
                 places.append(((x + near) % 4 * 8 + (y + far) % 4 * 2 + 1 - zh) * rows)
-    return jnp.stack(places), pieces
-
-
-def project_kernel(places_ref, rows_ref, *refs):
-    pieces, out_ref, ordered = refs[:-2], refs[-2], refs[-1]
-    width = out_ref.shape[1]
-    half = width // 2
+    return jnp.stack(places)
+
+
+def project_kernel(parts, places_ref, *refs):
+    row_refs, refs = refs[:parts], refs[parts:]
+    pieces, out_refs, ordered = refs[: -parts - 1], refs[-parts - 1 : -1], refs[-1]
+    half = out_refs[0].shape[1] // 2
     step = 128
 
     def take(first, count):
         for i in range(count):
             column = pl.multiple_of(places_ref[first + i], step)
-            ordered[:, i * step : (i + 1) * step] = rows_ref[:, pl.ds(column, step)]
-
-    def product(parts):
+            at = 0
+            for rows in row_refs:
+                ordered[at : at + rows.shape[0], i * step : (i + 1) * step] = rows[:, pl.ds(column, step)]
+                at += rows.shape[0]
+
+    def product(pieces):
         total, at = None, 0
-        for part in parts:
-            depth = part.shape[0]
-            term = jnp.dot(ordered[:, at : at + depth], part[...], preferred_element_type=jnp.float32)
+        for piece in pieces:
+            depth = piece.shape[0]
+            term = jnp.dot(ordered[:, at : at + depth], piece[...], preferred_element_type=jnp.float32)
             total = term if total is None else total + term
             at += depth
         return total
@@ -151,32 +190,35 @@
     out = product(pieces[:1])
     for side in range(2):
         take(16 + side * 16, 16)
-        other = product(pieces[1 + side * 5 : 6 + side * 5])
         columns = slice(side * half, (side + 1) * half)
-        out_ref[:, columns] = (out[:, columns] + other).astype(jnp.bfloat16)
+        here = (out[:, columns] + product(pieces[1 + side * 5 : 6 + side * 5])).astype(jnp.bfloat16)
+        at = 0
+        for out_ref in out_refs:
+            out_ref[:, columns] = here[at : at + out_ref.shape[0]]
+            at += out_ref.shape[0]
 
 
 def project(places, pieces, rows):
-    count, depth = rows.shape
+    count, depth = sum(r.shape[0] for r in rows), rows[0].shape[1]
     width = pieces[0].shape[1]
     whole = pl.BlockSpec(memory_space=pltpu.VMEM)
     return pl.pallas_call(
-        project_kernel,
-        out_shape=jax.ShapeDtypeStruct((count, width), jnp.bfloat16),
-        in_specs=[pl.BlockSpec(memory_space=pltpu.SMEM)] + [whole] * (1 + len(pieces)),
-        out_specs=whole,
+        functools.partial(project_kernel, len(rows)),
+        out_shape=[jax.ShapeDtypeStruct((r.shape[0], width), jnp.bfloat16) for r in rows],
+        in_specs=[pl.BlockSpec(memory_space=pltpu.SMEM)] + [whole] * (len(rows) + len(pieces)),
+        out_specs=[whole] * len(rows),
         scratch_shapes=[pltpu.VMEM((count, depth // 2), jnp.bfloat16)],
-        compiler_params=pltpu.CompilerParams(vmem_limit_bytes=24 * 2**20),
+        compiler_params=pltpu.CompilerParams(vmem_limit_bytes=16 * 2**20),
         cost_estimate=pl.CostEstimate(
             flops=2 * count * depth * width, bytes_accessed=2 * depth * (width + count), transcendentals=0
         ),
         name="project",
-    )(places, rows, *pieces)
+    )(places, *rows, *pieces)
 
 
 def attention_kernel(member_ref, lengths_ref, *refs):
-    lanes = refs[:4]
-    cos_ref, sin_ref, out_ref, queries, keys, values, mixed = refs[4:]
+    own_ref, near_ref, far_refs, last_refs = refs[0], refs[1], refs[2:6], refs[6:10]
+    cos_ref, sin_ref, out_ref, queries, keys, values, mixed = refs[10:]
     count = cos_ref.shape[0]
     blocks = count // BLOCK
     part = BLOCK // blocks
@@ -190,7 +232,8 @@
     wanted = lax.broadcasted_iota(jnp.int32, (BLOCK, BLOCK), 0)
     forward = jnp.where(wanted == placed, 1.0, 0.0).astype(jnp.bfloat16)
     for h in range(blocks):
-        chunk = jnp.concatenate([lane_ref[h * part : (h + 1) * part] for lane_ref in lanes], axis=0)
+        span = slice(h * part, (h + 1) * part)
+        chunk = jnp.concatenate([own_ref[span], near_ref[span], far_refs[h][...], last_refs[h][...]], axis=0)
         chunk = jnp.dot(forward, chunk, preferred_element_type=jnp.float32)
         for s in range(blocks):
             rows = slice(s * BLOCK + h * part, s * BLOCK + (h + 1) * part)
@@ -255,7 +298,7 @@
     return pl.pallas_call(
         attention_kernel,
         out_shape=jax.ShapeDtypeStruct((count, GROUP * HEAD_DIM), jnp.bfloat16),
-        in_specs=[scalars, scalars] + [whole] * 6,
+        in_specs=[scalars, scalars] + [whole] * (2 + len(lanes)),
         out_specs=whole,
         scratch_shapes=[
             pltpu.VMEM((GROUP, count, HEAD_DIM), jnp.bfloat16),
@@ -263,7 +306,7 @@
             pltpu.VMEM((count, HEAD_DIM), jnp.bfloat16),
             pltpu.VMEM((count, GROUP * HEAD_DIM), jnp.bfloat16),
         ],
-        compiler_params=pltpu.CompilerParams(vmem_limit_bytes=24 * 2**20),
+        compiler_params=pltpu.CompilerParams(vmem_limit_bytes=16 * 2**20),
         name="attend",
     )(member, lengths, *lanes, cosine, sine)
 
@@ -275,23 +318,46 @@
     groups = devices // members
     piece = row_count // devices
     member = lax.axis_index(CTX)
-
-    places, pieces = gather_weights(projection, member)
-    target = (placement[0][:, None] * piece + jnp.arange(piece, dtype=jnp.int32)[None, :]).reshape(row_count)
-    outgoing = sort_rows(tokens, target, groups)
+    across = [(0, 1), (1, 0)]
+    depth = projection.shape[0]
+    tie = lax.optimization_barrier
+
+    mine, theirs = columns_of(projection, [member, member ^ 2])
+    mine = lax.all_gather(mine, ("x", "y"), axis=0, tiled=True)
+    places = weight_places(depth)
+    outgoing = sort_rows(tokens, placement, groups)
     arrived = lax.all_to_all(outgoing, DP, 0, 0, tiled=True).reshape(row_count, width)
-    across = [(0, 1), (1, 0)]
-    far = lax.ppermute(arrived, "zl", across)
-    near = lax.ppermute(arrived, "core", across)
-    lanes = [project(places, pieces, arrived), project(places, pieces, near)]
+
+    theirs = lax.ppermute(theirs, ("zh", "zl"), [(0, 3), (3, 0), (1, 2), (2, 1)])
     tables = rotary_tables(doc_lengths[0], members * row_count)
-    far, lanes, tables = lax.optimization_barrier((far, lanes, tables))
-    last = lax.ppermute(far, "core", across)
-    lanes = lanes + [project(places, pieces, far), project(places, pieces, last)]
+    arrived, theirs, tables, places = tie((arrived, theirs, tables, places))
+
+    size = row_count // 4
+    near, far = [arrived], []
+
+    def exchange(step, *others):
+        near[0], sent, *others = tie((near[0], lax.ppermute(near[0][step * size : (step + 1) * size], "zl", across), *others))
+        far.append(sent)
+        return others
+
+    half = theirs.shape[1] // 2
+    first, second = exchange(0, ring_blocks(theirs[:, :half], "y"), ring_blocks(theirs[:, half:], "x"))
+    first, second = exchange(1, both_ways(first, "x"), both_ways(second, "y"))
+    first_far, second_far = exchange(2, far_halves(first, "x"), far_halves(second, "y"))
+    pieces = [mine, *first, *first_far, *second, *second_far]
+    own = near[0]
+    last_sent = lax.ppermute(own[3 * size :], "zl", across)
+    swapped = [lax.ppermute(rows, "core", across) for rows in (own, *far)]
+    done = project(places, pieces, [own, *far, *swapped])
+    last_sent, done = tie((last_sent, done))
+    last = project(places, pieces, [last_sent, lax.ppermute(last_sent, "core", across)])
+    lanes = [done[0], done[4], *done[1:4], last[0], *done[5:8], last[1]]
     mixed = attend(member.reshape(1), doc_lengths, lanes, *tables)
+
     returned = lax.all_to_all(
         mixed.reshape(devices, members * piece, GROUP * HEAD_DIM), EVERY, 0, 0, tiled=True
     )
+    target = (placement[0][:, None] * piece + jnp.arange(piece, dtype=jnp.int32)[None, :]).reshape(row_count)
     return unsort_rows(returned.reshape(groups, members, members * piece, GROUP * HEAD_DIM), target)
 
 

time: 173 us -> 204 us (1.18)
  Pallas kernels: 29.6 us -> 42.8 us
  local copies, waits for them, and re-layouts: 15.8 us -> 26.2 us
  starting transfers between devices: 42.3 us -> 49.6 us
    ppermute x20 -> x24, waiting for transfers between devices: 15.4 us -> 40.6 us  [the longest x1 17.1 us: on_device(): lax.ppermute(theirs, ('zh', 'zl'), [(0, 3), (3, 0), (1, 2), (2, 1)])]
    all_to_all x1, waiting for transfers between devices: 28.5 us -> 4.53 us  [on_device(): lax.all_to_all(outgoing, DP, 0, 0, tiled=True).reshape(row_count, width)]
    unnamed x20 -> x74, local copies, waits for them, and re-layouts: 8.63 us -> 25 us
    pallas_call x4 -> x3, Pallas kernels: 17.4 us -> 25.2 us  [the longest x1 13.7 us: columns_of(): pl.pallas_call(columns_kernel, out_shape=[shape] * len(members), in_specs...]
    ppermute x20 -> x24, starting transfers between devices: 25.3 us -> 33.1 us  [the longest x4 8.36 us: on_device(): swapped = [lax.ppermute(rows, 'core', across) for rows in (own, *far)]]
    pallas_call x1, Pallas kernels: 1.49 us -> 6.82 us  [sort_rows(): pl.pallas_call(sort_kernel, out_shape=jax.ShapeDtypeStruct((groups, rows,...]
    slice x9, local copies, waits for them, and re-layouts: 3.78 us -> 1.02 us  [the longest x1 0.81 us: on_device(): last_sent = lax.ppermute(own[3 * size:], 'zl', across)]
  transfers between devices with their start and end apart: 23 -> 27, of which waited for: 10 -> 15; matrix products, arithmetic and copies ran while one was open for 9% -> 3% of each run, Pallas kernels for 9% -> 8%
where the time goes in v4:
time: 204 us; the launch traced here: 202 us
  waiting for transfers between devices  64.2 us (31%)
  starting transfers between devices  49.6 us (24%)
  Pallas kernels  42.8 us (21%)
  local copies, waits for them, and re-layouts  26.2 us (13%)
  between operations  13.7 us (7%)
  other arithmetic  6.02 us (3%)
    unnamed x74, local copies, waits for them, and re-layouts  25 us
    all_to_all x1, waiting for transfers between devices, on_device(): lax.all_to_all(mixed.reshape(devices, members * piece, GROUP * HEAD_DIM),...  19.1 us
    ppermute x1, waiting for transfers between devices, on_device(): lax.ppermute(theirs, ('zh', 'zl'), [(0, 3), (3, 0), (1, 2), (2, 1)])  17.1 us
    pallas_call x1, Pallas kernels, columns_of(): pl.pallas_call(columns_kernel, out_shape=[shape] * len(members), in_specs...  13.7 us
    pallas_call x2, Pallas kernels, project(): pl.pallas_call(functools.partial(project_kernel, len(rows)), out_shape=[j...  11.5 us
    all_to_all x1, starting transfers between devices, on_device(): lax.all_to_all(outgoing, DP, 0, 0, tiled=True).reshape(row_count, width)  11.3 us
    ppermute x6, waiting for transfers between devices, ring_blocks(): others = [lax.ppermute(block, axis, way) for way in (UP, DOWN, OVER)]  8.5 us
    ppermute x2, waiting for transfers between devices, both_ways(): lax.ppermute(block, axis, DOWN)  8.46 us
  transfers between devices with their start and end apart: 27, of which 15 were waited for; matrix products, arithmetic and copies ran while one was open for 3% of the time, Pallas kernels for 8%

profile of v4, /device:TPU:1, one launch (start us, length us, event | category | flops | bytes accessed | tf_op | source)
XLA Modules:
  0.0 202.4 jit_solution(1766617495491875168)
XLA Ops:
  6.5 0.6 pad_add_fusion.members_ref
  7.1 13.7 %columns.1 = (bf16[128,768]{1,0:T(8,128)(2,1)}, bf16[128,768]{1,0:T(8,128)(2,1)}) custom-call(s32[2]{0:T(128)} %pad_add_fusion.members_ref, bf16[128,3072]{1,0:T(8,128)(2,1)} %projection_ref.1), custom_call_target="tpu_custom_call" | custom-call | tf_op jit(solution)/shard_map/columns/pallas_call | solution.py:124
  20.9 6.8 %sort_rows.1 = bf16[32,8,4096]{2,1,0:T(8,128)(2,1)} custom-call(s32[1,128]{1,0:T(1,128)} %placement_ref.1, bf16[256,4096]{1,0:T(8,128)(2,1)} %rows_ref.1), custom_call_target="tpu_custom_call" | custom-call | tf_op jit(solution)/shard_map/sort_rows/pallas_call | solution.py:63
  27.7 11.3 %all-to-all-start = ((bf16[32,8,4096]{2,1,0:T(8,128)(2,1)}), bf16[32,8,4096]{2,1,0:T(8,128)(2,1)S(1)}, u32[]{:S(2)}, u32[]{:S(2)}) async-start(bf16[32,8,4096]{2,1,0:T(8,128)(2,1)} %sort_rows.1), calls=%async_computation | async-start | bytes 4194304 | tf_op jit(solution)/shard_map/all_to_all | solution.py:329
  39.0 3.0 %collective-permute-start = (bf16[128,768]{1,0:T(8,128)(2,1)S(1)}, bf16[128,768]{1,0:T(8,128)(2,1)S(1)}, u32[]{:S(2)}, u32[]{:S(2)}) collective-permute-start(bf16[128,768]{1,0:T(8,128)(2,1)S(1)} %copy-done.36), channel_id=1, source_target_pairs={{0,6},{6,0},{2,4},{4,2},{1,7},{7,1},{3,5},{5,3},{8,14},{14,8},{10,... | collective-permute-start | bytes 589832 | tf_op jit(solution)/shard_map/ppermute | solution.py:331
  42.3 3.1 %fusion = (f32[1024,64]{1,0:T(8,128)}, f32[1024,64]{1,0:T(8,128)}, f32[1024,64]{1,0:T(8,128)}) fusion(f32[64]{0:T(128)S(1)} %multiply_power_fusion, f32[1024]{0:T(1024)S(1)} %subtract_convert_fusion), kind=kLoop, calls=%fused_computation.6 | loop fusion | flops 131072 | bytes 790784 | tf_op jit(solution)/shard_map/neg | solution.py:33
  45.6 1.9 pad_maximum_fusion
  47.4 17.1 %collective-permute-done = bf16[128,768]{1,0:T(8,128)(2,1)S(1)} collective-permute-done((bf16[128,768]{1,0:T(8,128)(2,1)S(1)}, bf16[128,768]{1,0:T(8,128)(2,1)S(1)}, u32[]{:S(2)}, u32[]{:S(2)}) %collective-permute-start) | collective-permute-done | bytes 196640 | tf_op jit(solution)/shard_map/ppermute | solution.py:331
  64.6 4.5 %all-to-all-done = bf16[32,8,4096]{2,1,0:T(8,128)(2,1)S(1)} async-done(((bf16[32,8,4096]{2,1,0:T(8,128)(2,1)}), bf16[32,8,4096]{2,1,0:T(8,128)(2,1)S(1)}, u32[]{:S(2)}, u32[]{:S(2)}) %all-to-all-start) | async-done | bytes 2097184 | tf_op jit(solution)/shard_map/all_to_all | solution.py:329
  69.1 1.4 collective-permute-start.1
  70.7 2.7 %collective-permute-start.6 = (bf16[128,384]{1,0:T(8,128)(2,1)S(1)}, bf16[128,384]{1,0:T(8,128)(2,1)S(1)}, u32[]{:S(2)}, u32[]{:S(2)}) collective-permute-start(bf16[128,384]{1,0:T(8,128)(2,1)S(1)} %get-tuple-element.93), channel_id=1, source_target_pairs={{0,96},{32,0},{64,32},{96,64},{1,97},{33,1},{65,33},{97,65},{2,98}... | collective-permute-start | bytes 294920 | tf_op jit(solution)/shard_map/ppermute | solution.py:138
  73.6 1.6 collective-permute-start.2
  75.3 2.1 %collective-permute-start.3 = (bf16[128,384]{1,0:T(8,128)(2,1)S(1)}, bf16[128,384]{1,0:T(8,128)(2,1)S(1)}, u32[]{:S(2)}, u32[]{:S(2)}) collective-permute-start(bf16[128,384]{1,0:T(8,128)(2,1)S(1)} %get-tuple-element.94), channel_id=1, source_target_pairs={{0,24},{8,0},{16,8},{24,16},{1,25},{9,1},{17,9},{25,17},{2,26},{10... | collective-permute-start | bytes 294920 | tf_op jit(solution)/shard_map/ppermute | solution.py:138
  77.7 0.6 collective-permute-start.4
  78.3 2.2 %collective-permute-done.7 = bf16[128,384]{1,0:T(8,128)(2,1)S(1)} collective-permute-done((bf16[128,384]{1,0:T(8,128)(2,1)S(1)}, bf16[128,384]{1,0:T(8,128)(2,1)S(1)}, u32[]{:S(2)}, u32[]{:S(2)}) %collective-permute-start.7) | collective-permute-done | bytes 98336 | tf_op jit(solution)/shard_map/ppermute | solution.py:138
  80.5 0.7 collective-permute-done.2
  81.2 5.2 %collective-permute-done.4 = bf16[128,384]{1,0:T(8,128)(2,1)S(1)} collective-permute-done((bf16[128,384]{1,0:T(8,128)(2,1)S(1)}, bf16[128,384]{1,0:T(8,128)(2,1)S(1)}, u32[]{:S(2)}, u32[]{:S(2)}) %collective-permute-start.4) | collective-permute-done | bytes 98336 | tf_op jit(solution)/shard_map/ppermute | solution.py:138
  86.5 1.6 collective-permute-start.8
  88.1 1.4 collective-permute-start.10
  89.6 2.5 %collective-permute-start.12 = (bf16[512,384]{1,0:T(8,128)(2,1)S(1)}, bf16[512,384]{1,0:T(8,128)(2,1)S(1)}, u32[]{:S(2)}, u32[]{:S(2)}) collective-permute-start(bf16[512,384]{1,0:T(8,128)(2,1)S(1)} %pad_maximum_fusion.3.refs_14_.refs_8_), channel_id=1, source_target_pairs={{0,24},{8,0},{16,8},{24,16},{1,25},{9,1},{17,9},{25,17},{2,26},{10... | collective-permute-start | bytes 1179656 | tf_op jit(solution)/shard_map/ppermute | solution.py:143
  92.2 8.5 %collective-permute-done.10.refs_11_.refs_5_ = bf16[512,384]{1,0:T(8,128)(2,1)S(1)} collective-permute-done((bf16[512,384]{1,0:T(8,128)(2,1)S(1)}, bf16[512,384]{1,0:T(8,128)(2,1)S(1)}, u32[]{:S(2)}, u32[]{:S(2)}) %collective-permute-start.10) | collective-permute-done | bytes 393248 | tf_op jit(solution)/shard_map/ppermute | solution.py:143
  100.8 1.0 collective-permute-start.13
  101.8 2.0 collective-permute-start.14
  103.9 0.8 collective-permute-start.15
  104.7 0.3 collective-permute-start.16
  105.0 2.6 %collective-permute-start.17 = (bf16[256,384]{1,0:T(8,128)(2,1)S(1)}, bf16[256,384]{1,0:T(8,128)(2,1)S(1)}, u32[]{:S(2)}, u32[]{:S(2)}) collective-permute-start(bf16[256,384]{1,0:T(8,128)(2,1)S(1)} %slice.38), channel_id=1, source_target_pairs={{0,24},{8,0},{16,8},{24,16},{1,25},{9,1},{17,9},{25,17},{2,26},{10... | collective-permute-start | bytes 589832 | tf_op jit(solution)/shard_map/ppermute | solution.py:148
  107.7 0.7 copy-done.12
  108.5 0.7 copy-done.14
  109.1 1.4 collective-permute-done.16.refs_17_.refs_11_
  110.5 0.7 copy-done.16
  111.2 0.7 copy-done.18
  111.9 7.8 %collective-permute-start.19 = (bf16[256,4096]{1,0:T(8,128)(2,1)S(1)}, bf16[256,4096]{1,0:T(8,128)(2,1)S(1)}, u32[]{:S(2)}, u32[]{:S(2)}) collective-permute-start(bf16[256,4096]{1,0:T(8,128)(2,1)S(1)} %bitcast.45), channel_id=1, source_target_pairs={{0,1},{1,0},{2,3},{3,2},{4,5},{5,4},{6,7},{7,6},{8,9},{9,8},{10,11... | collective-permute-start | bytes 6291464 | tf_op jit(solution)/shard_map/ppermute | solution.py:350
  119.7 0.4 collective-permute-start.21
  120.2 0.8 slice.39
  121.1 3.1 %collective-permute-done.20.refs_5_ = bf16[64,4096]{1,0:T(8,128)(2,1)S(1)} collective-permute-done((bf16[64,4096]{1,0:T(8,128)(2,1)S(1)}, bf16[64,4096]{1,0:T(8,128)(2,1)S(1)}, u32[]{:S(2)}, u32[]{:S(2)}) %collective-permute-start.20) | collective-permute-done | bytes 524320 | tf_op jit(solution)/shard_map/ppermute | solution.py:350
  124.2 0.8 copy-done.29
  125.0 0.8 copy-done.31
  125.9 0.8 copy-done.33
  126.7 1.3 copy-done.21
  128.0 1.9 copy-done
  129.9 1.0 copy-done.3
  130.9 1.0 copy-done.5
  131.9 1.0 copy-done.7
  132.9 1.0 copy-done.9
  133.9 1.0 copy-done.11
  134.9 0.9 copy-done.13
  135.8 0.9 copy-done.15
  136.7 0.9 copy-done.17
  137.7 0.9 copy-done.19
  138.6 1.6 copy-done.22
  140.2 1.0 copy-done.24
  141.2 1.0 copy-done.26
  142.3 1.0 copy-done.28
  143.3 1.0 copy-done.30
  144.4 1.0 copy-done.32
  145.4 1.0 copy-done.34
  146.4 9.0 %project.2 = (bf16[256,768]{1,0:T(8,128)(2,1)S(1)}, bf16[64,768]{1,0:T(8,128)(2,1)S(1)}, bf16[64,768]{1,0:T(8,128)(2,1)S(1)}, bf16[64,768]{1,0:T(8,128)(2,1)S(1)...) custom-call(s32[48]{0:T(128)S(1)} %stack.156.places_ref, ...), custom_call_target="tpu_custom_call" | custom-call | flops 5637144576 | bytes 13631488 | tf_op jit(solution)/shard_map/project/pallas_call | solution.py:205
  155.4 0.7 collective-permute-start.23
  156.1 1.7 collective-permute-done.23.refs_1_
  157.9 2.5 %project.3 = (bf16[64,768]{1,0:T(8,128)(2,1)S(1)}, bf16[64,768]{1,0:T(8,128)(2,1)S(1)}) custom-call(s32[48]{0:T(128)S(1)} %stack.156.places_ref, bf16[64,4096]{1,0:T(8,128)(2,1)} %collective-permute-done.18.refs_0_, bf16[64,4096]{1,0:T(8,128)(2,1)S(1)} %collective-permute-done.23.refs_1_, bf16[2048,768]{1,0:T(8,128)(2,1)S(1)} %copy-done.1, ...), custom_call_target="tpu_custom_call" | custom-call | flops 805306368 | bytes 7340032 | tf_op jit(solution)/shard_map/project/pallas_call | solution.py:205
  160.4 8.4 %attend.1 = bf16[1024,512]{1,0:T(8,128)(2,1)} custom-call(s32[1]{0:T(128)} %bitcast.1.member_ref, s32[1,8]{1,0:T(1,128)S(1)} %copy-done.20, bf16[256,768]{1,0:T(8,128)(2,1)S(1)} %get-tuple-element.80.refs_0_, bf16[256,768]{1,0:T(8,128)(2,1)S(1)} %get-tuple-element.81.refs_1_, bf16[64,768]{1,0:T(8,128)(2,1)S(1)} %get-tuple-element.82.refs_2_, ...), custom_call_target="tpu_custom_call" | custom-call | tf_op jit(solution)/shard_map/attend/pallas_call | solution.py:298
  168.8 5.2 %all-to-all-start.1 = ((bf16[128,8,512]{2,1,0:T(8,128)(2,1)}), bf16[128,8,512]{2,1,0:T(8,128)(2,1)S(1)}, u32[]{:S(2)}, u32[]{:S(2)}) async-start(bf16[128,8,512]{2,1,0:T(8,128)(2,1)} %bitcast.39), calls=%async_computation.1 | async-start | bytes 2097152 | tf_op jit(solution)/shard_map/all_to_all | solution.py:357
  174.2 19.1 %all-to-all-done.1 = bf16[128,8,512]{2,1,0:T(8,128)(2,1)S(1)} async-done(((bf16[128,8,512]{2,1,0:T(8,128)(2,1)}), bf16[128,8,512]{2,1,0:T(8,128)(2,1)S(1)}, u32[]{:S(2)}, u32[]{:S(2)}) %all-to-all-start.1) | async-done | bytes 1048608 | tf_op jit(solution)/shard_map/all_to_all | solution.py:357
  193.3 2.3 %unsort_rows.1 = bf16[256,2048]{1,0:T(8,128)(2,1)} custom-call(s32[256,1]{1,0:T(8,128)S(1)} %add.358.target_ref, bf16[32,4,8,512]{3,2,1,0:T(8,128)(2,1)S(1)} %bitcast.48), custom_call_target="tpu_custom_call" | custom-call | tf_op jit(solution)/shard_map/unsort_rows/pallas_call | solution.py:89
  (93 shorter events, 2.4 us)
Async XLA Ops:
  6.5 121.5 %all-gather.2.cloned.1.call-start = ((), (), s32[]{:S(2)}) async-start(), calls=%async_computation.2 | async-start | bytes 3342336 | tf_op jit(solution)/shard_map/all_gather | solution.py:326
  27.7 11.3 %copy-start.36 = (bf16[128,768]{1,0:T(8,128)(2,1)S(1)}, bf16[128,768]{1,0:T(8,128)(2,1)}, u32[]{:S(2)}) copy-start(bf16[128,768]{1,0:T(8,128)(2,1)} %get-tuple-element.49) | copy-start | bytes 589828
  27.7 14.3 %copy-start.20 = (s32[1,8]{1,0:T(1,128)S(1)}, s32[1,8]{1,0:T(1,128)}, u32[]{:S(2)}) copy-start(s32[1,8]{1,0:T(1,128)} %lengths_ref.1) | copy-start | bytes 100
  27.7 41.4 %all-to-all-start = ((bf16[32,8,4096]{2,1,0:T(8,128)(2,1)}), bf16[32,8,4096]{2,1,0:T(8,128)(2,1)S(1)}, u32[]{:S(2)}, u32[]{:S(2)}) async-start(bf16[32,8,4096]{2,1,0:T(8,128)(2,1)} %sort_rows.1), calls=%async_computation | async-start | bytes 4194304 | tf_op jit(solution)/shard_map/all_to_all | solution.py:329
  39.0 25.5 %collective-permute-start = (bf16[128,768]{1,0:T(8,128)(2,1)S(1)}, bf16[128,768]{1,0:T(8,128)(2,1)S(1)}, u32[]{:S(2)}, u32[]{:S(2)}) collective-permute-start(bf16[128,768]{1,0:T(8,128)(2,1)S(1)} %copy-done.36), channel_id=1, source_target_pairs={{0,6},{6,0},{2,4},{4,2},{1,7},{7,1},{3,5},{5,3},{8,14},{14,8},{10,... | collective-permute-start | bytes 589832 | tf_op jit(solution)/shard_map/ppermute | solution.py:331
  69.1 17.4 %collective-permute-start.1 = (bf16[64,4096]{1,0:T(8,128)(2,1)S(1)}, bf16[64,4096]{1,0:T(8,128)(2,1)S(1)}, u32[]{:S(2)}, u32[]{:S(2)}) collective-permute-start(bf16[64,4096]{1,0:T(8,128)(2,1)S(1)} %slice.30), channel_id=1, source_target_pairs={{0,2},{2,0},{1,3},{3,1},{4,6},{6,4},{5,7},{7,5},{8,10},{10,8},{9,1... | collective-permute-start | bytes 1572872 | tf_op jit(solution)/shard_map/ppermute | solution.py:339
  70.6 4.7 %collective-permute-start.5 = (bf16[128,384]{1,0:T(8,128)(2,1)S(1)}, bf16[128,384]{1,0:T(8,128)(2,1)S(1)}, u32[]{:S(2)}, u32[]{:S(2)}) collective-permute-start(bf16[128,384]{1,0:T(8,128)(2,1)S(1)} %get-tuple-element.93), channel_id=1, source_target_pairs={{0,32},{32,64},{64,96},{96,0},{1,33},{33,65},{65,97},{97,1},{2,34}... | collective-permute-start | bytes 294920 | tf_op jit(solution)/shard_map/ppermute | solution.py:138
  70.7 7.0 %collective-permute-start.6 = (bf16[128,384]{1,0:T(8,128)(2,1)S(1)}, bf16[128,384]{1,0:T(8,128)(2,1)S(1)}, u32[]{:S(2)}, u32[]{:S(2)}) collective-permute-start(bf16[128,384]{1,0:T(8,128)(2,1)S(1)} %get-tuple-element.93), channel_id=1, source_target_pairs={{0,96},{32,0},{64,32},{96,64},{1,97},{33,1},{65,33},{97,65},{2,98}... | collective-permute-start | bytes 294920 | tf_op jit(solution)/shard_map/ppermute | solution.py:138
  73.3 7.1 %collective-permute-start.7 = (bf16[128,384]{1,0:T(8,128)(2,1)S(1)}, bf16[128,384]{1,0:T(8,128)(2,1)S(1)}, u32[]{:S(2)}, u32[]{:S(2)}) collective-permute-start(bf16[128,384]{1,0:T(8,128)(2,1)S(1)} %get-tuple-element.93), channel_id=1, source_target_pairs={{0,64},{32,96},{64,0},{96,32},{1,65},{33,97},{65,1},{97,33},{2,66}... | collective-permute-start | bytes 294920 | tf_op jit(solution)/shard_map/ppermute | solution.py:138
  73.6 7.6 %collective-permute-start.2 = (bf16[128,384]{1,0:T(8,128)(2,1)S(1)}, bf16[128,384]{1,0:T(8,128)(2,1)S(1)}, u32[]{:S(2)}, u32[]{:S(2)}) collective-permute-start(bf16[128,384]{1,0:T(8,128)(2,1)S(1)} %get-tuple-element.94), channel_id=1, source_target_pairs={{0,8},{8,16},{16,24},{24,0},{1,9},{9,17},{17,25},{25,1},{2,10},{10... | collective-permute-start | bytes 294920 | tf_op jit(solution)/shard_map/ppermute | solution.py:138
  75.3 5.9 %collective-permute-start.3 = (bf16[128,384]{1,0:T(8,128)(2,1)S(1)}, bf16[128,384]{1,0:T(8,128)(2,1)S(1)}, u32[]{:S(2)}, u32[]{:S(2)}) collective-permute-start(bf16[128,384]{1,0:T(8,128)(2,1)S(1)} %get-tuple-element.94), channel_id=1, source_target_pairs={{0,24},{8,0},{16,8},{24,16},{1,25},{9,1},{17,9},{25,17},{2,26},{10... | collective-permute-start | bytes 294920 | tf_op jit(solution)/shard_map/ppermute | solution.py:138
  77.7 8.8 %collective-permute-start.4 = (bf16[128,384]{1,0:T(8,128)(2,1)S(1)}, bf16[128,384]{1,0:T(8,128)(2,1)S(1)}, u32[]{:S(2)}, u32[]{:S(2)}) collective-permute-start(bf16[128,384]{1,0:T(8,128)(2,1)S(1)} %get-tuple-element.94), channel_id=1, source_target_pairs={{0,16},{8,24},{16,0},{24,8},{1,17},{9,25},{17,1},{25,9},{2,18},{10... | collective-permute-start | bytes 294920 | tf_op jit(solution)/shard_map/ppermute | solution.py:138
  86.5 34.6 %copy-start.2 = (bf16[512,384]{1,0:T(8,128)(2,1)}, bf16[512,384]{1,0:T(8,128)(2,1)S(1)}, u32[]{:S(2)}) copy-start(bf16[512,384]{1,0:T(8,128)(2,1)S(1)} %pad_maximum_fusion.2.refs_9_.refs_3_) | copy-start | bytes 1179652
  86.5 34.6 %copy-start.23 = (bf16[64,4096]{1,0:T(8,128)(2,1)}, bf16[64,4096]{1,0:T(8,128)(2,1)S(1)}, u32[]{:S(2)}) copy-start(bf16[64,4096]{1,0:T(8,128)(2,1)S(1)} %collective-permute-done.1.refs_1_) | copy-start | bytes 1572868
  86.5 14.2 %collective-permute-start.8 = (bf16[64,4096]{1,0:T(8,128)(2,1)S(1)}, bf16[64,4096]{1,0:T(8,128)(2,1)S(1)}, u32[]{:S(2)}, u32[]{:S(2)}) collective-permute-start(bf16[64,4096]{1,0:T(8,128)(2,1)S(1)} %slice.33), channel_id=1, source_target_pairs={{0,2},{2,0},{1,3},{3,1},{4,6},{6,4},{5,7},{7,5},{8,10},{10,8},{9,1... | collective-permute-start | bytes 1572872 | tf_op jit(solution)/shard_map/ppermute | solution.py:339
  88.1 12.6 %collective-permute-start.10 = (bf16[512,384]{1,0:T(8,128)(2,1)S(1)}, bf16[512,384]{1,0:T(8,128)(2,1)S(1)}, u32[]{:S(2)}, u32[]{:S(2)}) collective-permute-start(bf16[512,384]{1,0:T(8,128)(2,1)S(1)} %pad_maximum_fusion.2.refs_9_.refs_3_), channel_id=1, source_target_pairs={{0,96},{32,0},{64,32},{96,64},{1,97},{33,1},{65,33},{97,65},{2,98}... | collective-permute-start | bytes 1179656 | tf_op jit(solution)/shard_map/ppermute | solution.py:143
  89.5 11.2 %collective-permute-start.11 = (bf16[512,384]{1,0:T(8,128)(2,1)S(1)}, bf16[512,384]{1,0:T(8,128)(2,1)S(1)}, u32[]{:S(2)}, u32[]{:S(2)}) collective-permute-start(bf16[512,384]{1,0:T(8,128)(2,1)S(1)} %pad_maximum_fusion.3.refs_14_.refs_8_), channel_id=1, source_target_pairs={{0,8},{8,16},{16,24},{24,0},{1,9},{9,17},{17,25},{25,1},{2,10},{10... | collective-permute-start | bytes 1179656 | tf_op jit(solution)/shard_map/ppermute | solution.py:143
  89.6 11.1 %collective-permute-start.12 = (bf16[512,384]{1,0:T(8,128)(2,1)S(1)}, bf16[512,384]{1,0:T(8,128)(2,1)S(1)}, u32[]{:S(2)}, u32[]{:S(2)}) collective-permute-start(bf16[512,384]{1,0:T(8,128)(2,1)S(1)} %pad_maximum_fusion.3.refs_14_.refs_8_), channel_id=1, source_target_pairs={{0,24},{8,0},{16,8},{24,16},{1,25},{9,1},{17,9},{25,17},{2,26},{10... | collective-permute-start | bytes 1179656 | tf_op jit(solution)/shard_map/ppermute | solution.py:143
  92.2 8.5 %collective-permute-start.9 = (bf16[512,384]{1,0:T(8,128)(2,1)S(1)}, bf16[512,384]{1,0:T(8,128)(2,1)S(1)}, u32[]{:S(2)}, u32[]{:S(2)}) collective-permute-start(bf16[512,384]{1,0:T(8,128)(2,1)S(1)} %pad_maximum_fusion.2.refs_9_.refs_3_), channel_id=1, source_target_pairs={{0,32},{32,64},{64,96},{96,0},{1,33},{33,65},{65,97},{97,1},{2,34}... | collective-permute-start | bytes 1179656 | tf_op jit(solution)/shard_map/ppermute | solution.py:143
  100.7 20.4 %copy-start.4 = (bf16[512,384]{1,0:T(8,128)(2,1)}, bf16[512,384]{1,0:T(8,128)(2,1)S(1)}, u32[]{:S(2)}) copy-start(bf16[512,384]{1,0:T(8,128)(2,1)S(1)} %collective-permute-done.10.refs_11_.refs_5_) | copy-start | bytes 1179652
  100.7 23.5 %copy-start.6 = (bf16[512,384]{1,0:T(8,128)(2,1)}, bf16[512,384]{1,0:T(8,128)(2,1)S(1)}, u32[]{:S(2)}) copy-start(bf16[512,384]{1,0:T(8,128)(2,1)S(1)} %collective-permute-done.11.refs_15_.refs_9_) | copy-start | bytes 1179652
  100.7 24.3 %copy-start.8 = (bf16[512,384]{1,0:T(8,128)(2,1)}, bf16[512,384]{1,0:T(8,128)(2,1)S(1)}, u32[]{:S(2)}) copy-start(bf16[512,384]{1,0:T(8,128)(2,1)S(1)} %collective-permute-done.12.refs_16_.refs_10_) | copy-start | bytes 1179652
  100.7 25.1 %copy-start.10 = (bf16[512,384]{1,0:T(8,128)(2,1)}, bf16[512,384]{1,0:T(8,128)(2,1)S(1)}, u32[]{:S(2)}) copy-start(bf16[512,384]{1,0:T(8,128)(2,1)S(1)} %collective-permute-done.9.refs_10_.refs_4_) | copy-start | bytes 1179652
  100.8 25.1 %copy-start.25 = (bf16[64,4096]{1,0:T(8,128)(2,1)}, bf16[64,4096]{1,0:T(8,128)(2,1)S(1)}, u32[]{:S(2)}) copy-start(bf16[64,4096]{1,0:T(8,128)(2,1)S(1)} %collective-permute-done.8.refs_2_) | copy-start | bytes 1572868
  100.8 11.1 %collective-permute-start.13 = (bf16[64,4096]{1,0:T(8,128)(2,1)S(1)}, bf16[64,4096]{1,0:T(8,128)(2,1)S(1)}, u32[]{:S(2)}, u32[]{:S(2)}) collective-permute-start(bf16[64,4096]{1,0:T(8,128)(2,1)S(1)} %slice.34), channel_id=1, source_target_pairs={{0,2},{2,0},{1,3},{3,1},{4,6},{6,4},{5,7},{7,5},{8,10},{10,8},{9,1... | collective-permute-start | bytes 1572872 | tf_op jit(solution)/shard_map/ppermute | solution.py:339
  101.8 5.8 %collective-permute-start.14 = (bf16[256,384]{1,0:T(8,128)(2,1)S(1)}, bf16[256,384]{1,0:T(8,128)(2,1)S(1)}, u32[]{:S(2)}, u32[]{:S(2)}) collective-permute-start(bf16[256,384]{1,0:T(8,128)(2,1)S(1)} %slice.35), channel_id=1, source_target_pairs={{0,32},{32,64},{64,96},{96,0},{1,33},{33,65},{65,97},{97,1},{2,34}... | collective-permute-start | bytes 589832 | tf_op jit(solution)/shard_map/ppermute | solution.py:148
  103.9 4.6 %collective-permute-start.15 = (bf16[256,384]{1,0:T(8,128)(2,1)S(1)}, bf16[256,384]{1,0:T(8,128)(2,1)S(1)}, u32[]{:S(2)}, u32[]{:S(2)}) collective-permute-start(bf16[256,384]{1,0:T(8,128)(2,1)S(1)} %slice.36), channel_id=1, source_target_pairs={{0,96},{32,0},{64,32},{96,64},{1,97},{33,1},{65,33},{97,65},{2,98}... | collective-permute-start | bytes 589832 | tf_op jit(solution)/shard_map/ppermute | solution.py:148
  104.7 5.8 %collective-permute-start.16 = (bf16[256,384]{1,0:T(8,128)(2,1)S(1)}, bf16[256,384]{1,0:T(8,128)(2,1)S(1)}, u32[]{:S(2)}, u32[]{:S(2)}) collective-permute-start(bf16[256,384]{1,0:T(8,128)(2,1)S(1)} %slice.37), channel_id=1, source_target_pairs={{0,8},{8,16},{16,24},{24,0},{1,9},{9,17},{17,25},{25,1},{2,10},{10... | collective-permute-start | bytes 589832 | tf_op jit(solution)/shard_map/ppermute | solution.py:148
  105.0 6.2 %collective-permute-start.17 = (bf16[256,384]{1,0:T(8,128)(2,1)S(1)}, bf16[256,384]{1,0:T(8,128)(2,1)S(1)}, u32[]{:S(2)}, u32[]{:S(2)}) collective-permute-start(bf16[256,384]{1,0:T(8,128)(2,1)S(1)} %slice.38), channel_id=1, source_target_pairs={{0,24},{8,0},{16,8},{24,16},{1,25},{9,1},{17,9},{25,17},{2,26},{10... | collective-permute-start | bytes 589832 | tf_op jit(solution)/shard_map/ppermute | solution.py:148
  107.6 0.7 copy-start.12
  108.5 0.7 copy-start.14
  110.5 0.7 copy-start.16
  111.2 0.7 copy-start.18
  111.9 14.0 %copy-start.27 = (bf16[64,4096]{1,0:T(8,128)(2,1)}, bf16[64,4096]{1,0:T(8,128)(2,1)S(1)}, u32[]{:S(2)}) copy-start(bf16[64,4096]{1,0:T(8,128)(2,1)S(1)} %collective-permute-done.13.refs_3_) | copy-start | bytes 1572868
  111.9 14.8 %collective-permute-start.19 = (bf16[256,4096]{1,0:T(8,128)(2,1)S(1)}, bf16[256,4096]{1,0:T(8,128)(2,1)S(1)}, u32[]{:S(2)}, u32[]{:S(2)}) collective-permute-start(bf16[256,4096]{1,0:T(8,128)(2,1)S(1)} %bitcast.45), channel_id=1, source_target_pairs={{0,1},{1,0},{2,3},{3,2},{4,5},{5,4},{6,7},{7,6},{8,9},{9,8},{10,11... | collective-permute-start | bytes 6291464 | tf_op jit(solution)/shard_map/ppermute | solution.py:350
  119.6 4.5 %collective-permute-start.20 = (bf16[64,4096]{1,0:T(8,128)(2,1)S(1)}, bf16[64,4096]{1,0:T(8,128)(2,1)S(1)}, u32[]{:S(2)}, u32[]{:S(2)}) collective-permute-start(bf16[64,4096]{1,0:T(8,128)(2,1)S(1)} %collective-permute-done.1.refs_1_), channel_id=1, source_target_pairs={{0,1},{1,0},{2,3},{3,2},{4,5},{5,4},{6,7},{7,6},{8,9},{9,8},{10,11... | collective-permute-start | bytes 1572872 | tf_op jit(solution)/shard_map/ppermute | solution.py:350
  119.7 5.3 %collective-permute-start.21 = (bf16[64,4096]{1,0:T(8,128)(2,1)S(1)}, bf16[64,4096]{1,0:T(8,128)(2,1)S(1)}, u32[]{:S(2)}, u32[]{:S(2)}) collective-permute-start(bf16[64,4096]{1,0:T(8,128)(2,1)S(1)} %collective-permute-done.8.refs_2_), channel_id=1, source_target_pairs={{0,1},{1,0},{2,3},{3,2},{4,5},{5,4},{6,7},{7,6},{8,9},{9,8},{10,11... | collective-permute-start | bytes 1572872 | tf_op jit(solution)/shard_map/ppermute | solution.py:350
  120.2 5.7 %collective-permute-start.22 = (bf16[64,4096]{1,0:T(8,128)(2,1)S(1)}, bf16[64,4096]{1,0:T(8,128)(2,1)S(1)}, u32[]{:S(2)}, u32[]{:S(2)}) collective-permute-start(bf16[64,4096]{1,0:T(8,128)(2,1)S(1)} %collective-permute-done.13.refs_3_), channel_id=1, source_target_pairs={{0,1},{1,0},{2,3},{3,2},{4,5},{5,4},{6,7},{7,6},{8,9},{9,8},{10,11... | collective-permute-start | bytes 1572872 | tf_op jit(solution)/shard_map/ppermute | solution.py:350
  121.1 34.4 %collective-permute-start.18 = (bf16[64,4096]{1,0:T(8,128)(2,1)}, bf16[64,4096]{1,0:T(8,128)(2,1)}, u32[]{:S(2)}, u32[]{:S(2)}) collective-permute-start(bf16[64,4096]{1,0:T(8,128)(2,1)} %slice.39), channel_id=1, source_target_pairs={{0,2},{2,0},{1,3},{3,1},{4,6},{6,4},{5,7},{7,5},{8,10},{10,8},{9,1... | collective-permute-start | bytes 1572872 | tf_op jit(solution)/shard_map/ppermute | solution.py:349
  124.2 0.8 copy-start.29
  125.0 0.8 copy-start.31
  125.9 0.8 copy-start.33
  126.7 1.3 copy-start.21
  128.0 1.9 copy-start
  129.9 1.0 copy-start.3
  130.9 1.0 copy-start.5
  131.9 1.0 copy-start.7
  132.9 1.0 copy-start.9
  133.9 1.0 copy-start.11
  134.9 0.9 copy-start.13
  135.8 0.9 copy-start.15
  136.7 0.9 copy-start.17
  137.7 0.9 copy-start.19
  138.6 1.6 copy-start.22
  140.2 1.0 copy-start.24
  141.2 1.0 copy-start.26
  142.3 1.0 copy-start.28
  143.3 1.0 copy-start.30
  144.4 1.0 copy-start.32
  145.4 1.0 copy-start.34
  146.4 11.4 %copy-start.1 = (bf16[2048,768]{1,0:T(8,128)(2,1)S(1)}, bf16[2048,768]{1,0:T(8,128)(2,1)}, u32[]{:S(2)}) copy-start(bf16[2048,768]{1,0:T(8,128)(2,1)} %all-gather.2.cloned.1.call-done.refs_8_.refs_2_) | copy-start | bytes 9437188
  155.4 2.4 %collective-permute-start.23 = (bf16[64,4096]{1,0:T(8,128)(2,1)}, bf16[64,4096]{1,0:T(8,128)(2,1)S(1)}, u32[]{:S(2)}, u32[]{:S(2)}) collective-permute-start(bf16[64,4096]{1,0:T(8,128)(2,1)} %collective-permute-done.18.refs_0_), channel_id=1, source_target_pairs={{0,1},{1,0},{2,3},{3,2},{4,5},{5,4},{6,7},{7,6},{8,9},{9,8},{10,11... | collective-permute-start | bytes 1572872 | tf_op jit(solution)/shard_map/ppermute | solution.py:353
  160.4 13.6 %copy-start.35 = (s32[1,128]{1,0:T(1,128)S(1)}, s32[1,128]{1,0:T(1,128)}, u32[]{:S(2)}) copy-start(s32[1,128]{1,0:T(1,128)} %placement_ref.1) | copy-start | bytes 1540
  168.8 24.5 %all-to-all-start.1 = ((bf16[128,8,512]{2,1,0:T(8,128)(2,1)}), bf16[128,8,512]{2,1,0:T(8,128)(2,1)S(1)}, u32[]{:S(2)}, u32[]{:S(2)}) async-start(bf16[128,8,512]{2,1,0:T(8,128)(2,1)} %bitcast.39), calls=%async_computation.1 | async-start | bytes 2097152 | tf_op jit(solution)/shard_map/all_to_all | solution.py:357
Sparse Core Ops, SparseCore 0:
  21.0 73.9 all-gather.1

commit v5 on v2

--- a/solution.py
+++ b/solution.py
@@ -29,8 +29,7 @@
     ends = jnp.cumsum(lengths)
     begins = jnp.sum(jnp.where(position[:, None] >= ends[None, :], lengths[None, :], 0), axis=1)
     angles = (position - begins).astype(jnp.float32)[:, None] * frequencies()[None, :]
-    cosine, sine = jnp.cos(angles), jnp.sin(angles)
-    return jnp.concatenate([cosine, cosine], axis=1), jnp.concatenate([-sine, sine], axis=1)
+    return jnp.cos(angles), jnp.sin(angles)
 
 
 def sort_kernel(target_ref, rows_ref, out_ref):
@@ -96,6 +95,11 @@
     )
 
 
+def ring_blocks(block, axis):
+    ways = [[(i, (i + d) % 4) for i in range(4)] for d in (1, 3, 2)]
+    return jnp.concatenate([block] + [lax.ppermute(block, axis, way) for way in ways], axis=0)
+
+
 def spread(block, axis):
     up, down = [(i, (i + 1) % 4) for i in range(4)], [(i, (i + 3) % 4) for i in range(4)]
     half = block.shape[0] // 2
@@ -109,17 +113,14 @@
 SPAN = ((0, (0, 1, 2, 3)), (3, (0, 1, 2, 3)), (1, (0, 1, 2, 3)), (2, (0, 1)), (2, (2, 3)))
 
 
-def gather_weights(projection, member):
+def gather_weights(mine, theirs, rows):
     x, y, zh = lax.axis_index("x"), lax.axis_index("y"), lax.axis_index("zh")
-    rows = projection.shape[0]
-    mine = lax.all_gather(own_columns(projection, member), ("x", "y"), axis=0, tiled=True)
-    theirs = lax.ppermute(own_columns(projection, member ^ 2), ("zh", "zl"), [(0, 3), (3, 0), (1, 2), (2, 1)])
     half = theirs.shape[1] // 2
     pieces = [mine]
     places = [(i * 2 + zh) * rows for i in range(16)]
     for side, (one, two) in enumerate((("y", "x"), ("x", "y"))):
         block = theirs[:, side * half : (side + 1) * half]
-        pieces += spread(jnp.concatenate(spread(block, one), axis=0), two)
+        pieces += spread(ring_blocks(block, one), two)
         for outer, inners in SPAN:
             for inner in inners:
                 near, far = (outer, RING[inner]) if side == 0 else (RING[inner], outer)
@@ -127,51 +128,78 @@
     return jnp.stack(places), pieces
 
 
-def project_kernel(places_ref, rows_ref, *refs):
-    pieces, out_ref, ordered = refs[:-2], refs[-2], refs[-1]
-    width = out_ref.shape[1]
-    half = width // 2
+def project_kernel(parts, places_ref, *refs):
+    row_refs, pieces, out_refs = refs[:parts], refs[parts : parts + 11], refs[parts + 11 : 2 * parts + 11]
+    held, ordered, weights, row_sems, sems = refs[2 * parts + 11], refs[2 * parts + 12], refs[-5:-2], refs[-2], refs[-1]
+    half = out_refs[0].shape[1] // 2
     step = 128
 
-    def take(first, count):
-        for i in range(count):
-            column = pl.multiple_of(places_ref[first + i], step)
-            ordered[:, i * step : (i + 1) * step] = rows_ref[:, pl.ds(column, step)]
-
-    def product(parts):
-        total, at = None, 0
-        for part in parts:
-            depth = part.shape[0]
-            term = jnp.dot(ordered[:, at : at + depth], part[...], preferred_element_type=jnp.float32)
-            total = term if total is None else total + term
-            at += depth
-        return total
-
-    take(0, 16)
-    out = product(pieces[:1])
-    for side in range(2):
-        take(16 + side * 16, 16)
-        other = product(pieces[1 + side * 5 : 6 + side * 5])
-        columns = slice(side * half, (side + 1) * half)
-        out_ref[:, columns] = (out[:, columns] + other).astype(jnp.bfloat16)
+    row_copies, at = [], 0
+    for i, rows in enumerate(row_refs):
+        row_copies.append(pltpu.make_async_copy(rows, held.at[pl.ds(at, rows.shape[0])], row_sems.at[i]))
+        row_copies[-1].start()
+        at += rows.shape[0]
+    copies = [[], [], []]
+    for i, piece in enumerate(pieces):
+        which = 0 if i == 0 else 1 + (i - 1) // 5
+        at = 0 if i in (0, 1, 6) else at
+        for first in range(0, piece.shape[0], 512):
+            count = min(512, piece.shape[0] - first)
+            copy = pltpu.make_async_copy(
+                piece.at[pl.ds(first, count)],
+                weights[which].at[pl.ds(at, count)],
+                sems.at[sum(len(c) for c in copies)],
+            )
+            copy.start()
+            copies[which].append(copy)
+            at += count
+
+    for copy in row_copies:
+        copy.wait()
+    total = None
+    for which in range(3):
+        for i in range(16):
+            column = pl.multiple_of(places_ref[which * 16 + i], step)
+            ordered[:, i * step : (i + 1) * step] = held[:, pl.ds(column, step)]
+        for copy in copies[which]:
+            copy.wait()
+        here = jnp.dot(ordered[...], weights[which][...], preferred_element_type=jnp.float32)
+        if which == 0:
+            total = here
+            continue
+        columns = slice((which - 1) * half, which * half)
+        here = (total[:, columns] + here).astype(jnp.bfloat16)
+        at = 0
+        for out_ref in out_refs:
+            out_ref[:, columns] = here[at : at + out_ref.shape[0]]
+            at += out_ref.shape[0]
 
 
 def project(places, pieces, rows):
-    count, depth = rows.shape
+    count, depth = sum(r.shape[0] for r in rows), rows[0].shape[1]
     width = pieces[0].shape[1]
     whole = pl.BlockSpec(memory_space=pltpu.VMEM)
+    anywhere = pl.BlockSpec(memory_space=pl.ANY)
     return pl.pallas_call(
-        project_kernel,
-        out_shape=jax.ShapeDtypeStruct((count, width), jnp.bfloat16),
-        in_specs=[pl.BlockSpec(memory_space=pltpu.SMEM)] + [whole] * (1 + len(pieces)),
-        out_specs=whole,
-        scratch_shapes=[pltpu.VMEM((count, depth // 2), jnp.bfloat16)],
-        compiler_params=pltpu.CompilerParams(vmem_limit_bytes=24 * 2**20),
+        functools.partial(project_kernel, len(rows)),
+        out_shape=[jax.ShapeDtypeStruct((r.shape[0], width), jnp.bfloat16) for r in rows],
+        in_specs=[pl.BlockSpec(memory_space=pltpu.SMEM)] + [anywhere] * (len(rows) + len(pieces)),
+        out_specs=[whole] * len(rows),
+        scratch_shapes=[
+            pltpu.VMEM((count, depth), jnp.bfloat16),
+            pltpu.VMEM((count, depth // 2), jnp.bfloat16),
+            pltpu.VMEM((depth // 2, width), jnp.bfloat16),
+            pltpu.VMEM((depth // 2, width // 2), jnp.bfloat16),
+            pltpu.VMEM((depth // 2, width // 2), jnp.bfloat16),
+            pltpu.SemaphoreType.DMA((len(rows),)),
+            pltpu.SemaphoreType.DMA((14,)),
+        ],
+        compiler_params=pltpu.CompilerParams(vmem_limit_bytes=60 * 2**20),
         cost_estimate=pl.CostEstimate(
             flops=2 * count * depth * width, bytes_accessed=2 * depth * (width + count), transcendentals=0
         ),
         name="project",
-    )(places, rows, *pieces)
+    )(places, *rows, *pieces)
 
 
 def attention_kernel(member_ref, lengths_ref, *refs):
@@ -195,7 +223,8 @@
         for s in range(blocks):
             rows = slice(s * BLOCK + h * part, s * BLOCK + (h + 1) * part)
             here = chunk[s * part : (s + 1) * part]
-            cosine, sine = cos_ref[rows], sin_ref[rows]
+            cosine = jnp.concatenate([cos_ref[rows]] * 2, axis=1)
+            sine = jnp.concatenate([-sin_ref[rows], sin_ref[rows]], axis=1)
 
             def rotate(x):
                 return (x * cosine + pltpu.roll(x, half, 1) * sine).astype(jnp.bfloat16)
@@ -276,18 +305,21 @@
     piece = row_count // devices
     member = lax.axis_index(CTX)
 
-    places, pieces = gather_weights(projection, member)
+    mine = lax.all_gather(own_columns(projection, member), ("x", "y"), axis=0, tiled=True)
+    theirs = lax.ppermute(own_columns(projection, member ^ 2), ("zh", "zl"), [(0, 3), (3, 0), (1, 2), (2, 1)])
+    tables = rotary_tables(doc_lengths[0], members * row_count)
     target = (placement[0][:, None] * piece + jnp.arange(piece, dtype=jnp.int32)[None, :]).reshape(row_count)
     outgoing = sort_rows(tokens, target, groups)
     arrived = lax.all_to_all(outgoing, DP, 0, 0, tiled=True).reshape(row_count, width)
+    arrived, theirs, tables = lax.optimization_barrier((arrived, theirs, tables))
+    places, pieces = gather_weights(mine, theirs, projection.shape[0])
     across = [(0, 1), (1, 0)]
     far = lax.ppermute(arrived, "zl", across)
     near = lax.ppermute(arrived, "core", across)
-    lanes = [project(places, pieces, arrived), project(places, pieces, near)]
-    tables = rotary_tables(doc_lengths[0], members * row_count)
-    far, lanes, tables = lax.optimization_barrier((far, lanes, tables))
+    lanes = project(places, pieces, [arrived, near])
+    far, lanes = lax.optimization_barrier((far, lanes))
     last = lax.ppermute(far, "core", across)
-    lanes = lanes + [project(places, pieces, far), project(places, pieces, last)]
+    lanes = lanes + project(places, pieces, [far]) + project(places, pieces, [last])
     mixed = attend(member.reshape(1), doc_lengths, lanes, *tables)
     returned = lax.all_to_all(
         mixed.reshape(devices, members * piece, GROUP * HEAD_DIM), EVERY, 0, 0, tiled=True

time: 173 us -> 189 us (1.092)
  waiting for transfers between devices: 63.1 us -> 78.3 us
  Pallas kernels: 29.6 us -> 41.1 us
  local copies, waits for them, and re-layouts: 15.8 us -> 7.45 us
  other arithmetic: 7.88 us -> 3.69 us
  starting transfers between devices: 42.3 us -> 44.4 us
    ppermute x1 -> x7, waiting for transfers between devices: 0.01 us -> 45.5 us  [the longest x6 24.7 us: ring_blocks(): lax.ppermute(block, axis, way)]
    all_to_all x1, waiting for transfers between devices: 28.5 us -> 5.4 us  [on_device(): lax.all_to_all(outgoing, DP, 0, 0, tiled=True).reshape(row_count, width)]
    ppermute x4 -> x2, waiting for transfers between devices: 11 us -> 0.36 us  [spread(): lax.ppermute(block, axis, up)]
    pallas_call x4 -> x3, Pallas kernels: 17.4 us -> 27.6 us  [project(): pl.pallas_call(functools.partial(project_kernel, len(rows)), out_shape=[j...]
    ppermute x1 -> x7, starting transfers between devices: 2.97 us -> 9.61 us  [the longest x6 6.71 us: ring_blocks(): lax.ppermute(block, axis, way)]
    unnamed x20 -> x24, local copies, waits for them, and re-layouts: 8.63 us -> 2.62 us
    ppermute x4 -> x2, starting transfers between devices: 7.99 us -> 2.05 us  [spread(): far_high = lax.ppermute(above[half:], axis, down)]
    ppermute x4 -> x2, starting transfers between devices: 7.34 us -> 2.87 us  [spread(): lax.ppermute(block, axis, down)]
  transfers between devices with their start and end apart: 23 -> 21, of which waited for: 10 -> 12; matrix products, arithmetic and copies ran while one was open for 9% -> 3% of each run, Pallas kernels for 9% -> 12%
where the time goes in v5:
time: 189 us
  waiting for transfers between devices  78.3 us (41%)
  starting transfers between devices  44.4 us (23%)
  Pallas kernels  41.1 us (22%)
  between operations  13.7 us (7%)
  local copies, waits for them, and re-layouts  7.45 us (4%)
  other arithmetic  3.69 us (2%)
    pallas_call x3, Pallas kernels, project(): pl.pallas_call(functools.partial(project_kernel, len(rows)), out_shape=[j...  27.6 us
    ppermute x6, waiting for transfers between devices, ring_blocks(): lax.ppermute(block, axis, way)  24.7 us
    ppermute x1, waiting for transfers between devices, on_device(): lax.ppermute(own_columns(projection, member ^ 2), ('zh', 'zl'), [(0, 3),...  20.8 us
    all_to_all x1, waiting for transfers between devices, on_device(): lax.all_to_all(mixed.reshape(devices, members * piece, GROUP * HEAD_DIM),...  19.2 us
    all_to_all x1, starting transfers between devices, on_device(): lax.all_to_all(outgoing, DP, 0, 0, tiled=True).reshape(row_count, width)  11.4 us
    all_to_all x1, starting transfers between devices, on_device(): lax.all_to_all(mixed.reshape(devices, members * piece, GROUP * HEAD_DIM),...  8.89 us
    pallas_call x1, Pallas kernels, attend(): pl.pallas_call(attention_kernel, out_shape=jax.ShapeDtypeStruct((count, G...  8.43 us
    ppermute x6, starting transfers between devices, ring_blocks(): lax.ppermute(block, axis, way)  6.71 us
  transfers between devices with their start and end apart: 21, of which 12 were waited for; matrix products, arithmetic and copies ran while one was open for 3% of the time, Pallas kernels for 12%

profile of v5, /device:TPU:1, one launch (start us, length us, event | category | flops | bytes accessed | tf_op | source)
XLA Modules:
  0.0 188.6 jit_solution(10401808985090096246)
XLA Ops:
  6.5 1.0 constant_dynamic-slice_fusion.1
  7.5 0.8 constant_dynamic-slice_fusion
  8.4 0.7 pad_maximum_fusion.3
  9.1 0.0 all-gather.2.cloned.1.call-update
  9.1 0.7 multiply_bitcast_fusion
  9.7 0.1 iota_add_fusion
  9.8 0.1 add.357.target_ref
  10.0 0.0 copy-start
  10.0 1.6 copy-done
  11.6 2.8 %sort_rows.1 = bf16[32,8,4096]{2,1,0:T(8,128)(2,1)} custom-call(s32[1,256]{1,0:T(1,128)S(1)} %add.357.target_ref, bf16[256,4096]{1,0:T(8,128)(2,1)S(1)} %copy-done), custom_call_target="tpu_custom_call" | custom-call | tf_op jit(solution)/shard_map/sort_rows/pallas_call | solution.py:47
  14.4 11.4 %all-to-all-start = ((bf16[32,8,4096]{2,1,0:T(8,128)(2,1)}), bf16[32,8,4096]{2,1,0:T(8,128)(2,1)}, u32[]{:S(2)}, u32[]{:S(2)}) async-start(bf16[32,8,4096]{2,1,0:T(8,128)(2,1)} %sort_rows.1), calls=%async_computation | async-start | bytes 4194304 | tf_op jit(solution)/shard_map/all_to_all | solution.py:313
  25.8 2.9 %collective-permute-start = (bf16[128,768]{1,0:T(8,128)(2,1)S(1)}, bf16[128,768]{1,0:T(8,128)(2,1)S(1)}, u32[]{:S(2)}, u32[]{:S(2)}) collective-permute-start(bf16[128,768]{1,0:T(8,128)(2,1)S(1)} %pad_maximum_fusion.2), channel_id=1, source_target_pairs={{0,6},{6,0},{2,4},{4,2},{1,7},{7,1},{3,5},{5,3},{8,14},{14,8},{10,... | collective-permute-start | bytes 589832 | tf_op jit(solution)/shard_map/ppermute | solution.py:309
  28.7 0.2 reduce-window.8
  28.9 0.1 select_reduce_fusion
  29.0 1.9 multiply_sine_fusion
  30.9 20.8 %collective-permute-done = bf16[128,768]{1,0:T(8,128)(2,1)S(1)} collective-permute-done((bf16[128,768]{1,0:T(8,128)(2,1)S(1)}, bf16[128,768]{1,0:T(8,128)(2,1)S(1)}, u32[]{:S(2)}, u32[]{:S(2)}) %collective-permute-start) | collective-permute-done | bytes 196640 | tf_op jit(solution)/shard_map/ppermute | solution.py:309
  51.7 5.4 %all-to-all-done = bf16[32,8,4096]{2,1,0:T(8,128)(2,1)} async-done(((bf16[32,8,4096]{2,1,0:T(8,128)(2,1)}), bf16[32,8,4096]{2,1,0:T(8,128)(2,1)}, u32[]{:S(2)}, u32[]{:S(2)}) %all-to-all-start) | async-done | bytes 2097184 | tf_op jit(solution)/shard_map/all_to_all | solution.py:313
  57.1 0.9 collective-permute-start.2
  58.1 0.9 collective-permute-start.1
  59.0 0.1 collective-permute-start.10
  59.0 2.7 %collective-permute-start.11 = (bf16[128,384]{1,0:T(8,128)(2,1)S(1)}, bf16[128,384]{1,0:T(8,128)(2,1)S(1)}, u32[]{:S(2)}, u32[]{:S(2)}) collective-permute-start(bf16[128,384]{1,0:T(8,128)(2,1)S(1)} %get-tuple-element.29), channel_id=1, source_target_pairs={{0,96},{32,0},{64,32},{96,64},{1,97},{33,1},{65,33},{97,65},{2,98}... | collective-permute-start | bytes 294920 | tf_op jit(solution)/shard_map/ppermute | solution.py:100
  61.7 0.0 collective-permute-start.12
  61.7 5.5 %collective-permute-done.10 = bf16[128,384]{1,0:T(8,128)(2,1)S(1)} collective-permute-done((bf16[128,384]{1,0:T(8,128)(2,1)S(1)}, bf16[128,384]{1,0:T(8,128)(2,1)S(1)}, u32[]{:S(2)}, u32[]{:S(2)}) %collective-permute-start.10) | collective-permute-done | bytes 98336 | tf_op jit(solution)/shard_map/ppermute | solution.py:100
  67.2 0.0 collective-permute-done.11
  67.2 2.8 %collective-permute-done.12 = bf16[128,384]{1,0:T(8,128)(2,1)S(1)} collective-permute-done((bf16[128,384]{1,0:T(8,128)(2,1)S(1)}, bf16[128,384]{1,0:T(8,128)(2,1)S(1)}, u32[]{:S(2)}, u32[]{:S(2)}) %collective-permute-start.12) | collective-permute-done | bytes 98336 | tf_op jit(solution)/shard_map/ppermute | solution.py:100
  70.1 0.6 collective-permute-start.13
  70.7 0.1 collective-permute-start.3
  70.8 2.6 %collective-permute-start.4 = (bf16[128,384]{1,0:T(8,128)(2,1)S(1)}, bf16[128,384]{1,0:T(8,128)(2,1)S(1)}, u32[]{:S(2)}, u32[]{:S(2)}) collective-permute-start(bf16[128,384]{1,0:T(8,128)(2,1)S(1)} %get-tuple-element.30), channel_id=1, source_target_pairs={{0,24},{8,0},{16,8},{24,16},{1,25},{9,1},{17,9},{25,17},{2,26},{10... | collective-permute-start | bytes 294920 | tf_op jit(solution)/shard_map/ppermute | solution.py:100
  73.4 14.2 %collective-permute-done.3 = bf16[128,384]{1,0:T(8,128)(2,1)S(1)} collective-permute-done((bf16[128,384]{1,0:T(8,128)(2,1)S(1)}, bf16[128,384]{1,0:T(8,128)(2,1)S(1)}, u32[]{:S(2)}, u32[]{:S(2)}) %collective-permute-start.3) | collective-permute-done | bytes 98336 | tf_op jit(solution)/shard_map/ppermute | solution.py:100
  87.6 1.3 collective-permute-start.5
  88.9 0.0 collective-permute-done.4
  88.9 1.5 collective-permute-start.14
  90.4 2.2 %collective-permute-done.5 = bf16[128,384]{1,0:T(8,128)(2,1)S(1)} collective-permute-done((bf16[128,384]{1,0:T(8,128)(2,1)S(1)}, bf16[128,384]{1,0:T(8,128)(2,1)S(1)}, u32[]{:S(2)}, u32[]{:S(2)}) %collective-permute-start.5) | collective-permute-done | bytes 98336 | tf_op jit(solution)/shard_map/ppermute | solution.py:100
  92.6 0.0 copy-start.7
  92.6 1.4 collective-permute-start.6
  94.0 0.0 collective-permute-done.13.refs_9_.refs_8_
  94.0 1.3 collective-permute-start.7
  95.4 4.0 %collective-permute-done.14.refs_10_.refs_9_ = bf16[512,384]{1,0:T(8,128)(2,1)S(1)} collective-permute-done((bf16[512,384]{1,0:T(8,128)(2,1)S(1)}, bf16[512,384]{1,0:T(8,128)(2,1)S(1)}, u32[]{:S(2)}, u32[]{:S(2)}) %collective-permute-start.14) | collective-permute-done | bytes 393248 | tf_op jit(solution)/shard_map/ppermute | solution.py:106
  99.4 1.8 collective-permute-start.15
  101.2 0.7 slice.27
  101.9 0.4 collective-permute-done.6.refs_4_.refs_3_
  102.3 0.5 collective-permute-start.16
  102.8 0.7 slice.24
  103.5 0.0 collective-permute-done.7.refs_5_.refs_4_
  103.5 0.4 collective-permute-start.8
  103.9 0.7 slice.25
  104.6 0.9 collective-permute-done.15.refs_11_.refs_10_
  105.5 1.6 collective-permute-start.9
  107.1 0.7 stack.147.places_ref
  107.8 0.0 collective-permute-done.16.refs_12_.refs_11_
  107.8 1.8 collective-permute-done.8.refs_6_.refs_5_
  109.5 1.1 collective-permute-done.9.refs_7_.refs_6_
  110.7 10.9 %project.3 = (bf16[256,768]{1,0:T(8,128)(2,1)}, bf16[256,768]{1,0:T(8,128)(2,1)}) custom-call(s32[48]{0:T(128)} %stack.147.places_ref, bf16[256,4096]{1,0:T(8,128)(2,1)} %bitcast.2.refs_0_, bf16[256,4096]{1,0:T(8,128)(2,1)} %collective-permute-done.2.refs_1_, bf16[2048,768]{1,0:T(8,128)(2,1)} %all-gather.2.cloned.1.call-done.refs_2_.refs_1_, ...), custom_call_target="tpu_custom_call" | custom-call | flops 3221225472 | bytes 10485760 | tf_op jit(solution)/shard_map/project/pallas_call | solution.py:183
  121.6 0.0 collective-permute-done.1.refs_0_
  121.6 3.4 %collective-permute-start.17 = (bf16[256,4096]{1,0:T(8,128)(2,1)}, bf16[256,4096]{1,0:T(8,128)(2,1)}, u32[]{:S(2)}, u32[]{:S(2)}) collective-permute-start(bf16[256,4096]{1,0:T(8,128)(2,1)} %collective-permute-done.1.refs_0_), channel_id=1, source_target_pairs={{0,1},{1,0},{2,3},{3,2},{4,5},{5,4},{6,7},{7,6},{8,9},{9,8},{10,11... | collective-permute-start | bytes 6291464 | tf_op jit(solution)/shard_map/ppermute | solution.py:321
  125.1 8.3 %project.4.refs_2_ = bf16[256,768]{1,0:T(8,128)(2,1)} custom-call(s32[48]{0:T(128)} %stack.147.places_ref, bf16[256,4096]{1,0:T(8,128)(2,1)} %collective-permute-done.1.refs_0_, bf16[2048,768]{1,0:T(8,128)(2,1)} %all-gather.2.cloned.1.call-done.refs_2_.refs_1_, bf16[512,384]{1,0:T(8,128)(2,1)} %copy-done.7, bf16[512,384]{1,0:T(8,128)(2,1)} %copy-done.10, ...), custom_call_target="tpu_custom_call" | custom-call | flops 1610612736 | bytes 8388608 | tf_op jit(solution)/shard_map/project/pallas_call | solution.py:183
  133.4 0.0 collective-permute-done.17.refs_0_
  133.4 8.4 %project.5.refs_3_ = bf16[256,768]{1,0:T(8,128)(2,1)} custom-call(s32[48]{0:T(128)} %stack.147.places_ref, bf16[256,4096]{1,0:T(8,128)(2,1)} %collective-permute-done.17.refs_0_, bf16[2048,768]{1,0:T(8,128)(2,1)} %all-gather.2.cloned.1.call-done.refs_2_.refs_1_, bf16[512,384]{1,0:T(8,128)(2,1)} %copy-done.7, bf16[512,384]{1,0:T(8,128)(2,1)} %copy-done.10, ...), custom_call_target="tpu_custom_call" | custom-call | flops 1610612736 | bytes 8388608 | tf_op jit(solution)/shard_map/project/pallas_call | solution.py:183
  141.9 1.0 copy-done.2
  142.8 8.4 %attend.1 = bf16[1024,512]{1,0:T(8,128)(2,1)} custom-call(s32[1]{0:T(128)} %bitcast.1.member_ref, s32[1,8]{1,0:T(1,128)S(1)} %copy-done.5, bf16[256,768]{1,0:T(8,128)(2,1)S(1)} %copy-done.3, bf16[256,768]{1,0:T(8,128)(2,1)S(1)} %copy-done.4, bf16[256,768]{1,0:T(8,128)(2,1)S(1)} %copy-done.1, bf16[256,768]{1,0:T(8,128)(2,1)S(1)} %copy-done.2, ...), custom_call_target="tpu_custom_call" | custom-call | tf_op jit(solution)/shard_map/attend/pallas_call | solution.py:284
  151.3 8.9 %all-to-all-start.1 = ((bf16[128,8,512]{2,1,0:T(8,128)(2,1)}), bf16[128,8,512]{2,1,0:T(8,128)(2,1)S(1)}, u32[]{:S(2)}, u32[]{:S(2)}) async-start(bf16[128,8,512]{2,1,0:T(8,128)(2,1)} %bitcast.38), calls=%async_computation.1 | async-start | bytes 2097152 | tf_op jit(solution)/shard_map/all_to_all | solution.py:324
  160.2 0.1 add.417.target_ref
  160.3 19.2 %all-to-all-done.1 = bf16[128,8,512]{2,1,0:T(8,128)(2,1)S(1)} async-done(((bf16[128,8,512]{2,1,0:T(8,128)(2,1)}), bf16[128,8,512]{2,1,0:T(8,128)(2,1)S(1)}, u32[]{:S(2)}, u32[]{:S(2)}) %all-to-all-start.1) | async-done | bytes 1048608 | tf_op jit(solution)/shard_map/all_to_all | solution.py:324
  179.5 2.3 %unsort_rows.1 = bf16[256,2048]{1,0:T(8,128)(2,1)} custom-call(s32[256,1]{1,0:T(8,128)S(1)} %add.417.target_ref, bf16[32,4,8,512]{3,2,1,0:T(8,128)(2,1)S(1)} %bitcast.41), custom_call_target="tpu_custom_call" | custom-call | tf_op jit(solution)/shard_map/unsort_rows/pallas_call | solution.py:72
  (30 shorter events, 0.2 us)
Async XLA Ops:
  6.5 104.1 %all-gather.2.cloned.1.call-start = ((), (), s32[]{:S(2)}) async-start(), calls=%async_computation.2 | async-start | bytes 3342336 | tf_op jit(solution)/shard_map/all_gather | solution.py:308
  10.0 1.6 copy-start
  14.4 14.4 %copy-start.5 = (s32[1,8]{1,0:T(1,128)S(1)}, s32[1,8]{1,0:T(1,128)}, u32[]{:S(2)}) copy-start(s32[1,8]{1,0:T(1,128)} %lengths_ref.1) | copy-start | bytes 100
  14.4 42.8 %all-to-all-start = ((bf16[32,8,4096]{2,1,0:T(8,128)(2,1)}), bf16[32,8,4096]{2,1,0:T(8,128)(2,1)}, u32[]{:S(2)}, u32[]{:S(2)}) async-start(bf16[32,8,4096]{2,1,0:T(8,128)(2,1)} %sort_rows.1), calls=%async_computation | async-start | bytes 4194304 | tf_op jit(solution)/shard_map/all_to_all | solution.py:313
  25.8 25.9 %collective-permute-start = (bf16[128,768]{1,0:T(8,128)(2,1)S(1)}, bf16[128,768]{1,0:T(8,128)(2,1)S(1)}, u32[]{:S(2)}, u32[]{:S(2)}) collective-permute-start(bf16[128,768]{1,0:T(8,128)(2,1)S(1)} %pad_maximum_fusion.2), channel_id=1, source_target_pairs={{0,6},{6,0},{2,4},{4,2},{1,7},{7,1},{3,5},{5,3},{8,14},{14,8},{10,... | collective-permute-start | bytes 589832 | tf_op jit(solution)/shard_map/ppermute | solution.py:309
  57.1 53.5 %collective-permute-start.2 = (bf16[256,4096]{1,0:T(8,128)(2,1)}, bf16[256,4096]{1,0:T(8,128)(2,1)}, u32[]{:S(2)}, u32[]{:S(2)}) collective-permute-start(bf16[256,4096]{1,0:T(8,128)(2,1)} %bitcast.2.refs_0_), channel_id=1, source_target_pairs={{0,1},{1,0},{2,3},{3,2},{4,5},{5,4},{6,7},{7,6},{8,9},{9,8},{10,11... | collective-permute-start | bytes 6291464 | tf_op jit(solution)/shard_map/ppermute | solution.py:318
  58.1 63.5 %collective-permute-start.1 = (bf16[256,4096]{1,0:T(8,128)(2,1)}, bf16[256,4096]{1,0:T(8,128)(2,1)}, u32[]{:S(2)}, u32[]{:S(2)}) collective-permute-start(bf16[256,4096]{1,0:T(8,128)(2,1)} %bitcast.2.refs_0_), channel_id=1, source_target_pairs={{0,2},{2,0},{1,3},{3,1},{4,6},{6,4},{5,7},{7,5},{8,10},{10,8},{9,1... | collective-permute-start | bytes 6291464 | tf_op jit(solution)/shard_map/ppermute | solution.py:317
  59.0 8.2 %collective-permute-start.10 = (bf16[128,384]{1,0:T(8,128)(2,1)S(1)}, bf16[128,384]{1,0:T(8,128)(2,1)S(1)}, u32[]{:S(2)}, u32[]{:S(2)}) collective-permute-start(bf16[128,384]{1,0:T(8,128)(2,1)S(1)} %get-tuple-element.29), channel_id=1, source_target_pairs={{0,32},{32,64},{64,96},{96,0},{1,33},{33,65},{65,97},{97,1},{2,34}... | collective-permute-start | bytes 294920 | tf_op jit(solution)/shard_map/ppermute | solution.py:100
  59.0 8.2 %collective-permute-start.11 = (bf16[128,384]{1,0:T(8,128)(2,1)S(1)}, bf16[128,384]{1,0:T(8,128)(2,1)S(1)}, u32[]{:S(2)}, u32[]{:S(2)}) collective-permute-start(bf16[128,384]{1,0:T(8,128)(2,1)S(1)} %get-tuple-element.29), channel_id=1, source_target_pairs={{0,96},{32,0},{64,32},{96,64},{1,97},{33,1},{65,33},{97,65},{2,98}... | collective-permute-start | bytes 294920 | tf_op jit(solution)/shard_map/ppermute | solution.py:100
  61.7 8.3 %collective-permute-start.12 = (bf16[128,384]{1,0:T(8,128)(2,1)S(1)}, bf16[128,384]{1,0:T(8,128)(2,1)S(1)}, u32[]{:S(2)}, u32[]{:S(2)}) collective-permute-start(bf16[128,384]{1,0:T(8,128)(2,1)S(1)} %get-tuple-element.29), channel_id=1, source_target_pairs={{0,64},{32,96},{64,0},{96,32},{1,65},{33,97},{65,1},{97,33},{2,66}... | collective-permute-start | bytes 294920 | tf_op jit(solution)/shard_map/ppermute | solution.py:100
  70.0 40.6 %copy-start.6 = (bf16[512,384]{1,0:T(8,128)(2,1)}, bf16[512,384]{1,0:T(8,128)(2,1)S(1)}, u32[]{:S(2)}) copy-start(bf16[512,384]{1,0:T(8,128)(2,1)S(1)} %pad_maximum_fusion.1.refs_8_.refs_7_) | copy-start | bytes 1179652
  70.1 24.0 %collective-permute-start.13 = (bf16[512,384]{1,0:T(8,128)(2,1)S(1)}, bf16[512,384]{1,0:T(8,128)(2,1)S(1)}, u32[]{:S(2)}, u32[]{:S(2)}) collective-permute-start(bf16[512,384]{1,0:T(8,128)(2,1)S(1)} %pad_maximum_fusion.1.refs_8_.refs_7_), channel_id=1, source_target_pairs={{0,8},{8,16},{16,24},{24,0},{1,9},{9,17},{17,25},{25,1},{2,10},{10... | collective-permute-start | bytes 1179656 | tf_op jit(solution)/shard_map/ppermute | solution.py:106
  70.7 16.9 %collective-permute-start.3 = (bf16[128,384]{1,0:T(8,128)(2,1)S(1)}, bf16[128,384]{1,0:T(8,128)(2,1)S(1)}, u32[]{:S(2)}, u32[]{:S(2)}) collective-permute-start(bf16[128,384]{1,0:T(8,128)(2,1)S(1)} %get-tuple-element.30), channel_id=1, source_target_pairs={{0,8},{8,16},{16,24},{24,0},{1,9},{9,17},{17,25},{25,1},{2,10},{10... | collective-permute-start | bytes 294920 | tf_op jit(solution)/shard_map/ppermute | solution.py:100
  70.8 18.1 %collective-permute-start.4 = (bf16[128,384]{1,0:T(8,128)(2,1)S(1)}, bf16[128,384]{1,0:T(8,128)(2,1)S(1)}, u32[]{:S(2)}, u32[]{:S(2)}) collective-permute-start(bf16[128,384]{1,0:T(8,128)(2,1)S(1)} %get-tuple-element.30), channel_id=1, source_target_pairs={{0,24},{8,0},{16,8},{24,16},{1,25},{9,1},{17,9},{25,17},{2,26},{10... | collective-permute-start | bytes 294920 | tf_op jit(solution)/shard_map/ppermute | solution.py:100
  87.6 5.0 %collective-permute-start.5 = (bf16[128,384]{1,0:T(8,128)(2,1)S(1)}, bf16[128,384]{1,0:T(8,128)(2,1)S(1)}, u32[]{:S(2)}, u32[]{:S(2)}) collective-permute-start(bf16[128,384]{1,0:T(8,128)(2,1)S(1)} %get-tuple-element.30), channel_id=1, source_target_pairs={{0,16},{8,24},{16,0},{24,8},{1,17},{9,25},{17,1},{25,9},{2,18},{10... | collective-permute-start | bytes 294920 | tf_op jit(solution)/shard_map/ppermute | solution.py:100
  88.9 10.5 %collective-permute-start.14 = (bf16[512,384]{1,0:T(8,128)(2,1)S(1)}, bf16[512,384]{1,0:T(8,128)(2,1)S(1)}, u32[]{:S(2)}, u32[]{:S(2)}) collective-permute-start(bf16[512,384]{1,0:T(8,128)(2,1)S(1)} %pad_maximum_fusion.1.refs_8_.refs_7_), channel_id=1, source_target_pairs={{0,24},{8,0},{16,8},{24,16},{1,25},{9,1},{17,9},{25,17},{2,26},{10... | collective-permute-start | bytes 1179656 | tf_op jit(solution)/shard_map/ppermute | solution.py:106
  92.6 18.1 %copy-start.7 = (bf16[512,384]{1,0:T(8,128)(2,1)}, bf16[512,384]{1,0:T(8,128)(2,1)S(1)}, u32[]{:S(2)}) copy-start(bf16[512,384]{1,0:T(8,128)(2,1)S(1)} %pad_maximum_fusion.refs_3_.refs_2_) | copy-start | bytes 1179652
  92.6 9.7 %collective-permute-start.6 = (bf16[512,384]{1,0:T(8,128)(2,1)S(1)}, bf16[512,384]{1,0:T(8,128)(2,1)S(1)}, u32[]{:S(2)}, u32[]{:S(2)}) collective-permute-start(bf16[512,384]{1,0:T(8,128)(2,1)S(1)} %pad_maximum_fusion.refs_3_.refs_2_), channel_id=1, source_target_pairs={{0,32},{32,64},{64,96},{96,0},{1,33},{33,65},{65,97},{97,1},{2,34}... | collective-permute-start | bytes 1179656 | tf_op jit(solution)/shard_map/ppermute | solution.py:106
  94.0 16.7 %copy-start.8 = (bf16[512,384]{1,0:T(8,128)(2,1)}, bf16[512,384]{1,0:T(8,128)(2,1)S(1)}, u32[]{:S(2)}) copy-start(bf16[512,384]{1,0:T(8,128)(2,1)S(1)} %collective-permute-done.13.refs_9_.refs_8_) | copy-start | bytes 1179652
  94.0 9.5 %collective-permute-start.7 = (bf16[512,384]{1,0:T(8,128)(2,1)S(1)}, bf16[512,384]{1,0:T(8,128)(2,1)S(1)}, u32[]{:S(2)}, u32[]{:S(2)}) collective-permute-start(bf16[512,384]{1,0:T(8,128)(2,1)S(1)} %pad_maximum_fusion.refs_3_.refs_2_), channel_id=1, source_target_pairs={{0,96},{32,0},{64,32},{96,64},{1,97},{33,1},{65,33},{97,65},{2,98}... | collective-permute-start | bytes 1179656 | tf_op jit(solution)/shard_map/ppermute | solution.py:106
  99.4 11.3 %copy-start.9 = (bf16[512,384]{1,0:T(8,128)(2,1)}, bf16[512,384]{1,0:T(8,128)(2,1)S(1)}, u32[]{:S(2)}) copy-start(bf16[512,384]{1,0:T(8,128)(2,1)S(1)} %collective-permute-done.14.refs_10_.refs_9_) | copy-start | bytes 1179652
  99.4 6.1 %collective-permute-start.15 = (bf16[256,384]{1,0:T(8,128)(2,1)S(1)}, bf16[256,384]{1,0:T(8,128)(2,1)}, u32[]{:S(2)}, u32[]{:S(2)}) collective-permute-start(bf16[256,384]{1,0:T(8,128)(2,1)S(1)} %slice.26), channel_id=1, source_target_pairs={{0,8},{8,16},{16,24},{24,0},{1,9},{9,17},{17,25},{25,1},{2,10},{10... | collective-permute-start | bytes 589832 | tf_op jit(solution)/shard_map/ppermute | solution.py:107
  102.3 8.4 %copy-start.10 = (bf16[512,384]{1,0:T(8,128)(2,1)}, bf16[512,384]{1,0:T(8,128)(2,1)S(1)}, u32[]{:S(2)}) copy-start(bf16[512,384]{1,0:T(8,128)(2,1)S(1)} %collective-permute-done.6.refs_4_.refs_3_) | copy-start | bytes 1179652
  102.3 5.5 %collective-permute-start.16 = (bf16[256,384]{1,0:T(8,128)(2,1)}, bf16[256,384]{1,0:T(8,128)(2,1)}, u32[]{:S(2)}, u32[]{:S(2)}) collective-permute-start(bf16[256,384]{1,0:T(8,128)(2,1)} %slice.27), channel_id=1, source_target_pairs={{0,24},{8,0},{16,8},{24,16},{1,25},{9,1},{17,9},{25,17},{2,26},{10... | collective-permute-start | bytes 589832 | tf_op jit(solution)/shard_map/ppermute | solution.py:108
  103.5 7.2 %copy-start.11 = (bf16[512,384]{1,0:T(8,128)(2,1)}, bf16[512,384]{1,0:T(8,128)(2,1)S(1)}, u32[]{:S(2)}) copy-start(bf16[512,384]{1,0:T(8,128)(2,1)S(1)} %collective-permute-done.7.refs_5_.refs_4_) | copy-start | bytes 1179652
  103.5 6.0 %collective-permute-start.8 = (bf16[256,384]{1,0:T(8,128)(2,1)}, bf16[256,384]{1,0:T(8,128)(2,1)}, u32[]{:S(2)}, u32[]{:S(2)}) collective-permute-start(bf16[256,384]{1,0:T(8,128)(2,1)} %slice.24), channel_id=1, source_target_pairs={{0,32},{32,64},{64,96},{96,0},{1,33},{33,65},{65,97},{97,1},{2,34}... | collective-permute-start | bytes 589832 | tf_op jit(solution)/shard_map/ppermute | solution.py:107
  105.5 5.1 %collective-permute-start.9 = (bf16[256,384]{1,0:T(8,128)(2,1)}, bf16[256,384]{1,0:T(8,128)(2,1)}, u32[]{:S(2)}, u32[]{:S(2)}) collective-permute-start(bf16[256,384]{1,0:T(8,128)(2,1)} %slice.25), channel_id=1, source_target_pairs={{0,96},{32,0},{64,32},{96,64},{1,97},{33,1},{65,33},{97,65},{2,98}... | collective-permute-start | bytes 589832 | tf_op jit(solution)/shard_map/ppermute | solution.py:108
  121.6 11.8 %collective-permute-start.17 = (bf16[256,4096]{1,0:T(8,128)(2,1)}, bf16[256,4096]{1,0:T(8,128)(2,1)}, u32[]{:S(2)}, u32[]{:S(2)}) collective-permute-start(bf16[256,4096]{1,0:T(8,128)(2,1)} %collective-permute-done.1.refs_0_), channel_id=1, source_target_pairs={{0,1},{1,0},{2,3},{3,2},{4,5},{5,4},{6,7},{7,6},{8,9},{9,8},{10,11... | collective-permute-start | bytes 6291464 | tf_op jit(solution)/shard_map/ppermute | solution.py:321
  133.3 8.5 %copy-start.1 = (bf16[256,768]{1,0:T(8,128)(2,1)S(1)}, bf16[256,768]{1,0:T(8,128)(2,1)}, u32[]{:S(2)}) copy-start(bf16[256,768]{1,0:T(8,128)(2,1)} %project.4.refs_2_) | copy-start | bytes 1179652
  133.4 8.5 %copy-start.3 = (bf16[256,768]{1,0:T(8,128)(2,1)S(1)}, bf16[256,768]{1,0:T(8,128)(2,1)}, u32[]{:S(2)}) copy-start(bf16[256,768]{1,0:T(8,128)(2,1)} %get-tuple-element.18.refs_0_) | copy-start | bytes 1179652
  133.4 8.5 %copy-start.4 = (bf16[256,768]{1,0:T(8,128)(2,1)S(1)}, bf16[256,768]{1,0:T(8,128)(2,1)}, u32[]{:S(2)}) copy-start(bf16[256,768]{1,0:T(8,128)(2,1)} %get-tuple-element.19.refs_1_) | copy-start | bytes 1179652
  141.8 1.0 copy-start.2
  151.3 28.2 %all-to-all-start.1 = ((bf16[128,8,512]{2,1,0:T(8,128)(2,1)}), bf16[128,8,512]{2,1,0:T(8,128)(2,1)S(1)}, u32[]{:S(2)}, u32[]{:S(2)}) async-start(bf16[128,8,512]{2,1,0:T(8,128)(2,1)} %bitcast.38), calls=%async_computation.1 | async-start | bytes 2097152 | tf_op jit(solution)/shard_map/all_to_all | solution.py:324
Sparse Core Ops, SparseCore 0:
  9.5 70.9 all-gather.1

commit v6 on v2

--- a/solution.py
+++ b/solution.py
@@ -96,6 +96,11 @@
     )
 
 
+def ring_blocks(block, axis):
+    ways = [[(i, (i + d) % 4) for i in range(4)] for d in (1, 3, 2)]
+    return jnp.concatenate([block] + [lax.ppermute(block, axis, way) for way in ways], axis=0)
+
+
 def spread(block, axis):
     up, down = [(i, (i + 1) % 4) for i in range(4)], [(i, (i + 3) % 4) for i in range(4)]
     half = block.shape[0] // 2
@@ -109,17 +114,14 @@
 SPAN = ((0, (0, 1, 2, 3)), (3, (0, 1, 2, 3)), (1, (0, 1, 2, 3)), (2, (0, 1)), (2, (2, 3)))
 
 
-def gather_weights(projection, member):
+def gather_weights(mine, theirs, rows):
     x, y, zh = lax.axis_index("x"), lax.axis_index("y"), lax.axis_index("zh")
-    rows = projection.shape[0]
-    mine = lax.all_gather(own_columns(projection, member), ("x", "y"), axis=0, tiled=True)
-    theirs = lax.ppermute(own_columns(projection, member ^ 2), ("zh", "zl"), [(0, 3), (3, 0), (1, 2), (2, 1)])
     half = theirs.shape[1] // 2
     pieces = [mine]
     places = [(i * 2 + zh) * rows for i in range(16)]
-    for side, (one, two) in enumerate((("y", "x"), ("x", "y"))):
-        block = theirs[:, side * half : (side + 1) * half]
-        pieces += spread(jnp.concatenate(spread(block, one), axis=0), two)
+    ready = lax.optimization_barrier([ring_blocks(theirs[:, :half], "y"), ring_blocks(theirs[:, half:], "x")])
+    for side, two in enumerate(("x", "y")):
+        pieces += spread(ready[side], two)
         for outer, inners in SPAN:
             for inner in inners:
                 near, far = (outer, RING[inner]) if side == 0 else (RING[inner], outer)
@@ -276,18 +278,21 @@
     piece = row_count // devices
     member = lax.axis_index(CTX)
 
-    places, pieces = gather_weights(projection, member)
+    mine = lax.all_gather(own_columns(projection, member), ("x", "y"), axis=0, tiled=True)
+    theirs = lax.ppermute(own_columns(projection, member ^ 2), ("zh", "zl"), [(0, 3), (3, 0), (1, 2), (2, 1)])
     target = (placement[0][:, None] * piece + jnp.arange(piece, dtype=jnp.int32)[None, :]).reshape(row_count)
     outgoing = sort_rows(tokens, target, groups)
     arrived = lax.all_to_all(outgoing, DP, 0, 0, tiled=True).reshape(row_count, width)
+    arrived, theirs = lax.optimization_barrier((arrived, theirs))
+    places, pieces = gather_weights(mine, theirs, projection.shape[0])
     across = [(0, 1), (1, 0)]
     far = lax.ppermute(arrived, "zl", across)
     near = lax.ppermute(arrived, "core", across)
-    lanes = [project(places, pieces, arrived), project(places, pieces, near)]
+    lanes = [project(places, pieces, arrived)]
     tables = rotary_tables(doc_lengths[0], members * row_count)
     far, lanes, tables = lax.optimization_barrier((far, lanes, tables))
     last = lax.ppermute(far, "core", across)
-    lanes = lanes + [project(places, pieces, far), project(places, pieces, last)]
+    lanes = lanes + [project(places, pieces, rows) for rows in (near, far, last)]
     mixed = attend(member.reshape(1), doc_lengths, lanes, *tables)
     returned = lax.all_to_all(
         mixed.reshape(devices, members * piece, GROUP * HEAD_DIM), EVERY, 0, 0, tiled=True

time: 173 us -> 171 us (0.988)
  local copies, waits for them, and re-layouts: 15.8 us -> 12.6 us
    ppermute x1 -> x7, waiting for transfers between devices: 0.01 us -> 30.4 us  [the longest x1 22.8 us: on_device(): lax.ppermute(own_columns(projection, member ^ 2), ('zh', 'zl'), [(0, 3),...]
    all_to_all x1, waiting for transfers between devices: 28.5 us -> 5.71 us  [on_device(): lax.all_to_all(outgoing, DP, 0, 0, tiled=True).reshape(row_count, width)]
    ppermute x4 -> x2, waiting for transfers between devices: 11 us -> 0.01 us  [spread(): lax.ppermute(block, axis, up)]
    ppermute x1 -> x7, starting transfers between devices: 2.97 us -> 10 us  [the longest x6 7.05 us: ring_blocks(): lax.ppermute(block, axis, way)]
    ppermute x4 -> x2, waiting for transfers between devices: 3.71 us -> 8.81 us  [spread(): lax.ppermute(block, axis, down)]
    ppermute x4 -> x2, starting transfers between devices: 7.99 us -> 4.15 us  [spread(): far_high = lax.ppermute(above[half:], axis, down)]
    unnamed x20 -> x14, local copies, waits for them, and re-layouts: 8.63 us -> 4.83 us
    ppermute x1, starting transfers between devices: 3.35 us -> 0.28 us  [on_device(): last = lax.ppermute(far, 'core', across)]
  transfers between devices with their start and end apart: 23 -> 21, of which waited for: 10 -> 8; matrix products, arithmetic and copies ran while one was open for 9% -> 8% of each run, Pallas kernels for 9% -> 9%
where the time goes in v6:
time: 171 us; the launch traced here: 170 us
  waiting for transfers between devices  64.2 us (38%)
  starting transfers between devices  42.2 us (25%)
  Pallas kernels  29.6 us (17%)
  between operations  13.6 us (8%)
  local copies, waits for them, and re-layouts  12.6 us (7%)
  other arithmetic  7.86 us (5%)
    ppermute x1, waiting for transfers between devices, on_device(): lax.ppermute(own_columns(projection, member ^ 2), ('zh', 'zl'), [(0, 3),...  22.8 us
    all_to_all x1, waiting for transfers between devices, on_device(): lax.all_to_all(mixed.reshape(devices, members * piece, GROUP * HEAD_DIM),...  19.2 us
    pallas_call x4, Pallas kernels, project(): pl.pallas_call(project_kernel, out_shape=jax.ShapeDtypeStruct((count, wid...  17.4 us
    all_to_all x1, starting transfers between devices, on_device(): lax.all_to_all(outgoing, DP, 0, 0, tiled=True).reshape(row_count, width)  11.2 us
    ppermute x2, waiting for transfers between devices, spread(): lax.ppermute(block, axis, down)  8.81 us
    pallas_call x1, Pallas kernels, attend(): pl.pallas_call(attention_kernel, out_shape=jax.ShapeDtypeStruct((count, G...  8.43 us
    all_to_all x1, starting transfers between devices, on_device(): lax.all_to_all(mixed.reshape(devices, members * piece, GROUP * HEAD_DIM),...  8.3 us
    ppermute x6, waiting for transfers between devices, ring_blocks(): lax.ppermute(block, axis, way)  7.58 us
  transfers between devices with their start and end apart: 21, of which 8 were waited for; matrix products, arithmetic and copies ran while one was open for 8% of the time, Pallas kernels for 9%

profile of v6, /device:TPU:1, one launch (start us, length us, event | category | flops | bytes accessed | tf_op | source)
XLA Modules:
  0.0 170.0 jit_solution(11740410591162785406)
XLA Ops:
  6.5 1.0 constant_dynamic-slice_fusion.2
  7.5 0.8 constant_dynamic-slice_fusion.1
  8.4 0.7 pad_maximum_fusion.5
  9.1 0.0 all-gather.2.cloned.1.call-update
  9.1 0.7 multiply_bitcast_fusion
  9.7 0.1 iota_add_fusion
  9.8 0.1 add.357.target_ref
  10.0 0.0 copy-start.3
  10.0 1.6 copy-done.3
  11.6 1.5 sort_rows.1
  13.1 1.3 copy-done.2
  14.4 11.2 %all-to-all-start = ((bf16[32,8,4096]{2,1,0:T(8,128)(2,1)}), bf16[32,8,4096]{2,1,0:T(8,128)(2,1)S(1)}, u32[]{:S(2)}, u32[]{:S(2)}) async-start(bf16[32,8,4096]{2,1,0:T(8,128)(2,1)} %copy-done.2), calls=%async_computation | async-start | bytes 4194304 | tf_op jit(solution)/shard_map/all_to_all | solution.py:285
  25.6 0.0 copy-start.6
  25.6 3.0 %collective-permute-start = (bf16[128,768]{1,0:T(8,128)(2,1)S(1)}, bf16[128,768]{1,0:T(8,128)(2,1)S(1)}, u32[]{:S(2)}, u32[]{:S(2)}) collective-permute-start(bf16[128,768]{1,0:T(8,128)(2,1)S(1)} %pad_maximum_fusion.4), channel_id=1, source_target_pairs={{0,6},{6,0},{2,4},{4,2},{1,7},{7,1},{3,5},{5,3},{8,14},{14,8},{10,... | collective-permute-start | bytes 589832 | tf_op jit(solution)/shard_map/ppermute | solution.py:282
  28.6 22.8 %collective-permute-done = bf16[128,768]{1,0:T(8,128)(2,1)S(1)} collective-permute-done((bf16[128,768]{1,0:T(8,128)(2,1)S(1)}, bf16[128,768]{1,0:T(8,128)(2,1)S(1)}, u32[]{:S(2)}, u32[]{:S(2)}) %collective-permute-start) | collective-permute-done | bytes 196640 | tf_op jit(solution)/shard_map/ppermute | solution.py:282
  51.4 5.7 %all-to-all-done = bf16[32,8,4096]{2,1,0:T(8,128)(2,1)S(1)} async-done(((bf16[32,8,4096]{2,1,0:T(8,128)(2,1)}), bf16[32,8,4096]{2,1,0:T(8,128)(2,1)S(1)}, u32[]{:S(2)}, u32[]{:S(2)}) %all-to-all-start) | async-done | bytes 2097184 | tf_op jit(solution)/shard_map/all_to_all | solution.py:285
  57.1 0.7 collective-permute-start.1
  57.9 1.3 collective-permute-start.7
  59.2 1.5 collective-permute-start.5
  60.7 2.5 %collective-permute-start.4 = (bf16[128,384]{1,0:T(8,128)(2,1)S(1)}, bf16[128,384]{1,0:T(8,128)(2,1)S(1)}, u32[]{:S(2)}, u32[]{:S(2)}) collective-permute-start(bf16[128,384]{1,0:T(8,128)(2,1)S(1)} %get-tuple-element.28), channel_id=1, source_target_pairs={{0,16},{8,24},{16,0},{24,8},{1,17},{9,25},{17,1},{25,9},{2,18},{10... | collective-permute-start | bytes 294920 | tf_op jit(solution)/shard_map/ppermute | solution.py:101
  63.2 0.9 collective-permute-start.3
  64.1 0.3 collective-permute-done.6
  64.4 0.9 collective-permute-start.2
  65.3 0.1 collective-permute-done.5
  65.5 2.7 %collective-permute-done.4 = bf16[128,384]{1,0:T(8,128)(2,1)S(1)} collective-permute-done((bf16[128,384]{1,0:T(8,128)(2,1)S(1)}, bf16[128,384]{1,0:T(8,128)(2,1)S(1)}, u32[]{:S(2)}, u32[]{:S(2)}) %collective-permute-start.4) | collective-permute-done | bytes 98336 | tf_op jit(solution)/shard_map/ppermute | solution.py:101
  68.2 4.4 %collective-permute-done.3 = bf16[128,384]{1,0:T(8,128)(2,1)S(1)} collective-permute-done((bf16[128,384]{1,0:T(8,128)(2,1)S(1)}, bf16[128,384]{1,0:T(8,128)(2,1)S(1)}, u32[]{:S(2)}, u32[]{:S(2)}) %collective-permute-start.3) | collective-permute-done | bytes 98336 | tf_op jit(solution)/shard_map/ppermute | solution.py:101
  72.6 3.3 %collective-permute-start.9 = (bf16[512,384]{1,0:T(8,128)(2,1)S(1)}, bf16[512,384]{1,0:T(8,128)(2,1)S(1)}, u32[]{:S(2)}, u32[]{:S(2)}) collective-permute-start(bf16[512,384]{1,0:T(8,128)(2,1)S(1)} %pad_maximum_fusion.2.refs_1_), channel_id=1, source_target_pairs={{0,96},{32,0},{64,32},{96,64},{1,97},{33,1},{65,33},{97,65},{2,98}... | collective-permute-start | bytes 1179656 | tf_op jit(solution)/shard_map/ppermute | solution.py:107
  75.9 0.0 collective-permute-start.8
  75.9 1.3 collective-permute-start.13
  77.2 0.1 collective-permute-start.12
  77.4 0.2 reduce-window.8
  77.6 0.1 select_reduce_fusion
  77.7 8.8 %collective-permute-done.9.refs_3_ = bf16[512,384]{1,0:T(8,128)(2,1)S(1)} collective-permute-done((bf16[512,384]{1,0:T(8,128)(2,1)S(1)}, bf16[512,384]{1,0:T(8,128)(2,1)S(1)}, u32[]{:S(2)}, u32[]{:S(2)}) %collective-permute-start.9) | collective-permute-done | bytes 393248 | tf_op jit(solution)/shard_map/ppermute | solution.py:107
  86.5 0.7 slice.25
  87.2 3.5 %collective-permute-start.11 = (bf16[256,384]{1,0:T(8,128)(2,1)}, bf16[256,384]{1,0:T(8,128)(2,1)S(1)}, u32[]{:S(2)}, u32[]{:S(2)}) collective-permute-start(bf16[256,384]{1,0:T(8,128)(2,1)} %slice.25), channel_id=1, source_target_pairs={{0,96},{32,0},{64,32},{96,64},{1,97},{33,1},{65,33},{97,65},{2,98}... | collective-permute-start | bytes 589832 | tf_op jit(solution)/shard_map/ppermute | solution.py:109
  90.7 1.6 slice.24
  92.3 0.0 collective-permute-start.10
  92.3 0.0 collective-permute-done.13.refs_8_
  92.3 1.6 slice.27
  94.0 0.6 collective-permute-start.15
  94.6 1.6 slice.26
  96.2 0.8 collective-permute-start.14
  97.1 3.1 %fusion = (f32[1024,64]{1,0:T(8,128)}, f32[1024,64]{1,0:T(8,128)}, f32[1024,64]{1,0:T(8,128)}) fusion(f32[64]{0:T(128)S(1)} %multiply_power_fusion, f32[1024]{0:T(1024)S(1)} %subtract_convert_fusion), kind=kLoop, calls=%fused_computation.8 | loop fusion | flops 131072 | bytes 790784 | tf_op jit(solution)/shard_map/neg | solution.py:33
  100.2 0.1 stack.147.places_ref
  100.3 2.9 %pad_maximum_fusion = (f32[1024,128]{1,0:T(8,128)}, f32[1024,128]{1,0:T(8,128)}) fusion(f32[1024,64]{1,0:T(8,128)} %get-tuple-element.31, f32[1024,64]{1,0:T(8,128)} %get-tuple-element.30, f32[1024,64]{1,0:T(8,128)} %get-tuple-element.29), kind=kLoop, calls=%fused_computation.2 | loop fusion | flops 262144 | bytes 1835008 | tf_op jit(solution)/shard_map/concatenate | solution.py:33
  103.2 0.0 collective-permute-done.11.refs_5_
  103.2 1.9 %collective-permute-start.16 = (bf16[256,4096]{1,0:T(8,128)(2,1)S(1)}, bf16[256,4096]{1,0:T(8,128)(2,1)}, u32[]{:S(2)}, u32[]{:S(2)}) collective-permute-start(bf16[256,4096]{1,0:T(8,128)(2,1)S(1)} %bitcast.42), channel_id=1, source_target_pairs={{0,1},{1,0},{2,3},{3,2},{4,5},{5,4},{6,7},{7,6},{8,9},{9,8},{10,11... | collective-permute-start | bytes 6291464 | tf_op jit(solution)/shard_map/ppermute | solution.py:290
  105.2 0.0 collective-permute-done.10.refs_4_
  105.2 0.0 collective-permute-done.15.refs_10_
  105.2 0.0 collective-permute-done.14.refs_9_
  105.2 0.0 all-gather.2.cloned.1.call-done.refs_0_
  105.2 1.9 %copy-done = bf16[2048,768]{1,0:T(8,128)(2,1)S(1)} copy-done((bf16[2048,768]{1,0:T(8,128)(2,1)S(1)}, bf16[2048,768]{1,0:T(8,128)(2,1)}, u32[]{:S(2)}) %copy-start) | copy-done | bytes 3145752
  107.1 4.1 %project.4.refs_0_ = bf16[256,768]{1,0:T(8,128)(2,1)S(1)} custom-call(s32[48]{0:T(128)S(1)} %stack.147.places_ref, bf16[256,4096]{1,0:T(8,128)(2,1)S(1)} %bitcast.43, bf16[2048,768]{1,0:T(8,128)(2,1)S(1)} %copy-done, bf16[512,384]{1,0:T(8,128)(2,1)S(1)} %pad_maximum_fusion.2.refs_1_, bf16[512,384]{1,0:T(8,128)(2,1)} %collective-permute-done.8.refs_2_, ...), custom_call_target="tpu_custom_call" | custom-call | flops 1610612736 | bytes 8388608 | tf_op jit(solution)/shard_map/project/pallas_call | solution.py:165
  111.3 0.0 collective-permute-done.1.rows_ref
  111.3 0.3 collective-permute-start.17
  111.5 4.6 %project.6.refs_2_ = bf16[256,768]{1,0:T(8,128)(2,1)S(1)} custom-call(s32[48]{0:T(128)S(1)} %stack.147.places_ref, bf16[256,4096]{1,0:T(8,128)(2,1)} %collective-permute-done.1.rows_ref, bf16[2048,768]{1,0:T(8,128)(2,1)S(1)} %copy-done.1, bf16[512,384]{1,0:T(8,128)(2,1)S(1)} %pad_maximum_fusion.2.refs_1_, bf16[512,384]{1,0:T(8,128)(2,1)} %collective-permute-done.8.refs_2_, ...), custom_call_target="tpu_custom_call" | custom-call | flops 1610612736 | bytes 8388608 | tf_op jit(solution)/shard_map/project/pallas_call | solution.py:165
  116.2 0.0 collective-permute-done.16.rows_ref
  116.2 4.6 %project.5.refs_1_ = bf16[256,768]{1,0:T(8,128)(2,1)S(1)} custom-call(s32[48]{0:T(128)S(1)} %stack.147.places_ref, bf16[256,4096]{1,0:T(8,128)(2,1)} %collective-permute-done.16.rows_ref, bf16[2048,768]{1,0:T(8,128)(2,1)S(1)} %copy-done.1, bf16[512,384]{1,0:T(8,128)(2,1)S(1)} %pad_maximum_fusion.2.refs_1_, bf16[512,384]{1,0:T(8,128)(2,1)} %collective-permute-done.8.refs_2_, ...), custom_call_target="tpu_custom_call" | custom-call | flops 1610612736 | bytes 8388608 | tf_op jit(solution)/shard_map/project/pallas_call | solution.py:165
  120.8 4.1 %project.7.refs_3_ = bf16[256,768]{1,0:T(8,128)(2,1)S(1)} custom-call(s32[48]{0:T(128)S(1)} %stack.147.places_ref, bf16[256,4096]{1,0:T(8,128)(2,1)S(1)} %collective-permute-done.17.rows_ref, bf16[2048,768]{1,0:T(8,128)(2,1)S(1)} %copy-done.1, bf16[512,384]{1,0:T(8,128)(2,1)S(1)} %pad_maximum_fusion.2.refs_1_, ...), custom_call_target="tpu_custom_call" | custom-call | flops 1610612736 | bytes 8388608 | tf_op jit(solution)/shard_map/project/pallas_call | solution.py:165
  124.9 8.4 %attend.1 = bf16[1024,512]{1,0:T(8,128)(2,1)} custom-call(s32[1]{0:T(128)} %bitcast.1.member_ref, s32[1,8]{1,0:T(1,128)S(1)} %copy-done.6, bf16[256,768]{1,0:T(8,128)(2,1)S(1)} %project.4.refs_0_, bf16[256,768]{1,0:T(8,128)(2,1)S(1)} %project.5.refs_1_, bf16[256,768]{1,0:T(8,128)(2,1)S(1)} %project.6.refs_2_, bf16[256,768]{1,0:T(8,128)(2,1)S(1)} %project.7.refs_3_, ...), custom_call_target="tpu_custom_call" | custom-call | tf_op jit(solution)/shard_map/attend/pallas_call | solution.py:257
  133.3 8.3 %all-to-all-start.1 = ((bf16[128,8,512]{2,1,0:T(8,128)(2,1)}), bf16[128,8,512]{2,1,0:T(8,128)(2,1)S(1)}, u32[]{:S(2)}, u32[]{:S(2)}) async-start(bf16[128,8,512]{2,1,0:T(8,128)(2,1)} %bitcast.38), calls=%async_computation.1 | async-start | bytes 2097152 | tf_op jit(solution)/shard_map/all_to_all | solution.py:297
  141.6 0.1 add.417.target_ref
  141.7 19.2 %all-to-all-done.1 = bf16[128,8,512]{2,1,0:T(8,128)(2,1)S(1)} async-done(((bf16[128,8,512]{2,1,0:T(8,128)(2,1)}), bf16[128,8,512]{2,1,0:T(8,128)(2,1)S(1)}, u32[]{:S(2)}, u32[]{:S(2)}) %all-to-all-start.1) | async-done | bytes 1048608 | tf_op jit(solution)/shard_map/all_to_all | solution.py:297
  160.9 2.3 %unsort_rows.1 = bf16[256,2048]{1,0:T(8,128)(2,1)} custom-call(s32[256,1]{1,0:T(8,128)S(1)} %add.417.target_ref, bf16[32,4,8,512]{3,2,1,0:T(8,128)(2,1)S(1)} %bitcast.44), custom_call_target="tpu_custom_call" | custom-call | tf_op jit(solution)/shard_map/unsort_rows/pallas_call | solution.py:73
  (22 shorter events, 0.2 us)
Async XLA Ops:
  6.5 98.7 %all-gather.2.cloned.1.call-start = ((), (), s32[]{:S(2)}) async-start(), calls=%async_computation.2 | async-start | bytes 3342336 | tf_op jit(solution)/shard_map/all_gather | solution.py:281
  10.0 1.6 copy-start.3
  13.1 1.3 copy-start.2
  14.4 42.7 %all-to-all-start = ((bf16[32,8,4096]{2,1,0:T(8,128)(2,1)}), bf16[32,8,4096]{2,1,0:T(8,128)(2,1)S(1)}, u32[]{:S(2)}, u32[]{:S(2)}) async-start(bf16[32,8,4096]{2,1,0:T(8,128)(2,1)} %copy-done.2), calls=%async_computation | async-start | bytes 4194304 | tf_op jit(solution)/shard_map/all_to_all | solution.py:285
  25.6 51.8 %copy-start.6 = (s32[1,8]{1,0:T(1,128)S(1)}, s32[1,8]{1,0:T(1,128)}, u32[]{:S(2)}) copy-start(s32[1,8]{1,0:T(1,128)} %lengths_ref.1) | copy-start | bytes 100
  25.6 25.8 %collective-permute-start = (bf16[128,768]{1,0:T(8,128)(2,1)S(1)}, bf16[128,768]{1,0:T(8,128)(2,1)S(1)}, u32[]{:S(2)}, u32[]{:S(2)}) collective-permute-start(bf16[128,768]{1,0:T(8,128)(2,1)S(1)} %pad_maximum_fusion.4), channel_id=1, source_target_pairs={{0,6},{6,0},{2,4},{4,2},{1,7},{7,1},{3,5},{5,3},{8,14},{14,8},{10,... | collective-permute-start | bytes 589832 | tf_op jit(solution)/shard_map/ppermute | solution.py:282
  57.1 54.1 %collective-permute-start.1 = (bf16[256,4096]{1,0:T(8,128)(2,1)S(1)}, bf16[256,4096]{1,0:T(8,128)(2,1)}, u32[]{:S(2)}, u32[]{:S(2)}) collective-permute-start(bf16[256,4096]{1,0:T(8,128)(2,1)S(1)} %bitcast.41), channel_id=1, source_target_pairs={{0,2},{2,0},{1,3},{3,1},{4,6},{6,4},{5,7},{7,5},{8,10},{10,8},{9,1... | collective-permute-start | bytes 6291464 | tf_op jit(solution)/shard_map/ppermute | solution.py:289
  57.9 5.3 %collective-permute-start.7 = (bf16[128,384]{1,0:T(8,128)(2,1)S(1)}, bf16[128,384]{1,0:T(8,128)(2,1)S(1)}, u32[]{:S(2)}, u32[]{:S(2)}) collective-permute-start(bf16[128,384]{1,0:T(8,128)(2,1)S(1)} %get-tuple-element.27), channel_id=1, source_target_pairs={{0,64},{32,96},{64,0},{96,32},{1,65},{33,97},{65,1},{97,33},{2,66}... | collective-permute-start | bytes 294920 | tf_op jit(solution)/shard_map/ppermute | solution.py:101
  59.2 5.2 %collective-permute-start.6 = (bf16[128,384]{1,0:T(8,128)(2,1)S(1)}, bf16[128,384]{1,0:T(8,128)(2,1)S(1)}, u32[]{:S(2)}, u32[]{:S(2)}) collective-permute-start(bf16[128,384]{1,0:T(8,128)(2,1)S(1)} %get-tuple-element.27), channel_id=1, source_target_pairs={{0,96},{32,0},{64,32},{96,64},{1,97},{33,1},{65,33},{97,65},{2,98}... | collective-permute-start | bytes 294920 | tf_op jit(solution)/shard_map/ppermute | solution.py:101
  59.2 6.2 %collective-permute-start.5 = (bf16[128,384]{1,0:T(8,128)(2,1)S(1)}, bf16[128,384]{1,0:T(8,128)(2,1)S(1)}, u32[]{:S(2)}, u32[]{:S(2)}) collective-permute-start(bf16[128,384]{1,0:T(8,128)(2,1)S(1)} %get-tuple-element.27), channel_id=1, source_target_pairs={{0,32},{32,64},{64,96},{96,0},{1,33},{33,65},{65,97},{97,1},{2,34}... | collective-permute-start | bytes 294920 | tf_op jit(solution)/shard_map/ppermute | solution.py:101
  60.7 7.5 %collective-permute-start.4 = (bf16[128,384]{1,0:T(8,128)(2,1)S(1)}, bf16[128,384]{1,0:T(8,128)(2,1)S(1)}, u32[]{:S(2)}, u32[]{:S(2)}) collective-permute-start(bf16[128,384]{1,0:T(8,128)(2,1)S(1)} %get-tuple-element.28), channel_id=1, source_target_pairs={{0,16},{8,24},{16,0},{24,8},{1,17},{9,25},{17,1},{25,9},{2,18},{10... | collective-permute-start | bytes 294920 | tf_op jit(solution)/shard_map/ppermute | solution.py:101
  63.2 9.3 %collective-permute-start.3 = (bf16[128,384]{1,0:T(8,128)(2,1)S(1)}, bf16[128,384]{1,0:T(8,128)(2,1)S(1)}, u32[]{:S(2)}, u32[]{:S(2)}) collective-permute-start(bf16[128,384]{1,0:T(8,128)(2,1)S(1)} %get-tuple-element.28), channel_id=1, source_target_pairs={{0,24},{8,0},{16,8},{24,16},{1,25},{9,1},{17,9},{25,17},{2,26},{10... | collective-permute-start | bytes 294920 | tf_op jit(solution)/shard_map/ppermute | solution.py:101
  64.4 8.1 %collective-permute-start.2 = (bf16[128,384]{1,0:T(8,128)(2,1)S(1)}, bf16[128,384]{1,0:T(8,128)(2,1)S(1)}, u32[]{:S(2)}, u32[]{:S(2)}) collective-permute-start(bf16[128,384]{1,0:T(8,128)(2,1)S(1)} %get-tuple-element.28), channel_id=1, source_target_pairs={{0,8},{8,16},{16,24},{24,0},{1,9},{9,17},{17,25},{25,1},{2,10},{10... | collective-permute-start | bytes 294920 | tf_op jit(solution)/shard_map/ppermute | solution.py:101
  72.6 13.9 %collective-permute-start.9 = (bf16[512,384]{1,0:T(8,128)(2,1)S(1)}, bf16[512,384]{1,0:T(8,128)(2,1)S(1)}, u32[]{:S(2)}, u32[]{:S(2)}) collective-permute-start(bf16[512,384]{1,0:T(8,128)(2,1)S(1)} %pad_maximum_fusion.2.refs_1_), channel_id=1, source_target_pairs={{0,96},{32,0},{64,32},{96,64},{1,97},{33,1},{65,33},{97,65},{2,98}... | collective-permute-start | bytes 1179656 | tf_op jit(solution)/shard_map/ppermute | solution.py:107
  75.9 14.8 %collective-permute-start.8 = (bf16[512,384]{1,0:T(8,128)(2,1)S(1)}, bf16[512,384]{1,0:T(8,128)(2,1)}, u32[]{:S(2)}, u32[]{:S(2)}) collective-permute-start(bf16[512,384]{1,0:T(8,128)(2,1)S(1)} %pad_maximum_fusion.2.refs_1_), channel_id=1, source_target_pairs={{0,32},{32,64},{64,96},{96,0},{1,33},{33,65},{65,97},{97,1},{2,34}... | collective-permute-start | bytes 1179656 | tf_op jit(solution)/shard_map/ppermute | solution.py:107
  75.9 16.4 %collective-permute-start.13 = (bf16[512,384]{1,0:T(8,128)(2,1)S(1)}, bf16[512,384]{1,0:T(8,128)(2,1)}, u32[]{:S(2)}, u32[]{:S(2)}) collective-permute-start(bf16[512,384]{1,0:T(8,128)(2,1)S(1)} %pad_maximum_fusion.3.refs_6_), channel_id=1, source_target_pairs={{0,24},{8,0},{16,8},{24,16},{1,25},{9,1},{17,9},{25,17},{2,26},{10... | collective-permute-start | bytes 1179656 | tf_op jit(solution)/shard_map/ppermute | solution.py:107
  77.2 17.4 %collective-permute-start.12 = (bf16[512,384]{1,0:T(8,128)(2,1)S(1)}, bf16[512,384]{1,0:T(8,128)(2,1)}, u32[]{:S(2)}, u32[]{:S(2)}) collective-permute-start(bf16[512,384]{1,0:T(8,128)(2,1)S(1)} %pad_maximum_fusion.3.refs_6_), channel_id=1, source_target_pairs={{0,8},{8,16},{16,24},{24,0},{1,9},{9,17},{17,25},{25,1},{2,10},{10... | collective-permute-start | bytes 1179656 | tf_op jit(solution)/shard_map/ppermute | solution.py:107
  87.2 16.1 %collective-permute-start.11 = (bf16[256,384]{1,0:T(8,128)(2,1)}, bf16[256,384]{1,0:T(8,128)(2,1)S(1)}, u32[]{:S(2)}, u32[]{:S(2)}) collective-permute-start(bf16[256,384]{1,0:T(8,128)(2,1)} %slice.25), channel_id=1, source_target_pairs={{0,96},{32,0},{64,32},{96,64},{1,97},{33,1},{65,33},{97,65},{2,98}... | collective-permute-start | bytes 589832 | tf_op jit(solution)/shard_map/ppermute | solution.py:109
  92.3 12.9 %collective-permute-start.10 = (bf16[256,384]{1,0:T(8,128)(2,1)}, bf16[256,384]{1,0:T(8,128)(2,1)}, u32[]{:S(2)}, u32[]{:S(2)}) collective-permute-start(bf16[256,384]{1,0:T(8,128)(2,1)} %slice.24), channel_id=1, source_target_pairs={{0,32},{32,64},{64,96},{96,0},{1,33},{33,65},{65,97},{97,1},{2,34}... | collective-permute-start | bytes 589832 | tf_op jit(solution)/shard_map/ppermute | solution.py:108
  94.0 11.2 %collective-permute-start.15 = (bf16[256,384]{1,0:T(8,128)(2,1)}, bf16[256,384]{1,0:T(8,128)(2,1)}, u32[]{:S(2)}, u32[]{:S(2)}) collective-permute-start(bf16[256,384]{1,0:T(8,128)(2,1)} %slice.27), channel_id=1, source_target_pairs={{0,24},{8,0},{16,8},{24,16},{1,25},{9,1},{17,9},{25,17},{2,26},{10... | collective-permute-start | bytes 589832 | tf_op jit(solution)/shard_map/ppermute | solution.py:109
  96.2 9.0 %collective-permute-start.14 = (bf16[256,384]{1,0:T(8,128)(2,1)}, bf16[256,384]{1,0:T(8,128)(2,1)}, u32[]{:S(2)}, u32[]{:S(2)}) collective-permute-start(bf16[256,384]{1,0:T(8,128)(2,1)} %slice.26), channel_id=1, source_target_pairs={{0,8},{8,16},{16,24},{24,0},{1,9},{9,17},{17,25},{25,1},{2,10},{10... | collective-permute-start | bytes 589832 | tf_op jit(solution)/shard_map/ppermute | solution.py:108
  103.2 12.9 %collective-permute-start.16 = (bf16[256,4096]{1,0:T(8,128)(2,1)S(1)}, bf16[256,4096]{1,0:T(8,128)(2,1)}, u32[]{:S(2)}, u32[]{:S(2)}) collective-permute-start(bf16[256,4096]{1,0:T(8,128)(2,1)S(1)} %bitcast.42), channel_id=1, source_target_pairs={{0,1},{1,0},{2,3},{3,2},{4,5},{5,4},{6,7},{7,6},{8,9},{9,8},{10,11... | collective-permute-start | bytes 6291464 | tf_op jit(solution)/shard_map/ppermute | solution.py:290
  105.2 1.9 %copy-start = (bf16[2048,768]{1,0:T(8,128)(2,1)S(1)}, bf16[2048,768]{1,0:T(8,128)(2,1)}, u32[]{:S(2)}) copy-start(bf16[2048,768]{1,0:T(8,128)(2,1)} %all-gather.2.cloned.1.call-done.refs_0_) | copy-start | bytes 9437188
  107.1 4.4 %copy-start.1 = (bf16[2048,768]{1,0:T(8,128)(2,1)S(1)}, bf16[2048,768]{1,0:T(8,128)(2,1)}, u32[]{:S(2)}) copy-start(bf16[2048,768]{1,0:T(8,128)(2,1)} %all-gather.2.cloned.1.call-done.refs_0_) | copy-start | bytes 9437188
  111.3 9.5 %collective-permute-start.17 = (bf16[256,4096]{1,0:T(8,128)(2,1)}, bf16[256,4096]{1,0:T(8,128)(2,1)S(1)}, u32[]{:S(2)}, u32[]{:S(2)}) collective-permute-start(bf16[256,4096]{1,0:T(8,128)(2,1)} %collective-permute-done.1.rows_ref), channel_id=1, source_target_pairs={{0,1},{1,0},{2,3},{3,2},{4,5},{5,4},{6,7},{7,6},{8,9},{9,8},{10,11... | collective-permute-start | bytes 6291464 | tf_op jit(solution)/shard_map/ppermute | solution.py:294
  120.8 4.1 %copy-start.4 = (f32[1024,128]{1,0:T(8,128)S(1)}, f32[1024,128]{1,0:T(8,128)}, u32[]{:S(2)}) copy-start(f32[1024,128]{1,0:T(8,128)} %get-tuple-element.19.refs_4_) | copy-start | bytes 1572868
  120.8 4.1 %copy-start.5 = (f32[1024,128]{1,0:T(8,128)S(1)}, f32[1024,128]{1,0:T(8,128)}, u32[]{:S(2)}) copy-start(f32[1024,128]{1,0:T(8,128)} %get-tuple-element.20.refs_5_) | copy-start | bytes 1572868
  133.3 27.6 %all-to-all-start.1 = ((bf16[128,8,512]{2,1,0:T(8,128)(2,1)}), bf16[128,8,512]{2,1,0:T(8,128)(2,1)S(1)}, u32[]{:S(2)}, u32[]{:S(2)}) async-start(bf16[128,8,512]{2,1,0:T(8,128)(2,1)} %bitcast.38), calls=%async_computation.1 | async-start | bytes 2097152 | tf_op jit(solution)/shard_map/all_to_all | solution.py:297
Sparse Core Ops, SparseCore 0:
  9.5 73.7 all-gather.1

commit v7 on v6

--- a/solution.py
+++ b/solution.py
@@ -1,7 +1,9 @@
 import functools
+import math
 
 import jax
 import jax.numpy as jnp
+import numpy as np
 from jax import lax
 from jax.experimental import pallas as pl
 from jax.experimental.pallas import tpu as pltpu
@@ -19,44 +21,80 @@
 BLOCK = 256
 
 
-def frequencies():
-    half = HEAD_DIM // 2
-    return THETA ** (-2.0 * jnp.arange(half, dtype=jnp.float32) / HEAD_DIM)
+def tables_kernel(lengths_ref, frequency_ref, cos_ref, sin_ref):
+    count, width = cos_ref.shape
+    step = 128
+
+    @pl.loop(0, count // step)
+    def _(i):
+        position = i * step + lax.broadcasted_iota(jnp.int32, (step, width), 0)
+        begin, end = jnp.zeros_like(position), jnp.int32(0)
+        for j in range(lengths_ref.shape[1]):
+            end = end + lengths_ref[0, j]
+            begin = jnp.where(position >= end, end, begin)
+        angle = (position - begin).astype(jnp.float32) * frequency_ref[...]
+        rows = pl.ds(pl.multiple_of(i * step, step), step)
+        cos_ref[rows] = jnp.cos(angle)
+        sine = jnp.sin(angle)
+        first = lax.broadcasted_iota(jnp.int32, (step, width), 1) < width // 2
+        sin_ref[rows] = jnp.where(first, -sine, sine)
 
 
 def rotary_tables(lengths, count):
-    position = jnp.arange(count, dtype=jnp.int32)
-    ends = jnp.cumsum(lengths)
-    begins = jnp.sum(jnp.where(position[:, None] >= ends[None, :], lengths[None, :], 0), axis=1)
-    angles = (position - begins).astype(jnp.float32)[:, None] * frequencies()[None, :]
-    cosine, sine = jnp.cos(angles), jnp.sin(angles)
-    return jnp.concatenate([cosine, cosine], axis=1), jnp.concatenate([-sine, sine], axis=1)
-
-
-def sort_kernel(target_ref, rows_ref, out_ref):
-    count = rows_ref.shape[0]
+    frequency = THETA ** (-2.0 * np.arange(HEAD_DIM // 2) / HEAD_DIM)
+    frequency = np.concatenate([frequency, frequency])[None].astype(np.float32)
+    whole = pl.BlockSpec(memory_space=pltpu.VMEM)
+    shape = jax.ShapeDtypeStruct((count, HEAD_DIM), jnp.float32)
+    return pl.pallas_call(
+        tables_kernel,
+        out_shape=[shape] * 2,
+        in_specs=[pl.BlockSpec(memory_space=pltpu.SMEM), whole],
+        out_specs=[pl.BlockSpec((count, HEAD_DIM), lambda: (0, 0))] * 2,
+        compiler_params=pltpu.CompilerParams(vmem_limit_bytes=60 * 2**20),
+        name="rotary_tables",
+    )(lengths, frequency)
+
+
+def sort_kernel(target_ref, rows_ref, out_ref, held, moved, in_sems, out_sems):
+    count = held.shape[0]
+    arriving, leaving = [], []
+    for i in range(8):
+        rows = pl.ds(i * (count // 8), count // 8)
+        arriving.append(pltpu.make_async_copy(rows_ref.at[rows], held.at[rows], in_sems.at[i]))
+        arriving[-1].start()
     order = lax.broadcasted_iota(jnp.int32, (count, count), 0)
     one_hot = jnp.where(order == target_ref[...], 1.0, 0.0).astype(jnp.bfloat16)
-    moved = jnp.dot(one_hot, rows_ref[...], preferred_element_type=jnp.float32).astype(jnp.bfloat16)
-    out_ref[...] = moved.reshape(out_ref.shape)
+    for copy in arriving:
+        copy.wait()
+    for i in range(2):
+        half = slice(i * (count // 2), (i + 1) * (count // 2))
+        moved[half] = jnp.dot(one_hot[half], held[...], preferred_element_type=jnp.float32).astype(jnp.bfloat16)
+        for j in range(4):
+            rows = pl.ds((i * 4 + j) * (count // 8), count // 8)
+            leaving.append(pltpu.make_async_copy(moved.at[rows], out_ref.at[rows], out_sems.at[i * 4 + j]))
+            leaving[-1].start()
+    for copy in leaving:
+        copy.wait()
 
 
 def sort_rows(tokens, target, groups):
     count, width = tokens.shape
-    rows = count // groups
-    tile = 1024
-    return pl.pallas_call(
+    anywhere = pl.BlockSpec(memory_space=pl.ANY)
+    moved = pl.pallas_call(
         sort_kernel,
-        out_shape=jax.ShapeDtypeStruct((groups, rows, width), tokens.dtype),
-        grid=(width // tile,),
-        in_specs=[
-            pl.BlockSpec((1, count), lambda i: (0, 0)),
-            pl.BlockSpec((count, tile), lambda i: (0, i)),
+        out_shape=jax.ShapeDtypeStruct(tokens.shape, tokens.dtype),
+        in_specs=[pl.BlockSpec(memory_space=pltpu.VMEM), anywhere],
+        out_specs=anywhere,
+        scratch_shapes=[
+            pltpu.VMEM(tokens.shape, tokens.dtype),
+            pltpu.VMEM(tokens.shape, tokens.dtype),
+            pltpu.SemaphoreType.DMA((8,)),
+            pltpu.SemaphoreType.DMA((8,)),
         ],
-        out_specs=pl.BlockSpec((groups, rows, tile), lambda i: (0, 0, i)),
-        compiler_params=pltpu.CompilerParams(vmem_limit_bytes=32 * 2**20),
+        compiler_params=pltpu.CompilerParams(vmem_limit_bytes=60 * 2**20),
         name="sort_rows",
     )(target.reshape(1, count), tokens)
+    return moved.reshape(groups, count // groups, width)
 
 
 def unsort_kernel(target_ref, rows_ref, out_ref):
@@ -129,22 +167,25 @@
     return jnp.stack(places), pieces
 
 
-def project_kernel(places_ref, rows_ref, *refs):
-    pieces, out_ref, ordered = refs[:-2], refs[-2], refs[-1]
-    width = out_ref.shape[1]
-    half = width // 2
+def project_kernel(parts, places_ref, *refs):
+    row_refs, refs = refs[:parts], refs[parts:]
+    pieces, out_refs, ordered = refs[: -parts - 1], refs[-parts - 1 : -1], refs[-1]
+    half = out_refs[0].shape[1] // 2
     step = 128
 
     def take(first, count):
         for i in range(count):
             column = pl.multiple_of(places_ref[first + i], step)
-            ordered[:, i * step : (i + 1) * step] = rows_ref[:, pl.ds(column, step)]
-
-    def product(parts):
+            at = 0
+            for rows in row_refs:
+                ordered[at : at + rows.shape[0], i * step : (i + 1) * step] = rows[:, pl.ds(column, step)]
+                at += rows.shape[0]
+
+    def product(pieces):
         total, at = None, 0
-        for part in parts:
-            depth = part.shape[0]
-            term = jnp.dot(ordered[:, at : at + depth], part[...], preferred_element_type=jnp.float32)
+        for piece in pieces:
+            depth = piece.shape[0]
+            term = jnp.dot(ordered[:, at : at + depth], piece[...], preferred_element_type=jnp.float32)
             total = term if total is None else total + term
             at += depth
         return total
@@ -153,27 +194,30 @@
     out = product(pieces[:1])
     for side in range(2):
         take(16 + side * 16, 16)
-        other = product(pieces[1 + side * 5 : 6 + side * 5])
         columns = slice(side * half, (side + 1) * half)
-        out_ref[:, columns] = (out[:, columns] + other).astype(jnp.bfloat16)
+        here = (out[:, columns] + product(pieces[1 + side * 5 : 6 + side * 5])).astype(jnp.bfloat16)
+        at = 0
+        for out_ref in out_refs:
+            out_ref[:, columns] = here[at : at + out_ref.shape[0]]
+            at += out_ref.shape[0]
 
 
 def project(places, pieces, rows):
-    count, depth = rows.shape
+    count, depth = sum(r.shape[0] for r in rows), rows[0].shape[1]
     width = pieces[0].shape[1]
     whole = pl.BlockSpec(memory_space=pltpu.VMEM)
     return pl.pallas_call(
-        project_kernel,
-        out_shape=jax.ShapeDtypeStruct((count, width), jnp.bfloat16),
-        in_specs=[pl.BlockSpec(memory_space=pltpu.SMEM)] + [whole] * (1 + len(pieces)),
-        out_specs=whole,
+        functools.partial(project_kernel, len(rows)),
+        out_shape=[jax.ShapeDtypeStruct((r.shape[0], width), jnp.bfloat16) for r in rows],
+        in_specs=[pl.BlockSpec(memory_space=pltpu.SMEM)] + [whole] * (len(rows) + len(pieces)),
+        out_specs=[whole] * len(rows),
         scratch_shapes=[pltpu.VMEM((count, depth // 2), jnp.bfloat16)],
         compiler_params=pltpu.CompilerParams(vmem_limit_bytes=24 * 2**20),
         cost_estimate=pl.CostEstimate(
             flops=2 * count * depth * width, bytes_accessed=2 * depth * (width + count), transcendentals=0
         ),
         name="project",
-    )(places, rows, *pieces)
+    )(places, *rows, *pieces)
 
 
 def attention_kernel(member_ref, lengths_ref, *refs):
@@ -207,7 +251,7 @@
             keys[rows] = rotate(here[:, GROUP * HEAD_DIM : (GROUP + 1) * HEAD_DIM])
             values[rows] = here[:, (GROUP + 1) * HEAD_DIM :].astype(jnp.bfloat16)
 
-    scale = HEAD_DIM ** (-0.5)
+    scale = HEAD_DIM ** (-0.5) * math.log2(math.e)
     reach = (MOST - 1 + BLOCK - 1) // BLOCK
     for b in range(blocks):
         first = max(0, b - reach)
@@ -228,8 +272,8 @@
                 (((1,), (1,)), ((), ())),
                 preferred_element_type=jnp.float32,
             )
-            scores = jnp.where(allowed, scores * scale, -1e30)
-            weights = jnp.exp(scores - jnp.max(scores, axis=1, keepdims=True))
+            scores = jnp.where(allowed, scores, -1e30)
+            weights = jnp.exp2((scores - jnp.max(scores, axis=1, keepdims=True)) * scale)
             total = jnp.sum(weights, axis=1, keepdims=True)
             weighted = jnp.dot(
                 weights.astype(jnp.bfloat16), value_block, preferred_element_type=jnp.float32
@@ -283,16 +327,16 @@
     target = (placement[0][:, None] * piece + jnp.arange(piece, dtype=jnp.int32)[None, :]).reshape(row_count)
     outgoing = sort_rows(tokens, target, groups)
     arrived = lax.all_to_all(outgoing, DP, 0, 0, tiled=True).reshape(row_count, width)
-    arrived, theirs = lax.optimization_barrier((arrived, theirs))
+    tables = rotary_tables(doc_lengths, members * row_count)
+    arrived, theirs, tables = lax.optimization_barrier((arrived, theirs, tables))
     places, pieces = gather_weights(mine, theirs, projection.shape[0])
     across = [(0, 1), (1, 0)]
     far = lax.ppermute(arrived, "zl", across)
     near = lax.ppermute(arrived, "core", across)
-    lanes = [project(places, pieces, arrived)]
-    tables = rotary_tables(doc_lengths[0], members * row_count)
-    far, lanes, tables = lax.optimization_barrier((far, lanes, tables))
+    lanes = project(places, pieces, [arrived])
+    far, lanes = lax.optimization_barrier((far, lanes))
     last = lax.ppermute(far, "core", across)
-    lanes = lanes + [project(places, pieces, rows) for rows in (near, far, last)]
+    lanes = lanes + project(places, pieces, [near, far]) + project(places, pieces, [last])
     mixed = attend(member.reshape(1), doc_lengths, lanes, *tables)
     returned = lax.all_to_all(
         mixed.reshape(devices, members * piece, GROUP * HEAD_DIM), EVERY, 0, 0, tiled=True

time: 171 us -> 166 us (0.971)
  other arithmetic: 7.86 us -> 1.53 us
  Pallas kernels: 29.6 us -> 33.6 us
  local copies, waits for them, and re-layouts: 12.6 us -> 9.96 us
    pallas_call x5, Pallas kernels: 18.9 us -> 22.9 us  [the longest x3 14.8 us: project(): pl.pallas_call(functools.partial(project_kernel, len(rows)), out_shape=[j...]
    ppermute x1, waiting for transfers between devices: 22.8 us -> 18.8 us  [on_device(): lax.ppermute(own_columns(projection, member ^ 2), ('zh', 'zl'), [(0, 3),...]
    neg x1 -> x0, other arithmetic: 3.12 us -> none  [rotary_tables(): -sine]
    ppermute x2, waiting for transfers between devices: 0.01 us -> 3.06 us  [spread(): far_low = lax.ppermute(below[:half], axis, up)]
    concatenate x1 -> x0, other arithmetic: 2.93 us -> none  [rotary_tables(): jnp.concatenate([cosine, cosine], axis=1)]
    ppermute x1, starting transfers between devices: 0.28 us -> 3.01 us  [on_device(): last = lax.ppermute(far, 'core', across)]
    all_to_all x1, starting transfers between devices: 8.3 us -> 6.45 us  [on_device(): lax.all_to_all(mixed.reshape(devices, members * piece, GROUP * HEAD_DIM),...]
    slice x2, local copies, waits for them, and re-layouts: 3.24 us -> 1.51 us  [spread(): far_low = lax.ppermute(below[:half], axis, up)]
  transfers between devices with their start and end apart: 21 -> 21, of which waited for: 8 -> 8; matrix products, arithmetic and copies ran while one was open for 8% -> 2% of each run, Pallas kernels for 9% -> 12%
where the time goes in v7:
time: 166 us
  waiting for transfers between devices  63.4 us (38%)
  starting transfers between devices  43.5 us (26%)
  Pallas kernels  33.6 us (20%)
  between operations  13.6 us (8%)
  local copies, waits for them, and re-layouts  9.96 us (6%)
    all_to_all x1, waiting for transfers between devices, on_device(): lax.all_to_all(mixed.reshape(devices, members * piece, GROUP * HEAD_DIM),...  19.2 us
    ppermute x1, waiting for transfers between devices, on_device(): lax.ppermute(own_columns(projection, member ^ 2), ('zh', 'zl'), [(0, 3),...  18.8 us
    pallas_call x3, Pallas kernels, project(): pl.pallas_call(functools.partial(project_kernel, len(rows)), out_shape=[j...  14.8 us
    all_to_all x1, starting transfers between devices, on_device(): lax.all_to_all(outgoing, DP, 0, 0, tiled=True).reshape(row_count, width)  11.2 us
    ppermute x2, waiting for transfers between devices, spread(): lax.ppermute(block, axis, down)  9.26 us
    pallas_call x1, Pallas kernels, attend(): pl.pallas_call(attention_kernel, out_shape=jax.ShapeDtypeStruct((count, G...  8.32 us
    ppermute x6, waiting for transfers between devices, ring_blocks(): lax.ppermute(block, axis, way)  7.42 us
    ppermute x6, starting transfers between devices, ring_blocks(): lax.ppermute(block, axis, way)  7.17 us
  transfers between devices with their start and end apart: 21, of which 8 were waited for; matrix products, arithmetic and copies ran while one was open for 2% of the time, Pallas kernels for 12%

profile of v7, /device:TPU:1, one launch (start us, length us, event | category | flops | bytes accessed | tf_op | source)
XLA Modules:
  0.0 165.6 jit_solution(5999843498100058157)
XLA Ops:
  6.5 1.0 constant_dynamic-slice_fusion.2
  7.5 0.8 constant_dynamic-slice_fusion.1
  8.4 0.7 pad_maximum_fusion.3
  9.1 0.0 all-gather.2.cloned.1.call-update
  9.1 0.7 multiply_bitcast_fusion
  9.7 0.1 iota_add_fusion
  9.8 0.7 add.357.target_ref
  10.5 4.1 %sort_rows.1 = bf16[256,4096]{1,0:T(8,128)(2,1)} custom-call(s32[1,256]{1,0:T(1,128)} %add.357.target_ref, bf16[256,4096]{1,0:T(8,128)(2,1)} %rows_ref.1), custom_call_target="tpu_custom_call" | custom-call | tf_op jit(solution)/shard_map/sort_rows/pallas_call | solution.py:83
  14.6 11.2 %all-to-all-start = ((bf16[32,8,4096]{2,1,0:T(8,128)(2,1)}), bf16[32,8,4096]{2,1,0:T(8,128)(2,1)S(1)}, u32[]{:S(2)}, u32[]{:S(2)}) async-start(bf16[32,8,4096]{2,1,0:T(8,128)(2,1)} %bitcast.43), calls=%async_computation | async-start | bytes 4194304 | tf_op jit(solution)/shard_map/all_to_all | solution.py:329
  25.9 3.0 %collective-permute-start = (bf16[128,768]{1,0:T(8,128)(2,1)S(1)}, bf16[128,768]{1,0:T(8,128)(2,1)S(1)}, u32[]{:S(2)}, u32[]{:S(2)}) collective-permute-start(bf16[128,768]{1,0:T(8,128)(2,1)S(1)} %pad_maximum_fusion.2), channel_id=1, source_target_pairs={{0,6},{6,0},{2,4},{4,2},{1,7},{7,1},{3,5},{5,3},{8,14},{14,8},{10,... | collective-permute-start | bytes 589832 | tf_op jit(solution)/shard_map/ppermute | solution.py:326
  28.8 4.1 %rotary_tables.1 = (f32[1024,128]{1,0:T(8,128)}, f32[1024,128]{1,0:T(8,128)}) custom-call(s32[1,8]{1,0:T(1,128)} %lengths_ref.3, f32[1,128]{1,0:T(1,128)} %constant.223.clone.frequency_ref), custom_call_target="tpu_custom_call" | custom-call | tf_op jit(solution)/shard_map/rotary_tables/pallas_call | solution.py:48
  32.9 18.8 %collective-permute-done = bf16[128,768]{1,0:T(8,128)(2,1)S(1)} collective-permute-done((bf16[128,768]{1,0:T(8,128)(2,1)S(1)}, bf16[128,768]{1,0:T(8,128)(2,1)S(1)}, u32[]{:S(2)}, u32[]{:S(2)}) %collective-permute-start) | collective-permute-done | bytes 196640 | tf_op jit(solution)/shard_map/ppermute | solution.py:326
  51.8 5.6 %all-to-all-done = bf16[32,8,4096]{2,1,0:T(8,128)(2,1)S(1)} async-done(((bf16[32,8,4096]{2,1,0:T(8,128)(2,1)}), bf16[32,8,4096]{2,1,0:T(8,128)(2,1)S(1)}, u32[]{:S(2)}, u32[]{:S(2)}) %all-to-all-start) | async-done | bytes 2097184 | tf_op jit(solution)/shard_map/all_to_all | solution.py:329
  57.4 0.7 collective-permute-start.1
  58.1 1.2 collective-permute-start.7
  59.4 0.0 collective-permute-start.6
  59.4 1.5 collective-permute-start.5
  60.8 2.6 %collective-permute-start.4 = (bf16[128,384]{1,0:T(8,128)(2,1)S(1)}, bf16[128,384]{1,0:T(8,128)(2,1)S(1)}, u32[]{:S(2)}, u32[]{:S(2)}) collective-permute-start(bf16[128,384]{1,0:T(8,128)(2,1)S(1)} %get-tuple-element.36), channel_id=1, source_target_pairs={{0,16},{8,24},{16,0},{24,8},{1,17},{9,25},{17,1},{25,9},{2,18},{10... | collective-permute-start | bytes 294920 | tf_op jit(solution)/shard_map/ppermute | solution.py:139
  63.5 0.0 collective-permute-done.7
  63.5 0.8 collective-permute-start.3
  64.3 0.0 collective-permute-done.6
  64.3 1.0 collective-permute-start.2
  65.3 0.0 collective-permute-done.5
  65.4 2.8 %collective-permute-done.4 = bf16[128,384]{1,0:T(8,128)(2,1)S(1)} collective-permute-done((bf16[128,384]{1,0:T(8,128)(2,1)S(1)}, bf16[128,384]{1,0:T(8,128)(2,1)S(1)}, u32[]{:S(2)}, u32[]{:S(2)}) %collective-permute-start.4) | collective-permute-done | bytes 98336 | tf_op jit(solution)/shard_map/ppermute | solution.py:139
  68.2 4.6 %collective-permute-done.3 = bf16[128,384]{1,0:T(8,128)(2,1)S(1)} collective-permute-done((bf16[128,384]{1,0:T(8,128)(2,1)S(1)}, bf16[128,384]{1,0:T(8,128)(2,1)S(1)}, u32[]{:S(2)}, u32[]{:S(2)}) %collective-permute-start.3) | collective-permute-done | bytes 98336 | tf_op jit(solution)/shard_map/ppermute | solution.py:139
  72.8 0.0 collective-permute-done.2
  72.8 3.4 %collective-permute-start.9 = (bf16[512,384]{1,0:T(8,128)(2,1)S(1)}, bf16[512,384]{1,0:T(8,128)(2,1)S(1)}, u32[]{:S(2)}, u32[]{:S(2)}) collective-permute-start(bf16[512,384]{1,0:T(8,128)(2,1)S(1)} %pad_maximum_fusion.refs_2_.refs_3_), channel_id=1, source_target_pairs={{0,96},{32,0},{64,32},{96,64},{1,97},{33,1},{65,33},{97,65},{2,98}... | collective-permute-start | bytes 1179656 | tf_op jit(solution)/shard_map/ppermute | solution.py:145
  76.2 0.0 collective-permute-start.8
  76.2 1.3 collective-permute-start.13
  77.5 0.2 collective-permute-start.12
  77.7 9.3 %collective-permute-done.9.refs_4_.refs_5_ = bf16[512,384]{1,0:T(8,128)(2,1)S(1)} collective-permute-done((bf16[512,384]{1,0:T(8,128)(2,1)S(1)}, bf16[512,384]{1,0:T(8,128)(2,1)S(1)}, u32[]{:S(2)}, u32[]{:S(2)}) %collective-permute-start.9) | collective-permute-done | bytes 393248 | tf_op jit(solution)/shard_map/ppermute | solution.py:145
  86.9 3.5 %collective-permute-start.11 = (bf16[256,384]{1,0:T(8,128)(2,1)S(1)}, bf16[256,384]{1,0:T(8,128)(2,1)S(1)}, u32[]{:S(2)}, u32[]{:S(2)}) collective-permute-start(bf16[256,384]{1,0:T(8,128)(2,1)S(1)} %slice.25), channel_id=1, source_target_pairs={{0,96},{32,0},{64,32},{96,64},{1,97},{33,1},{65,33},{97,65},{2,98}... | collective-permute-start | bytes 589832 | tf_op jit(solution)/shard_map/ppermute | solution.py:147
  90.4 0.0 collective-permute-done.8.refs_3_.refs_4_
  90.4 0.8 slice.24
  91.2 0.0 collective-permute-start.10
  91.2 0.0 collective-permute-done.13.refs_9_.refs_10_
  91.2 0.8 slice.27
  92.0 0.5 collective-permute-start.15
  92.5 0.0 collective-permute-done.12.refs_8_.refs_9_
  92.5 0.7 slice.26
  93.2 1.0 collective-permute-start.14
  94.2 0.0 collective-permute-done.11.refs_6_.refs_7_
  94.2 2.2 %collective-permute-start.16 = (bf16[256,4096]{1,0:T(8,128)(2,1)S(1)}, bf16[256,4096]{1,0:T(8,128)(2,1)}, u32[]{:S(2)}, u32[]{:S(2)}) collective-permute-start(bf16[256,4096]{1,0:T(8,128)(2,1)S(1)} %bitcast.40), channel_id=1, source_target_pairs={{0,1},{1,0},{2,3},{3,2},{4,5},{5,4},{6,7},{7,6},{8,9},{9,8},{10,11... | collective-permute-start | bytes 6291464 | tf_op jit(solution)/shard_map/ppermute | solution.py:335
  96.4 0.1 stack.147.places_ref
  96.5 1.1 collective-permute-done.10.refs_5_.refs_6_
  97.6 0.0 collective-permute-done.15.refs_11_.refs_12_
  97.6 1.9 %collective-permute-done.14.refs_10_.refs_11_ = bf16[256,384]{1,0:T(8,128)(2,1)} collective-permute-done((bf16[256,384]{1,0:T(8,128)(2,1)}, bf16[256,384]{1,0:T(8,128)(2,1)}, u32[]{:S(2)}, u32[]{:S(2)}) %collective-permute-start.14) | collective-permute-done | bytes 196640 | tf_op jit(solution)/shard_map/ppermute | solution.py:146
  99.6 1.9 %copy-done = bf16[2048,768]{1,0:T(8,128)(2,1)S(1)} copy-done((bf16[2048,768]{1,0:T(8,128)(2,1)S(1)}, bf16[2048,768]{1,0:T(8,128)(2,1)}, u32[]{:S(2)}) %copy-start) | copy-done | bytes 3145752
  101.5 1.0 copy-done.3
  102.5 1.0 copy-done.6
  103.4 1.0 copy-done.9
  104.5 3.8 %project.3.refs_0_ = bf16[256,768]{1,0:T(8,128)(2,1)S(1)} custom-call(s32[48]{0:T(128)S(1)} %stack.147.places_ref, bf16[256,4096]{1,0:T(8,128)(2,1)S(1)} %bitcast.41, bf16[2048,768]{1,0:T(8,128)(2,1)S(1)} %copy-done, bf16[512,384]{1,0:T(8,128)(2,1)S(1)} %pad_maximum_fusion.refs_2_.refs_3_, bf16[512,384]{1,0:T(8,128)(2,1)S(1)} %copy-done.3, ...), custom_call_target="tpu_custom_call" | custom-call | flops 1610612736 | bytes 8388608 | tf_op jit(solution)/shard_map/project/pallas_call | solution.py:209
  108.2 0.0 collective-permute-done.1.refs_1_
  108.2 3.0 %collective-permute-start.17 = (bf16[256,4096]{1,0:T(8,128)(2,1)}, bf16[256,4096]{1,0:T(8,128)(2,1)S(1)}, u32[]{:S(2)}, u32[]{:S(2)}) collective-permute-start(bf16[256,4096]{1,0:T(8,128)(2,1)} %collective-permute-done.1.refs_1_), channel_id=1, source_target_pairs={{0,1},{1,0},{2,3},{3,2},{4,5},{5,4},{6,7},{7,6},{8,9},{9,8},{10,11... | collective-permute-start | bytes 6291464 | tf_op jit(solution)/shard_map/ppermute | solution.py:338
  111.3 7.3 %project.4 = (bf16[256,768]{1,0:T(8,128)(2,1)S(1)}, bf16[256,768]{1,0:T(8,128)(2,1)S(1)}) custom-call(s32[48]{0:T(128)S(1)} %stack.147.places_ref, bf16[256,4096]{1,0:T(8,128)(2,1)} %collective-permute-done.16.refs_0_, bf16[256,4096]{1,0:T(8,128)(2,1)} %collective-permute-done.1.refs_1_, bf16[2048,768]{1,0:T(8,128)(2,1)S(1)} %copy-done.1, ...), custom_call_target="tpu_custom_call" | custom-call | flops 3221225472 | bytes 10485760 | tf_op jit(solution)/shard_map/project/pallas_call | solution.py:209
  118.6 0.0 copy-start.11
  118.6 0.0 copy-start.13
  118.6 0.0 collective-permute-done.17.refs_0_
  118.6 3.7 %project.5.refs_3_ = bf16[256,768]{1,0:T(8,128)(2,1)S(1)} custom-call(s32[48]{0:T(128)S(1)} %stack.147.places_ref, bf16[256,4096]{1,0:T(8,128)(2,1)S(1)} %collective-permute-done.17.refs_0_, bf16[2048,768]{1,0:T(8,128)(2,1)S(1)} %copy-done.1, bf16[512,384]{1,0:T(8,128)(2,1)S(1)} %pad_maximum_fusion.refs_2_.refs_3_, bf16[512,384]{1,0:T(8,128)(2,1)S(1)} %copy-done.4, ...), custom_call_target="tpu_custom_call" | custom-call | flops 1610612736 | bytes 8388608 | tf_op jit(solution)/shard_map/project/pallas_call | solution.py:209
  122.4 8.3 %attend.1 = bf16[1024,512]{1,0:T(8,128)(2,1)} custom-call(s32[1]{0:T(128)} %bitcast.1.member_ref, s32[1,8]{1,0:T(1,128)S(1)} %copy-done.13, bf16[256,768]{1,0:T(8,128)(2,1)S(1)} %project.3.refs_0_, bf16[256,768]{1,0:T(8,128)(2,1)S(1)} %get-tuple-element.25.refs_1_, bf16[256,768]{1,0:T(8,128)(2,1)S(1)} %get-tuple-element.26.refs_2_, ...), custom_call_target="tpu_custom_call" | custom-call | tf_op jit(solution)/shard_map/attend/pallas_call | solution.py:301
  130.7 6.5 %all-to-all-start.1 = ((bf16[128,8,512]{2,1,0:T(8,128)(2,1)}), bf16[128,8,512]{2,1,0:T(8,128)(2,1)S(1)}, u32[]{:S(2)}, u32[]{:S(2)}) async-start(bf16[128,8,512]{2,1,0:T(8,128)(2,1)} %bitcast.36), calls=%async_computation.1 | async-start | bytes 2097152 | tf_op jit(solution)/shard_map/all_to_all | solution.py:341
  137.2 0.1 add.417.target_ref
  137.3 19.2 %all-to-all-done.1 = bf16[128,8,512]{2,1,0:T(8,128)(2,1)S(1)} async-done(((bf16[128,8,512]{2,1,0:T(8,128)(2,1)}), bf16[128,8,512]{2,1,0:T(8,128)(2,1)S(1)}, u32[]{:S(2)}, u32[]{:S(2)}) %all-to-all-start.1) | async-done | bytes 1048608 | tf_op jit(solution)/shard_map/all_to_all | solution.py:341
  156.4 2.3 %unsort_rows.1 = bf16[256,2048]{1,0:T(8,128)(2,1)} custom-call(s32[256,1]{1,0:T(8,128)S(1)} %add.417.target_ref, bf16[32,4,8,512]{3,2,1,0:T(8,128)(2,1)S(1)} %bitcast.42), custom_call_target="tpu_custom_call" | custom-call | tf_op jit(solution)/shard_map/unsort_rows/pallas_call | solution.py:111
  (30 shorter events, 0.2 us)
Async XLA Ops:
  6.5 93.0 %all-gather.2.cloned.1.call-start = ((), (), s32[]{:S(2)}) async-start(), calls=%async_computation.2 | async-start | bytes 3342336 | tf_op jit(solution)/shard_map/all_gather | solution.py:325
  14.6 42.7 %all-to-all-start = ((bf16[32,8,4096]{2,1,0:T(8,128)(2,1)}), bf16[32,8,4096]{2,1,0:T(8,128)(2,1)S(1)}, u32[]{:S(2)}, u32[]{:S(2)}) async-start(bf16[32,8,4096]{2,1,0:T(8,128)(2,1)} %bitcast.43), calls=%async_computation | async-start | bytes 4194304 | tf_op jit(solution)/shard_map/all_to_all | solution.py:329
  25.9 25.9 %collective-permute-start = (bf16[128,768]{1,0:T(8,128)(2,1)S(1)}, bf16[128,768]{1,0:T(8,128)(2,1)S(1)}, u32[]{:S(2)}, u32[]{:S(2)}) collective-permute-start(bf16[128,768]{1,0:T(8,128)(2,1)S(1)} %pad_maximum_fusion.2), channel_id=1, source_target_pairs={{0,6},{6,0},{2,4},{4,2},{1,7},{7,1},{3,5},{5,3},{8,14},{14,8},{10,... | collective-permute-start | bytes 589832 | tf_op jit(solution)/shard_map/ppermute | solution.py:326
  57.4 50.9 %collective-permute-start.1 = (bf16[256,4096]{1,0:T(8,128)(2,1)S(1)}, bf16[256,4096]{1,0:T(8,128)(2,1)}, u32[]{:S(2)}, u32[]{:S(2)}) collective-permute-start(bf16[256,4096]{1,0:T(8,128)(2,1)S(1)} %bitcast.39), channel_id=1, source_target_pairs={{0,2},{2,0},{1,3},{3,1},{4,6},{6,4},{5,7},{7,5},{8,10},{10,8},{9,1... | collective-permute-start | bytes 6291464 | tf_op jit(solution)/shard_map/ppermute | solution.py:334
  58.1 5.3 %collective-permute-start.7 = (bf16[128,384]{1,0:T(8,128)(2,1)S(1)}, bf16[128,384]{1,0:T(8,128)(2,1)S(1)}, u32[]{:S(2)}, u32[]{:S(2)}) collective-permute-start(bf16[128,384]{1,0:T(8,128)(2,1)S(1)} %get-tuple-element.35), channel_id=1, source_target_pairs={{0,64},{32,96},{64,0},{96,32},{1,65},{33,97},{65,1},{97,33},{2,66}... | collective-permute-start | bytes 294920 | tf_op jit(solution)/shard_map/ppermute | solution.py:139
  59.4 4.9 %collective-permute-start.6 = (bf16[128,384]{1,0:T(8,128)(2,1)S(1)}, bf16[128,384]{1,0:T(8,128)(2,1)S(1)}, u32[]{:S(2)}, u32[]{:S(2)}) collective-permute-start(bf16[128,384]{1,0:T(8,128)(2,1)S(1)} %get-tuple-element.35), channel_id=1, source_target_pairs={{0,96},{32,0},{64,32},{96,64},{1,97},{33,1},{65,33},{97,65},{2,98}... | collective-permute-start | bytes 294920 | tf_op jit(solution)/shard_map/ppermute | solution.py:139
  59.4 5.9 %collective-permute-start.5 = (bf16[128,384]{1,0:T(8,128)(2,1)S(1)}, bf16[128,384]{1,0:T(8,128)(2,1)S(1)}, u32[]{:S(2)}, u32[]{:S(2)}) collective-permute-start(bf16[128,384]{1,0:T(8,128)(2,1)S(1)} %get-tuple-element.35), channel_id=1, source_target_pairs={{0,32},{32,64},{64,96},{96,0},{1,33},{33,65},{65,97},{97,1},{2,34}... | collective-permute-start | bytes 294920 | tf_op jit(solution)/shard_map/ppermute | solution.py:139
  60.8 7.3 %collective-permute-start.4 = (bf16[128,384]{1,0:T(8,128)(2,1)S(1)}, bf16[128,384]{1,0:T(8,128)(2,1)S(1)}, u32[]{:S(2)}, u32[]{:S(2)}) collective-permute-start(bf16[128,384]{1,0:T(8,128)(2,1)S(1)} %get-tuple-element.36), channel_id=1, source_target_pairs={{0,16},{8,24},{16,0},{24,8},{1,17},{9,25},{17,1},{25,9},{2,18},{10... | collective-permute-start | bytes 294920 | tf_op jit(solution)/shard_map/ppermute | solution.py:139
  63.5 9.3 %collective-permute-start.3 = (bf16[128,384]{1,0:T(8,128)(2,1)S(1)}, bf16[128,384]{1,0:T(8,128)(2,1)S(1)}, u32[]{:S(2)}, u32[]{:S(2)}) collective-permute-start(bf16[128,384]{1,0:T(8,128)(2,1)S(1)} %get-tuple-element.36), channel_id=1, source_target_pairs={{0,24},{8,0},{16,8},{24,16},{1,25},{9,1},{17,9},{25,17},{2,26},{10... | collective-permute-start | bytes 294920 | tf_op jit(solution)/shard_map/ppermute | solution.py:139
  64.3 8.5 %collective-permute-start.2 = (bf16[128,384]{1,0:T(8,128)(2,1)S(1)}, bf16[128,384]{1,0:T(8,128)(2,1)S(1)}, u32[]{:S(2)}, u32[]{:S(2)}) collective-permute-start(bf16[128,384]{1,0:T(8,128)(2,1)S(1)} %get-tuple-element.36), channel_id=1, source_target_pairs={{0,8},{8,16},{16,24},{24,0},{1,9},{9,17},{17,25},{25,1},{2,10},{10... | collective-permute-start | bytes 294920 | tf_op jit(solution)/shard_map/ppermute | solution.py:139
  72.8 14.1 %collective-permute-start.9 = (bf16[512,384]{1,0:T(8,128)(2,1)S(1)}, bf16[512,384]{1,0:T(8,128)(2,1)S(1)}, u32[]{:S(2)}, u32[]{:S(2)}) collective-permute-start(bf16[512,384]{1,0:T(8,128)(2,1)S(1)} %pad_maximum_fusion.refs_2_.refs_3_), channel_id=1, source_target_pairs={{0,96},{32,0},{64,32},{96,64},{1,97},{33,1},{65,33},{97,65},{2,98}... | collective-permute-start | bytes 1179656 | tf_op jit(solution)/shard_map/ppermute | solution.py:145
  76.2 14.2 %collective-permute-start.8 = (bf16[512,384]{1,0:T(8,128)(2,1)S(1)}, bf16[512,384]{1,0:T(8,128)(2,1)S(1)}, u32[]{:S(2)}, u32[]{:S(2)}) collective-permute-start(bf16[512,384]{1,0:T(8,128)(2,1)S(1)} %pad_maximum_fusion.refs_2_.refs_3_), channel_id=1, source_target_pairs={{0,32},{32,64},{64,96},{96,0},{1,33},{33,65},{65,97},{97,1},{2,34}... | collective-permute-start | bytes 1179656 | tf_op jit(solution)/shard_map/ppermute | solution.py:145
  76.2 15.0 %collective-permute-start.13 = (bf16[512,384]{1,0:T(8,128)(2,1)S(1)}, bf16[512,384]{1,0:T(8,128)(2,1)S(1)}, u32[]{:S(2)}, u32[]{:S(2)}) collective-permute-start(bf16[512,384]{1,0:T(8,128)(2,1)S(1)} %pad_maximum_fusion.1.refs_7_.refs_8_), channel_id=1, source_target_pairs={{0,24},{8,0},{16,8},{24,16},{1,25},{9,1},{17,9},{25,17},{2,26},{10... | collective-permute-start | bytes 1179656 | tf_op jit(solution)/shard_map/ppermute | solution.py:145
  77.5 15.0 %collective-permute-start.12 = (bf16[512,384]{1,0:T(8,128)(2,1)S(1)}, bf16[512,384]{1,0:T(8,128)(2,1)S(1)}, u32[]{:S(2)}, u32[]{:S(2)}) collective-permute-start(bf16[512,384]{1,0:T(8,128)(2,1)S(1)} %pad_maximum_fusion.1.refs_7_.refs_8_), channel_id=1, source_target_pairs={{0,8},{8,16},{16,24},{24,0},{1,9},{9,17},{17,25},{25,1},{2,10},{10... | collective-permute-start | bytes 1179656 | tf_op jit(solution)/shard_map/ppermute | solution.py:145
  86.9 7.2 %collective-permute-start.11 = (bf16[256,384]{1,0:T(8,128)(2,1)S(1)}, bf16[256,384]{1,0:T(8,128)(2,1)S(1)}, u32[]{:S(2)}, u32[]{:S(2)}) collective-permute-start(bf16[256,384]{1,0:T(8,128)(2,1)S(1)} %slice.25), channel_id=1, source_target_pairs={{0,96},{32,0},{64,32},{96,64},{1,97},{33,1},{65,33},{97,65},{2,98}... | collective-permute-start | bytes 589832 | tf_op jit(solution)/shard_map/ppermute | solution.py:147
  90.4 3.8 %copy-start.2 = (bf16[512,384]{1,0:T(8,128)(2,1)}, bf16[512,384]{1,0:T(8,128)(2,1)S(1)}, u32[]{:S(2)}) copy-start(bf16[512,384]{1,0:T(8,128)(2,1)S(1)} %collective-permute-done.8.refs_3_.refs_4_) | copy-start | bytes 1179652
  91.2 6.4 %collective-permute-start.10 = (bf16[256,384]{1,0:T(8,128)(2,1)}, bf16[256,384]{1,0:T(8,128)(2,1)}, u32[]{:S(2)}, u32[]{:S(2)}) collective-permute-start(bf16[256,384]{1,0:T(8,128)(2,1)} %slice.24), channel_id=1, source_target_pairs={{0,32},{32,64},{64,96},{96,0},{1,33},{33,65},{65,97},{97,1},{2,34}... | collective-permute-start | bytes 589832 | tf_op jit(solution)/shard_map/ppermute | solution.py:146
  91.2 3.0 %copy-start.5 = (bf16[512,384]{1,0:T(8,128)(2,1)}, bf16[512,384]{1,0:T(8,128)(2,1)S(1)}, u32[]{:S(2)}) copy-start(bf16[512,384]{1,0:T(8,128)(2,1)S(1)} %collective-permute-done.13.refs_9_.refs_10_) | copy-start | bytes 1179652
  92.0 5.6 %collective-permute-start.15 = (bf16[256,384]{1,0:T(8,128)(2,1)}, bf16[256,384]{1,0:T(8,128)(2,1)}, u32[]{:S(2)}, u32[]{:S(2)}) collective-permute-start(bf16[256,384]{1,0:T(8,128)(2,1)} %slice.27), channel_id=1, source_target_pairs={{0,24},{8,0},{16,8},{24,16},{1,25},{9,1},{17,9},{25,17},{2,26},{10... | collective-permute-start | bytes 589832 | tf_op jit(solution)/shard_map/ppermute | solution.py:147
  92.5 1.7 %copy-start.8 = (bf16[512,384]{1,0:T(8,128)(2,1)}, bf16[512,384]{1,0:T(8,128)(2,1)S(1)}, u32[]{:S(2)}) copy-start(bf16[512,384]{1,0:T(8,128)(2,1)S(1)} %collective-permute-done.12.refs_8_.refs_9_) | copy-start | bytes 1179652
  93.2 6.3 %collective-permute-start.14 = (bf16[256,384]{1,0:T(8,128)(2,1)}, bf16[256,384]{1,0:T(8,128)(2,1)}, u32[]{:S(2)}, u32[]{:S(2)}) collective-permute-start(bf16[256,384]{1,0:T(8,128)(2,1)} %slice.26), channel_id=1, source_target_pairs={{0,8},{8,16},{16,24},{24,0},{1,9},{9,17},{17,25},{25,1},{2,10},{10... | collective-permute-start | bytes 589832 | tf_op jit(solution)/shard_map/ppermute | solution.py:146
  94.2 17.1 %collective-permute-start.16 = (bf16[256,4096]{1,0:T(8,128)(2,1)S(1)}, bf16[256,4096]{1,0:T(8,128)(2,1)}, u32[]{:S(2)}, u32[]{:S(2)}) collective-permute-start(bf16[256,4096]{1,0:T(8,128)(2,1)S(1)} %bitcast.40), channel_id=1, source_target_pairs={{0,1},{1,0},{2,3},{3,2},{4,5},{5,4},{6,7},{7,6},{8,9},{9,8},{10,11... | collective-permute-start | bytes 6291464 | tf_op jit(solution)/shard_map/ppermute | solution.py:335
  99.6 1.9 %copy-start = (bf16[2048,768]{1,0:T(8,128)(2,1)S(1)}, bf16[2048,768]{1,0:T(8,128)(2,1)}, u32[]{:S(2)}) copy-start(bf16[2048,768]{1,0:T(8,128)(2,1)} %all-gather.2.cloned.1.call-done.refs_1_.refs_2_) | copy-start | bytes 9437188
  101.5 1.0 copy-start.3
  102.5 1.0 copy-start.6
  103.4 1.0 copy-start.9
  104.4 6.8 %copy-start.1 = (bf16[2048,768]{1,0:T(8,128)(2,1)S(1)}, bf16[2048,768]{1,0:T(8,128)(2,1)}, u32[]{:S(2)}) copy-start(bf16[2048,768]{1,0:T(8,128)(2,1)} %all-gather.2.cloned.1.call-done.refs_1_.refs_2_) | copy-start | bytes 9437188
  104.4 6.8 %copy-start.4 = (bf16[512,384]{1,0:T(8,128)(2,1)S(1)}, bf16[512,384]{1,0:T(8,128)(2,1)}, u32[]{:S(2)}) copy-start(bf16[512,384]{1,0:T(8,128)(2,1)} %copy-done.2) | copy-start | bytes 1179652
  104.4 6.8 %copy-start.7 = (bf16[512,384]{1,0:T(8,128)(2,1)S(1)}, bf16[512,384]{1,0:T(8,128)(2,1)}, u32[]{:S(2)}) copy-start(bf16[512,384]{1,0:T(8,128)(2,1)} %copy-done.5) | copy-start | bytes 1179652
  104.5 6.8 %copy-start.10 = (bf16[512,384]{1,0:T(8,128)(2,1)S(1)}, bf16[512,384]{1,0:T(8,128)(2,1)}, u32[]{:S(2)}) copy-start(bf16[512,384]{1,0:T(8,128)(2,1)} %copy-done.8) | copy-start | bytes 1179652
  108.2 10.4 %collective-permute-start.17 = (bf16[256,4096]{1,0:T(8,128)(2,1)}, bf16[256,4096]{1,0:T(8,128)(2,1)S(1)}, u32[]{:S(2)}, u32[]{:S(2)}) collective-permute-start(bf16[256,4096]{1,0:T(8,128)(2,1)} %collective-permute-done.1.refs_1_), channel_id=1, source_target_pairs={{0,1},{1,0},{2,3},{3,2},{4,5},{5,4},{6,7},{7,6},{8,9},{9,8},{10,11... | collective-permute-start | bytes 6291464 | tf_op jit(solution)/shard_map/ppermute | solution.py:338
  118.6 3.8 %copy-start.11 = (f32[1024,128]{1,0:T(8,128)S(1)}, f32[1024,128]{1,0:T(8,128)}, u32[]{:S(2)}) copy-start(f32[1024,128]{1,0:T(8,128)} %get-tuple-element.27.refs_4_) | copy-start | bytes 1572868
  118.6 3.8 %copy-start.12 = (f32[1024,128]{1,0:T(8,128)S(1)}, f32[1024,128]{1,0:T(8,128)}, u32[]{:S(2)}) copy-start(f32[1024,128]{1,0:T(8,128)} %get-tuple-element.28.refs_5_) | copy-start | bytes 1572868
  118.6 3.8 %copy-start.13 = (s32[1,8]{1,0:T(1,128)S(1)}, s32[1,8]{1,0:T(1,128)}, u32[]{:S(2)}) copy-start(s32[1,8]{1,0:T(1,128)} %lengths_ref.3) | copy-start | bytes 100
  130.7 25.7 %all-to-all-start.1 = ((bf16[128,8,512]{2,1,0:T(8,128)(2,1)}), bf16[128,8,512]{2,1,0:T(8,128)(2,1)S(1)}, u32[]{:S(2)}, u32[]{:S(2)}) async-start(bf16[128,8,512]{2,1,0:T(8,128)(2,1)} %bitcast.36), calls=%async_computation.1 | async-start | bytes 2097152 | tf_op jit(solution)/shard_map/all_to_all | solution.py:341
Sparse Core Ops, SparseCore 0:
  9.5 74.0 all-gather.1

commit v8 on v7

--- a/solution.py
+++ b/solution.py
@@ -50,20 +50,50 @@
         out_shape=[shape] * 2,
         in_specs=[pl.BlockSpec(memory_space=pltpu.SMEM), whole],
         out_specs=[pl.BlockSpec((count, HEAD_DIM), lambda: (0, 0))] * 2,
-        compiler_params=pltpu.CompilerParams(vmem_limit_bytes=60 * 2**20),
+        compiler_params=pltpu.CompilerParams(vmem_limit_bytes=63 * 2**20),
         name="rotary_tables",
     )(lengths, frequency)
 
 
-def sort_kernel(target_ref, rows_ref, out_ref, held, moved, in_sems, out_sems):
-    count = held.shape[0]
+def sort_kernel(member_ref, placement_ref, rows_ref, projection_ref, out_ref, mine_ref, theirs_ref, held, moved, columns, *sems):
+    in_sems, out_sems, column_sems, head_sems = sems
+    count, devices = held.shape[0], placement_ref.shape[1]
+    piece = count // devices
     arriving, leaving = [], []
     for i in range(8):
         rows = pl.ds(i * (count // 8), count // 8)
         arriving.append(pltpu.make_async_copy(rows_ref.at[rows], held.at[rows], in_sems.at[i]))
         arriving[-1].start()
-    order = lax.broadcasted_iota(jnp.int32, (count, count), 0)
-    one_hot = jnp.where(order == target_ref[...], 1.0, 0.0).astype(jnp.bfloat16)
+    taking = []
+    for i, member in enumerate((member_ref[0], member_ref[0] ^ 2)):
+        at, source = 0, 0
+        for heads, width in ((KV_HEADS, GROUP * HEAD_DIM), (KV_HEADS, HEAD_DIM), (KV_HEADS, HEAD_DIM)):
+            copy = pltpu.make_async_copy(
+                projection_ref.at[:, pl.ds(pl.multiple_of(source + member * width, HEAD_DIM), width)],
+                columns.at[i, :, pl.ds(at, width)],
+                column_sems.at[len(taking)],
+            )
+            copy.start()
+            taking.append(copy)
+            at, source = at + width, source + heads * width
+
+    device = lax.broadcasted_iota(jnp.int32, (devices, devices), 0)
+    pieces = jnp.where(device == placement_ref[...], 1.0, 0.0).astype(jnp.bfloat16)
+    down = lax.broadcasted_iota(jnp.int32, (count, devices), 0) // piece
+    tall = jnp.where(down == lax.broadcasted_iota(jnp.int32, (count, devices), 1), 1.0, 0.0).astype(jnp.bfloat16)
+    along = lax.broadcasted_iota(jnp.int32, (devices, count), 1) // piece
+    wide = jnp.where(along == lax.broadcasted_iota(jnp.int32, (devices, count), 0), 1.0, 0.0).astype(jnp.bfloat16)
+    tall = jnp.dot(tall, pieces, preferred_element_type=jnp.float32).astype(jnp.bfloat16)
+    both = jnp.dot(tall, wide, preferred_element_type=jnp.float32)
+    row = lax.broadcasted_iota(jnp.int32, (count, count), 0) % piece
+    same = row == lax.broadcasted_iota(jnp.int32, (count, count), 1) % piece
+    one_hot = jnp.where(same, both, 0.0).astype(jnp.bfloat16)
+
+    for copy in taking:
+        copy.wait()
+    for i, out in enumerate((mine_ref, theirs_ref)):
+        leaving.append(pltpu.make_async_copy(columns.at[i], out, head_sems.at[i]))
+        leaving[-1].start()
     for copy in arriving:
         copy.wait()
     for i in range(2):
@@ -77,24 +107,31 @@
         copy.wait()
 
 
-def sort_rows(tokens, target, groups):
-    count, width = tokens.shape
+def sort_rows(tokens, placement, projection, member):
     anywhere = pl.BlockSpec(memory_space=pl.ANY)
-    moved = pl.pallas_call(
+    columns = (projection.shape[0], (GROUP + 2) * HEAD_DIM)
+    return pl.pallas_call(
         sort_kernel,
-        out_shape=jax.ShapeDtypeStruct(tokens.shape, tokens.dtype),
-        in_specs=[pl.BlockSpec(memory_space=pltpu.VMEM), anywhere],
-        out_specs=anywhere,
+        out_shape=[jax.ShapeDtypeStruct(shape, tokens.dtype) for shape in (tokens.shape, columns, columns)],
+        in_specs=[
+            pl.BlockSpec(memory_space=pltpu.SMEM),
+            pl.BlockSpec(memory_space=pltpu.VMEM),
+            anywhere,
+            anywhere,
+        ],
+        out_specs=[anywhere] * 3,
         scratch_shapes=[
             pltpu.VMEM(tokens.shape, tokens.dtype),
             pltpu.VMEM(tokens.shape, tokens.dtype),
+            pltpu.VMEM((2,) + columns, tokens.dtype),
             pltpu.SemaphoreType.DMA((8,)),
             pltpu.SemaphoreType.DMA((8,)),
+            pltpu.SemaphoreType.DMA((6,)),
+            pltpu.SemaphoreType.DMA((2,)),
         ],
         compiler_params=pltpu.CompilerParams(vmem_limit_bytes=60 * 2**20),
         name="sort_rows",
-    )(target.reshape(1, count), tokens)
-    return moved.reshape(groups, count // groups, width)
+    )(member.reshape(1), placement, tokens, projection)
 
 
 def unsort_kernel(target_ref, rows_ref, out_ref):
@@ -122,30 +159,20 @@
     )(target.reshape(count, 1), returned)
 
 
-def own_columns(projection, member):
-    query_width, key_width = HEADS * HEAD_DIM, KV_HEADS * HEAD_DIM
-    return jnp.concatenate(
-        [
-            lax.dynamic_slice_in_dim(projection, member * GROUP * HEAD_DIM, GROUP * HEAD_DIM, 1),
-            lax.dynamic_slice_in_dim(projection, query_width + member * HEAD_DIM, HEAD_DIM, 1),
-            lax.dynamic_slice_in_dim(projection, query_width + key_width + member * HEAD_DIM, HEAD_DIM, 1),
-        ],
-        axis=1,
-    )
-
-
 def ring_blocks(block, axis):
     ways = [[(i, (i + d) % 4) for i in range(4)] for d in (1, 3, 2)]
     return jnp.concatenate([block] + [lax.ppermute(block, axis, way) for way in ways], axis=0)
 
 
-def spread(block, axis):
-    up, down = [(i, (i + 1) % 4) for i in range(4)], [(i, (i + 3) % 4) for i in range(4)]
-    half = block.shape[0] // 2
-    below, above = lax.ppermute(block, axis, up), lax.ppermute(block, axis, down)
-    far_low = lax.ppermute(below[:half], axis, up)
-    far_high = lax.ppermute(above[half:], axis, down)
-    return [block, below, above, far_low, far_high]
+UP, DOWN = [(i, (i + 1) % 4) for i in range(4)], [(i, (i + 3) % 4) for i in range(4)]
+
+
+def spread(blocks):
+    pairs = [(lax.ppermute(b, axis, UP), lax.ppermute(b, axis, DOWN)) for b, axis in zip(blocks, ("x", "y"))]
+    half = blocks[0].shape[0] // 2
+    halves = [h for below, above in pairs for h in (below[:half], above[half:])]
+    far = [lax.ppermute(h, axis, way) for h, axis, way in zip(halves, ("x", "x", "y", "y"), (UP, DOWN, UP, DOWN))]
+    return [[blocks[i], *pairs[i], *far[2 * i : 2 * i + 2]] for i in range(2)]
 
 
 RING = (0, 3, 1, 2)
@@ -158,8 +185,8 @@
     pieces = [mine]
     places = [(i * 2 + zh) * rows for i in range(16)]
     ready = lax.optimization_barrier([ring_blocks(theirs[:, :half], "y"), ring_blocks(theirs[:, half:], "x")])
-    for side, two in enumerate(("x", "y")):
-        pieces += spread(ready[side], two)
+    for side, spreads in enumerate(spread(ready)):
+        pieces += spreads
         for outer, inners in SPAN:
             for inner in inners:
                 near, far = (outer, RING[inner]) if side == 0 else (RING[inner], outer)
@@ -322,10 +349,11 @@
     piece = row_count // devices
     member = lax.axis_index(CTX)
 
-    mine = lax.all_gather(own_columns(projection, member), ("x", "y"), axis=0, tiled=True)
-    theirs = lax.ppermute(own_columns(projection, member ^ 2), ("zh", "zl"), [(0, 3), (3, 0), (1, 2), (2, 1)])
+    outgoing, mine, theirs = sort_rows(tokens, placement, projection, member)
+    outgoing = outgoing.reshape(groups, row_count // groups, width)
+    mine = lax.all_gather(mine, ("x", "y"), axis=0, tiled=True)
+    theirs = lax.ppermute(theirs, ("zh", "zl"), [(0, 3), (3, 0), (1, 2), (2, 1)])
     target = (placement[0][:, None] * piece + jnp.arange(piece, dtype=jnp.int32)[None, :]).reshape(row_count)
-    outgoing = sort_rows(tokens, target, groups)
     arrived = lax.all_to_all(outgoing, DP, 0, 0, tiled=True).reshape(row_count, width)
     tables = rotary_tables(doc_lengths, members * row_count)
     arrived, theirs, tables = lax.optimization_barrier((arrived, theirs, tables))

time: 166 us -> 158 us (0.952)
  local copies, waits for them, and re-layouts: 9.96 us -> 2.91 us
  waiting for transfers between devices: 63.4 us -> 65.4 us
    unnamed x28 -> x14, local copies, waits for them, and re-layouts: 4.92 us -> 1.92 us
    ppermute x9, waiting for transfers between devices: 31.2 us -> 33.9 us  [the longest x1 18.8 us: on_device(): lax.ppermute(theirs, ('zh', 'zl'), [(0, 3), (3, 0), (1, 2), (2, 1)])]
    dynamic_slice x2 -> x0, local copies, waits for them, and re-layouts: 1.82 us -> none  [the longest x1 0.99 us: own_columns(): lax.dynamic_slice_in_dim(projection, member * GROUP * HEAD_DIM, GROUP * H...]
  transfers between devices with their start and end apart: 21 -> 21, of which waited for: 8 -> 9; matrix products, arithmetic and copies ran while one was open for 2% -> 1% of each run, Pallas kernels for 12% -> 10%
where the time goes in v8:
time: 158 us
  waiting for transfers between devices  65.4 us (41%)
  starting transfers between devices  42.2 us (27%)
  Pallas kernels  33.4 us (21%)
  between operations  13.6 us (9%)
  local copies, waits for them, and re-layouts  2.91 us (2%)
    all_to_all x1, waiting for transfers between devices, on_device(): lax.all_to_all(mixed.reshape(devices, members * piece, GROUP * HEAD_DIM),...  19.1 us
    ppermute x1, waiting for transfers between devices, on_device(): lax.ppermute(theirs, ('zh', 'zl'), [(0, 3), (3, 0), (1, 2), (2, 1)])  18.8 us
    pallas_call x3, Pallas kernels, project(): pl.pallas_call(functools.partial(project_kernel, len(rows)), out_shape=[j...  14.5 us
    ppermute x2, waiting for transfers between devices, spread(): lax.ppermute(b, axis, DOWN)  11.7 us
    all_to_all x1, starting transfers between devices, on_device(): lax.all_to_all(outgoing, DP, 0, 0, tiled=True).reshape(row_count, width)  11.5 us
    pallas_call x1, Pallas kernels, attend(): pl.pallas_call(attention_kernel, out_shape=jax.ShapeDtypeStruct((count, G...  8.39 us
    ppermute x6, starting transfers between devices, ring_blocks(): lax.ppermute(block, axis, way)  6.91 us
    ppermute x6, waiting for transfers between devices, ring_blocks(): lax.ppermute(block, axis, way)  6.69 us
  transfers between devices with their start and end apart: 21, of which 9 were waited for; matrix products, arithmetic and copies ran while one was open for 1% of the time, Pallas kernels for 10%

profile of v8, /device:TPU:1, one launch (start us, length us, event | category | flops | bytes accessed | tf_op | source)
XLA Modules:
  0.0 157.8 jit_solution(14948260681785392675)
XLA Ops:
  6.5 0.0 all-gather.2.cloned.1.call-start
  6.5 4.3 %sort_rows.1 = (bf16[256,4096]{1,0:T(8,128)(2,1)}, bf16[128,768]{1,0:T(8,128)(2,1)}, bf16[128,768]{1,0:T(8,128)(2,1)}) custom-call(s32[1]{0:T(128)} %bitcast.1.member_ref, s32[1,128]{1,0:T(1,128)} %placement_ref.1, bf16[256,4096]{1,0:T(8,128)(2,1)} %rows_ref.1, bf16[128,3072]{1,0:T(8,128)(2,1)} %projection_ref.1), custom_call_target="tpu_custom_call" | custom-call | tf_op jit(solution)/shard_map/sort_rows/pallas_call | solution.py:113
  10.8 0.0 all-gather.2.cloned.1.call-update
  10.8 0.0 copy-start.6
  10.9 11.5 %all-to-all-start = ((bf16[32,8,4096]{2,1,0:T(8,128)(2,1)}), bf16[32,8,4096]{2,1,0:T(8,128)(2,1)}, u32[]{:S(2)}, u32[]{:S(2)}) async-start(bf16[32,8,4096]{2,1,0:T(8,128)(2,1)} %bitcast.40), calls=%async_computation | async-start | bytes 4194304 | tf_op jit(solution)/shard_map/all_to_all | solution.py:357
  22.3 0.0 copy-done.6
  22.3 2.9 %collective-permute-start = (bf16[128,768]{1,0:T(8,128)(2,1)S(1)}, bf16[128,768]{1,0:T(8,128)(2,1)S(1)}, u32[]{:S(2)}, u32[]{:S(2)}) collective-permute-start(bf16[128,768]{1,0:T(8,128)(2,1)S(1)} %copy-done.6), channel_id=1, source_target_pairs={{0,6},{6,0},{2,4},{4,2},{1,7},{7,1},{3,5},{5,3},{8,14},{14,8},{10,... | collective-permute-start | bytes 589832 | tf_op jit(solution)/shard_map/ppermute | solution.py:355
  25.2 4.0 %rotary_tables.1 = (f32[1024,128]{1,0:T(8,128)}, f32[1024,128]{1,0:T(8,128)}) custom-call(s32[1,8]{1,0:T(1,128)} %lengths_ref.3, f32[1,128]{1,0:T(1,128)} %constant.207.clone.frequency_ref), custom_call_target="tpu_custom_call" | custom-call | tf_op jit(solution)/shard_map/rotary_tables/pallas_call | solution.py:48
  29.2 18.8 %collective-permute-done = bf16[128,768]{1,0:T(8,128)(2,1)S(1)} collective-permute-done((bf16[128,768]{1,0:T(8,128)(2,1)S(1)}, bf16[128,768]{1,0:T(8,128)(2,1)S(1)}, u32[]{:S(2)}, u32[]{:S(2)}) %collective-permute-start) | collective-permute-done | bytes 196640 | tf_op jit(solution)/shard_map/ppermute | solution.py:355
  48.1 5.7 %all-to-all-done = bf16[32,8,4096]{2,1,0:T(8,128)(2,1)} async-done(((bf16[32,8,4096]{2,1,0:T(8,128)(2,1)}), bf16[32,8,4096]{2,1,0:T(8,128)(2,1)}, u32[]{:S(2)}, u32[]{:S(2)}) %all-to-all-start) | async-done | bytes 2097184 | tf_op jit(solution)/shard_map/all_to_all | solution.py:357
  53.8 0.5 collective-permute-start.1
  54.4 0.8 collective-permute-start.7
  55.1 0.5 collective-permute-start.6
  55.7 0.9 collective-permute-start.5
  56.6 3.2 %collective-permute-start.4 = (bf16[128,384]{1,0:T(8,128)(2,1)S(1)}, bf16[128,384]{1,0:T(8,128)(2,1)S(1)}, u32[]{:S(2)}, u32[]{:S(2)}) collective-permute-start(bf16[128,384]{1,0:T(8,128)(2,1)S(1)} %get-tuple-element.36), channel_id=1, source_target_pairs={{0,16},{8,24},{16,0},{24,8},{1,17},{9,25},{17,1},{25,9},{2,18},{10... | collective-permute-start | bytes 294920 | tf_op jit(solution)/shard_map/ppermute | solution.py:164
  59.8 0.0 collective-permute-done.7
  59.8 0.6 collective-permute-start.3
  60.4 0.0 collective-permute-done.6
  60.4 0.9 collective-permute-start.2
  61.3 0.0 collective-permute-done.5
  61.3 2.1 %collective-permute-done.4 = bf16[128,384]{1,0:T(8,128)(2,1)S(1)} collective-permute-done((bf16[128,384]{1,0:T(8,128)(2,1)S(1)}, bf16[128,384]{1,0:T(8,128)(2,1)S(1)}, u32[]{:S(2)}, u32[]{:S(2)}) %collective-permute-start.4) | collective-permute-done | bytes 98336 | tf_op jit(solution)/shard_map/ppermute | solution.py:164
  63.4 4.4 %collective-permute-done.3 = bf16[128,384]{1,0:T(8,128)(2,1)S(1)} collective-permute-done((bf16[128,384]{1,0:T(8,128)(2,1)S(1)}, bf16[128,384]{1,0:T(8,128)(2,1)S(1)}, u32[]{:S(2)}, u32[]{:S(2)}) %collective-permute-start.3) | collective-permute-done | bytes 98336 | tf_op jit(solution)/shard_map/ppermute | solution.py:164
  67.8 0.3 collective-permute-done.2
  68.1 3.1 %collective-permute-start.9 = (bf16[512,384]{1,0:T(8,128)(2,1)S(1)}, bf16[512,384]{1,0:T(8,128)(2,1)S(1)}, u32[]{:S(2)}, u32[]{:S(2)}) collective-permute-start(bf16[512,384]{1,0:T(8,128)(2,1)S(1)} %pad_maximum_fusion.refs_2_.refs_3_), channel_id=1, source_target_pairs={{0,96},{32,0},{64,32},{96,64},{1,97},{33,1},{65,33},{97,65},{2,98}... | collective-permute-start | bytes 1179656 | tf_op jit(solution)/shard_map/ppermute | solution.py:171
  71.2 0.0 collective-permute-start.8
  71.2 0.5 collective-permute-start.13
  71.7 0.9 collective-permute-start.12
  72.6 11.7 %collective-permute-done.9.refs_4_.refs_5_ = bf16[512,384]{1,0:T(8,128)(2,1)S(1)} collective-permute-done((bf16[512,384]{1,0:T(8,128)(2,1)S(1)}, bf16[512,384]{1,0:T(8,128)(2,1)S(1)}, u32[]{:S(2)}, u32[]{:S(2)}) %collective-permute-start.9) | collective-permute-done | bytes 393248 | tf_op jit(solution)/shard_map/ppermute | solution.py:171
  84.4 2.2 %collective-permute-start.11 = (bf16[256,384]{1,0:T(8,128)(2,1)S(1)}, bf16[256,384]{1,0:T(8,128)(2,1)S(1)}, u32[]{:S(2)}, u32[]{:S(2)}) collective-permute-start(bf16[256,384]{1,0:T(8,128)(2,1)S(1)} %slice.25), channel_id=1, source_target_pairs={{0,96},{32,0},{64,32},{96,64},{1,97},{33,1},{65,33},{97,65},{2,98}... | collective-permute-start | bytes 589832 | tf_op jit(solution)/shard_map/ppermute | solution.py:174
  86.6 0.0 collective-permute-done.8.refs_3_.refs_4_
  86.6 0.1 collective-permute-start.10
  86.7 0.0 collective-permute-done.13.refs_9_.refs_10_
  86.8 2.0 %collective-permute-start.15 = (bf16[256,384]{1,0:T(8,128)(2,1)S(1)}, bf16[256,384]{1,0:T(8,128)(2,1)S(1)}, u32[]{:S(2)}, u32[]{:S(2)}) collective-permute-start(bf16[256,384]{1,0:T(8,128)(2,1)S(1)} %slice.27), channel_id=1, source_target_pairs={{0,24},{8,0},{16,8},{24,16},{1,25},{9,1},{17,9},{25,17},{2,26},{10... | collective-permute-start | bytes 589832 | tf_op jit(solution)/shard_map/ppermute | solution.py:174
  88.8 0.0 collective-permute-done.12.refs_8_.refs_9_
  88.8 0.7 slice.26
  89.5 0.0 collective-permute-start.14
  89.5 0.0 collective-permute-done.11.refs_6_.refs_7_
  89.5 2.7 %collective-permute-start.16 = (bf16[256,4096]{1,0:T(8,128)(2,1)}, bf16[256,4096]{1,0:T(8,128)(2,1)}, u32[]{:S(2)}, u32[]{:S(2)}) collective-permute-start(bf16[256,4096]{1,0:T(8,128)(2,1)} %bitcast.3.refs_0_), channel_id=1, source_target_pairs={{0,1},{1,0},{2,3},{3,2},{4,5},{5,4},{6,7},{7,6},{8,9},{9,8},{10,11... | collective-permute-start | bytes 6291464 | tf_op jit(solution)/shard_map/ppermute | solution.py:363
  92.2 0.1 stack.147.places_ref
  92.3 0.1 collective-permute-done.10.refs_5_.refs_6_
  92.4 0.0 collective-permute-done.15.refs_11_.refs_12_
  92.4 3.2 %collective-permute-done.14.refs_10_.refs_11_ = bf16[256,384]{1,0:T(8,128)(2,1)S(1)} collective-permute-done((bf16[256,384]{1,0:T(8,128)(2,1)}, bf16[256,384]{1,0:T(8,128)(2,1)S(1)}, u32[]{:S(2)}, u32[]{:S(2)}) %collective-permute-start.14) | collective-permute-done | bytes 196640 | tf_op jit(solution)/shard_map/ppermute | solution.py:174
  95.6 1.9 %copy-done = bf16[2048,768]{1,0:T(8,128)(2,1)S(1)} copy-done((bf16[2048,768]{1,0:T(8,128)(2,1)S(1)}, bf16[2048,768]{1,0:T(8,128)(2,1)}, u32[]{:S(2)}) %copy-start) | copy-done | bytes 3145752
  97.5 4.3 %project.3.refs_0_ = bf16[256,768]{1,0:T(8,128)(2,1)S(1)} custom-call(s32[48]{0:T(128)S(1)} %stack.147.places_ref, bf16[256,4096]{1,0:T(8,128)(2,1)} %bitcast.3.refs_0_, bf16[2048,768]{1,0:T(8,128)(2,1)S(1)} %copy-done, bf16[512,384]{1,0:T(8,128)(2,1)S(1)} %pad_maximum_fusion.refs_2_.refs_3_, bf16[512,384]{1,0:T(8,128)(2,1)S(1)} %collective-permute-done.8.refs_3_.refs_4_, ...), custom_call_target="tpu_custom_call" | custom-call | flops 1610612736 | bytes 8388608 | tf_op jit(solution)/shard_map/project/pallas_call | solution.py:236
  101.8 0.0 collective-permute-done.1.refs_1_
  101.8 3.5 %collective-permute-start.17 = (bf16[256,4096]{1,0:T(8,128)(2,1)}, bf16[256,4096]{1,0:T(8,128)(2,1)S(1)}, u32[]{:S(2)}, u32[]{:S(2)}) collective-permute-start(bf16[256,4096]{1,0:T(8,128)(2,1)} %collective-permute-done.1.refs_1_), channel_id=1, source_target_pairs={{0,1},{1,0},{2,3},{3,2},{4,5},{5,4},{6,7},{7,6},{8,9},{9,8},{10,11... | collective-permute-start | bytes 6291464 | tf_op jit(solution)/shard_map/ppermute | solution.py:366
  105.3 0.0 collective-permute-done.16.refs_0_
  105.3 0.0 copy-done.1
  105.3 7.2 %project.4 = (bf16[256,768]{1,0:T(8,128)(2,1)S(1)}, bf16[256,768]{1,0:T(8,128)(2,1)S(1)}) custom-call(s32[48]{0:T(128)S(1)} %stack.147.places_ref, bf16[256,4096]{1,0:T(8,128)(2,1)} %collective-permute-done.16.refs_0_, bf16[256,4096]{1,0:T(8,128)(2,1)} %collective-permute-done.1.refs_1_, bf16[2048,768]{1,0:T(8,128)(2,1)S(1)} %copy-done.1, ...), custom_call_target="tpu_custom_call" | custom-call | flops 3221225472 | bytes 10485760 | tf_op jit(solution)/shard_map/project/pallas_call | solution.py:236
  112.5 0.0 copy-start.2
  112.5 0.0 copy-start.3
  112.5 0.0 copy-start.4
  112.5 0.0 collective-permute-done.17.refs_0_
  112.6 3.0 %project.5.refs_3_ = bf16[256,768]{1,0:T(8,128)(2,1)S(1)} custom-call(s32[48]{0:T(128)S(1)} %stack.147.places_ref, bf16[256,4096]{1,0:T(8,128)(2,1)S(1)} %collective-permute-done.17.refs_0_, bf16[2048,768]{1,0:T(8,128)(2,1)S(1)} %copy-done.1, bf16[512,384]{1,0:T(8,128)(2,1)S(1)} %pad_maximum_fusion.refs_2_.refs_3_, ...), custom_call_target="tpu_custom_call" | custom-call | flops 1610612736 | bytes 8388608 | tf_op jit(solution)/shard_map/project/pallas_call | solution.py:236
  115.5 0.0 copy-done.2
  115.6 0.0 copy-done.3
  115.6 0.0 copy-done.4
  115.6 0.0 copy-start.5
  115.6 8.4 %attend.1 = bf16[1024,512]{1,0:T(8,128)(2,1)} custom-call(s32[1]{0:T(128)} %bitcast.1.member_ref, s32[1,8]{1,0:T(1,128)S(1)} %copy-done.4, bf16[256,768]{1,0:T(8,128)(2,1)S(1)} %project.3.refs_0_, bf16[256,768]{1,0:T(8,128)(2,1)S(1)} %get-tuple-element.31.refs_1_, bf16[256,768]{1,0:T(8,128)(2,1)S(1)} %get-tuple-element.32.refs_2_, ...), custom_call_target="tpu_custom_call" | custom-call | tf_op jit(solution)/shard_map/attend/pallas_call | solution.py:328
  124.0 5.4 %all-to-all-start.1 = ((bf16[128,8,512]{2,1,0:T(8,128)(2,1)}), bf16[128,8,512]{2,1,0:T(8,128)(2,1)S(1)}, u32[]{:S(2)}, u32[]{:S(2)}) async-start(bf16[128,8,512]{2,1,0:T(8,128)(2,1)} %bitcast.36), calls=%async_computation.1 | async-start | bytes 2097152 | tf_op jit(solution)/shard_map/all_to_all | solution.py:369
  129.4 0.1 iota_add_fusion
  129.5 0.1 add.358.target_ref
  129.5 19.1 %all-to-all-done.1 = bf16[128,8,512]{2,1,0:T(8,128)(2,1)S(1)} async-done(((bf16[128,8,512]{2,1,0:T(8,128)(2,1)}), bf16[128,8,512]{2,1,0:T(8,128)(2,1)S(1)}, u32[]{:S(2)}, u32[]{:S(2)}) %all-to-all-start.1) | async-done | bytes 1048608 | tf_op jit(solution)/shard_map/all_to_all | solution.py:369
  148.6 2.3 %unsort_rows.1 = bf16[256,2048]{1,0:T(8,128)(2,1)} custom-call(s32[256,1]{1,0:T(8,128)S(1)} %add.358.target_ref, bf16[32,4,8,512]{3,2,1,0:T(8,128)(2,1)S(1)} %bitcast.39), custom_call_target="tpu_custom_call" | custom-call | tf_op jit(solution)/shard_map/unsort_rows/pallas_call | solution.py:148
  (11 shorter events, 0.2 us)
Async XLA Ops:
  6.5 89.1 %all-gather.2.cloned.1.call-start = ((), (), s32[]{:S(2)}) async-start(), calls=%async_computation.2 | async-start | bytes 3342336 | tf_op jit(solution)/shard_map/all_gather | solution.py:354
  10.8 11.5 %copy-start.6 = (bf16[128,768]{1,0:T(8,128)(2,1)S(1)}, bf16[128,768]{1,0:T(8,128)(2,1)}, u32[]{:S(2)}) copy-start(bf16[128,768]{1,0:T(8,128)(2,1)} %get-tuple-element.21) | copy-start | bytes 589828
  10.9 43.0 %all-to-all-start = ((bf16[32,8,4096]{2,1,0:T(8,128)(2,1)}), bf16[32,8,4096]{2,1,0:T(8,128)(2,1)}, u32[]{:S(2)}, u32[]{:S(2)}) async-start(bf16[32,8,4096]{2,1,0:T(8,128)(2,1)} %bitcast.40), calls=%async_computation | async-start | bytes 4194304 | tf_op jit(solution)/shard_map/all_to_all | solution.py:357
  22.3 25.7 %collective-permute-start = (bf16[128,768]{1,0:T(8,128)(2,1)S(1)}, bf16[128,768]{1,0:T(8,128)(2,1)S(1)}, u32[]{:S(2)}, u32[]{:S(2)}) collective-permute-start(bf16[128,768]{1,0:T(8,128)(2,1)S(1)} %copy-done.6), channel_id=1, source_target_pairs={{0,6},{6,0},{2,4},{4,2},{1,7},{7,1},{3,5},{5,3},{8,14},{14,8},{10,... | collective-permute-start | bytes 589832 | tf_op jit(solution)/shard_map/ppermute | solution.py:355
  53.8 48.0 %collective-permute-start.1 = (bf16[256,4096]{1,0:T(8,128)(2,1)}, bf16[256,4096]{1,0:T(8,128)(2,1)}, u32[]{:S(2)}, u32[]{:S(2)}) collective-permute-start(bf16[256,4096]{1,0:T(8,128)(2,1)} %bitcast.3.refs_0_), channel_id=1, source_target_pairs={{0,2},{2,0},{1,3},{3,1},{4,6},{6,4},{5,7},{7,5},{8,10},{10,8},{9,1... | collective-permute-start | bytes 6291464 | tf_op jit(solution)/shard_map/ppermute | solution.py:362
  54.4 5.4 %collective-permute-start.7 = (bf16[128,384]{1,0:T(8,128)(2,1)S(1)}, bf16[128,384]{1,0:T(8,128)(2,1)S(1)}, u32[]{:S(2)}, u32[]{:S(2)}) collective-permute-start(bf16[128,384]{1,0:T(8,128)(2,1)S(1)} %get-tuple-element.35), channel_id=1, source_target_pairs={{0,64},{32,96},{64,0},{96,32},{1,65},{33,97},{65,1},{97,33},{2,66}... | collective-permute-start | bytes 294920 | tf_op jit(solution)/shard_map/ppermute | solution.py:164
  55.1 5.3 %collective-permute-start.6 = (bf16[128,384]{1,0:T(8,128)(2,1)S(1)}, bf16[128,384]{1,0:T(8,128)(2,1)S(1)}, u32[]{:S(2)}, u32[]{:S(2)}) collective-permute-start(bf16[128,384]{1,0:T(8,128)(2,1)S(1)} %get-tuple-element.35), channel_id=1, source_target_pairs={{0,96},{32,0},{64,32},{96,64},{1,97},{33,1},{65,33},{97,65},{2,98}... | collective-permute-start | bytes 294920 | tf_op jit(solution)/shard_map/ppermute | solution.py:164
  55.7 5.6 %collective-permute-start.5 = (bf16[128,384]{1,0:T(8,128)(2,1)S(1)}, bf16[128,384]{1,0:T(8,128)(2,1)S(1)}, u32[]{:S(2)}, u32[]{:S(2)}) collective-permute-start(bf16[128,384]{1,0:T(8,128)(2,1)S(1)} %get-tuple-element.35), channel_id=1, source_target_pairs={{0,32},{32,64},{64,96},{96,0},{1,33},{33,65},{65,97},{97,1},{2,34}... | collective-permute-start | bytes 294920 | tf_op jit(solution)/shard_map/ppermute | solution.py:164
  56.6 6.8 %collective-permute-start.4 = (bf16[128,384]{1,0:T(8,128)(2,1)S(1)}, bf16[128,384]{1,0:T(8,128)(2,1)S(1)}, u32[]{:S(2)}, u32[]{:S(2)}) collective-permute-start(bf16[128,384]{1,0:T(8,128)(2,1)S(1)} %get-tuple-element.36), channel_id=1, source_target_pairs={{0,16},{8,24},{16,0},{24,8},{1,17},{9,25},{17,1},{25,9},{2,18},{10... | collective-permute-start | bytes 294920 | tf_op jit(solution)/shard_map/ppermute | solution.py:164
  59.8 7.9 %collective-permute-start.3 = (bf16[128,384]{1,0:T(8,128)(2,1)S(1)}, bf16[128,384]{1,0:T(8,128)(2,1)S(1)}, u32[]{:S(2)}, u32[]{:S(2)}) collective-permute-start(bf16[128,384]{1,0:T(8,128)(2,1)S(1)} %get-tuple-element.36), channel_id=1, source_target_pairs={{0,24},{8,0},{16,8},{24,16},{1,25},{9,1},{17,9},{25,17},{2,26},{10... | collective-permute-start | bytes 294920 | tf_op jit(solution)/shard_map/ppermute | solution.py:164
  60.4 7.6 %collective-permute-start.2 = (bf16[128,384]{1,0:T(8,128)(2,1)S(1)}, bf16[128,384]{1,0:T(8,128)(2,1)S(1)}, u32[]{:S(2)}, u32[]{:S(2)}) collective-permute-start(bf16[128,384]{1,0:T(8,128)(2,1)S(1)} %get-tuple-element.36), channel_id=1, source_target_pairs={{0,8},{8,16},{16,24},{24,0},{1,9},{9,17},{17,25},{25,1},{2,10},{10... | collective-permute-start | bytes 294920 | tf_op jit(solution)/shard_map/ppermute | solution.py:164
  68.1 16.3 %collective-permute-start.9 = (bf16[512,384]{1,0:T(8,128)(2,1)S(1)}, bf16[512,384]{1,0:T(8,128)(2,1)S(1)}, u32[]{:S(2)}, u32[]{:S(2)}) collective-permute-start(bf16[512,384]{1,0:T(8,128)(2,1)S(1)} %pad_maximum_fusion.refs_2_.refs_3_), channel_id=1, source_target_pairs={{0,96},{32,0},{64,32},{96,64},{1,97},{33,1},{65,33},{97,65},{2,98}... | collective-permute-start | bytes 1179656 | tf_op jit(solution)/shard_map/ppermute | solution.py:171
  71.2 15.4 %collective-permute-start.8 = (bf16[512,384]{1,0:T(8,128)(2,1)S(1)}, bf16[512,384]{1,0:T(8,128)(2,1)S(1)}, u32[]{:S(2)}, u32[]{:S(2)}) collective-permute-start(bf16[512,384]{1,0:T(8,128)(2,1)S(1)} %pad_maximum_fusion.refs_2_.refs_3_), channel_id=1, source_target_pairs={{0,32},{32,64},{64,96},{96,0},{1,33},{33,65},{65,97},{97,1},{2,34}... | collective-permute-start | bytes 1179656 | tf_op jit(solution)/shard_map/ppermute | solution.py:171
  71.2 15.5 %collective-permute-start.13 = (bf16[512,384]{1,0:T(8,128)(2,1)S(1)}, bf16[512,384]{1,0:T(8,128)(2,1)S(1)}, u32[]{:S(2)}, u32[]{:S(2)}) collective-permute-start(bf16[512,384]{1,0:T(8,128)(2,1)S(1)} %pad_maximum_fusion.1.refs_7_.refs_8_), channel_id=1, source_target_pairs={{0,24},{8,0},{16,8},{24,16},{1,25},{9,1},{17,9},{25,17},{2,26},{10... | collective-permute-start | bytes 1179656 | tf_op jit(solution)/shard_map/ppermute | solution.py:171
  71.7 17.1 %collective-permute-start.12 = (bf16[512,384]{1,0:T(8,128)(2,1)S(1)}, bf16[512,384]{1,0:T(8,128)(2,1)S(1)}, u32[]{:S(2)}, u32[]{:S(2)}) collective-permute-start(bf16[512,384]{1,0:T(8,128)(2,1)S(1)} %pad_maximum_fusion.1.refs_7_.refs_8_), channel_id=1, source_target_pairs={{0,8},{8,16},{16,24},{24,0},{1,9},{9,17},{17,25},{25,1},{2,10},{10... | collective-permute-start | bytes 1179656 | tf_op jit(solution)/shard_map/ppermute | solution.py:171
  84.4 5.1 %collective-permute-start.11 = (bf16[256,384]{1,0:T(8,128)(2,1)S(1)}, bf16[256,384]{1,0:T(8,128)(2,1)S(1)}, u32[]{:S(2)}, u32[]{:S(2)}) collective-permute-start(bf16[256,384]{1,0:T(8,128)(2,1)S(1)} %slice.25), channel_id=1, source_target_pairs={{0,96},{32,0},{64,32},{96,64},{1,97},{33,1},{65,33},{97,65},{2,98}... | collective-permute-start | bytes 589832 | tf_op jit(solution)/shard_map/ppermute | solution.py:174
  86.6 5.8 %collective-permute-start.10 = (bf16[256,384]{1,0:T(8,128)(2,1)S(1)}, bf16[256,384]{1,0:T(8,128)(2,1)S(1)}, u32[]{:S(2)}, u32[]{:S(2)}) collective-permute-start(bf16[256,384]{1,0:T(8,128)(2,1)S(1)} %slice.24), channel_id=1, source_target_pairs={{0,32},{32,64},{64,96},{96,0},{1,33},{33,65},{65,97},{97,1},{2,34}... | collective-permute-start | bytes 589832 | tf_op jit(solution)/shard_map/ppermute | solution.py:174
  86.8 5.7 %collective-permute-start.15 = (bf16[256,384]{1,0:T(8,128)(2,1)S(1)}, bf16[256,384]{1,0:T(8,128)(2,1)S(1)}, u32[]{:S(2)}, u32[]{:S(2)}) collective-permute-start(bf16[256,384]{1,0:T(8,128)(2,1)S(1)} %slice.27), channel_id=1, source_target_pairs={{0,24},{8,0},{16,8},{24,16},{1,25},{9,1},{17,9},{25,17},{2,26},{10... | collective-permute-start | bytes 589832 | tf_op jit(solution)/shard_map/ppermute | solution.py:174
  89.5 6.1 %collective-permute-start.14 = (bf16[256,384]{1,0:T(8,128)(2,1)}, bf16[256,384]{1,0:T(8,128)(2,1)S(1)}, u32[]{:S(2)}, u32[]{:S(2)}) collective-permute-start(bf16[256,384]{1,0:T(8,128)(2,1)} %slice.26), channel_id=1, source_target_pairs={{0,8},{8,16},{16,24},{24,0},{1,9},{9,17},{17,25},{25,1},{2,10},{10... | collective-permute-start | bytes 589832 | tf_op jit(solution)/shard_map/ppermute | solution.py:174
  89.5 15.8 %collective-permute-start.16 = (bf16[256,4096]{1,0:T(8,128)(2,1)}, bf16[256,4096]{1,0:T(8,128)(2,1)}, u32[]{:S(2)}, u32[]{:S(2)}) collective-permute-start(bf16[256,4096]{1,0:T(8,128)(2,1)} %bitcast.3.refs_0_), channel_id=1, source_target_pairs={{0,1},{1,0},{2,3},{3,2},{4,5},{5,4},{6,7},{7,6},{8,9},{9,8},{10,11... | collective-permute-start | bytes 6291464 | tf_op jit(solution)/shard_map/ppermute | solution.py:363
  95.6 1.9 %copy-start = (bf16[2048,768]{1,0:T(8,128)(2,1)S(1)}, bf16[2048,768]{1,0:T(8,128)(2,1)}, u32[]{:S(2)}) copy-start(bf16[2048,768]{1,0:T(8,128)(2,1)} %all-gather.2.cloned.1.call-done.refs_1_.refs_2_) | copy-start | bytes 9437188
  97.5 7.8 %copy-start.1 = (bf16[2048,768]{1,0:T(8,128)(2,1)S(1)}, bf16[2048,768]{1,0:T(8,128)(2,1)}, u32[]{:S(2)}) copy-start(bf16[2048,768]{1,0:T(8,128)(2,1)} %all-gather.2.cloned.1.call-done.refs_1_.refs_2_) | copy-start | bytes 9437188
  101.8 10.8 %collective-permute-start.17 = (bf16[256,4096]{1,0:T(8,128)(2,1)}, bf16[256,4096]{1,0:T(8,128)(2,1)S(1)}, u32[]{:S(2)}, u32[]{:S(2)}) collective-permute-start(bf16[256,4096]{1,0:T(8,128)(2,1)} %collective-permute-done.1.refs_1_), channel_id=1, source_target_pairs={{0,1},{1,0},{2,3},{3,2},{4,5},{5,4},{6,7},{7,6},{8,9},{9,8},{10,11... | collective-permute-start | bytes 6291464 | tf_op jit(solution)/shard_map/ppermute | solution.py:366
  112.5 3.0 %copy-start.2 = (f32[1024,128]{1,0:T(8,128)S(1)}, f32[1024,128]{1,0:T(8,128)}, u32[]{:S(2)}) copy-start(f32[1024,128]{1,0:T(8,128)} %get-tuple-element.33.refs_4_) | copy-start | bytes 1572868
  112.5 3.0 %copy-start.3 = (f32[1024,128]{1,0:T(8,128)S(1)}, f32[1024,128]{1,0:T(8,128)}, u32[]{:S(2)}) copy-start(f32[1024,128]{1,0:T(8,128)} %get-tuple-element.34.refs_5_) | copy-start | bytes 1572868
  112.5 3.0 %copy-start.4 = (s32[1,8]{1,0:T(1,128)S(1)}, s32[1,8]{1,0:T(1,128)}, u32[]{:S(2)}) copy-start(s32[1,8]{1,0:T(1,128)} %lengths_ref.3) | copy-start | bytes 100
  115.6 13.8 %copy-start.5 = (s32[1,128]{1,0:T(1,128)S(1)}, s32[1,128]{1,0:T(1,128)}, u32[]{:S(2)}) copy-start(s32[1,128]{1,0:T(1,128)} %placement_ref.1) | copy-start | bytes 1540
  124.0 24.6 %all-to-all-start.1 = ((bf16[128,8,512]{2,1,0:T(8,128)(2,1)}), bf16[128,8,512]{2,1,0:T(8,128)(2,1)S(1)}, u32[]{:S(2)}, u32[]{:S(2)}) async-start(bf16[128,8,512]{2,1,0:T(8,128)(2,1)} %bitcast.36), calls=%async_computation.1 | async-start | bytes 2097152 | tf_op jit(solution)/shard_map/all_to_all | solution.py:369
Sparse Core Ops, SparseCore 0:
  11.0 71.9 all-gather.1

commit v9 on v8

--- a/solution.py
+++ b/solution.py
@@ -279,34 +279,37 @@
             values[rows] = here[:, (GROUP + 1) * HEAD_DIM :].astype(jnp.bfloat16)
 
     scale = HEAD_DIM ** (-0.5) * math.log2(math.e)
-    reach = (MOST - 1 + BLOCK - 1) // BLOCK
-    for b in range(blocks):
+    tile = 128
+    reach = (MOST - 1 + tile - 1) // tile
+    for b in range(count // tile):
         first = max(0, b - reach)
-        width = (b + 1 - first) * BLOCK
-        position = b * BLOCK + lax.broadcasted_iota(jnp.int32, (BLOCK, 1), 0)
+        width = (b + 1 - first) * tile
+        position = b * tile + lax.broadcasted_iota(jnp.int32, (tile, 1), 0)
         begin, end = jnp.zeros_like(position), jnp.int32(0)
         for j in range(lengths_ref.shape[1]):
             end = end + lengths_ref[0, j]
             begin = jnp.where(position >= end, end, begin)
-        key_at = first * BLOCK + lax.broadcasted_iota(jnp.int32, (BLOCK, width), 1)
+        key_at = first * tile + lax.broadcasted_iota(jnp.int32, (tile, width), 1)
         allowed = (key_at >= begin) & (key_at <= position)
-        key_block = keys[first * BLOCK : (b + 1) * BLOCK]
-        value_block = values[first * BLOCK : (b + 1) * BLOCK]
+        key_block = keys[first * tile : (b + 1) * tile]
+        value_block = values[first * tile : (b + 1) * tile]
+        rows = slice(b * tile, (b + 1) * tile)
+        stacked = jnp.concatenate([queries[g, rows] for g in range(GROUP)], axis=0)
+        all_scores = lax.dot_general(
+            stacked, key_block, (((1,), (1,)), ((), ())), preferred_element_type=jnp.float32
+        )
+        stacked_weights, totals = [], []
         for g in range(GROUP):
-            scores = lax.dot_general(
-                queries[g, b * BLOCK : (b + 1) * BLOCK],
-                key_block,
-                (((1,), (1,)), ((), ())),
-                preferred_element_type=jnp.float32,
-            )
-            scores = jnp.where(allowed, scores, -1e30)
+            scores = jnp.where(allowed, all_scores[g * tile : (g + 1) * tile], -1e30)
             weights = jnp.exp2((scores - jnp.max(scores, axis=1, keepdims=True)) * scale)
-            total = jnp.sum(weights, axis=1, keepdims=True)
-            weighted = jnp.dot(
-                weights.astype(jnp.bfloat16), value_block, preferred_element_type=jnp.float32
-            )
-            mixed[b * BLOCK : (b + 1) * BLOCK, g * HEAD_DIM : (g + 1) * HEAD_DIM] = (
-                weighted / total
+            totals.append(jnp.sum(weights, axis=1, keepdims=True))
+            stacked_weights.append(weights.astype(jnp.bfloat16))
+        weighted = jnp.dot(
+            jnp.concatenate(stacked_weights, axis=0), value_block, preferred_element_type=jnp.float32
+        )
+        for g in range(GROUP):
+            mixed[rows, g * HEAD_DIM : (g + 1) * HEAD_DIM] = (
+                weighted[g * tile : (g + 1) * tile] / totals[g]
             ).astype(jnp.bfloat16)
 
     left = lax.broadcasted_iota(jnp.int32, (BLOCK, BLOCK), 0)
@@ -361,10 +364,10 @@
     across = [(0, 1), (1, 0)]
     far = lax.ppermute(arrived, "zl", across)
     near = lax.ppermute(arrived, "core", across)
-    lanes = project(places, pieces, [arrived])
+    lanes = project(places, pieces, [arrived, near])
     far, lanes = lax.optimization_barrier((far, lanes))
     last = lax.ppermute(far, "core", across)
-    lanes = lanes + project(places, pieces, [near, far]) + project(places, pieces, [last])
+    lanes = lanes + project(places, pieces, [far]) + project(places, pieces, [last])
     mixed = attend(member.reshape(1), doc_lengths, lanes, *tables)
     returned = lax.all_to_all(
         mixed.reshape(devices, members * piece, GROUP * HEAD_DIM), EVERY, 0, 0, tiled=True

time: 158 us -> 166 us (1.051)
  waiting for transfers between devices: 65.4 us -> 71.9 us
  starting transfers between devices: 42.2 us -> 45.7 us
  Pallas kernels: 33.4 us -> 31.5 us
    ppermute x6, waiting for transfers between devices: 6.69 us -> 15.1 us  [ring_blocks(): lax.ppermute(block, axis, way)]
    ppermute x2, waiting for transfers between devices: 11.7 us -> 3.55 us  [spread(): lax.ppermute(b, axis, DOWN)]
    ppermute x2, waiting for transfers between devices: 0.01 us -> 6.78 us  [spread(): lax.ppermute(b, axis, UP)]
    ppermute x6, starting transfers between devices: 6.91 us -> 3.04 us  [ring_blocks(): lax.ppermute(block, axis, way)]
    ppermute x2, starting transfers between devices: 3.64 us -> 7.05 us  [spread(): lax.ppermute(b, axis, DOWN)]
    pallas_call x1, Pallas kernels: 8.39 us -> 6.45 us  [attend(): pl.pallas_call(attention_kernel, out_shape=jax.ShapeDtypeStruct((count, G...]
    ppermute x4, starting transfers between devices: 4.28 us -> 6.22 us  [spread(): lax.ppermute(h, axis, way)]
  transfers between devices with their start and end apart: 21 -> 21, of which waited for: 9 -> 13; matrix products, arithmetic and copies ran while one was open for 1% -> 1% of each run, Pallas kernels for 10% -> 9%
where the time goes in v9:
time: 166 us
  waiting for transfers between devices  71.9 us (43%)
  starting transfers between devices  45.7 us (28%)
  Pallas kernels  31.5 us (19%)
  between operations  13.6 us (8%)
  local copies, waits for them, and re-layouts  2.91 us (2%)
    all_to_all x1, waiting for transfers between devices, on_device(): lax.all_to_all(mixed.reshape(devices, members * piece, GROUP * HEAD_DIM),...  19.1 us
    ppermute x1, waiting for transfers between devices, on_device(): lax.ppermute(theirs, ('zh', 'zl'), [(0, 3), (3, 0), (1, 2), (2, 1)])  18.8 us
    ppermute x6, waiting for transfers between devices, ring_blocks(): lax.ppermute(block, axis, way)  15.1 us
    pallas_call x3, Pallas kernels, project(): pl.pallas_call(functools.partial(project_kernel, len(rows)), out_shape=[j...  14.5 us
    all_to_all x1, starting transfers between devices, on_device(): lax.all_to_all(outgoing, DP, 0, 0, tiled=True).reshape(row_count, width)  11.5 us
    ppermute x2, starting transfers between devices, spread(): lax.ppermute(b, axis, DOWN)  7.05 us
    ppermute x2, waiting for transfers between devices, spread(): lax.ppermute(b, axis, UP)  6.78 us
    pallas_call x1, Pallas kernels, attend(): pl.pallas_call(attention_kernel, out_shape=jax.ShapeDtypeStruct((count, G...  6.45 us
  transfers between devices with their start and end apart: 21, of which 13 were waited for; matrix products, arithmetic and copies ran while one was open for 1% of the time, Pallas kernels for 9%

profile of v9, /device:TPU:1, one launch (start us, length us, event | category | flops | bytes accessed | tf_op | source)
XLA Modules:
  0.0 165.9 jit_solution(1504313378202634959)
XLA Ops:
  6.5 0.0 all-gather.2.cloned.1.call-start
  6.5 4.3 %sort_rows.1 = (bf16[256,4096]{1,0:T(8,128)(2,1)}, bf16[128,768]{1,0:T(8,128)(2,1)}, bf16[128,768]{1,0:T(8,128)(2,1)}) custom-call(s32[1]{0:T(128)} %bitcast.1.member_ref, s32[1,128]{1,0:T(1,128)} %placement_ref.1, bf16[256,4096]{1,0:T(8,128)(2,1)} %rows_ref.1, bf16[128,3072]{1,0:T(8,128)(2,1)} %projection_ref.1), custom_call_target="tpu_custom_call" | custom-call | tf_op jit(solution)/shard_map/sort_rows/pallas_call | solution.py:113
  10.8 0.0 all-gather.2.cloned.1.call-update
  10.8 0.0 copy-start.6
  10.9 11.5 %all-to-all-start = ((bf16[32,8,4096]{2,1,0:T(8,128)(2,1)}), bf16[32,8,4096]{2,1,0:T(8,128)(2,1)}, u32[]{:S(2)}, u32[]{:S(2)}) async-start(bf16[32,8,4096]{2,1,0:T(8,128)(2,1)} %bitcast.40), calls=%async_computation | async-start | bytes 4194304 | tf_op jit(solution)/shard_map/all_to_all | solution.py:360
  22.3 0.0 copy-done.6
  22.3 2.9 %collective-permute-start = (bf16[128,768]{1,0:T(8,128)(2,1)S(1)}, bf16[128,768]{1,0:T(8,128)(2,1)S(1)}, u32[]{:S(2)}, u32[]{:S(2)}) collective-permute-start(bf16[128,768]{1,0:T(8,128)(2,1)S(1)} %copy-done.6), channel_id=1, source_target_pairs={{0,6},{6,0},{2,4},{4,2},{1,7},{7,1},{3,5},{5,3},{8,14},{14,8},{10,... | collective-permute-start | bytes 589832 | tf_op jit(solution)/shard_map/ppermute | solution.py:358
  25.2 4.0 %rotary_tables.1 = (f32[1024,128]{1,0:T(8,128)}, f32[1024,128]{1,0:T(8,128)}) custom-call(s32[1,8]{1,0:T(1,128)} %lengths_ref.3, f32[1,128]{1,0:T(1,128)} %constant.207.clone.frequency_ref), custom_call_target="tpu_custom_call" | custom-call | tf_op jit(solution)/shard_map/rotary_tables/pallas_call | solution.py:48
  29.2 18.8 %collective-permute-done = bf16[128,768]{1,0:T(8,128)(2,1)S(1)} collective-permute-done((bf16[128,768]{1,0:T(8,128)(2,1)S(1)}, bf16[128,768]{1,0:T(8,128)(2,1)S(1)}, u32[]{:S(2)}, u32[]{:S(2)}) %collective-permute-start) | collective-permute-done | bytes 196640 | tf_op jit(solution)/shard_map/ppermute | solution.py:358
  48.1 5.7 %all-to-all-done = bf16[32,8,4096]{2,1,0:T(8,128)(2,1)} async-done(((bf16[32,8,4096]{2,1,0:T(8,128)(2,1)}), bf16[32,8,4096]{2,1,0:T(8,128)(2,1)}, u32[]{:S(2)}, u32[]{:S(2)}) %all-to-all-start) | async-done | bytes 2097184 | tf_op jit(solution)/shard_map/all_to_all | solution.py:360
  53.8 2.5 %collective-permute-start.2 = (bf16[256,4096]{1,0:T(8,128)(2,1)}, bf16[256,4096]{1,0:T(8,128)(2,1)}, u32[]{:S(2)}, u32[]{:S(2)}) collective-permute-start(bf16[256,4096]{1,0:T(8,128)(2,1)} %bitcast.3.refs_0_), channel_id=1, source_target_pairs={{0,1},{1,0},{2,3},{3,2},{4,5},{5,4},{6,7},{7,6},{8,9},{9,8},{10,11... | collective-permute-start | bytes 6291464 | tf_op jit(solution)/shard_map/ppermute | solution.py:366
  56.3 0.7 collective-permute-start.1
  57.0 0.1 collective-permute-start.6
  57.1 2.7 %collective-permute-start.7 = (bf16[128,384]{1,0:T(8,128)(2,1)S(1)}, bf16[128,384]{1,0:T(8,128)(2,1)S(1)}, u32[]{:S(2)}, u32[]{:S(2)}) collective-permute-start(bf16[128,384]{1,0:T(8,128)(2,1)S(1)} %get-tuple-element.37), channel_id=1, source_target_pairs={{0,96},{32,0},{64,32},{96,64},{1,97},{33,1},{65,33},{97,65},{2,98}... | collective-permute-start | bytes 294920 | tf_op jit(solution)/shard_map/ppermute | solution.py:164
  59.8 0.0 collective-permute-start.8
  59.8 2.6 %collective-permute-done.6 = bf16[128,384]{1,0:T(8,128)(2,1)S(1)} collective-permute-done((bf16[128,384]{1,0:T(8,128)(2,1)S(1)}, bf16[128,384]{1,0:T(8,128)(2,1)S(1)}, u32[]{:S(2)}, u32[]{:S(2)}) %collective-permute-start.6) | collective-permute-done | bytes 98336 | tf_op jit(solution)/shard_map/ppermute | solution.py:164
  62.4 0.3 collective-permute-start.3
  62.7 3.1 %collective-permute-done.7 = bf16[128,384]{1,0:T(8,128)(2,1)S(1)} collective-permute-done((bf16[128,384]{1,0:T(8,128)(2,1)S(1)}, bf16[128,384]{1,0:T(8,128)(2,1)S(1)}, u32[]{:S(2)}, u32[]{:S(2)}) %collective-permute-start.7) | collective-permute-done | bytes 98336 | tf_op jit(solution)/shard_map/ppermute | solution.py:164
  65.8 0.0 collective-permute-start.4
  65.8 1.8 %collective-permute-done.8 = bf16[128,384]{1,0:T(8,128)(2,1)S(1)} collective-permute-done((bf16[128,384]{1,0:T(8,128)(2,1)S(1)}, bf16[128,384]{1,0:T(8,128)(2,1)S(1)}, u32[]{:S(2)}, u32[]{:S(2)}) %collective-permute-start.8) | collective-permute-done | bytes 98336 | tf_op jit(solution)/shard_map/ppermute | solution.py:164
  67.6 0.0 collective-permute-start.5
  67.6 2.5 %collective-permute-done.3 = bf16[128,384]{1,0:T(8,128)(2,1)S(1)} collective-permute-done((bf16[128,384]{1,0:T(8,128)(2,1)S(1)}, bf16[128,384]{1,0:T(8,128)(2,1)S(1)}, u32[]{:S(2)}, u32[]{:S(2)}) %collective-permute-start.3) | collective-permute-done | bytes 98336 | tf_op jit(solution)/shard_map/ppermute | solution.py:164
  70.1 2.2 %collective-permute-done.4 = bf16[128,384]{1,0:T(8,128)(2,1)S(1)} collective-permute-done((bf16[128,384]{1,0:T(8,128)(2,1)S(1)}, bf16[128,384]{1,0:T(8,128)(2,1)S(1)}, u32[]{:S(2)}, u32[]{:S(2)}) %collective-permute-start.4) | collective-permute-done | bytes 98336 | tf_op jit(solution)/shard_map/ppermute | solution.py:164
  72.3 2.9 %collective-permute-done.5 = bf16[128,384]{1,0:T(8,128)(2,1)S(1)} collective-permute-done((bf16[128,384]{1,0:T(8,128)(2,1)S(1)}, bf16[128,384]{1,0:T(8,128)(2,1)S(1)}, u32[]{:S(2)}, u32[]{:S(2)}) %collective-permute-start.5) | collective-permute-done | bytes 98336 | tf_op jit(solution)/shard_map/ppermute | solution.py:164
  75.3 0.1 collective-permute-start.9
  75.4 2.7 %collective-permute-start.10 = (bf16[512,384]{1,0:T(8,128)(2,1)S(1)}, bf16[512,384]{1,0:T(8,128)(2,1)S(1)}, u32[]{:S(2)}, u32[]{:S(2)}) collective-permute-start(bf16[512,384]{1,0:T(8,128)(2,1)S(1)} %pad_maximum_fusion.refs_3_.refs_2_), channel_id=1, source_target_pairs={{0,96},{32,0},{64,32},{96,64},{1,97},{33,1},{65,33},{97,65},{2,98}... | collective-permute-start | bytes 1179656 | tf_op jit(solution)/shard_map/ppermute | solution.py:171
  78.0 1.9 %collective-permute-start.13 = (bf16[512,384]{1,0:T(8,128)(2,1)S(1)}, bf16[512,384]{1,0:T(8,128)(2,1)S(1)}, u32[]{:S(2)}, u32[]{:S(2)}) collective-permute-start(bf16[512,384]{1,0:T(8,128)(2,1)S(1)} %pad_maximum_fusion.1.refs_8_.refs_7_), channel_id=1, source_target_pairs={{0,8},{8,16},{16,24},{24,0},{1,9},{9,17},{17,25},{25,1},{2,10},{10... | collective-permute-start | bytes 1179656 | tf_op jit(solution)/shard_map/ppermute | solution.py:171
  80.0 6.8 %collective-permute-done.9.refs_4_.refs_3_ = bf16[512,384]{1,0:T(8,128)(2,1)S(1)} collective-permute-done((bf16[512,384]{1,0:T(8,128)(2,1)S(1)}, bf16[512,384]{1,0:T(8,128)(2,1)S(1)}, u32[]{:S(2)}, u32[]{:S(2)}) %collective-permute-start.9) | collective-permute-done | bytes 393248 | tf_op jit(solution)/shard_map/ppermute | solution.py:171
  86.7 4.4 %collective-permute-start.14 = (bf16[512,384]{1,0:T(8,128)(2,1)S(1)}, bf16[512,384]{1,0:T(8,128)(2,1)S(1)}, u32[]{:S(2)}, u32[]{:S(2)}) collective-permute-start(bf16[512,384]{1,0:T(8,128)(2,1)S(1)} %pad_maximum_fusion.1.refs_8_.refs_7_), channel_id=1, source_target_pairs={{0,24},{8,0},{16,8},{24,16},{1,25},{9,1},{17,9},{25,17},{2,26},{10... | collective-permute-start | bytes 1179656 | tf_op jit(solution)/shard_map/ppermute | solution.py:171
  91.1 0.0 collective-permute-done.10.refs_5_.refs_4_
  91.1 0.1 collective-permute-start.11
  91.3 0.0 collective-permute-done.13.refs_9_.refs_8_
  91.3 2.7 %collective-permute-start.12 = (bf16[256,384]{1,0:T(8,128)(2,1)S(1)}, bf16[256,384]{1,0:T(8,128)(2,1)S(1)}, u32[]{:S(2)}, u32[]{:S(2)}) collective-permute-start(bf16[256,384]{1,0:T(8,128)(2,1)S(1)} %slice.25), channel_id=1, source_target_pairs={{0,96},{32,0},{64,32},{96,64},{1,97},{33,1},{65,33},{97,65},{2,98}... | collective-permute-start | bytes 589832 | tf_op jit(solution)/shard_map/ppermute | solution.py:174
  94.0 3.5 %collective-permute-done.14.refs_10_.refs_9_ = bf16[512,384]{1,0:T(8,128)(2,1)S(1)} collective-permute-done((bf16[512,384]{1,0:T(8,128)(2,1)S(1)}, bf16[512,384]{1,0:T(8,128)(2,1)S(1)}, u32[]{:S(2)}, u32[]{:S(2)}) %collective-permute-start.14) | collective-permute-done | bytes 393248 | tf_op jit(solution)/shard_map/ppermute | solution.py:171
  97.6 0.0 collective-permute-start.15
  97.6 0.7 slice.27
  98.3 0.0 collective-permute-done.11.refs_6_.refs_5_
  98.3 3.4 %collective-permute-start.16 = (bf16[256,384]{1,0:T(8,128)(2,1)}, bf16[256,384]{1,0:T(8,128)(2,1)S(1)}, u32[]{:S(2)}, u32[]{:S(2)}) collective-permute-start(bf16[256,384]{1,0:T(8,128)(2,1)} %slice.27), channel_id=1, source_target_pairs={{0,24},{8,0},{16,8},{24,16},{1,25},{9,1},{17,9},{25,17},{2,26},{10... | collective-permute-start | bytes 589832 | tf_op jit(solution)/shard_map/ppermute | solution.py:174
  101.7 0.1 stack.147.places_ref
  101.8 0.0 collective-permute-done.12.refs_7_.refs_6_
  101.8 2.2 %collective-permute-done.15.refs_11_.refs_10_ = bf16[256,384]{1,0:T(8,128)(2,1)S(1)} collective-permute-done((bf16[256,384]{1,0:T(8,128)(2,1)S(1)}, bf16[256,384]{1,0:T(8,128)(2,1)S(1)}, u32[]{:S(2)}, u32[]{:S(2)}) %collective-permute-start.15) | collective-permute-done | bytes 196640 | tf_op jit(solution)/shard_map/ppermute | solution.py:174
  104.0 0.6 collective-permute-done.16.refs_12_.refs_11_
  104.6 0.0 collective-permute-done.2.refs_1_
  104.6 1.9 %copy-done = bf16[2048,768]{1,0:T(8,128)(2,1)S(1)} copy-done((bf16[2048,768]{1,0:T(8,128)(2,1)S(1)}, bf16[2048,768]{1,0:T(8,128)(2,1)}, u32[]{:S(2)}) %copy-start) | copy-done | bytes 3145752
  106.5 7.4 %project.3 = (bf16[256,768]{1,0:T(8,128)(2,1)S(1)}, bf16[256,768]{1,0:T(8,128)(2,1)S(1)}) custom-call(s32[48]{0:T(128)S(1)} %stack.147.places_ref, bf16[256,4096]{1,0:T(8,128)(2,1)} %bitcast.3.refs_0_, bf16[256,4096]{1,0:T(8,128)(2,1)} %collective-permute-done.2.refs_1_, bf16[2048,768]{1,0:T(8,128)(2,1)S(1)} %copy-done, ...), custom_call_target="tpu_custom_call" | custom-call | flops 3221225472 | bytes 10485760 | tf_op jit(solution)/shard_map/project/pallas_call | solution.py:236
  113.9 0.0 collective-permute-done.1.refs_0_
  113.9 3.8 %collective-permute-start.17 = (bf16[256,4096]{1,0:T(8,128)(2,1)}, bf16[256,4096]{1,0:T(8,128)(2,1)S(1)}, u32[]{:S(2)}, u32[]{:S(2)}) collective-permute-start(bf16[256,4096]{1,0:T(8,128)(2,1)} %collective-permute-done.1.refs_0_), channel_id=1, source_target_pairs={{0,1},{1,0},{2,3},{3,2},{4,5},{5,4},{6,7},{7,6},{8,9},{9,8},{10,11... | collective-permute-start | bytes 6291464 | tf_op jit(solution)/shard_map/ppermute | solution.py:369
  117.7 0.0 copy-done.1
  117.7 4.1 %project.4.refs_2_ = bf16[256,768]{1,0:T(8,128)(2,1)S(1)} custom-call(s32[48]{0:T(128)S(1)} %stack.147.places_ref, bf16[256,4096]{1,0:T(8,128)(2,1)} %collective-permute-done.1.refs_0_, bf16[2048,768]{1,0:T(8,128)(2,1)S(1)} %copy-done.1, bf16[512,384]{1,0:T(8,128)(2,1)S(1)} %pad_maximum_fusion.refs_3_.refs_2_, ...), custom_call_target="tpu_custom_call" | custom-call | flops 1610612736 | bytes 8388608 | tf_op jit(solution)/shard_map/project/pallas_call | solution.py:236
  121.8 0.0 copy-start.2
  121.9 0.0 copy-start.3
  121.9 0.0 copy-start.4
  121.9 0.0 collective-permute-done.17.refs_0_
  121.9 3.0 %project.5.refs_3_ = bf16[256,768]{1,0:T(8,128)(2,1)S(1)} custom-call(s32[48]{0:T(128)S(1)} %stack.147.places_ref, bf16[256,4096]{1,0:T(8,128)(2,1)S(1)} %collective-permute-done.17.refs_0_, bf16[2048,768]{1,0:T(8,128)(2,1)S(1)} %copy-done.1, bf16[512,384]{1,0:T(8,128)(2,1)S(1)} %pad_maximum_fusion.refs_3_.refs_2_, ...), custom_call_target="tpu_custom_call" | custom-call | flops 1610612736 | bytes 8388608 | tf_op jit(solution)/shard_map/project/pallas_call | solution.py:236
  124.9 0.0 copy-done.2
  124.9 0.0 copy-done.3
  124.9 0.0 copy-done.4
  124.9 0.0 copy-start.5
  124.9 6.4 %attend.1 = bf16[1024,512]{1,0:T(8,128)(2,1)} custom-call(s32[1]{0:T(128)} %bitcast.1.member_ref, s32[1,8]{1,0:T(1,128)S(1)} %copy-done.4, bf16[256,768]{1,0:T(8,128)(2,1)S(1)} %get-tuple-element.32.refs_0_, bf16[256,768]{1,0:T(8,128)(2,1)S(1)} %get-tuple-element.33.refs_1_, bf16[256,768]{1,0:T(8,128)(2,1)S(1)} %project.4.refs_2_, ...), custom_call_target="tpu_custom_call" | custom-call | tf_op jit(solution)/shard_map/attend/pallas_call | solution.py:331
  131.4 6.1 %all-to-all-start.1 = ((bf16[128,8,512]{2,1,0:T(8,128)(2,1)}), bf16[128,8,512]{2,1,0:T(8,128)(2,1)S(1)}, u32[]{:S(2)}, u32[]{:S(2)}) async-start(bf16[128,8,512]{2,1,0:T(8,128)(2,1)} %bitcast.36), calls=%async_computation.1 | async-start | bytes 2097152 | tf_op jit(solution)/shard_map/all_to_all | solution.py:372
  137.5 0.1 iota_add_fusion
  137.6 0.1 add.358.target_ref
  137.6 19.1 %all-to-all-done.1 = bf16[128,8,512]{2,1,0:T(8,128)(2,1)S(1)} async-done(((bf16[128,8,512]{2,1,0:T(8,128)(2,1)}), bf16[128,8,512]{2,1,0:T(8,128)(2,1)S(1)}, u32[]{:S(2)}, u32[]{:S(2)}) %all-to-all-start.1) | async-done | bytes 1048608 | tf_op jit(solution)/shard_map/all_to_all | solution.py:372
  156.7 2.3 %unsort_rows.1 = bf16[256,2048]{1,0:T(8,128)(2,1)} custom-call(s32[256,1]{1,0:T(8,128)S(1)} %add.358.target_ref, bf16[32,4,8,512]{3,2,1,0:T(8,128)(2,1)S(1)} %bitcast.39), custom_call_target="tpu_custom_call" | custom-call | tf_op jit(solution)/shard_map/unsort_rows/pallas_call | solution.py:148
  (11 shorter events, 0.2 us)
Async XLA Ops:
  6.5 98.1 %all-gather.2.cloned.1.call-start = ((), (), s32[]{:S(2)}) async-start(), calls=%async_computation.2 | async-start | bytes 3342336 | tf_op jit(solution)/shard_map/all_gather | solution.py:357
  10.8 11.5 %copy-start.6 = (bf16[128,768]{1,0:T(8,128)(2,1)S(1)}, bf16[128,768]{1,0:T(8,128)(2,1)}, u32[]{:S(2)}) copy-start(bf16[128,768]{1,0:T(8,128)(2,1)} %get-tuple-element.22) | copy-start | bytes 589828
  10.9 43.0 %all-to-all-start = ((bf16[32,8,4096]{2,1,0:T(8,128)(2,1)}), bf16[32,8,4096]{2,1,0:T(8,128)(2,1)}, u32[]{:S(2)}, u32[]{:S(2)}) async-start(bf16[32,8,4096]{2,1,0:T(8,128)(2,1)} %bitcast.40), calls=%async_computation | async-start | bytes 4194304 | tf_op jit(solution)/shard_map/all_to_all | solution.py:360
  22.3 25.7 %collective-permute-start = (bf16[128,768]{1,0:T(8,128)(2,1)S(1)}, bf16[128,768]{1,0:T(8,128)(2,1)S(1)}, u32[]{:S(2)}, u32[]{:S(2)}) collective-permute-start(bf16[128,768]{1,0:T(8,128)(2,1)S(1)} %copy-done.6), channel_id=1, source_target_pairs={{0,6},{6,0},{2,4},{4,2},{1,7},{7,1},{3,5},{5,3},{8,14},{14,8},{10,... | collective-permute-start | bytes 589832 | tf_op jit(solution)/shard_map/ppermute | solution.py:358
  53.8 50.8 %collective-permute-start.2 = (bf16[256,4096]{1,0:T(8,128)(2,1)}, bf16[256,4096]{1,0:T(8,128)(2,1)}, u32[]{:S(2)}, u32[]{:S(2)}) collective-permute-start(bf16[256,4096]{1,0:T(8,128)(2,1)} %bitcast.3.refs_0_), channel_id=1, source_target_pairs={{0,1},{1,0},{2,3},{3,2},{4,5},{5,4},{6,7},{7,6},{8,9},{9,8},{10,11... | collective-permute-start | bytes 6291464 | tf_op jit(solution)/shard_map/ppermute | solution.py:366
  56.3 57.6 %collective-permute-start.1 = (bf16[256,4096]{1,0:T(8,128)(2,1)}, bf16[256,4096]{1,0:T(8,128)(2,1)}, u32[]{:S(2)}, u32[]{:S(2)}) collective-permute-start(bf16[256,4096]{1,0:T(8,128)(2,1)} %bitcast.3.refs_0_), channel_id=1, source_target_pairs={{0,2},{2,0},{1,3},{3,1},{4,6},{6,4},{5,7},{7,5},{8,10},{10,8},{9,1... | collective-permute-start | bytes 6291464 | tf_op jit(solution)/shard_map/ppermute | solution.py:365
  57.0 5.4 %collective-permute-start.6 = (bf16[128,384]{1,0:T(8,128)(2,1)S(1)}, bf16[128,384]{1,0:T(8,128)(2,1)S(1)}, u32[]{:S(2)}, u32[]{:S(2)}) collective-permute-start(bf16[128,384]{1,0:T(8,128)(2,1)S(1)} %get-tuple-element.37), channel_id=1, source_target_pairs={{0,32},{32,64},{64,96},{96,0},{1,33},{33,65},{65,97},{97,1},{2,34}... | collective-permute-start | bytes 294920 | tf_op jit(solution)/shard_map/ppermute | solution.py:164
  57.1 8.7 %collective-permute-start.7 = (bf16[128,384]{1,0:T(8,128)(2,1)S(1)}, bf16[128,384]{1,0:T(8,128)(2,1)S(1)}, u32[]{:S(2)}, u32[]{:S(2)}) collective-permute-start(bf16[128,384]{1,0:T(8,128)(2,1)S(1)} %get-tuple-element.37), channel_id=1, source_target_pairs={{0,96},{32,0},{64,32},{96,64},{1,97},{33,1},{65,33},{97,65},{2,98}... | collective-permute-start | bytes 294920 | tf_op jit(solution)/shard_map/ppermute | solution.py:164
  59.8 7.8 %collective-permute-start.8 = (bf16[128,384]{1,0:T(8,128)(2,1)S(1)}, bf16[128,384]{1,0:T(8,128)(2,1)S(1)}, u32[]{:S(2)}, u32[]{:S(2)}) collective-permute-start(bf16[128,384]{1,0:T(8,128)(2,1)S(1)} %get-tuple-element.37), channel_id=1, source_target_pairs={{0,64},{32,96},{64,0},{96,32},{1,65},{33,97},{65,1},{97,33},{2,66}... | collective-permute-start | bytes 294920 | tf_op jit(solution)/shard_map/ppermute | solution.py:164
  62.4 7.7 %collective-permute-start.3 = (bf16[128,384]{1,0:T(8,128)(2,1)S(1)}, bf16[128,384]{1,0:T(8,128)(2,1)S(1)}, u32[]{:S(2)}, u32[]{:S(2)}) collective-permute-start(bf16[128,384]{1,0:T(8,128)(2,1)S(1)} %get-tuple-element.38), channel_id=1, source_target_pairs={{0,8},{8,16},{16,24},{24,0},{1,9},{9,17},{17,25},{25,1},{2,10},{10... | collective-permute-start | bytes 294920 | tf_op jit(solution)/shard_map/ppermute | solution.py:164
  65.8 6.5 %collective-permute-start.4 = (bf16[128,384]{1,0:T(8,128)(2,1)S(1)}, bf16[128,384]{1,0:T(8,128)(2,1)S(1)}, u32[]{:S(2)}, u32[]{:S(2)}) collective-permute-start(bf16[128,384]{1,0:T(8,128)(2,1)S(1)} %get-tuple-element.38), channel_id=1, source_target_pairs={{0,24},{8,0},{16,8},{24,16},{1,25},{9,1},{17,9},{25,17},{2,26},{10... | collective-permute-start | bytes 294920 | tf_op jit(solution)/shard_map/ppermute | solution.py:164
  67.6 7.7 %collective-permute-start.5 = (bf16[128,384]{1,0:T(8,128)(2,1)S(1)}, bf16[128,384]{1,0:T(8,128)(2,1)S(1)}, u32[]{:S(2)}, u32[]{:S(2)}) collective-permute-start(bf16[128,384]{1,0:T(8,128)(2,1)S(1)} %get-tuple-element.38), channel_id=1, source_target_pairs={{0,16},{8,24},{16,0},{24,8},{1,17},{9,25},{17,1},{25,9},{2,18},{10... | collective-permute-start | bytes 294920 | tf_op jit(solution)/shard_map/ppermute | solution.py:164
  75.3 11.4 %collective-permute-start.9 = (bf16[512,384]{1,0:T(8,128)(2,1)S(1)}, bf16[512,384]{1,0:T(8,128)(2,1)S(1)}, u32[]{:S(2)}, u32[]{:S(2)}) collective-permute-start(bf16[512,384]{1,0:T(8,128)(2,1)S(1)} %pad_maximum_fusion.refs_3_.refs_2_), channel_id=1, source_target_pairs={{0,32},{32,64},{64,96},{96,0},{1,33},{33,65},{65,97},{97,1},{2,34}... | collective-permute-start | bytes 1179656 | tf_op jit(solution)/shard_map/ppermute | solution.py:171
  75.4 15.8 %collective-permute-start.10 = (bf16[512,384]{1,0:T(8,128)(2,1)S(1)}, bf16[512,384]{1,0:T(8,128)(2,1)S(1)}, u32[]{:S(2)}, u32[]{:S(2)}) collective-permute-start(bf16[512,384]{1,0:T(8,128)(2,1)S(1)} %pad_maximum_fusion.refs_3_.refs_2_), channel_id=1, source_target_pairs={{0,96},{32,0},{64,32},{96,64},{1,97},{33,1},{65,33},{97,65},{2,98}... | collective-permute-start | bytes 1179656 | tf_op jit(solution)/shard_map/ppermute | solution.py:171
  78.0 13.2 %collective-permute-start.13 = (bf16[512,384]{1,0:T(8,128)(2,1)S(1)}, bf16[512,384]{1,0:T(8,128)(2,1)S(1)}, u32[]{:S(2)}, u32[]{:S(2)}) collective-permute-start(bf16[512,384]{1,0:T(8,128)(2,1)S(1)} %pad_maximum_fusion.1.refs_8_.refs_7_), channel_id=1, source_target_pairs={{0,8},{8,16},{16,24},{24,0},{1,9},{9,17},{17,25},{25,1},{2,10},{10... | collective-permute-start | bytes 1179656 | tf_op jit(solution)/shard_map/ppermute | solution.py:171
  86.7 10.8 %collective-permute-start.14 = (bf16[512,384]{1,0:T(8,128)(2,1)S(1)}, bf16[512,384]{1,0:T(8,128)(2,1)S(1)}, u32[]{:S(2)}, u32[]{:S(2)}) collective-permute-start(bf16[512,384]{1,0:T(8,128)(2,1)S(1)} %pad_maximum_fusion.1.refs_8_.refs_7_), channel_id=1, source_target_pairs={{0,24},{8,0},{16,8},{24,16},{1,25},{9,1},{17,9},{25,17},{2,26},{10... | collective-permute-start | bytes 1179656 | tf_op jit(solution)/shard_map/ppermute | solution.py:171
  91.1 7.1 %collective-permute-start.11 = (bf16[256,384]{1,0:T(8,128)(2,1)S(1)}, bf16[256,384]{1,0:T(8,128)(2,1)S(1)}, u32[]{:S(2)}, u32[]{:S(2)}) collective-permute-start(bf16[256,384]{1,0:T(8,128)(2,1)S(1)} %slice.24), channel_id=1, source_target_pairs={{0,32},{32,64},{64,96},{96,0},{1,33},{33,65},{65,97},{97,1},{2,34}... | collective-permute-start | bytes 589832 | tf_op jit(solution)/shard_map/ppermute | solution.py:174
  91.3 10.6 %collective-permute-start.12 = (bf16[256,384]{1,0:T(8,128)(2,1)S(1)}, bf16[256,384]{1,0:T(8,128)(2,1)S(1)}, u32[]{:S(2)}, u32[]{:S(2)}) collective-permute-start(bf16[256,384]{1,0:T(8,128)(2,1)S(1)} %slice.25), channel_id=1, source_target_pairs={{0,96},{32,0},{64,32},{96,64},{1,97},{33,1},{65,33},{97,65},{2,98}... | collective-permute-start | bytes 589832 | tf_op jit(solution)/shard_map/ppermute | solution.py:174
  97.6 6.5 %collective-permute-start.15 = (bf16[256,384]{1,0:T(8,128)(2,1)S(1)}, bf16[256,384]{1,0:T(8,128)(2,1)S(1)}, u32[]{:S(2)}, u32[]{:S(2)}) collective-permute-start(bf16[256,384]{1,0:T(8,128)(2,1)S(1)} %slice.26), channel_id=1, source_target_pairs={{0,8},{8,16},{16,24},{24,0},{1,9},{9,17},{17,25},{25,1},{2,10},{10... | collective-permute-start | bytes 589832 | tf_op jit(solution)/shard_map/ppermute | solution.py:174
  98.3 6.3 %collective-permute-start.16 = (bf16[256,384]{1,0:T(8,128)(2,1)}, bf16[256,384]{1,0:T(8,128)(2,1)S(1)}, u32[]{:S(2)}, u32[]{:S(2)}) collective-permute-start(bf16[256,384]{1,0:T(8,128)(2,1)} %slice.27), channel_id=1, source_target_pairs={{0,24},{8,0},{16,8},{24,16},{1,25},{9,1},{17,9},{25,17},{2,26},{10... | collective-permute-start | bytes 589832 | tf_op jit(solution)/shard_map/ppermute | solution.py:174
  104.6 1.9 %copy-start = (bf16[2048,768]{1,0:T(8,128)(2,1)S(1)}, bf16[2048,768]{1,0:T(8,128)(2,1)}, u32[]{:S(2)}) copy-start(bf16[2048,768]{1,0:T(8,128)(2,1)} %all-gather.2.cloned.1.call-done.refs_2_.refs_1_) | copy-start | bytes 9437188
  106.5 11.2 %copy-start.1 = (bf16[2048,768]{1,0:T(8,128)(2,1)S(1)}, bf16[2048,768]{1,0:T(8,128)(2,1)}, u32[]{:S(2)}) copy-start(bf16[2048,768]{1,0:T(8,128)(2,1)} %all-gather.2.cloned.1.call-done.refs_2_.refs_1_) | copy-start | bytes 9437188
  113.9 8.0 %collective-permute-start.17 = (bf16[256,4096]{1,0:T(8,128)(2,1)}, bf16[256,4096]{1,0:T(8,128)(2,1)S(1)}, u32[]{:S(2)}, u32[]{:S(2)}) collective-permute-start(bf16[256,4096]{1,0:T(8,128)(2,1)} %collective-permute-done.1.refs_0_), channel_id=1, source_target_pairs={{0,1},{1,0},{2,3},{3,2},{4,5},{5,4},{6,7},{7,6},{8,9},{9,8},{10,11... | collective-permute-start | bytes 6291464 | tf_op jit(solution)/shard_map/ppermute | solution.py:369
  121.8 3.0 %copy-start.2 = (f32[1024,128]{1,0:T(8,128)S(1)}, f32[1024,128]{1,0:T(8,128)}, u32[]{:S(2)}) copy-start(f32[1024,128]{1,0:T(8,128)} %get-tuple-element.35.refs_4_) | copy-start | bytes 1572868
  121.9 3.0 %copy-start.3 = (f32[1024,128]{1,0:T(8,128)S(1)}, f32[1024,128]{1,0:T(8,128)}, u32[]{:S(2)}) copy-start(f32[1024,128]{1,0:T(8,128)} %get-tuple-element.36.refs_5_) | copy-start | bytes 1572868
  121.9 3.0 %copy-start.4 = (s32[1,8]{1,0:T(1,128)S(1)}, s32[1,8]{1,0:T(1,128)}, u32[]{:S(2)}) copy-start(s32[1,8]{1,0:T(1,128)} %lengths_ref.3) | copy-start | bytes 100
  124.9 12.5 %copy-start.5 = (s32[1,128]{1,0:T(1,128)S(1)}, s32[1,128]{1,0:T(1,128)}, u32[]{:S(2)}) copy-start(s32[1,128]{1,0:T(1,128)} %placement_ref.1) | copy-start | bytes 1540
  131.4 25.4 %all-to-all-start.1 = ((bf16[128,8,512]{2,1,0:T(8,128)(2,1)}), bf16[128,8,512]{2,1,0:T(8,128)(2,1)S(1)}, u32[]{:S(2)}, u32[]{:S(2)}) async-start(bf16[128,8,512]{2,1,0:T(8,128)(2,1)} %bitcast.36), calls=%async_computation.1 | async-start | bytes 2097152 | tf_op jit(solution)/shard_map/all_to_all | solution.py:372
Sparse Core Ops, SparseCore 0:
  11.0 70.5 all-gather.1

commit v10 on v9

--- a/solution.py
+++ b/solution.py
@@ -60,9 +60,13 @@
     count, devices = held.shape[0], placement_ref.shape[1]
     piece = count // devices
     arriving, leaving = [], []
-    for i in range(8):
-        rows = pl.ds(i * (count // 8), count // 8)
-        arriving.append(pltpu.make_async_copy(rows_ref.at[rows], held.at[rows], in_sems.at[i]))
+    parts = [
+        (pl.ds(half * (count // 2), count // 2), pl.ds(block * (held.shape[1] // 4), held.shape[1] // 4))
+        for block in range(4)
+        for half in range(2)
+    ]
+    for i, part in enumerate(parts):
+        arriving.append(pltpu.make_async_copy(rows_ref.at[part], held.at[part], in_sems.at[i]))
         arriving[-1].start()
     taking = []
     for i, member in enumerate((member_ref[0], member_ref[0] ^ 2)):
@@ -94,14 +98,15 @@
     for i, out in enumerate((mine_ref, theirs_ref)):
         leaving.append(pltpu.make_async_copy(columns.at[i], out, head_sems.at[i]))
         leaving[-1].start()
-    for copy in arriving:
-        copy.wait()
-    for i in range(2):
-        half = slice(i * (count // 2), (i + 1) * (count // 2))
-        moved[half] = jnp.dot(one_hot[half], held[...], preferred_element_type=jnp.float32).astype(jnp.bfloat16)
-        for j in range(4):
-            rows = pl.ds((i * 4 + j) * (count // 8), count // 8)
-            leaving.append(pltpu.make_async_copy(moved.at[rows], out_ref.at[rows], out_sems.at[i * 4 + j]))
+    for block in range(4):
+        columns_here = parts[2 * block][1]
+        for copy in arriving[2 * block : 2 * block + 2]:
+            copy.wait()
+        moved[:, columns_here] = jnp.dot(
+            one_hot, held[:, columns_here], preferred_element_type=jnp.float32
+        ).astype(jnp.bfloat16)
+        for i in (2 * block, 2 * block + 1):
+            leaving.append(pltpu.make_async_copy(moved.at[parts[i]], out_ref.at[parts[i]], out_sems.at[i]))
             leaving[-1].start()
     for copy in leaving:
         copy.wait()
@@ -364,10 +369,10 @@
     across = [(0, 1), (1, 0)]
     far = lax.ppermute(arrived, "zl", across)
     near = lax.ppermute(arrived, "core", across)
-    lanes = project(places, pieces, [arrived, near])
+    lanes = project(places, pieces, [arrived])
     far, lanes = lax.optimization_barrier((far, lanes))
     last = lax.ppermute(far, "core", across)
-    lanes = lanes + project(places, pieces, [far]) + project(places, pieces, [last])
+    lanes = lanes + project(places, pieces, [near, far]) + project(places, pieces, [last])
     mixed = attend(member.reshape(1), doc_lengths, lanes, *tables)
     returned = lax.all_to_all(
         mixed.reshape(devices, members * piece, GROUP * HEAD_DIM), EVERY, 0, 0, tiled=True

time: 166 us -> 156 us (0.940)
  waiting for transfers between devices: 71.9 us -> 65.2 us
  starting transfers between devices: 45.7 us -> 42.4 us
    ppermute x6, waiting for transfers between devices: 15.1 us -> 6.68 us  [ring_blocks(): lax.ppermute(block, axis, way)]
    ppermute x2, waiting for transfers between devices: 3.55 us -> 11.7 us  [spread(): lax.ppermute(b, axis, DOWN)]
    ppermute x2, waiting for transfers between devices: 6.78 us -> 0.01 us  [spread(): lax.ppermute(b, axis, UP)]
    ppermute x6, starting transfers between devices: 3.04 us -> 6.91 us  [ring_blocks(): lax.ppermute(block, axis, way)]
    ppermute x2, starting transfers between devices: 7.05 us -> 3.66 us  [spread(): lax.ppermute(b, axis, DOWN)]
    ppermute x4, starting transfers between devices: 6.22 us -> 4.28 us  [spread(): lax.ppermute(h, axis, way)]
  transfers between devices with their start and end apart: 21 -> 21, of which waited for: 13 -> 9; matrix products, arithmetic and copies ran while one was open for 1% -> 1% of each run, Pallas kernels for 9% -> 10%
where the time goes in v10:
time: 156 us
  waiting for transfers between devices  65.2 us (42%)
  starting transfers between devices  42.4 us (27%)
  Pallas kernels  31.7 us (20%)
  between operations  13.6 us (9%)
  local copies, waits for them, and re-layouts  2.91 us (2%)
    all_to_all x1, waiting for transfers between devices, on_device(): lax.all_to_all(mixed.reshape(devices, members * piece, GROUP * HEAD_DIM),...  19.1 us
    ppermute x1, waiting for transfers between devices, on_device(): lax.ppermute(theirs, ('zh', 'zl'), [(0, 3), (3, 0), (1, 2), (2, 1)])  18.8 us
    pallas_call x3, Pallas kernels, project(): pl.pallas_call(functools.partial(project_kernel, len(rows)), out_shape=[j...  14.5 us
    ppermute x2, waiting for transfers between devices, spread(): lax.ppermute(b, axis, DOWN)  11.7 us
    all_to_all x1, starting transfers between devices, on_device(): lax.all_to_all(outgoing, DP, 0, 0, tiled=True).reshape(row_count, width)  11.5 us
    ppermute x6, starting transfers between devices, ring_blocks(): lax.ppermute(block, axis, way)  6.91 us
    ppermute x6, waiting for transfers between devices, ring_blocks(): lax.ppermute(block, axis, way)  6.68 us
    pallas_call x1, Pallas kernels, attend(): pl.pallas_call(attention_kernel, out_shape=jax.ShapeDtypeStruct((count, G...  6.45 us
  transfers between devices with their start and end apart: 21, of which 9 were waited for; matrix products, arithmetic and copies ran while one was open for 1% of the time, Pallas kernels for 10%

profile of v10, /device:TPU:1, one launch (start us, length us, event | category | flops | bytes accessed | tf_op | source)
XLA Modules:
  0.0 156.0 jit_solution(7353217874861791825)
XLA Ops:
  6.5 0.0 all-gather.2.cloned.1.call-start
  6.5 4.5 %sort_rows.1 = (bf16[256,4096]{1,0:T(8,128)(2,1)}, bf16[128,768]{1,0:T(8,128)(2,1)}, bf16[128,768]{1,0:T(8,128)(2,1)}) custom-call(s32[1]{0:T(128)} %bitcast.1.member_ref, s32[1,128]{1,0:T(1,128)} %placement_ref.1, bf16[256,4096]{1,0:T(8,128)(2,1)} %rows_ref.1, bf16[128,3072]{1,0:T(8,128)(2,1)} %projection_ref.1), custom_call_target="tpu_custom_call" | custom-call | tf_op jit(solution)/shard_map/sort_rows/pallas_call | solution.py:118
  11.0 0.0 all-gather.2.cloned.1.call-update
  11.0 0.0 copy-start.6
  11.0 11.5 %all-to-all-start = ((bf16[32,8,4096]{2,1,0:T(8,128)(2,1)}), bf16[32,8,4096]{2,1,0:T(8,128)(2,1)}, u32[]{:S(2)}, u32[]{:S(2)}) async-start(bf16[32,8,4096]{2,1,0:T(8,128)(2,1)} %bitcast.40), calls=%async_computation | async-start | bytes 4194304 | tf_op jit(solution)/shard_map/all_to_all | solution.py:365
  22.5 0.0 copy-done.6
  22.5 2.9 %collective-permute-start = (bf16[128,768]{1,0:T(8,128)(2,1)S(1)}, bf16[128,768]{1,0:T(8,128)(2,1)S(1)}, u32[]{:S(2)}, u32[]{:S(2)}) collective-permute-start(bf16[128,768]{1,0:T(8,128)(2,1)S(1)} %copy-done.6), channel_id=1, source_target_pairs={{0,6},{6,0},{2,4},{4,2},{1,7},{7,1},{3,5},{5,3},{8,14},{14,8},{10,... | collective-permute-start | bytes 589832 | tf_op jit(solution)/shard_map/ppermute | solution.py:363
  25.4 4.0 %rotary_tables.1 = (f32[1024,128]{1,0:T(8,128)}, f32[1024,128]{1,0:T(8,128)}) custom-call(s32[1,8]{1,0:T(1,128)} %lengths_ref.3, f32[1,128]{1,0:T(1,128)} %constant.207.clone.frequency_ref), custom_call_target="tpu_custom_call" | custom-call | tf_op jit(solution)/shard_map/rotary_tables/pallas_call | solution.py:48
  29.4 18.8 %collective-permute-done = bf16[128,768]{1,0:T(8,128)(2,1)S(1)} collective-permute-done((bf16[128,768]{1,0:T(8,128)(2,1)S(1)}, bf16[128,768]{1,0:T(8,128)(2,1)S(1)}, u32[]{:S(2)}, u32[]{:S(2)}) %collective-permute-start) | collective-permute-done | bytes 196640 | tf_op jit(solution)/shard_map/ppermute | solution.py:363
  48.2 5.6 %all-to-all-done = bf16[32,8,4096]{2,1,0:T(8,128)(2,1)} async-done(((bf16[32,8,4096]{2,1,0:T(8,128)(2,1)}), bf16[32,8,4096]{2,1,0:T(8,128)(2,1)}, u32[]{:S(2)}, u32[]{:S(2)}) %all-to-all-start) | async-done | bytes 2097184 | tf_op jit(solution)/shard_map/all_to_all | solution.py:365
  53.9 0.6 collective-permute-start.1
  54.5 0.8 collective-permute-start.7
  55.3 0.5 collective-permute-start.6
  55.8 0.9 collective-permute-start.5
  56.8 3.2 %collective-permute-start.4 = (bf16[128,384]{1,0:T(8,128)(2,1)S(1)}, bf16[128,384]{1,0:T(8,128)(2,1)S(1)}, u32[]{:S(2)}, u32[]{:S(2)}) collective-permute-start(bf16[128,384]{1,0:T(8,128)(2,1)S(1)} %get-tuple-element.36), channel_id=1, source_target_pairs={{0,16},{8,24},{16,0},{24,8},{1,17},{9,25},{17,1},{25,9},{2,18},{10... | collective-permute-start | bytes 294920 | tf_op jit(solution)/shard_map/ppermute | solution.py:169
  60.0 0.0 collective-permute-done.7
  60.0 0.6 collective-permute-start.3
  60.6 0.0 collective-permute-done.6
  60.6 0.9 collective-permute-start.2
  61.5 0.0 collective-permute-done.5
  61.5 2.1 %collective-permute-done.4 = bf16[128,384]{1,0:T(8,128)(2,1)S(1)} collective-permute-done((bf16[128,384]{1,0:T(8,128)(2,1)S(1)}, bf16[128,384]{1,0:T(8,128)(2,1)S(1)}, u32[]{:S(2)}, u32[]{:S(2)}) %collective-permute-start.4) | collective-permute-done | bytes 98336 | tf_op jit(solution)/shard_map/ppermute | solution.py:169
  63.6 4.4 %collective-permute-done.3 = bf16[128,384]{1,0:T(8,128)(2,1)S(1)} collective-permute-done((bf16[128,384]{1,0:T(8,128)(2,1)S(1)}, bf16[128,384]{1,0:T(8,128)(2,1)S(1)}, u32[]{:S(2)}, u32[]{:S(2)}) %collective-permute-start.3) | collective-permute-done | bytes 98336 | tf_op jit(solution)/shard_map/ppermute | solution.py:169
  67.9 0.2 collective-permute-done.2
  68.2 3.1 %collective-permute-start.9 = (bf16[512,384]{1,0:T(8,128)(2,1)S(1)}, bf16[512,384]{1,0:T(8,128)(2,1)S(1)}, u32[]{:S(2)}, u32[]{:S(2)}) collective-permute-start(bf16[512,384]{1,0:T(8,128)(2,1)S(1)} %pad_maximum_fusion.refs_2_.refs_3_), channel_id=1, source_target_pairs={{0,96},{32,0},{64,32},{96,64},{1,97},{33,1},{65,33},{97,65},{2,98}... | collective-permute-start | bytes 1179656 | tf_op jit(solution)/shard_map/ppermute | solution.py:176
  71.4 0.0 collective-permute-start.8
  71.4 0.5 collective-permute-start.13
  71.9 0.9 collective-permute-start.12
  72.8 11.7 %collective-permute-done.9.refs_4_.refs_5_ = bf16[512,384]{1,0:T(8,128)(2,1)S(1)} collective-permute-done((bf16[512,384]{1,0:T(8,128)(2,1)S(1)}, bf16[512,384]{1,0:T(8,128)(2,1)S(1)}, u32[]{:S(2)}, u32[]{:S(2)}) %collective-permute-start.9) | collective-permute-done | bytes 393248 | tf_op jit(solution)/shard_map/ppermute | solution.py:176
  84.5 2.3 %collective-permute-start.11 = (bf16[256,384]{1,0:T(8,128)(2,1)S(1)}, bf16[256,384]{1,0:T(8,128)(2,1)S(1)}, u32[]{:S(2)}, u32[]{:S(2)}) collective-permute-start(bf16[256,384]{1,0:T(8,128)(2,1)S(1)} %slice.25), channel_id=1, source_target_pairs={{0,96},{32,0},{64,32},{96,64},{1,97},{33,1},{65,33},{97,65},{2,98}... | collective-permute-start | bytes 589832 | tf_op jit(solution)/shard_map/ppermute | solution.py:179
  86.8 0.0 collective-permute-done.8.refs_3_.refs_4_
  86.9 0.1 collective-permute-start.10
  86.9 0.0 collective-permute-done.13.refs_9_.refs_10_
  87.0 1.9 %collective-permute-start.15 = (bf16[256,384]{1,0:T(8,128)(2,1)S(1)}, bf16[256,384]{1,0:T(8,128)(2,1)S(1)}, u32[]{:S(2)}, u32[]{:S(2)}) collective-permute-start(bf16[256,384]{1,0:T(8,128)(2,1)S(1)} %slice.27), channel_id=1, source_target_pairs={{0,24},{8,0},{16,8},{24,16},{1,25},{9,1},{17,9},{25,17},{2,26},{10... | collective-permute-start | bytes 589832 | tf_op jit(solution)/shard_map/ppermute | solution.py:179
  88.9 0.0 collective-permute-done.12.refs_8_.refs_9_
  88.9 0.7 slice.26
  89.6 0.0 collective-permute-start.14
  89.6 0.0 collective-permute-done.11.refs_6_.refs_7_
  89.6 2.8 %collective-permute-start.16 = (bf16[256,4096]{1,0:T(8,128)(2,1)}, bf16[256,4096]{1,0:T(8,128)(2,1)}, u32[]{:S(2)}, u32[]{:S(2)}) collective-permute-start(bf16[256,4096]{1,0:T(8,128)(2,1)} %bitcast.3.refs_0_), channel_id=1, source_target_pairs={{0,1},{1,0},{2,3},{3,2},{4,5},{5,4},{6,7},{7,6},{8,9},{9,8},{10,11... | collective-permute-start | bytes 6291464 | tf_op jit(solution)/shard_map/ppermute | solution.py:371
  92.4 0.1 stack.147.places_ref
  92.5 0.1 collective-permute-done.10.refs_5_.refs_6_
  92.7 0.0 collective-permute-done.15.refs_11_.refs_12_
  92.7 3.1 %collective-permute-done.14.refs_10_.refs_11_ = bf16[256,384]{1,0:T(8,128)(2,1)S(1)} collective-permute-done((bf16[256,384]{1,0:T(8,128)(2,1)}, bf16[256,384]{1,0:T(8,128)(2,1)S(1)}, u32[]{:S(2)}, u32[]{:S(2)}) %collective-permute-start.14) | collective-permute-done | bytes 196640 | tf_op jit(solution)/shard_map/ppermute | solution.py:179
  95.8 1.9 %copy-done = bf16[2048,768]{1,0:T(8,128)(2,1)S(1)} copy-done((bf16[2048,768]{1,0:T(8,128)(2,1)S(1)}, bf16[2048,768]{1,0:T(8,128)(2,1)}, u32[]{:S(2)}) %copy-start) | copy-done | bytes 3145752
  97.7 4.3 %project.3.refs_0_ = bf16[256,768]{1,0:T(8,128)(2,1)S(1)} custom-call(s32[48]{0:T(128)S(1)} %stack.147.places_ref, bf16[256,4096]{1,0:T(8,128)(2,1)} %bitcast.3.refs_0_, bf16[2048,768]{1,0:T(8,128)(2,1)S(1)} %copy-done, bf16[512,384]{1,0:T(8,128)(2,1)S(1)} %pad_maximum_fusion.refs_2_.refs_3_, bf16[512,384]{1,0:T(8,128)(2,1)S(1)} %collective-permute-done.8.refs_3_.refs_4_, ...), custom_call_target="tpu_custom_call" | custom-call | flops 1610612736 | bytes 8388608 | tf_op jit(solution)/shard_map/project/pallas_call | solution.py:241
  102.0 0.0 collective-permute-done.1.refs_1_
  102.0 3.4 %collective-permute-start.17 = (bf16[256,4096]{1,0:T(8,128)(2,1)}, bf16[256,4096]{1,0:T(8,128)(2,1)S(1)}, u32[]{:S(2)}, u32[]{:S(2)}) collective-permute-start(bf16[256,4096]{1,0:T(8,128)(2,1)} %collective-permute-done.1.refs_1_), channel_id=1, source_target_pairs={{0,1},{1,0},{2,3},{3,2},{4,5},{5,4},{6,7},{7,6},{8,9},{9,8},{10,11... | collective-permute-start | bytes 6291464 | tf_op jit(solution)/shard_map/ppermute | solution.py:374
  105.4 0.0 collective-permute-done.16.refs_0_
  105.4 0.0 copy-done.1
  105.4 7.2 %project.4 = (bf16[256,768]{1,0:T(8,128)(2,1)S(1)}, bf16[256,768]{1,0:T(8,128)(2,1)S(1)}) custom-call(s32[48]{0:T(128)S(1)} %stack.147.places_ref, bf16[256,4096]{1,0:T(8,128)(2,1)} %collective-permute-done.16.refs_0_, bf16[256,4096]{1,0:T(8,128)(2,1)} %collective-permute-done.1.refs_1_, bf16[2048,768]{1,0:T(8,128)(2,1)S(1)} %copy-done.1, ...), custom_call_target="tpu_custom_call" | custom-call | flops 3221225472 | bytes 10485760 | tf_op jit(solution)/shard_map/project/pallas_call | solution.py:241
  112.7 0.0 copy-start.2
  112.7 0.0 copy-start.3
  112.7 0.0 copy-start.4
  112.7 0.0 collective-permute-done.17.refs_0_
  112.7 3.0 %project.5.refs_3_ = bf16[256,768]{1,0:T(8,128)(2,1)S(1)} custom-call(s32[48]{0:T(128)S(1)} %stack.147.places_ref, bf16[256,4096]{1,0:T(8,128)(2,1)S(1)} %collective-permute-done.17.refs_0_, bf16[2048,768]{1,0:T(8,128)(2,1)S(1)} %copy-done.1, bf16[512,384]{1,0:T(8,128)(2,1)S(1)} %pad_maximum_fusion.refs_2_.refs_3_, ...), custom_call_target="tpu_custom_call" | custom-call | flops 1610612736 | bytes 8388608 | tf_op jit(solution)/shard_map/project/pallas_call | solution.py:241
  115.7 0.0 copy-done.2
  115.7 0.0 copy-done.3
  115.7 0.0 copy-start.5
  115.7 6.5 %attend.1 = bf16[1024,512]{1,0:T(8,128)(2,1)} custom-call(s32[1]{0:T(128)} %bitcast.1.member_ref, s32[1,8]{1,0:T(1,128)S(1)} %copy-done.4, bf16[256,768]{1,0:T(8,128)(2,1)S(1)} %project.3.refs_0_, bf16[256,768]{1,0:T(8,128)(2,1)S(1)} %get-tuple-element.31.refs_1_, bf16[256,768]{1,0:T(8,128)(2,1)S(1)} %get-tuple-element.32.refs_2_, ...), custom_call_target="tpu_custom_call" | custom-call | tf_op jit(solution)/shard_map/attend/pallas_call | solution.py:336
  122.2 5.4 %all-to-all-start.1 = ((bf16[128,8,512]{2,1,0:T(8,128)(2,1)}), bf16[128,8,512]{2,1,0:T(8,128)(2,1)S(1)}, u32[]{:S(2)}, u32[]{:S(2)}) async-start(bf16[128,8,512]{2,1,0:T(8,128)(2,1)} %bitcast.36), calls=%async_computation.1 | async-start | bytes 2097152 | tf_op jit(solution)/shard_map/all_to_all | solution.py:377
  127.6 0.0 copy-done.5
  127.6 0.1 iota_add_fusion
  127.7 0.1 add.358.target_ref
  127.8 19.1 %all-to-all-done.1 = bf16[128,8,512]{2,1,0:T(8,128)(2,1)S(1)} async-done(((bf16[128,8,512]{2,1,0:T(8,128)(2,1)}), bf16[128,8,512]{2,1,0:T(8,128)(2,1)S(1)}, u32[]{:S(2)}, u32[]{:S(2)}) %all-to-all-start.1) | async-done | bytes 1048608 | tf_op jit(solution)/shard_map/all_to_all | solution.py:377
  146.9 2.3 %unsort_rows.1 = bf16[256,2048]{1,0:T(8,128)(2,1)} custom-call(s32[256,1]{1,0:T(8,128)S(1)} %add.358.target_ref, bf16[32,4,8,512]{3,2,1,0:T(8,128)(2,1)S(1)} %bitcast.39), custom_call_target="tpu_custom_call" | custom-call | tf_op jit(solution)/shard_map/unsort_rows/pallas_call | solution.py:153
  (11 shorter events, 0.2 us)
Async XLA Ops:
  6.5 89.3 %all-gather.2.cloned.1.call-start = ((), (), s32[]{:S(2)}) async-start(), calls=%async_computation.2 | async-start | bytes 3342336 | tf_op jit(solution)/shard_map/all_gather | solution.py:362
  11.0 11.5 %copy-start.6 = (bf16[128,768]{1,0:T(8,128)(2,1)S(1)}, bf16[128,768]{1,0:T(8,128)(2,1)}, u32[]{:S(2)}) copy-start(bf16[128,768]{1,0:T(8,128)(2,1)} %get-tuple-element.21) | copy-start | bytes 589828
  11.0 42.9 %all-to-all-start = ((bf16[32,8,4096]{2,1,0:T(8,128)(2,1)}), bf16[32,8,4096]{2,1,0:T(8,128)(2,1)}, u32[]{:S(2)}, u32[]{:S(2)}) async-start(bf16[32,8,4096]{2,1,0:T(8,128)(2,1)} %bitcast.40), calls=%async_computation | async-start | bytes 4194304 | tf_op jit(solution)/shard_map/all_to_all | solution.py:365
  22.5 25.7 %collective-permute-start = (bf16[128,768]{1,0:T(8,128)(2,1)S(1)}, bf16[128,768]{1,0:T(8,128)(2,1)S(1)}, u32[]{:S(2)}, u32[]{:S(2)}) collective-permute-start(bf16[128,768]{1,0:T(8,128)(2,1)S(1)} %copy-done.6), channel_id=1, source_target_pairs={{0,6},{6,0},{2,4},{4,2},{1,7},{7,1},{3,5},{5,3},{8,14},{14,8},{10,... | collective-permute-start | bytes 589832 | tf_op jit(solution)/shard_map/ppermute | solution.py:363
  53.9 48.1 %collective-permute-start.1 = (bf16[256,4096]{1,0:T(8,128)(2,1)}, bf16[256,4096]{1,0:T(8,128)(2,1)}, u32[]{:S(2)}, u32[]{:S(2)}) collective-permute-start(bf16[256,4096]{1,0:T(8,128)(2,1)} %bitcast.3.refs_0_), channel_id=1, source_target_pairs={{0,2},{2,0},{1,3},{3,1},{4,6},{6,4},{5,7},{7,5},{8,10},{10,8},{9,1... | collective-permute-start | bytes 6291464 | tf_op jit(solution)/shard_map/ppermute | solution.py:370
  54.5 5.4 %collective-permute-start.7 = (bf16[128,384]{1,0:T(8,128)(2,1)S(1)}, bf16[128,384]{1,0:T(8,128)(2,1)S(1)}, u32[]{:S(2)}, u32[]{:S(2)}) collective-permute-start(bf16[128,384]{1,0:T(8,128)(2,1)S(1)} %get-tuple-element.35), channel_id=1, source_target_pairs={{0,64},{32,96},{64,0},{96,32},{1,65},{33,97},{65,1},{97,33},{2,66}... | collective-permute-start | bytes 294920 | tf_op jit(solution)/shard_map/ppermute | solution.py:169
  55.3 5.3 %collective-permute-start.6 = (bf16[128,384]{1,0:T(8,128)(2,1)S(1)}, bf16[128,384]{1,0:T(8,128)(2,1)S(1)}, u32[]{:S(2)}, u32[]{:S(2)}) collective-permute-start(bf16[128,384]{1,0:T(8,128)(2,1)S(1)} %get-tuple-element.35), channel_id=1, source_target_pairs={{0,96},{32,0},{64,32},{96,64},{1,97},{33,1},{65,33},{97,65},{2,98}... | collective-permute-start | bytes 294920 | tf_op jit(solution)/shard_map/ppermute | solution.py:169
  55.8 5.6 %collective-permute-start.5 = (bf16[128,384]{1,0:T(8,128)(2,1)S(1)}, bf16[128,384]{1,0:T(8,128)(2,1)S(1)}, u32[]{:S(2)}, u32[]{:S(2)}) collective-permute-start(bf16[128,384]{1,0:T(8,128)(2,1)S(1)} %get-tuple-element.35), channel_id=1, source_target_pairs={{0,32},{32,64},{64,96},{96,0},{1,33},{33,65},{65,97},{97,1},{2,34}... | collective-permute-start | bytes 294920 | tf_op jit(solution)/shard_map/ppermute | solution.py:169
  56.8 6.8 %collective-permute-start.4 = (bf16[128,384]{1,0:T(8,128)(2,1)S(1)}, bf16[128,384]{1,0:T(8,128)(2,1)S(1)}, u32[]{:S(2)}, u32[]{:S(2)}) collective-permute-start(bf16[128,384]{1,0:T(8,128)(2,1)S(1)} %get-tuple-element.36), channel_id=1, source_target_pairs={{0,16},{8,24},{16,0},{24,8},{1,17},{9,25},{17,1},{25,9},{2,18},{10... | collective-permute-start | bytes 294920 | tf_op jit(solution)/shard_map/ppermute | solution.py:169
  60.0 7.9 %collective-permute-start.3 = (bf16[128,384]{1,0:T(8,128)(2,1)S(1)}, bf16[128,384]{1,0:T(8,128)(2,1)S(1)}, u32[]{:S(2)}, u32[]{:S(2)}) collective-permute-start(bf16[128,384]{1,0:T(8,128)(2,1)S(1)} %get-tuple-element.36), channel_id=1, source_target_pairs={{0,24},{8,0},{16,8},{24,16},{1,25},{9,1},{17,9},{25,17},{2,26},{10... | collective-permute-start | bytes 294920 | tf_op jit(solution)/shard_map/ppermute | solution.py:169
  60.6 7.6 %collective-permute-start.2 = (bf16[128,384]{1,0:T(8,128)(2,1)S(1)}, bf16[128,384]{1,0:T(8,128)(2,1)S(1)}, u32[]{:S(2)}, u32[]{:S(2)}) collective-permute-start(bf16[128,384]{1,0:T(8,128)(2,1)S(1)} %get-tuple-element.36), channel_id=1, source_target_pairs={{0,8},{8,16},{16,24},{24,0},{1,9},{9,17},{17,25},{25,1},{2,10},{10... | collective-permute-start | bytes 294920 | tf_op jit(solution)/shard_map/ppermute | solution.py:169
  68.2 16.3 %collective-permute-start.9 = (bf16[512,384]{1,0:T(8,128)(2,1)S(1)}, bf16[512,384]{1,0:T(8,128)(2,1)S(1)}, u32[]{:S(2)}, u32[]{:S(2)}) collective-permute-start(bf16[512,384]{1,0:T(8,128)(2,1)S(1)} %pad_maximum_fusion.refs_2_.refs_3_), channel_id=1, source_target_pairs={{0,96},{32,0},{64,32},{96,64},{1,97},{33,1},{65,33},{97,65},{2,98}... | collective-permute-start | bytes 1179656 | tf_op jit(solution)/shard_map/ppermute | solution.py:176
  71.4 15.5 %collective-permute-start.8 = (bf16[512,384]{1,0:T(8,128)(2,1)S(1)}, bf16[512,384]{1,0:T(8,128)(2,1)S(1)}, u32[]{:S(2)}, u32[]{:S(2)}) collective-permute-start(bf16[512,384]{1,0:T(8,128)(2,1)S(1)} %pad_maximum_fusion.refs_2_.refs_3_), channel_id=1, source_target_pairs={{0,32},{32,64},{64,96},{96,0},{1,33},{33,65},{65,97},{97,1},{2,34}... | collective-permute-start | bytes 1179656 | tf_op jit(solution)/shard_map/ppermute | solution.py:176
  71.4 15.6 %collective-permute-start.13 = (bf16[512,384]{1,0:T(8,128)(2,1)S(1)}, bf16[512,384]{1,0:T(8,128)(2,1)S(1)}, u32[]{:S(2)}, u32[]{:S(2)}) collective-permute-start(bf16[512,384]{1,0:T(8,128)(2,1)S(1)} %pad_maximum_fusion.1.refs_7_.refs_8_), channel_id=1, source_target_pairs={{0,24},{8,0},{16,8},{24,16},{1,25},{9,1},{17,9},{25,17},{2,26},{10... | collective-permute-start | bytes 1179656 | tf_op jit(solution)/shard_map/ppermute | solution.py:176
  71.9 17.0 %collective-permute-start.12 = (bf16[512,384]{1,0:T(8,128)(2,1)S(1)}, bf16[512,384]{1,0:T(8,128)(2,1)S(1)}, u32[]{:S(2)}, u32[]{:S(2)}) collective-permute-start(bf16[512,384]{1,0:T(8,128)(2,1)S(1)} %pad_maximum_fusion.1.refs_7_.refs_8_), channel_id=1, source_target_pairs={{0,8},{8,16},{16,24},{24,0},{1,9},{9,17},{17,25},{25,1},{2,10},{10... | collective-permute-start | bytes 1179656 | tf_op jit(solution)/shard_map/ppermute | solution.py:176
  84.5 5.1 %collective-permute-start.11 = (bf16[256,384]{1,0:T(8,128)(2,1)S(1)}, bf16[256,384]{1,0:T(8,128)(2,1)S(1)}, u32[]{:S(2)}, u32[]{:S(2)}) collective-permute-start(bf16[256,384]{1,0:T(8,128)(2,1)S(1)} %slice.25), channel_id=1, source_target_pairs={{0,96},{32,0},{64,32},{96,64},{1,97},{33,1},{65,33},{97,65},{2,98}... | collective-permute-start | bytes 589832 | tf_op jit(solution)/shard_map/ppermute | solution.py:179
  86.9 5.8 %collective-permute-start.10 = (bf16[256,384]{1,0:T(8,128)(2,1)S(1)}, bf16[256,384]{1,0:T(8,128)(2,1)S(1)}, u32[]{:S(2)}, u32[]{:S(2)}) collective-permute-start(bf16[256,384]{1,0:T(8,128)(2,1)S(1)} %slice.24), channel_id=1, source_target_pairs={{0,32},{32,64},{64,96},{96,0},{1,33},{33,65},{65,97},{97,1},{2,34}... | collective-permute-start | bytes 589832 | tf_op jit(solution)/shard_map/ppermute | solution.py:179
  87.0 5.7 %collective-permute-start.15 = (bf16[256,384]{1,0:T(8,128)(2,1)S(1)}, bf16[256,384]{1,0:T(8,128)(2,1)S(1)}, u32[]{:S(2)}, u32[]{:S(2)}) collective-permute-start(bf16[256,384]{1,0:T(8,128)(2,1)S(1)} %slice.27), channel_id=1, source_target_pairs={{0,24},{8,0},{16,8},{24,16},{1,25},{9,1},{17,9},{25,17},{2,26},{10... | collective-permute-start | bytes 589832 | tf_op jit(solution)/shard_map/ppermute | solution.py:179
  89.6 6.2 %collective-permute-start.14 = (bf16[256,384]{1,0:T(8,128)(2,1)}, bf16[256,384]{1,0:T(8,128)(2,1)S(1)}, u32[]{:S(2)}, u32[]{:S(2)}) collective-permute-start(bf16[256,384]{1,0:T(8,128)(2,1)} %slice.26), channel_id=1, source_target_pairs={{0,8},{8,16},{16,24},{24,0},{1,9},{9,17},{17,25},{25,1},{2,10},{10... | collective-permute-start | bytes 589832 | tf_op jit(solution)/shard_map/ppermute | solution.py:179
  89.6 15.8 %collective-permute-start.16 = (bf16[256,4096]{1,0:T(8,128)(2,1)}, bf16[256,4096]{1,0:T(8,128)(2,1)}, u32[]{:S(2)}, u32[]{:S(2)}) collective-permute-start(bf16[256,4096]{1,0:T(8,128)(2,1)} %bitcast.3.refs_0_), channel_id=1, source_target_pairs={{0,1},{1,0},{2,3},{3,2},{4,5},{5,4},{6,7},{7,6},{8,9},{9,8},{10,11... | collective-permute-start | bytes 6291464 | tf_op jit(solution)/shard_map/ppermute | solution.py:371
  95.8 1.9 %copy-start = (bf16[2048,768]{1,0:T(8,128)(2,1)S(1)}, bf16[2048,768]{1,0:T(8,128)(2,1)}, u32[]{:S(2)}) copy-start(bf16[2048,768]{1,0:T(8,128)(2,1)} %all-gather.2.cloned.1.call-done.refs_1_.refs_2_) | copy-start | bytes 9437188
  97.7 7.7 %copy-start.1 = (bf16[2048,768]{1,0:T(8,128)(2,1)S(1)}, bf16[2048,768]{1,0:T(8,128)(2,1)}, u32[]{:S(2)}) copy-start(bf16[2048,768]{1,0:T(8,128)(2,1)} %all-gather.2.cloned.1.call-done.refs_1_.refs_2_) | copy-start | bytes 9437188
  102.0 10.7 %collective-permute-start.17 = (bf16[256,4096]{1,0:T(8,128)(2,1)}, bf16[256,4096]{1,0:T(8,128)(2,1)S(1)}, u32[]{:S(2)}, u32[]{:S(2)}) collective-permute-start(bf16[256,4096]{1,0:T(8,128)(2,1)} %collective-permute-done.1.refs_1_), channel_id=1, source_target_pairs={{0,1},{1,0},{2,3},{3,2},{4,5},{5,4},{6,7},{7,6},{8,9},{9,8},{10,11... | collective-permute-start | bytes 6291464 | tf_op jit(solution)/shard_map/ppermute | solution.py:374
  112.7 3.0 %copy-start.2 = (f32[1024,128]{1,0:T(8,128)S(1)}, f32[1024,128]{1,0:T(8,128)}, u32[]{:S(2)}) copy-start(f32[1024,128]{1,0:T(8,128)} %get-tuple-element.33.refs_4_) | copy-start | bytes 1572868
  112.7 3.0 %copy-start.3 = (f32[1024,128]{1,0:T(8,128)S(1)}, f32[1024,128]{1,0:T(8,128)}, u32[]{:S(2)}) copy-start(f32[1024,128]{1,0:T(8,128)} %get-tuple-element.34.refs_5_) | copy-start | bytes 1572868
  112.7 3.0 %copy-start.4 = (s32[1,8]{1,0:T(1,128)S(1)}, s32[1,8]{1,0:T(1,128)}, u32[]{:S(2)}) copy-start(s32[1,8]{1,0:T(1,128)} %lengths_ref.3) | copy-start | bytes 100
  115.7 11.9 %copy-start.5 = (s32[1,128]{1,0:T(1,128)S(1)}, s32[1,128]{1,0:T(1,128)}, u32[]{:S(2)}) copy-start(s32[1,128]{1,0:T(1,128)} %placement_ref.1) | copy-start | bytes 1540
  122.2 24.7 %all-to-all-start.1 = ((bf16[128,8,512]{2,1,0:T(8,128)(2,1)}), bf16[128,8,512]{2,1,0:T(8,128)(2,1)S(1)}, u32[]{:S(2)}, u32[]{:S(2)}) async-start(bf16[128,8,512]{2,1,0:T(8,128)(2,1)} %bitcast.36), calls=%async_computation.1 | async-start | bytes 2097152 | tf_op jit(solution)/shard_map/all_to_all | solution.py:377
Sparse Core Ops, SparseCore 0:
  11.1 71.8 all-gather.1

commit v11 on v10

--- a/solution.py
+++ b/solution.py
@@ -93,11 +93,6 @@
     same = row == lax.broadcasted_iota(jnp.int32, (count, count), 1) % piece
     one_hot = jnp.where(same, both, 0.0).astype(jnp.bfloat16)
 
-    for copy in taking:
-        copy.wait()
-    for i, out in enumerate((mine_ref, theirs_ref)):
-        leaving.append(pltpu.make_async_copy(columns.at[i], out, head_sems.at[i]))
-        leaving[-1].start()
     for block in range(4):
         columns_here = parts[2 * block][1]
         for copy in arriving[2 * block : 2 * block + 2]:
@@ -108,6 +103,11 @@
         for i in (2 * block, 2 * block + 1):
             leaving.append(pltpu.make_async_copy(moved.at[parts[i]], out_ref.at[parts[i]], out_sems.at[i]))
             leaving[-1].start()
+    for copy in taking:
+        copy.wait()
+    for i, out in enumerate((mine_ref, theirs_ref)):
+        leaving.append(pltpu.make_async_copy(columns.at[i], out, head_sems.at[i]))
+        leaving[-1].start()
     for copy in leaving:
         copy.wait()
 
@@ -141,25 +141,26 @@
 
 def unsort_kernel(target_ref, rows_ref, out_ref):
     count = out_ref.shape[0]
+    blocks, width = rows_ref.shape[1], rows_ref.shape[3]
     order = lax.broadcasted_iota(jnp.int32, (count, count), 1)
     one_hot = jnp.where(order == target_ref[...], 1.0, 0.0).astype(jnp.bfloat16)
-    rows = rows_ref[...].reshape(count, out_ref.shape[1])
-    out_ref[...] = jnp.dot(one_hot, rows, preferred_element_type=jnp.float32).astype(jnp.bfloat16)
+    for i in range(blocks):
+        rows = rows_ref[:, i].reshape(count, width)
+        out_ref[:, i * width : (i + 1) * width] = jnp.dot(
+            one_hot, rows, preferred_element_type=jnp.float32
+        ).astype(jnp.bfloat16)
 
 
 def unsort_rows(returned, target):
     groups, blocks, rows, width = returned.shape
     count = groups * rows
+    whole = pl.BlockSpec(memory_space=pltpu.VMEM)
     return pl.pallas_call(
         unsort_kernel,
         out_shape=jax.ShapeDtypeStruct((count, blocks * width), returned.dtype),
-        grid=(blocks,),
-        in_specs=[
-            pl.BlockSpec((count, 1), lambda i: (0, 0)),
-            pl.BlockSpec((groups, None, rows, width), lambda i: (0, i, 0, 0)),
-        ],
-        out_specs=pl.BlockSpec((count, width), lambda i: (0, i)),
-        compiler_params=pltpu.CompilerParams(vmem_limit_bytes=32 * 2**20),
+        in_specs=[whole, whole],
+        out_specs=pl.BlockSpec((count, blocks * width), lambda: (0, 0)),
+        compiler_params=pltpu.CompilerParams(vmem_limit_bytes=16 * 2**20),
         name="unsort_rows",
     )(target.reshape(count, 1), returned)
 

time: 156 us -> 155 us (level)
  no operation moved by 1% of the time
where the time goes in v11:
time: 155 us
  waiting for transfers between devices  65.3 us (42%)
  starting transfers between devices  42.3 us (27%)
  Pallas kernels  30.4 us (20%)
  between operations  13.6 us (9%)
  local copies, waits for them, and re-layouts  2.91 us (2%)
    all_to_all x1, waiting for transfers between devices, on_device(): lax.all_to_all(mixed.reshape(devices, members * piece, GROUP * HEAD_DIM),...  19.1 us
    ppermute x1, waiting for transfers between devices, on_device(): lax.ppermute(theirs, ('zh', 'zl'), [(0, 3), (3, 0), (1, 2), (2, 1)])  18.8 us
    pallas_call x3, Pallas kernels, project(): pl.pallas_call(functools.partial(project_kernel, len(rows)), out_shape=[j...  14.5 us
    ppermute x2, waiting for transfers between devices, spread(): lax.ppermute(b, axis, DOWN)  11.8 us
    all_to_all x1, starting transfers between devices, on_device(): lax.all_to_all(outgoing, DP, 0, 0, tiled=True).reshape(row_count, width)  11.5 us
    ppermute x6, starting transfers between devices, ring_blocks(): lax.ppermute(block, axis, way)  6.89 us
    ppermute x6, waiting for transfers between devices, ring_blocks(): lax.ppermute(block, axis, way)  6.69 us
    pallas_call x1, Pallas kernels, attend(): pl.pallas_call(attention_kernel, out_shape=jax.ShapeDtypeStruct((count, G...  6.45 us
  transfers between devices with their start and end apart: 21, of which 9 were waited for; matrix products, arithmetic and copies ran while one was open for 1% of the time, Pallas kernels for 10%

profile of v11, /device:TPU:1, one launch (start us, length us, event | category | flops | bytes accessed | tf_op | source)
XLA Modules:
  0.0 154.8 jit_solution(497955908165518842)
XLA Ops:
  6.5 0.0 all-gather.2.cloned.1.call-start
  6.5 4.1 %sort_rows.1 = (bf16[256,4096]{1,0:T(8,128)(2,1)}, bf16[128,768]{1,0:T(8,128)(2,1)}, bf16[128,768]{1,0:T(8,128)(2,1)}) custom-call(s32[1]{0:T(128)} %bitcast.1.member_ref, s32[1,128]{1,0:T(1,128)} %placement_ref.1, bf16[256,4096]{1,0:T(8,128)(2,1)} %rows_ref.1, bf16[128,3072]{1,0:T(8,128)(2,1)} %projection_ref.1), custom_call_target="tpu_custom_call" | custom-call | tf_op jit(solution)/shard_map/sort_rows/pallas_call | solution.py:118
  10.6 0.0 all-gather.2.cloned.1.call-update
  10.6 0.0 copy-start.6
  10.6 11.5 %all-to-all-start = ((bf16[32,8,4096]{2,1,0:T(8,128)(2,1)}), bf16[32,8,4096]{2,1,0:T(8,128)(2,1)}, u32[]{:S(2)}, u32[]{:S(2)}) async-start(bf16[32,8,4096]{2,1,0:T(8,128)(2,1)} %bitcast.40), calls=%async_computation | async-start | bytes 4194304 | tf_op jit(solution)/shard_map/all_to_all | solution.py:366
  22.1 0.0 copy-done.6
  22.1 2.9 %collective-permute-start = (bf16[128,768]{1,0:T(8,128)(2,1)S(1)}, bf16[128,768]{1,0:T(8,128)(2,1)S(1)}, u32[]{:S(2)}, u32[]{:S(2)}) collective-permute-start(bf16[128,768]{1,0:T(8,128)(2,1)S(1)} %copy-done.6), channel_id=1, source_target_pairs={{0,6},{6,0},{2,4},{4,2},{1,7},{7,1},{3,5},{5,3},{8,14},{14,8},{10,... | collective-permute-start | bytes 589832 | tf_op jit(solution)/shard_map/ppermute | solution.py:364
  25.0 4.0 %rotary_tables.1 = (f32[1024,128]{1,0:T(8,128)}, f32[1024,128]{1,0:T(8,128)}) custom-call(s32[1,8]{1,0:T(1,128)} %lengths_ref.3, f32[1,128]{1,0:T(1,128)} %constant.207.clone.frequency_ref), custom_call_target="tpu_custom_call" | custom-call | tf_op jit(solution)/shard_map/rotary_tables/pallas_call | solution.py:48
  29.0 18.8 %collective-permute-done = bf16[128,768]{1,0:T(8,128)(2,1)S(1)} collective-permute-done((bf16[128,768]{1,0:T(8,128)(2,1)S(1)}, bf16[128,768]{1,0:T(8,128)(2,1)S(1)}, u32[]{:S(2)}, u32[]{:S(2)}) %collective-permute-start) | collective-permute-done | bytes 196640 | tf_op jit(solution)/shard_map/ppermute | solution.py:364
  47.8 5.6 %all-to-all-done = bf16[32,8,4096]{2,1,0:T(8,128)(2,1)} async-done(((bf16[32,8,4096]{2,1,0:T(8,128)(2,1)}), bf16[32,8,4096]{2,1,0:T(8,128)(2,1)}, u32[]{:S(2)}, u32[]{:S(2)}) %all-to-all-start) | async-done | bytes 2097184 | tf_op jit(solution)/shard_map/all_to_all | solution.py:366
  53.5 0.6 collective-permute-start.1
  54.2 0.8 collective-permute-start.7
  54.9 0.5 collective-permute-start.6
  55.5 0.9 collective-permute-start.5
  56.4 3.2 %collective-permute-start.4 = (bf16[128,384]{1,0:T(8,128)(2,1)S(1)}, bf16[128,384]{1,0:T(8,128)(2,1)S(1)}, u32[]{:S(2)}, u32[]{:S(2)}) collective-permute-start(bf16[128,384]{1,0:T(8,128)(2,1)S(1)} %get-tuple-element.36), channel_id=1, source_target_pairs={{0,16},{8,24},{16,0},{24,8},{1,17},{9,25},{17,1},{25,9},{2,18},{10... | collective-permute-start | bytes 294920 | tf_op jit(solution)/shard_map/ppermute | solution.py:170
  59.6 0.0 collective-permute-done.7
  59.6 0.6 collective-permute-start.3
  60.2 0.0 collective-permute-done.6
  60.2 0.9 collective-permute-start.2
  61.1 0.0 collective-permute-done.5
  61.1 2.1 %collective-permute-done.4 = bf16[128,384]{1,0:T(8,128)(2,1)S(1)} collective-permute-done((bf16[128,384]{1,0:T(8,128)(2,1)S(1)}, bf16[128,384]{1,0:T(8,128)(2,1)S(1)}, u32[]{:S(2)}, u32[]{:S(2)}) %collective-permute-start.4) | collective-permute-done | bytes 98336 | tf_op jit(solution)/shard_map/ppermute | solution.py:170
  63.2 4.3 %collective-permute-done.3 = bf16[128,384]{1,0:T(8,128)(2,1)S(1)} collective-permute-done((bf16[128,384]{1,0:T(8,128)(2,1)S(1)}, bf16[128,384]{1,0:T(8,128)(2,1)S(1)}, u32[]{:S(2)}, u32[]{:S(2)}) %collective-permute-start.3) | collective-permute-done | bytes 98336 | tf_op jit(solution)/shard_map/ppermute | solution.py:170
  67.5 0.3 collective-permute-done.2
  67.8 3.1 %collective-permute-start.9 = (bf16[512,384]{1,0:T(8,128)(2,1)S(1)}, bf16[512,384]{1,0:T(8,128)(2,1)S(1)}, u32[]{:S(2)}, u32[]{:S(2)}) collective-permute-start(bf16[512,384]{1,0:T(8,128)(2,1)S(1)} %pad_maximum_fusion.refs_2_.refs_3_), channel_id=1, source_target_pairs={{0,96},{32,0},{64,32},{96,64},{1,97},{33,1},{65,33},{97,65},{2,98}... | collective-permute-start | bytes 1179656 | tf_op jit(solution)/shard_map/ppermute | solution.py:177
  71.0 0.0 collective-permute-start.8
  71.0 0.5 collective-permute-start.13
  71.5 0.9 collective-permute-start.12
  72.4 11.8 %collective-permute-done.9.refs_4_.refs_5_ = bf16[512,384]{1,0:T(8,128)(2,1)S(1)} collective-permute-done((bf16[512,384]{1,0:T(8,128)(2,1)S(1)}, bf16[512,384]{1,0:T(8,128)(2,1)S(1)}, u32[]{:S(2)}, u32[]{:S(2)}) %collective-permute-start.9) | collective-permute-done | bytes 393248 | tf_op jit(solution)/shard_map/ppermute | solution.py:177
  84.2 2.2 %collective-permute-start.11 = (bf16[256,384]{1,0:T(8,128)(2,1)S(1)}, bf16[256,384]{1,0:T(8,128)(2,1)S(1)}, u32[]{:S(2)}, u32[]{:S(2)}) collective-permute-start(bf16[256,384]{1,0:T(8,128)(2,1)S(1)} %slice.25), channel_id=1, source_target_pairs={{0,96},{32,0},{64,32},{96,64},{1,97},{33,1},{65,33},{97,65},{2,98}... | collective-permute-start | bytes 589832 | tf_op jit(solution)/shard_map/ppermute | solution.py:180
  86.4 0.0 collective-permute-done.8.refs_3_.refs_4_
  86.4 0.1 collective-permute-start.10
  86.5 0.0 collective-permute-done.13.refs_9_.refs_10_
  86.5 2.0 %collective-permute-start.15 = (bf16[256,384]{1,0:T(8,128)(2,1)S(1)}, bf16[256,384]{1,0:T(8,128)(2,1)S(1)}, u32[]{:S(2)}, u32[]{:S(2)}) collective-permute-start(bf16[256,384]{1,0:T(8,128)(2,1)S(1)} %slice.27), channel_id=1, source_target_pairs={{0,24},{8,0},{16,8},{24,16},{1,25},{9,1},{17,9},{25,17},{2,26},{10... | collective-permute-start | bytes 589832 | tf_op jit(solution)/shard_map/ppermute | solution.py:180
  88.6 0.0 collective-permute-done.12.refs_8_.refs_9_
  88.6 0.7 slice.26
  89.3 0.0 collective-permute-start.14
  89.3 0.0 collective-permute-done.11.refs_6_.refs_7_
  89.3 2.7 %collective-permute-start.16 = (bf16[256,4096]{1,0:T(8,128)(2,1)}, bf16[256,4096]{1,0:T(8,128)(2,1)}, u32[]{:S(2)}, u32[]{:S(2)}) collective-permute-start(bf16[256,4096]{1,0:T(8,128)(2,1)} %bitcast.3.refs_0_), channel_id=1, source_target_pairs={{0,1},{1,0},{2,3},{3,2},{4,5},{5,4},{6,7},{7,6},{8,9},{9,8},{10,11... | collective-permute-start | bytes 6291464 | tf_op jit(solution)/shard_map/ppermute | solution.py:372
  92.0 0.1 stack.147.places_ref
  92.1 0.1 collective-permute-done.10.refs_5_.refs_6_
  92.2 0.0 collective-permute-done.15.refs_11_.refs_12_
  92.2 3.2 %collective-permute-done.14.refs_10_.refs_11_ = bf16[256,384]{1,0:T(8,128)(2,1)S(1)} collective-permute-done((bf16[256,384]{1,0:T(8,128)(2,1)}, bf16[256,384]{1,0:T(8,128)(2,1)S(1)}, u32[]{:S(2)}, u32[]{:S(2)}) %collective-permute-start.14) | collective-permute-done | bytes 196640 | tf_op jit(solution)/shard_map/ppermute | solution.py:180
  95.4 1.9 %copy-done = bf16[2048,768]{1,0:T(8,128)(2,1)S(1)} copy-done((bf16[2048,768]{1,0:T(8,128)(2,1)S(1)}, bf16[2048,768]{1,0:T(8,128)(2,1)}, u32[]{:S(2)}) %copy-start) | copy-done | bytes 3145752
  97.3 4.3 %project.3.refs_0_ = bf16[256,768]{1,0:T(8,128)(2,1)S(1)} custom-call(s32[48]{0:T(128)S(1)} %stack.147.places_ref, bf16[256,4096]{1,0:T(8,128)(2,1)} %bitcast.3.refs_0_, bf16[2048,768]{1,0:T(8,128)(2,1)S(1)} %copy-done, bf16[512,384]{1,0:T(8,128)(2,1)S(1)} %pad_maximum_fusion.refs_2_.refs_3_, bf16[512,384]{1,0:T(8,128)(2,1)S(1)} %collective-permute-done.8.refs_3_.refs_4_, ...), custom_call_target="tpu_custom_call" | custom-call | flops 1610612736 | bytes 8388608 | tf_op jit(solution)/shard_map/project/pallas_call | solution.py:242
  101.6 0.0 collective-permute-done.1.refs_1_
  101.6 3.5 %collective-permute-start.17 = (bf16[256,4096]{1,0:T(8,128)(2,1)}, bf16[256,4096]{1,0:T(8,128)(2,1)S(1)}, u32[]{:S(2)}, u32[]{:S(2)}) collective-permute-start(bf16[256,4096]{1,0:T(8,128)(2,1)} %collective-permute-done.1.refs_1_), channel_id=1, source_target_pairs={{0,1},{1,0},{2,3},{3,2},{4,5},{5,4},{6,7},{7,6},{8,9},{9,8},{10,11... | collective-permute-start | bytes 6291464 | tf_op jit(solution)/shard_map/ppermute | solution.py:375
  105.0 0.0 collective-permute-done.16.refs_0_
  105.1 0.0 copy-done.1
  105.1 7.2 %project.4 = (bf16[256,768]{1,0:T(8,128)(2,1)S(1)}, bf16[256,768]{1,0:T(8,128)(2,1)S(1)}) custom-call(s32[48]{0:T(128)S(1)} %stack.147.places_ref, bf16[256,4096]{1,0:T(8,128)(2,1)} %collective-permute-done.16.refs_0_, bf16[256,4096]{1,0:T(8,128)(2,1)} %collective-permute-done.1.refs_1_, bf16[2048,768]{1,0:T(8,128)(2,1)S(1)} %copy-done.1, ...), custom_call_target="tpu_custom_call" | custom-call | flops 3221225472 | bytes 10485760 | tf_op jit(solution)/shard_map/project/pallas_call | solution.py:242
  112.3 0.0 copy-start.2
  112.3 0.0 copy-start.3
  112.3 0.0 copy-start.4
  112.3 0.0 collective-permute-done.17.refs_0_
  112.3 3.0 %project.5.refs_3_ = bf16[256,768]{1,0:T(8,128)(2,1)S(1)} custom-call(s32[48]{0:T(128)S(1)} %stack.147.places_ref, bf16[256,4096]{1,0:T(8,128)(2,1)S(1)} %collective-permute-done.17.refs_0_, bf16[2048,768]{1,0:T(8,128)(2,1)S(1)} %copy-done.1, bf16[512,384]{1,0:T(8,128)(2,1)S(1)} %pad_maximum_fusion.refs_2_.refs_3_, ...), custom_call_target="tpu_custom_call" | custom-call | flops 1610612736 | bytes 8388608 | tf_op jit(solution)/shard_map/project/pallas_call | solution.py:242
  115.3 0.0 copy-done.2
  115.3 0.0 copy-done.3
  115.4 0.0 copy-done.4
  115.4 0.0 copy-start.5
  115.4 6.5 %attend.1 = bf16[1024,512]{1,0:T(8,128)(2,1)} custom-call(s32[1]{0:T(128)} %bitcast.1.member_ref, s32[1,8]{1,0:T(1,128)S(1)} %copy-done.4, bf16[256,768]{1,0:T(8,128)(2,1)S(1)} %project.3.refs_0_, bf16[256,768]{1,0:T(8,128)(2,1)S(1)} %get-tuple-element.31.refs_1_, bf16[256,768]{1,0:T(8,128)(2,1)S(1)} %get-tuple-element.32.refs_2_, ...), custom_call_target="tpu_custom_call" | custom-call | tf_op jit(solution)/shard_map/attend/pallas_call | solution.py:337
  121.8 5.4 %all-to-all-start.1 = ((bf16[128,8,512]{2,1,0:T(8,128)(2,1)}), bf16[128,8,512]{2,1,0:T(8,128)(2,1)S(1)}, u32[]{:S(2)}, u32[]{:S(2)}) async-start(bf16[128,8,512]{2,1,0:T(8,128)(2,1)} %bitcast.36), calls=%async_computation.1 | async-start | bytes 2097152 | tf_op jit(solution)/shard_map/all_to_all | solution.py:378
  127.2 0.1 iota_add_fusion
  127.3 0.1 add.358.target_ref
  127.4 19.1 %all-to-all-done.1 = bf16[128,8,512]{2,1,0:T(8,128)(2,1)S(1)} async-done(((bf16[128,8,512]{2,1,0:T(8,128)(2,1)}), bf16[128,8,512]{2,1,0:T(8,128)(2,1)S(1)}, u32[]{:S(2)}, u32[]{:S(2)}) %all-to-all-start.1) | async-done | bytes 1048608 | tf_op jit(solution)/shard_map/all_to_all | solution.py:378
  146.5 1.4 unsort_rows.1
  (11 shorter events, 0.2 us)
Async XLA Ops:
  6.5 88.9 %all-gather.2.cloned.1.call-start = ((), (), s32[]{:S(2)}) async-start(), calls=%async_computation.2 | async-start | bytes 3342336 | tf_op jit(solution)/shard_map/all_gather | solution.py:363
  10.6 11.5 %copy-start.6 = (bf16[128,768]{1,0:T(8,128)(2,1)S(1)}, bf16[128,768]{1,0:T(8,128)(2,1)}, u32[]{:S(2)}) copy-start(bf16[128,768]{1,0:T(8,128)(2,1)} %get-tuple-element.21) | copy-start | bytes 589828
  10.6 42.8 %all-to-all-start = ((bf16[32,8,4096]{2,1,0:T(8,128)(2,1)}), bf16[32,8,4096]{2,1,0:T(8,128)(2,1)}, u32[]{:S(2)}, u32[]{:S(2)}) async-start(bf16[32,8,4096]{2,1,0:T(8,128)(2,1)} %bitcast.40), calls=%async_computation | async-start | bytes 4194304 | tf_op jit(solution)/shard_map/all_to_all | solution.py:366
  22.1 25.7 %collective-permute-start = (bf16[128,768]{1,0:T(8,128)(2,1)S(1)}, bf16[128,768]{1,0:T(8,128)(2,1)S(1)}, u32[]{:S(2)}, u32[]{:S(2)}) collective-permute-start(bf16[128,768]{1,0:T(8,128)(2,1)S(1)} %copy-done.6), channel_id=1, source_target_pairs={{0,6},{6,0},{2,4},{4,2},{1,7},{7,1},{3,5},{5,3},{8,14},{14,8},{10,... | collective-permute-start | bytes 589832 | tf_op jit(solution)/shard_map/ppermute | solution.py:364
  53.5 48.1 %collective-permute-start.1 = (bf16[256,4096]{1,0:T(8,128)(2,1)}, bf16[256,4096]{1,0:T(8,128)(2,1)}, u32[]{:S(2)}, u32[]{:S(2)}) collective-permute-start(bf16[256,4096]{1,0:T(8,128)(2,1)} %bitcast.3.refs_0_), channel_id=1, source_target_pairs={{0,2},{2,0},{1,3},{3,1},{4,6},{6,4},{5,7},{7,5},{8,10},{10,8},{9,1... | collective-permute-start | bytes 6291464 | tf_op jit(solution)/shard_map/ppermute | solution.py:371
  54.2 5.4 %collective-permute-start.7 = (bf16[128,384]{1,0:T(8,128)(2,1)S(1)}, bf16[128,384]{1,0:T(8,128)(2,1)S(1)}, u32[]{:S(2)}, u32[]{:S(2)}) collective-permute-start(bf16[128,384]{1,0:T(8,128)(2,1)S(1)} %get-tuple-element.35), channel_id=1, source_target_pairs={{0,64},{32,96},{64,0},{96,32},{1,65},{33,97},{65,1},{97,33},{2,66}... | collective-permute-start | bytes 294920 | tf_op jit(solution)/shard_map/ppermute | solution.py:170
  54.9 5.3 %collective-permute-start.6 = (bf16[128,384]{1,0:T(8,128)(2,1)S(1)}, bf16[128,384]{1,0:T(8,128)(2,1)S(1)}, u32[]{:S(2)}, u32[]{:S(2)}) collective-permute-start(bf16[128,384]{1,0:T(8,128)(2,1)S(1)} %get-tuple-element.35), channel_id=1, source_target_pairs={{0,96},{32,0},{64,32},{96,64},{1,97},{33,1},{65,33},{97,65},{2,98}... | collective-permute-start | bytes 294920 | tf_op jit(solution)/shard_map/ppermute | solution.py:170
  55.5 5.6 %collective-permute-start.5 = (bf16[128,384]{1,0:T(8,128)(2,1)S(1)}, bf16[128,384]{1,0:T(8,128)(2,1)S(1)}, u32[]{:S(2)}, u32[]{:S(2)}) collective-permute-start(bf16[128,384]{1,0:T(8,128)(2,1)S(1)} %get-tuple-element.35), channel_id=1, source_target_pairs={{0,32},{32,64},{64,96},{96,0},{1,33},{33,65},{65,97},{97,1},{2,34}... | collective-permute-start | bytes 294920 | tf_op jit(solution)/shard_map/ppermute | solution.py:170
  56.4 6.8 %collective-permute-start.4 = (bf16[128,384]{1,0:T(8,128)(2,1)S(1)}, bf16[128,384]{1,0:T(8,128)(2,1)S(1)}, u32[]{:S(2)}, u32[]{:S(2)}) collective-permute-start(bf16[128,384]{1,0:T(8,128)(2,1)S(1)} %get-tuple-element.36), channel_id=1, source_target_pairs={{0,16},{8,24},{16,0},{24,8},{1,17},{9,25},{17,1},{25,9},{2,18},{10... | collective-permute-start | bytes 294920 | tf_op jit(solution)/shard_map/ppermute | solution.py:170
  59.6 7.9 %collective-permute-start.3 = (bf16[128,384]{1,0:T(8,128)(2,1)S(1)}, bf16[128,384]{1,0:T(8,128)(2,1)S(1)}, u32[]{:S(2)}, u32[]{:S(2)}) collective-permute-start(bf16[128,384]{1,0:T(8,128)(2,1)S(1)} %get-tuple-element.36), channel_id=1, source_target_pairs={{0,24},{8,0},{16,8},{24,16},{1,25},{9,1},{17,9},{25,17},{2,26},{10... | collective-permute-start | bytes 294920 | tf_op jit(solution)/shard_map/ppermute | solution.py:170
  60.2 7.6 %collective-permute-start.2 = (bf16[128,384]{1,0:T(8,128)(2,1)S(1)}, bf16[128,384]{1,0:T(8,128)(2,1)S(1)}, u32[]{:S(2)}, u32[]{:S(2)}) collective-permute-start(bf16[128,384]{1,0:T(8,128)(2,1)S(1)} %get-tuple-element.36), channel_id=1, source_target_pairs={{0,8},{8,16},{16,24},{24,0},{1,9},{9,17},{17,25},{25,1},{2,10},{10... | collective-permute-start | bytes 294920 | tf_op jit(solution)/shard_map/ppermute | solution.py:170
  67.8 16.4 %collective-permute-start.9 = (bf16[512,384]{1,0:T(8,128)(2,1)S(1)}, bf16[512,384]{1,0:T(8,128)(2,1)S(1)}, u32[]{:S(2)}, u32[]{:S(2)}) collective-permute-start(bf16[512,384]{1,0:T(8,128)(2,1)S(1)} %pad_maximum_fusion.refs_2_.refs_3_), channel_id=1, source_target_pairs={{0,96},{32,0},{64,32},{96,64},{1,97},{33,1},{65,33},{97,65},{2,98}... | collective-permute-start | bytes 1179656 | tf_op jit(solution)/shard_map/ppermute | solution.py:177
  71.0 15.4 %collective-permute-start.8 = (bf16[512,384]{1,0:T(8,128)(2,1)S(1)}, bf16[512,384]{1,0:T(8,128)(2,1)S(1)}, u32[]{:S(2)}, u32[]{:S(2)}) collective-permute-start(bf16[512,384]{1,0:T(8,128)(2,1)S(1)} %pad_maximum_fusion.refs_2_.refs_3_), channel_id=1, source_target_pairs={{0,32},{32,64},{64,96},{96,0},{1,33},{33,65},{65,97},{97,1},{2,34}... | collective-permute-start | bytes 1179656 | tf_op jit(solution)/shard_map/ppermute | solution.py:177
  71.0 15.5 %collective-permute-start.13 = (bf16[512,384]{1,0:T(8,128)(2,1)S(1)}, bf16[512,384]{1,0:T(8,128)(2,1)S(1)}, u32[]{:S(2)}, u32[]{:S(2)}) collective-permute-start(bf16[512,384]{1,0:T(8,128)(2,1)S(1)} %pad_maximum_fusion.1.refs_7_.refs_8_), channel_id=1, source_target_pairs={{0,24},{8,0},{16,8},{24,16},{1,25},{9,1},{17,9},{25,17},{2,26},{10... | collective-permute-start | bytes 1179656 | tf_op jit(solution)/shard_map/ppermute | solution.py:177
  71.5 17.1 %collective-permute-start.12 = (bf16[512,384]{1,0:T(8,128)(2,1)S(1)}, bf16[512,384]{1,0:T(8,128)(2,1)S(1)}, u32[]{:S(2)}, u32[]{:S(2)}) collective-permute-start(bf16[512,384]{1,0:T(8,128)(2,1)S(1)} %pad_maximum_fusion.1.refs_7_.refs_8_), channel_id=1, source_target_pairs={{0,8},{8,16},{16,24},{24,0},{1,9},{9,17},{17,25},{25,1},{2,10},{10... | collective-permute-start | bytes 1179656 | tf_op jit(solution)/shard_map/ppermute | solution.py:177
  84.2 5.0 %collective-permute-start.11 = (bf16[256,384]{1,0:T(8,128)(2,1)S(1)}, bf16[256,384]{1,0:T(8,128)(2,1)S(1)}, u32[]{:S(2)}, u32[]{:S(2)}) collective-permute-start(bf16[256,384]{1,0:T(8,128)(2,1)S(1)} %slice.25), channel_id=1, source_target_pairs={{0,96},{32,0},{64,32},{96,64},{1,97},{33,1},{65,33},{97,65},{2,98}... | collective-permute-start | bytes 589832 | tf_op jit(solution)/shard_map/ppermute | solution.py:180
  86.4 5.8 %collective-permute-start.10 = (bf16[256,384]{1,0:T(8,128)(2,1)S(1)}, bf16[256,384]{1,0:T(8,128)(2,1)S(1)}, u32[]{:S(2)}, u32[]{:S(2)}) collective-permute-start(bf16[256,384]{1,0:T(8,128)(2,1)S(1)} %slice.24), channel_id=1, source_target_pairs={{0,32},{32,64},{64,96},{96,0},{1,33},{33,65},{65,97},{97,1},{2,34}... | collective-permute-start | bytes 589832 | tf_op jit(solution)/shard_map/ppermute | solution.py:180
  86.5 5.7 %collective-permute-start.15 = (bf16[256,384]{1,0:T(8,128)(2,1)S(1)}, bf16[256,384]{1,0:T(8,128)(2,1)S(1)}, u32[]{:S(2)}, u32[]{:S(2)}) collective-permute-start(bf16[256,384]{1,0:T(8,128)(2,1)S(1)} %slice.27), channel_id=1, source_target_pairs={{0,24},{8,0},{16,8},{24,16},{1,25},{9,1},{17,9},{25,17},{2,26},{10... | collective-permute-start | bytes 589832 | tf_op jit(solution)/shard_map/ppermute | solution.py:180
  89.3 6.1 %collective-permute-start.14 = (bf16[256,384]{1,0:T(8,128)(2,1)}, bf16[256,384]{1,0:T(8,128)(2,1)S(1)}, u32[]{:S(2)}, u32[]{:S(2)}) collective-permute-start(bf16[256,384]{1,0:T(8,128)(2,1)} %slice.26), channel_id=1, source_target_pairs={{0,8},{8,16},{16,24},{24,0},{1,9},{9,17},{17,25},{25,1},{2,10},{10... | collective-permute-start | bytes 589832 | tf_op jit(solution)/shard_map/ppermute | solution.py:180
  89.3 15.8 %collective-permute-start.16 = (bf16[256,4096]{1,0:T(8,128)(2,1)}, bf16[256,4096]{1,0:T(8,128)(2,1)}, u32[]{:S(2)}, u32[]{:S(2)}) collective-permute-start(bf16[256,4096]{1,0:T(8,128)(2,1)} %bitcast.3.refs_0_), channel_id=1, source_target_pairs={{0,1},{1,0},{2,3},{3,2},{4,5},{5,4},{6,7},{7,6},{8,9},{9,8},{10,11... | collective-permute-start | bytes 6291464 | tf_op jit(solution)/shard_map/ppermute | solution.py:372
  95.4 1.9 %copy-start = (bf16[2048,768]{1,0:T(8,128)(2,1)S(1)}, bf16[2048,768]{1,0:T(8,128)(2,1)}, u32[]{:S(2)}) copy-start(bf16[2048,768]{1,0:T(8,128)(2,1)} %all-gather.2.cloned.1.call-done.refs_1_.refs_2_) | copy-start | bytes 9437188
  97.3 7.8 %copy-start.1 = (bf16[2048,768]{1,0:T(8,128)(2,1)S(1)}, bf16[2048,768]{1,0:T(8,128)(2,1)}, u32[]{:S(2)}) copy-start(bf16[2048,768]{1,0:T(8,128)(2,1)} %all-gather.2.cloned.1.call-done.refs_1_.refs_2_) | copy-start | bytes 9437188
  101.6 10.8 %collective-permute-start.17 = (bf16[256,4096]{1,0:T(8,128)(2,1)}, bf16[256,4096]{1,0:T(8,128)(2,1)S(1)}, u32[]{:S(2)}, u32[]{:S(2)}) collective-permute-start(bf16[256,4096]{1,0:T(8,128)(2,1)} %collective-permute-done.1.refs_1_), channel_id=1, source_target_pairs={{0,1},{1,0},{2,3},{3,2},{4,5},{5,4},{6,7},{7,6},{8,9},{9,8},{10,11... | collective-permute-start | bytes 6291464 | tf_op jit(solution)/shard_map/ppermute | solution.py:375
  112.3 3.0 %copy-start.2 = (f32[1024,128]{1,0:T(8,128)S(1)}, f32[1024,128]{1,0:T(8,128)}, u32[]{:S(2)}) copy-start(f32[1024,128]{1,0:T(8,128)} %get-tuple-element.33.refs_4_) | copy-start | bytes 1572868
  112.3 3.0 %copy-start.3 = (f32[1024,128]{1,0:T(8,128)S(1)}, f32[1024,128]{1,0:T(8,128)}, u32[]{:S(2)}) copy-start(f32[1024,128]{1,0:T(8,128)} %get-tuple-element.34.refs_5_) | copy-start | bytes 1572868
  112.3 3.0 %copy-start.4 = (s32[1,8]{1,0:T(1,128)S(1)}, s32[1,8]{1,0:T(1,128)}, u32[]{:S(2)}) copy-start(s32[1,8]{1,0:T(1,128)} %lengths_ref.3) | copy-start | bytes 100
  115.4 11.8 %copy-start.5 = (s32[1,128]{1,0:T(1,128)S(1)}, s32[1,128]{1,0:T(1,128)}, u32[]{:S(2)}) copy-start(s32[1,128]{1,0:T(1,128)} %placement_ref.1) | copy-start | bytes 1540
  121.8 24.6 %all-to-all-start.1 = ((bf16[128,8,512]{2,1,0:T(8,128)(2,1)}), bf16[128,8,512]{2,1,0:T(8,128)(2,1)S(1)}, u32[]{:S(2)}, u32[]{:S(2)}) async-start(bf16[128,8,512]{2,1,0:T(8,128)(2,1)} %bitcast.36), calls=%async_computation.1 | async-start | bytes 2097152 | tf_op jit(solution)/shard_map/all_to_all | solution.py:378
Sparse Core Ops, SparseCore 0:
  10.7 71.9 all-gather.1

commit v12 on v11

--- a/solution.py
+++ b/solution.py
@@ -60,14 +60,6 @@
     count, devices = held.shape[0], placement_ref.shape[1]
     piece = count // devices
     arriving, leaving = [], []
-    parts = [
-        (pl.ds(half * (count // 2), count // 2), pl.ds(block * (held.shape[1] // 4), held.shape[1] // 4))
-        for block in range(4)
-        for half in range(2)
-    ]
-    for i, part in enumerate(parts):
-        arriving.append(pltpu.make_async_copy(rows_ref.at[part], held.at[part], in_sems.at[i]))
-        arriving[-1].start()
     taking = []
     for i, member in enumerate((member_ref[0], member_ref[0] ^ 2)):
         at, source = 0, 0
@@ -81,6 +73,14 @@
             taking.append(copy)
             at, source = at + width, source + heads * width
 
+    parts = [
+        (pl.ds(half * (count // 2), count // 2), pl.ds(block * (held.shape[1] // 4), held.shape[1] // 4))
+        for block in range(4)
+        for half in range(2)
+    ]
+    for i, part in enumerate(parts):
+        arriving.append(pltpu.make_async_copy(rows_ref.at[part], held.at[part], in_sems.at[i]))
+        arriving[-1].start()
     device = lax.broadcasted_iota(jnp.int32, (devices, devices), 0)
     pieces = jnp.where(device == placement_ref[...], 1.0, 0.0).astype(jnp.bfloat16)
     down = lax.broadcasted_iota(jnp.int32, (count, devices), 0) // piece

time: 155 us -> 155 us (level)
  no operation moved by 1% of the time
where the time goes in v12:
time: 155 us
  waiting for transfers between devices  65.3 us (42%)
  starting transfers between devices  42.3 us (27%)
  Pallas kernels  30.4 us (20%)
  between operations  13.6 us (9%)
  local copies, waits for them, and re-layouts  2.91 us (2%)
    all_to_all x1, waiting for transfers between devices, on_device(): lax.all_to_all(mixed.reshape(devices, members * piece, GROUP * HEAD_DIM),...  19.1 us
    ppermute x1, waiting for transfers between devices, on_device(): lax.ppermute(theirs, ('zh', 'zl'), [(0, 3), (3, 0), (1, 2), (2, 1)])  18.8 us
    pallas_call x3, Pallas kernels, project(): pl.pallas_call(functools.partial(project_kernel, len(rows)), out_shape=[j...  14.5 us
    ppermute x2, waiting for transfers between devices, spread(): lax.ppermute(b, axis, DOWN)  11.8 us
    all_to_all x1, starting transfers between devices, on_device(): lax.all_to_all(outgoing, DP, 0, 0, tiled=True).reshape(row_count, width)  11.5 us
    ppermute x6, starting transfers between devices, ring_blocks(): lax.ppermute(block, axis, way)  6.89 us
    ppermute x6, waiting for transfers between devices, ring_blocks(): lax.ppermute(block, axis, way)  6.69 us
    pallas_call x1, Pallas kernels, attend(): pl.pallas_call(attention_kernel, out_shape=jax.ShapeDtypeStruct((count, G...  6.45 us
  transfers between devices with their start and end apart: 21, of which 9 were waited for; matrix products, arithmetic and copies ran while one was open for 1% of the time, Pallas kernels for 10%

profile of v12, /device:TPU:1, one launch (start us, length us, event | category | flops | bytes accessed | tf_op | source)
XLA Modules:
  0.0 154.8 jit_solution(6928465071285201930)
XLA Ops:
  6.5 0.0 all-gather.2.cloned.1.call-start
  6.5 4.1 %sort_rows.1 = (bf16[256,4096]{1,0:T(8,128)(2,1)}, bf16[128,768]{1,0:T(8,128)(2,1)}, bf16[128,768]{1,0:T(8,128)(2,1)}) custom-call(s32[1]{0:T(128)} %bitcast.1.member_ref, s32[1,128]{1,0:T(1,128)} %placement_ref.1, bf16[256,4096]{1,0:T(8,128)(2,1)} %rows_ref.1, bf16[128,3072]{1,0:T(8,128)(2,1)} %projection_ref.1), custom_call_target="tpu_custom_call" | custom-call | tf_op jit(solution)/shard_map/sort_rows/pallas_call | solution.py:118
  10.6 0.0 all-gather.2.cloned.1.call-update
  10.6 0.0 copy-start.6
  10.6 11.5 %all-to-all-start = ((bf16[32,8,4096]{2,1,0:T(8,128)(2,1)}), bf16[32,8,4096]{2,1,0:T(8,128)(2,1)}, u32[]{:S(2)}, u32[]{:S(2)}) async-start(bf16[32,8,4096]{2,1,0:T(8,128)(2,1)} %bitcast.40), calls=%async_computation | async-start | bytes 4194304 | tf_op jit(solution)/shard_map/all_to_all | solution.py:366
  22.1 0.0 copy-done.6
  22.1 2.9 %collective-permute-start = (bf16[128,768]{1,0:T(8,128)(2,1)S(1)}, bf16[128,768]{1,0:T(8,128)(2,1)S(1)}, u32[]{:S(2)}, u32[]{:S(2)}) collective-permute-start(bf16[128,768]{1,0:T(8,128)(2,1)S(1)} %copy-done.6), channel_id=1, source_target_pairs={{0,6},{6,0},{2,4},{4,2},{1,7},{7,1},{3,5},{5,3},{8,14},{14,8},{10,... | collective-permute-start | bytes 589832 | tf_op jit(solution)/shard_map/ppermute | solution.py:364
  25.0 4.0 %rotary_tables.1 = (f32[1024,128]{1,0:T(8,128)}, f32[1024,128]{1,0:T(8,128)}) custom-call(s32[1,8]{1,0:T(1,128)} %lengths_ref.3, f32[1,128]{1,0:T(1,128)} %constant.207.clone.frequency_ref), custom_call_target="tpu_custom_call" | custom-call | tf_op jit(solution)/shard_map/rotary_tables/pallas_call | solution.py:48
  29.0 18.8 %collective-permute-done = bf16[128,768]{1,0:T(8,128)(2,1)S(1)} collective-permute-done((bf16[128,768]{1,0:T(8,128)(2,1)S(1)}, bf16[128,768]{1,0:T(8,128)(2,1)S(1)}, u32[]{:S(2)}, u32[]{:S(2)}) %collective-permute-start) | collective-permute-done | bytes 196640 | tf_op jit(solution)/shard_map/ppermute | solution.py:364
  47.8 5.6 %all-to-all-done = bf16[32,8,4096]{2,1,0:T(8,128)(2,1)} async-done(((bf16[32,8,4096]{2,1,0:T(8,128)(2,1)}), bf16[32,8,4096]{2,1,0:T(8,128)(2,1)}, u32[]{:S(2)}, u32[]{:S(2)}) %all-to-all-start) | async-done | bytes 2097184 | tf_op jit(solution)/shard_map/all_to_all | solution.py:366
  53.5 0.6 collective-permute-start.1
  54.2 0.8 collective-permute-start.7
  54.9 0.5 collective-permute-start.6
  55.5 0.9 collective-permute-start.5
  56.4 3.2 %collective-permute-start.4 = (bf16[128,384]{1,0:T(8,128)(2,1)S(1)}, bf16[128,384]{1,0:T(8,128)(2,1)S(1)}, u32[]{:S(2)}, u32[]{:S(2)}) collective-permute-start(bf16[128,384]{1,0:T(8,128)(2,1)S(1)} %get-tuple-element.36), channel_id=1, source_target_pairs={{0,16},{8,24},{16,0},{24,8},{1,17},{9,25},{17,1},{25,9},{2,18},{10... | collective-permute-start | bytes 294920 | tf_op jit(solution)/shard_map/ppermute | solution.py:170
  59.6 0.0 collective-permute-done.7
  59.6 0.6 collective-permute-start.3
  60.2 0.0 collective-permute-done.6
  60.2 0.9 collective-permute-start.2
  61.1 0.0 collective-permute-done.5
  61.1 2.1 %collective-permute-done.4 = bf16[128,384]{1,0:T(8,128)(2,1)S(1)} collective-permute-done((bf16[128,384]{1,0:T(8,128)(2,1)S(1)}, bf16[128,384]{1,0:T(8,128)(2,1)S(1)}, u32[]{:S(2)}, u32[]{:S(2)}) %collective-permute-start.4) | collective-permute-done | bytes 98336 | tf_op jit(solution)/shard_map/ppermute | solution.py:170
  63.2 4.3 %collective-permute-done.3 = bf16[128,384]{1,0:T(8,128)(2,1)S(1)} collective-permute-done((bf16[128,384]{1,0:T(8,128)(2,1)S(1)}, bf16[128,384]{1,0:T(8,128)(2,1)S(1)}, u32[]{:S(2)}, u32[]{:S(2)}) %collective-permute-start.3) | collective-permute-done | bytes 98336 | tf_op jit(solution)/shard_map/ppermute | solution.py:170
  67.5 0.3 collective-permute-done.2
  67.8 3.1 %collective-permute-start.9 = (bf16[512,384]{1,0:T(8,128)(2,1)S(1)}, bf16[512,384]{1,0:T(8,128)(2,1)S(1)}, u32[]{:S(2)}, u32[]{:S(2)}) collective-permute-start(bf16[512,384]{1,0:T(8,128)(2,1)S(1)} %pad_maximum_fusion.refs_2_.refs_3_), channel_id=1, source_target_pairs={{0,96},{32,0},{64,32},{96,64},{1,97},{33,1},{65,33},{97,65},{2,98}... | collective-permute-start | bytes 1179656 | tf_op jit(solution)/shard_map/ppermute | solution.py:177
  71.0 0.0 collective-permute-start.8
  71.0 0.5 collective-permute-start.13
  71.5 0.9 collective-permute-start.12
  72.4 11.8 %collective-permute-done.9.refs_4_.refs_5_ = bf16[512,384]{1,0:T(8,128)(2,1)S(1)} collective-permute-done((bf16[512,384]{1,0:T(8,128)(2,1)S(1)}, bf16[512,384]{1,0:T(8,128)(2,1)S(1)}, u32[]{:S(2)}, u32[]{:S(2)}) %collective-permute-start.9) | collective-permute-done | bytes 393248 | tf_op jit(solution)/shard_map/ppermute | solution.py:177
  84.2 2.2 %collective-permute-start.11 = (bf16[256,384]{1,0:T(8,128)(2,1)S(1)}, bf16[256,384]{1,0:T(8,128)(2,1)S(1)}, u32[]{:S(2)}, u32[]{:S(2)}) collective-permute-start(bf16[256,384]{1,0:T(8,128)(2,1)S(1)} %slice.25), channel_id=1, source_target_pairs={{0,96},{32,0},{64,32},{96,64},{1,97},{33,1},{65,33},{97,65},{2,98}... | collective-permute-start | bytes 589832 | tf_op jit(solution)/shard_map/ppermute | solution.py:180
  86.4 0.0 collective-permute-done.8.refs_3_.refs_4_
  86.4 0.1 collective-permute-start.10
  86.5 0.0 collective-permute-done.13.refs_9_.refs_10_
  86.5 2.0 %collective-permute-start.15 = (bf16[256,384]{1,0:T(8,128)(2,1)S(1)}, bf16[256,384]{1,0:T(8,128)(2,1)S(1)}, u32[]{:S(2)}, u32[]{:S(2)}) collective-permute-start(bf16[256,384]{1,0:T(8,128)(2,1)S(1)} %slice.27), channel_id=1, source_target_pairs={{0,24},{8,0},{16,8},{24,16},{1,25},{9,1},{17,9},{25,17},{2,26},{10... | collective-permute-start | bytes 589832 | tf_op jit(solution)/shard_map/ppermute | solution.py:180
  88.6 0.0 collective-permute-done.12.refs_8_.refs_9_
  88.6 0.7 slice.26
  89.3 0.0 collective-permute-start.14
  89.3 0.0 collective-permute-done.11.refs_6_.refs_7_
  89.3 2.7 %collective-permute-start.16 = (bf16[256,4096]{1,0:T(8,128)(2,1)}, bf16[256,4096]{1,0:T(8,128)(2,1)}, u32[]{:S(2)}, u32[]{:S(2)}) collective-permute-start(bf16[256,4096]{1,0:T(8,128)(2,1)} %bitcast.3.refs_0_), channel_id=1, source_target_pairs={{0,1},{1,0},{2,3},{3,2},{4,5},{5,4},{6,7},{7,6},{8,9},{9,8},{10,11... | collective-permute-start | bytes 6291464 | tf_op jit(solution)/shard_map/ppermute | solution.py:372
  92.0 0.1 stack.147.places_ref
  92.1 0.1 collective-permute-done.10.refs_5_.refs_6_
  92.2 0.0 collective-permute-done.15.refs_11_.refs_12_
  92.2 3.2 %collective-permute-done.14.refs_10_.refs_11_ = bf16[256,384]{1,0:T(8,128)(2,1)S(1)} collective-permute-done((bf16[256,384]{1,0:T(8,128)(2,1)}, bf16[256,384]{1,0:T(8,128)(2,1)S(1)}, u32[]{:S(2)}, u32[]{:S(2)}) %collective-permute-start.14) | collective-permute-done | bytes 196640 | tf_op jit(solution)/shard_map/ppermute | solution.py:180
  95.4 1.9 %copy-done = bf16[2048,768]{1,0:T(8,128)(2,1)S(1)} copy-done((bf16[2048,768]{1,0:T(8,128)(2,1)S(1)}, bf16[2048,768]{1,0:T(8,128)(2,1)}, u32[]{:S(2)}) %copy-start) | copy-done | bytes 3145752
  97.3 4.3 %project.3.refs_0_ = bf16[256,768]{1,0:T(8,128)(2,1)S(1)} custom-call(s32[48]{0:T(128)S(1)} %stack.147.places_ref, bf16[256,4096]{1,0:T(8,128)(2,1)} %bitcast.3.refs_0_, bf16[2048,768]{1,0:T(8,128)(2,1)S(1)} %copy-done, bf16[512,384]{1,0:T(8,128)(2,1)S(1)} %pad_maximum_fusion.refs_2_.refs_3_, bf16[512,384]{1,0:T(8,128)(2,1)S(1)} %collective-permute-done.8.refs_3_.refs_4_, ...), custom_call_target="tpu_custom_call" | custom-call | flops 1610612736 | bytes 8388608 | tf_op jit(solution)/shard_map/project/pallas_call | solution.py:242
  101.6 0.0 collective-permute-done.1.refs_1_
  101.6 3.5 %collective-permute-start.17 = (bf16[256,4096]{1,0:T(8,128)(2,1)}, bf16[256,4096]{1,0:T(8,128)(2,1)S(1)}, u32[]{:S(2)}, u32[]{:S(2)}) collective-permute-start(bf16[256,4096]{1,0:T(8,128)(2,1)} %collective-permute-done.1.refs_1_), channel_id=1, source_target_pairs={{0,1},{1,0},{2,3},{3,2},{4,5},{5,4},{6,7},{7,6},{8,9},{9,8},{10,11... | collective-permute-start | bytes 6291464 | tf_op jit(solution)/shard_map/ppermute | solution.py:375
  105.0 0.0 collective-permute-done.16.refs_0_
  105.1 0.0 copy-done.1
  105.1 7.2 %project.4 = (bf16[256,768]{1,0:T(8,128)(2,1)S(1)}, bf16[256,768]{1,0:T(8,128)(2,1)S(1)}) custom-call(s32[48]{0:T(128)S(1)} %stack.147.places_ref, bf16[256,4096]{1,0:T(8,128)(2,1)} %collective-permute-done.16.refs_0_, bf16[256,4096]{1,0:T(8,128)(2,1)} %collective-permute-done.1.refs_1_, bf16[2048,768]{1,0:T(8,128)(2,1)S(1)} %copy-done.1, ...), custom_call_target="tpu_custom_call" | custom-call | flops 3221225472 | bytes 10485760 | tf_op jit(solution)/shard_map/project/pallas_call | solution.py:242
  112.3 0.0 copy-start.2
  112.3 0.0 copy-start.3
  112.3 0.0 copy-start.4
  112.3 0.0 collective-permute-done.17.refs_0_
  112.3 3.0 %project.5.refs_3_ = bf16[256,768]{1,0:T(8,128)(2,1)S(1)} custom-call(s32[48]{0:T(128)S(1)} %stack.147.places_ref, bf16[256,4096]{1,0:T(8,128)(2,1)S(1)} %collective-permute-done.17.refs_0_, bf16[2048,768]{1,0:T(8,128)(2,1)S(1)} %copy-done.1, bf16[512,384]{1,0:T(8,128)(2,1)S(1)} %pad_maximum_fusion.refs_2_.refs_3_, ...), custom_call_target="tpu_custom_call" | custom-call | flops 1610612736 | bytes 8388608 | tf_op jit(solution)/shard_map/project/pallas_call | solution.py:242
  115.3 0.0 copy-done.2
  115.3 0.0 copy-done.3
  115.4 0.0 copy-done.4
  115.4 0.0 copy-start.5
  115.4 6.5 %attend.1 = bf16[1024,512]{1,0:T(8,128)(2,1)} custom-call(s32[1]{0:T(128)} %bitcast.1.member_ref, s32[1,8]{1,0:T(1,128)S(1)} %copy-done.4, bf16[256,768]{1,0:T(8,128)(2,1)S(1)} %project.3.refs_0_, bf16[256,768]{1,0:T(8,128)(2,1)S(1)} %get-tuple-element.31.refs_1_, bf16[256,768]{1,0:T(8,128)(2,1)S(1)} %get-tuple-element.32.refs_2_, ...), custom_call_target="tpu_custom_call" | custom-call | tf_op jit(solution)/shard_map/attend/pallas_call | solution.py:337
  121.8 5.4 %all-to-all-start.1 = ((bf16[128,8,512]{2,1,0:T(8,128)(2,1)}), bf16[128,8,512]{2,1,0:T(8,128)(2,1)S(1)}, u32[]{:S(2)}, u32[]{:S(2)}) async-start(bf16[128,8,512]{2,1,0:T(8,128)(2,1)} %bitcast.36), calls=%async_computation.1 | async-start | bytes 2097152 | tf_op jit(solution)/shard_map/all_to_all | solution.py:378
  127.2 0.1 iota_add_fusion
  127.3 0.1 add.358.target_ref
  127.4 19.1 %all-to-all-done.1 = bf16[128,8,512]{2,1,0:T(8,128)(2,1)S(1)} async-done(((bf16[128,8,512]{2,1,0:T(8,128)(2,1)}), bf16[128,8,512]{2,1,0:T(8,128)(2,1)S(1)}, u32[]{:S(2)}, u32[]{:S(2)}) %all-to-all-start.1) | async-done | bytes 1048608 | tf_op jit(solution)/shard_map/all_to_all | solution.py:378
  146.5 1.4 unsort_rows.1
  (11 shorter events, 0.2 us)
Async XLA Ops:
  6.5 88.9 %all-gather.2.cloned.1.call-start = ((), (), s32[]{:S(2)}) async-start(), calls=%async_computation.2 | async-start | bytes 3342336 | tf_op jit(solution)/shard_map/all_gather | solution.py:363
  10.6 11.5 %copy-start.6 = (bf16[128,768]{1,0:T(8,128)(2,1)S(1)}, bf16[128,768]{1,0:T(8,128)(2,1)}, u32[]{:S(2)}) copy-start(bf16[128,768]{1,0:T(8,128)(2,1)} %get-tuple-element.21) | copy-start | bytes 589828
  10.6 42.8 %all-to-all-start = ((bf16[32,8,4096]{2,1,0:T(8,128)(2,1)}), bf16[32,8,4096]{2,1,0:T(8,128)(2,1)}, u32[]{:S(2)}, u32[]{:S(2)}) async-start(bf16[32,8,4096]{2,1,0:T(8,128)(2,1)} %bitcast.40), calls=%async_computation | async-start | bytes 4194304 | tf_op jit(solution)/shard_map/all_to_all | solution.py:366
  22.1 25.7 %collective-permute-start = (bf16[128,768]{1,0:T(8,128)(2,1)S(1)}, bf16[128,768]{1,0:T(8,128)(2,1)S(1)}, u32[]{:S(2)}, u32[]{:S(2)}) collective-permute-start(bf16[128,768]{1,0:T(8,128)(2,1)S(1)} %copy-done.6), channel_id=1, source_target_pairs={{0,6},{6,0},{2,4},{4,2},{1,7},{7,1},{3,5},{5,3},{8,14},{14,8},{10,... | collective-permute-start | bytes 589832 | tf_op jit(solution)/shard_map/ppermute | solution.py:364
  53.5 48.1 %collective-permute-start.1 = (bf16[256,4096]{1,0:T(8,128)(2,1)}, bf16[256,4096]{1,0:T(8,128)(2,1)}, u32[]{:S(2)}, u32[]{:S(2)}) collective-permute-start(bf16[256,4096]{1,0:T(8,128)(2,1)} %bitcast.3.refs_0_), channel_id=1, source_target_pairs={{0,2},{2,0},{1,3},{3,1},{4,6},{6,4},{5,7},{7,5},{8,10},{10,8},{9,1... | collective-permute-start | bytes 6291464 | tf_op jit(solution)/shard_map/ppermute | solution.py:371
  54.2 5.4 %collective-permute-start.7 = (bf16[128,384]{1,0:T(8,128)(2,1)S(1)}, bf16[128,384]{1,0:T(8,128)(2,1)S(1)}, u32[]{:S(2)}, u32[]{:S(2)}) collective-permute-start(bf16[128,384]{1,0:T(8,128)(2,1)S(1)} %get-tuple-element.35), channel_id=1, source_target_pairs={{0,64},{32,96},{64,0},{96,32},{1,65},{33,97},{65,1},{97,33},{2,66}... | collective-permute-start | bytes 294920 | tf_op jit(solution)/shard_map/ppermute | solution.py:170
  54.9 5.3 %collective-permute-start.6 = (bf16[128,384]{1,0:T(8,128)(2,1)S(1)}, bf16[128,384]{1,0:T(8,128)(2,1)S(1)}, u32[]{:S(2)}, u32[]{:S(2)}) collective-permute-start(bf16[128,384]{1,0:T(8,128)(2,1)S(1)} %get-tuple-element.35), channel_id=1, source_target_pairs={{0,96},{32,0},{64,32},{96,64},{1,97},{33,1},{65,33},{97,65},{2,98}... | collective-permute-start | bytes 294920 | tf_op jit(solution)/shard_map/ppermute | solution.py:170
  55.5 5.6 %collective-permute-start.5 = (bf16[128,384]{1,0:T(8,128)(2,1)S(1)}, bf16[128,384]{1,0:T(8,128)(2,1)S(1)}, u32[]{:S(2)}, u32[]{:S(2)}) collective-permute-start(bf16[128,384]{1,0:T(8,128)(2,1)S(1)} %get-tuple-element.35), channel_id=1, source_target_pairs={{0,32},{32,64},{64,96},{96,0},{1,33},{33,65},{65,97},{97,1},{2,34}... | collective-permute-start | bytes 294920 | tf_op jit(solution)/shard_map/ppermute | solution.py:170
  56.4 6.8 %collective-permute-start.4 = (bf16[128,384]{1,0:T(8,128)(2,1)S(1)}, bf16[128,384]{1,0:T(8,128)(2,1)S(1)}, u32[]{:S(2)}, u32[]{:S(2)}) collective-permute-start(bf16[128,384]{1,0:T(8,128)(2,1)S(1)} %get-tuple-element.36), channel_id=1, source_target_pairs={{0,16},{8,24},{16,0},{24,8},{1,17},{9,25},{17,1},{25,9},{2,18},{10... | collective-permute-start | bytes 294920 | tf_op jit(solution)/shard_map/ppermute | solution.py:170
  59.6 7.9 %collective-permute-start.3 = (bf16[128,384]{1,0:T(8,128)(2,1)S(1)}, bf16[128,384]{1,0:T(8,128)(2,1)S(1)}, u32[]{:S(2)}, u32[]{:S(2)}) collective-permute-start(bf16[128,384]{1,0:T(8,128)(2,1)S(1)} %get-tuple-element.36), channel_id=1, source_target_pairs={{0,24},{8,0},{16,8},{24,16},{1,25},{9,1},{17,9},{25,17},{2,26},{10... | collective-permute-start | bytes 294920 | tf_op jit(solution)/shard_map/ppermute | solution.py:170
  60.2 7.6 %collective-permute-start.2 = (bf16[128,384]{1,0:T(8,128)(2,1)S(1)}, bf16[128,384]{1,0:T(8,128)(2,1)S(1)}, u32[]{:S(2)}, u32[]{:S(2)}) collective-permute-start(bf16[128,384]{1,0:T(8,128)(2,1)S(1)} %get-tuple-element.36), channel_id=1, source_target_pairs={{0,8},{8,16},{16,24},{24,0},{1,9},{9,17},{17,25},{25,1},{2,10},{10... | collective-permute-start | bytes 294920 | tf_op jit(solution)/shard_map/ppermute | solution.py:170
  67.8 16.4 %collective-permute-start.9 = (bf16[512,384]{1,0:T(8,128)(2,1)S(1)}, bf16[512,384]{1,0:T(8,128)(2,1)S(1)}, u32[]{:S(2)}, u32[]{:S(2)}) collective-permute-start(bf16[512,384]{1,0:T(8,128)(2,1)S(1)} %pad_maximum_fusion.refs_2_.refs_3_), channel_id=1, source_target_pairs={{0,96},{32,0},{64,32},{96,64},{1,97},{33,1},{65,33},{97,65},{2,98}... | collective-permute-start | bytes 1179656 | tf_op jit(solution)/shard_map/ppermute | solution.py:177
  71.0 15.4 %collective-permute-start.8 = (bf16[512,384]{1,0:T(8,128)(2,1)S(1)}, bf16[512,384]{1,0:T(8,128)(2,1)S(1)}, u32[]{:S(2)}, u32[]{:S(2)}) collective-permute-start(bf16[512,384]{1,0:T(8,128)(2,1)S(1)} %pad_maximum_fusion.refs_2_.refs_3_), channel_id=1, source_target_pairs={{0,32},{32,64},{64,96},{96,0},{1,33},{33,65},{65,97},{97,1},{2,34}... | collective-permute-start | bytes 1179656 | tf_op jit(solution)/shard_map/ppermute | solution.py:177
  71.0 15.5 %collective-permute-start.13 = (bf16[512,384]{1,0:T(8,128)(2,1)S(1)}, bf16[512,384]{1,0:T(8,128)(2,1)S(1)}, u32[]{:S(2)}, u32[]{:S(2)}) collective-permute-start(bf16[512,384]{1,0:T(8,128)(2,1)S(1)} %pad_maximum_fusion.1.refs_7_.refs_8_), channel_id=1, source_target_pairs={{0,24},{8,0},{16,8},{24,16},{1,25},{9,1},{17,9},{25,17},{2,26},{10... | collective-permute-start | bytes 1179656 | tf_op jit(solution)/shard_map/ppermute | solution.py:177
  71.5 17.1 %collective-permute-start.12 = (bf16[512,384]{1,0:T(8,128)(2,1)S(1)}, bf16[512,384]{1,0:T(8,128)(2,1)S(1)}, u32[]{:S(2)}, u32[]{:S(2)}) collective-permute-start(bf16[512,384]{1,0:T(8,128)(2,1)S(1)} %pad_maximum_fusion.1.refs_7_.refs_8_), channel_id=1, source_target_pairs={{0,8},{8,16},{16,24},{24,0},{1,9},{9,17},{17,25},{25,1},{2,10},{10... | collective-permute-start | bytes 1179656 | tf_op jit(solution)/shard_map/ppermute | solution.py:177
  84.2 5.0 %collective-permute-start.11 = (bf16[256,384]{1,0:T(8,128)(2,1)S(1)}, bf16[256,384]{1,0:T(8,128)(2,1)S(1)}, u32[]{:S(2)}, u32[]{:S(2)}) collective-permute-start(bf16[256,384]{1,0:T(8,128)(2,1)S(1)} %slice.25), channel_id=1, source_target_pairs={{0,96},{32,0},{64,32},{96,64},{1,97},{33,1},{65,33},{97,65},{2,98}... | collective-permute-start | bytes 589832 | tf_op jit(solution)/shard_map/ppermute | solution.py:180
  86.4 5.8 %collective-permute-start.10 = (bf16[256,384]{1,0:T(8,128)(2,1)S(1)}, bf16[256,384]{1,0:T(8,128)(2,1)S(1)}, u32[]{:S(2)}, u32[]{:S(2)}) collective-permute-start(bf16[256,384]{1,0:T(8,128)(2,1)S(1)} %slice.24), channel_id=1, source_target_pairs={{0,32},{32,64},{64,96},{96,0},{1,33},{33,65},{65,97},{97,1},{2,34}... | collective-permute-start | bytes 589832 | tf_op jit(solution)/shard_map/ppermute | solution.py:180
  86.5 5.7 %collective-permute-start.15 = (bf16[256,384]{1,0:T(8,128)(2,1)S(1)}, bf16[256,384]{1,0:T(8,128)(2,1)S(1)}, u32[]{:S(2)}, u32[]{:S(2)}) collective-permute-start(bf16[256,384]{1,0:T(8,128)(2,1)S(1)} %slice.27), channel_id=1, source_target_pairs={{0,24},{8,0},{16,8},{24,16},{1,25},{9,1},{17,9},{25,17},{2,26},{10... | collective-permute-start | bytes 589832 | tf_op jit(solution)/shard_map/ppermute | solution.py:180
  89.3 6.1 %collective-permute-start.14 = (bf16[256,384]{1,0:T(8,128)(2,1)}, bf16[256,384]{1,0:T(8,128)(2,1)S(1)}, u32[]{:S(2)}, u32[]{:S(2)}) collective-permute-start(bf16[256,384]{1,0:T(8,128)(2,1)} %slice.26), channel_id=1, source_target_pairs={{0,8},{8,16},{16,24},{24,0},{1,9},{9,17},{17,25},{25,1},{2,10},{10... | collective-permute-start | bytes 589832 | tf_op jit(solution)/shard_map/ppermute | solution.py:180
  89.3 15.8 %collective-permute-start.16 = (bf16[256,4096]{1,0:T(8,128)(2,1)}, bf16[256,4096]{1,0:T(8,128)(2,1)}, u32[]{:S(2)}, u32[]{:S(2)}) collective-permute-start(bf16[256,4096]{1,0:T(8,128)(2,1)} %bitcast.3.refs_0_), channel_id=1, source_target_pairs={{0,1},{1,0},{2,3},{3,2},{4,5},{5,4},{6,7},{7,6},{8,9},{9,8},{10,11... | collective-permute-start | bytes 6291464 | tf_op jit(solution)/shard_map/ppermute | solution.py:372
  95.4 1.9 %copy-start = (bf16[2048,768]{1,0:T(8,128)(2,1)S(1)}, bf16[2048,768]{1,0:T(8,128)(2,1)}, u32[]{:S(2)}) copy-start(bf16[2048,768]{1,0:T(8,128)(2,1)} %all-gather.2.cloned.1.call-done.refs_1_.refs_2_) | copy-start | bytes 9437188
  97.3 7.8 %copy-start.1 = (bf16[2048,768]{1,0:T(8,128)(2,1)S(1)}, bf16[2048,768]{1,0:T(8,128)(2,1)}, u32[]{:S(2)}) copy-start(bf16[2048,768]{1,0:T(8,128)(2,1)} %all-gather.2.cloned.1.call-done.refs_1_.refs_2_) | copy-start | bytes 9437188
  101.6 10.8 %collective-permute-start.17 = (bf16[256,4096]{1,0:T(8,128)(2,1)}, bf16[256,4096]{1,0:T(8,128)(2,1)S(1)}, u32[]{:S(2)}, u32[]{:S(2)}) collective-permute-start(bf16[256,4096]{1,0:T(8,128)(2,1)} %collective-permute-done.1.refs_1_), channel_id=1, source_target_pairs={{0,1},{1,0},{2,3},{3,2},{4,5},{5,4},{6,7},{7,6},{8,9},{9,8},{10,11... | collective-permute-start | bytes 6291464 | tf_op jit(solution)/shard_map/ppermute | solution.py:375
  112.3 3.0 %copy-start.2 = (f32[1024,128]{1,0:T(8,128)S(1)}, f32[1024,128]{1,0:T(8,128)}, u32[]{:S(2)}) copy-start(f32[1024,128]{1,0:T(8,128)} %get-tuple-element.33.refs_4_) | copy-start | bytes 1572868
  112.3 3.0 %copy-start.3 = (f32[1024,128]{1,0:T(8,128)S(1)}, f32[1024,128]{1,0:T(8,128)}, u32[]{:S(2)}) copy-start(f32[1024,128]{1,0:T(8,128)} %get-tuple-element.34.refs_5_) | copy-start | bytes 1572868
  112.3 3.0 %copy-start.4 = (s32[1,8]{1,0:T(1,128)S(1)}, s32[1,8]{1,0:T(1,128)}, u32[]{:S(2)}) copy-start(s32[1,8]{1,0:T(1,128)} %lengths_ref.3) | copy-start | bytes 100
  115.4 11.8 %copy-start.5 = (s32[1,128]{1,0:T(1,128)S(1)}, s32[1,128]{1,0:T(1,128)}, u32[]{:S(2)}) copy-start(s32[1,128]{1,0:T(1,128)} %placement_ref.1) | copy-start | bytes 1540
  121.8 24.6 %all-to-all-start.1 = ((bf16[128,8,512]{2,1,0:T(8,128)(2,1)}), bf16[128,8,512]{2,1,0:T(8,128)(2,1)S(1)}, u32[]{:S(2)}, u32[]{:S(2)}) async-start(bf16[128,8,512]{2,1,0:T(8,128)(2,1)} %bitcast.36), calls=%async_computation.1 | async-start | bytes 2097152 | tf_op jit(solution)/shard_map/all_to_all | solution.py:378
Sparse Core Ops, SparseCore 0:
  10.7 71.9 all-gather.1
